TPU v7x, 128 devices: a whole 4x4x4 slice. The times are simulated.
128 devices in a mesh: lat: 8 (over z, x_lo), lon: 16 (over y, x_hi, core).
Axes of the slice: x: 4 (x_hi: 2, x_lo: 2; x = x_hi * 2 + x_lo), y: 4, z: 4, core: 2. Of those that a mesh axis runs over, the one named last changes fastest.
Arguments:
- tokens: bfloat16 [2, 96, 192, 512], P(None, 'lat', 'lon'), may hold values from -6 to 6
- window_ids: int32 [96, 192], P('lat', 'lon'), may hold values from 0 to 3, as said below
- cotangent: bfloat16 [2, 48, 96, 1024], P(None, 'lat', 'lon'), may hold values from -6 to 6
- w_qkv: bfloat16 [512, 1536], replicated, may hold values from -0.25 to 0.25
- w_out: bfloat16 [512, 512], replicated, may hold values from -0.25 to 0.25
- w_up: bfloat16 [512, 2048], replicated, may hold values from -0.25 to 0.25
- w_down: bfloat16 [2048, 512], replicated, may hold values from -0.125 to 0.125
- w_merge: bfloat16 [2048, 1024], replicated, may hold values from -0.125 to 0.125
Outputs:
- level_two: bfloat16 [2, 48, 96, 1024], P(None, 'lat', 'lon')
- grad_tokens: bfloat16 [2, 96, 192, 512], P(None, 'lat', 'lon')
- grad_qkv: float32 [512, 1536], P(('lat', 'lon'))
- grad_out: float32 [512, 512], P(('lat', 'lon'))
- grad_up: float32 [512, 2048], P(('lat', 'lon'))
- grad_down: float32 [2048, 512], P(('lat', 'lon'))
- grad_merge: float32 [2048, 1024], P(('lat', 'lon'))
Inputs may be any that keep to these rules, and one draw needn't show every extreme that they name: window_ids gives the shift regions of the rolled grid: latitude rows below 84 have label 0; in each longitude column, rows 84 to 89 share one label of 1 to 3 and the last 6 rows, which wrapped from the other end, share another label of 1 to 3, different from the first; these two labels are drawn for each column.
All inputs are finite; a program needn't handle non-finite values.
Results may differ from a plain program's by a relative error of at most 0.018.
Values may be sent and summed in bfloat16 or wider, within the bound.
No kernel may reach another device: no remote copies, remote signals or barrier semaphores. Data moves between devices by JAX's collectives and lax.ppermute only.
A program may use at most 128 MiB of HBM per device.

v0:
```python
import jax
import jax.numpy as jnp
from jax import lax
from jax.sharding import PartitionSpec as P

HEAD = 32
WIN = 12


EPS = 1e-05


def shifted(block, axis, distance):
    devices = range(lax.axis_size(axis))
    route = [((i - distance) % len(devices), i) for i in devices]
    return lax.ppermute(block, axis, route)


def normalize(values):
    wide = values.astype(jnp.float32)
    centered = wide - jnp.mean(wide, axis=-1, keepdims=True)
    inverse_std = lax.rsqrt(jnp.mean(centered * centered, axis=-1, keepdims=True) + EPS)
    return (centered * inverse_std, inverse_std)


def norm_back(normed, inverse_std, upstream):
    mean_grad = jnp.mean(upstream, axis=-1, keepdims=True)
    mean_cross = jnp.mean(upstream * normed, axis=-1, keepdims=True)
    return inverse_std * (upstream - mean_grad - normed * mean_cross)


def gelu_slope(values):
    cumulative = 0.5 * (1.0 + jax.scipy.special.erf(values * 0.7071067811865476))
    return cumulative + values * jnp.exp(-0.5 * values * values) * 0.3989422804014327


def matmul(left, right):
    return lax.dot_general(
        left, right, (((left.ndim - 1,), (0,)), ((), ())), preferred_element_type=jnp.float32
    )


def matmul_t(left, right):
    return lax.dot_general(
        left, right, (((left.ndim - 1,), (1,)), ((), ())), preferred_element_type=jnp.float32
    )


def reduce_grad(activations, upstream):
    fan_in = activations.shape[-1]
    flat_left = activations.reshape(-1, fan_in)
    flat_right = upstream.reshape(-1, upstream.shape[-1])
    return lax.psum_scatter(
        lax.dot_general(
            flat_left, flat_right, (((0,), (0,)), ((), ())), preferred_element_type=jnp.float32
        ),
        ("lat", "lon"),
        scatter_dimension=0,
        tiled=True,
    )


def roll_rims(field, direction):
    half_win = WIN // 2
    lat_rows = field.shape[1]
    moving = field[:, :half_win] if direction < 0 else field[:, lat_rows - half_win :]
    arrived = shifted(moving, "lat", direction)
    if direction < 0:
        field = jnp.concatenate([field[:, half_win:], arrived], axis=1)
    else:
        field = jnp.concatenate([arrived, field[:, : lat_rows - half_win]], axis=1)
    lon_cols = field.shape[2]
    moving = field[:, :, :half_win] if direction < 0 else field[:, :, lon_cols - half_win :]
    arrived = shifted(moving, "lon", direction)
    if direction < 0:
        field = jnp.concatenate([field[:, :, half_win:], arrived], axis=2)
    else:
        field = jnp.concatenate([arrived, field[:, :, : lon_cols - half_win]], axis=2)
    return field


def to_windows(packed, window):
    levels, lat_rows, lon_cols, channels = packed.shape
    shaped = packed.reshape(
        levels, lat_rows // window, window, lon_cols // window, window, channels
    )
    return shaped.transpose(1, 3, 0, 2, 4, 5).reshape(-1, levels * window * window, channels)


def from_windows(windowed, levels, lat_rows, lon_cols, window):
    channels = windowed.shape[-1]
    shaped = windowed.reshape(
        lat_rows // window, lon_cols // window, levels, window, window, channels
    )
    return shaped.transpose(2, 0, 3, 1, 4, 5).reshape(levels, lat_rows, lon_cols, channels)


def window_labels(grid, levels, window):
    lat_rows, lon_cols = grid.shape
    tiles = grid.reshape(lat_rows // window, window, lon_cols // window, window).transpose(
        0, 2, 1, 3
    )
    tiles = tiles.reshape(-1, 1, window * window)
    tiles = jnp.broadcast_to(tiles, (tiles.shape[0], levels, window * window))
    return tiles.reshape(-1, levels * window * window)


def split_heads(packed):
    num_windows, win_tokens, channels = packed.shape
    features = channels // 3
    heads = features // HEAD
    query = packed[:, :, :features].reshape(num_windows, win_tokens, heads, HEAD)
    keys = packed[:, :, features : 2 * features].reshape(num_windows, win_tokens, heads, HEAD)
    values = packed[:, :, 2 * features :].reshape(num_windows, win_tokens, heads, HEAD)
    return (query, keys, values)


def attention_weights(query, keys, labels):
    scores = jnp.einsum(
        "nqhd,nkhd->nhqk", query, keys, preferred_element_type=jnp.float32
    ) * HEAD ** (-0.5)
    allowed = labels[:, None, :, None] == labels[:, None, None, :]
    scores = jnp.where(allowed, scores, -1e30)
    return jax.nn.softmax(scores, axis=-1)


def window_forward(packed, labels):
    num_windows, win_tokens, channels = packed.shape
    query, keys, values = split_heads(packed)
    probs = attention_weights(query, keys, labels)
    weights = probs.astype(jnp.bfloat16)
    mixed = jnp.einsum("nhqk,nkhd->nqhd", weights, values, preferred_element_type=jnp.float32)
    return mixed.astype(jnp.bfloat16).reshape(num_windows, win_tokens, channels // 3)


def window_backward(packed, labels, upstream):
    num_windows, win_tokens, channels = packed.shape
    query, keys, values = split_heads(packed)
    probs = attention_weights(query, keys, labels)
    weights = probs.astype(jnp.bfloat16)
    grad_heads = upstream.reshape(query.shape)
    grad_values = jnp.einsum(
        "nhqk,nqhd->nkhd", weights, grad_heads, preferred_element_type=jnp.float32
    )
    grad_weights = jnp.einsum(
        "nqhd,nkhd->nhqk", grad_heads, values, preferred_element_type=jnp.float32
    )
    total = jnp.sum(grad_weights * probs, axis=-1, keepdims=True)
    grad_scores = (probs * (grad_weights - total) * HEAD ** (-0.5)).astype(jnp.bfloat16)
    grad_query = jnp.einsum(
        "nhqk,nkhd->nqhd", grad_scores, keys, preferred_element_type=jnp.float32
    )
    grad_keys = jnp.einsum(
        "nhqk,nqhd->nkhd", grad_scores, query, preferred_element_type=jnp.float32
    )
    shape_out = (num_windows, win_tokens, channels // 3)
    return jnp.concatenate(
        [
            grad_query.astype(jnp.bfloat16).reshape(shape_out),
            grad_keys.astype(jnp.bfloat16).reshape(shape_out),
            grad_values.astype(jnp.bfloat16).reshape(shape_out),
        ],
        axis=-1,
    )


def merge_pairs(field):
    levels, lat_rows, lon_cols, features = field.shape
    shaped = field.reshape(levels, lat_rows // 2, 2, lon_cols // 2, 2, features)
    return shaped.transpose(0, 1, 3, 4, 2, 5).reshape(
        levels, lat_rows // 2, lon_cols // 2, 4 * features
    )


def split_pairs(field):
    levels, half_rows, half_cols, channels = field.shape
    shaped = field.reshape(levels, half_rows, half_cols, 2, 2, channels // 4)
    return shaped.transpose(0, 1, 4, 2, 3, 5).reshape(
        levels, 2 * half_rows, 2 * half_cols, channels // 4
    )


def body(tokens, window_ids, cotangent, w_qkv, w_out, w_up, w_down, w_merge):
    levels, lat_rows, lon_cols, features = tokens.shape
    normed_in, inverse_in = normalize(tokens)
    first_norm = normed_in.astype(jnp.bfloat16)
    rolled = roll_rims(first_norm, -1)
    packed = matmul(rolled, w_qkv).astype(jnp.bfloat16)
    labels = window_labels(window_ids, levels, WIN)
    packed_win = to_windows(packed, WIN)
    attended = from_windows(window_forward(packed_win, labels), levels, lat_rows, lon_cols, WIN)
    attn_out = matmul(attended, w_out).astype(jnp.bfloat16)
    returned = roll_rims(attn_out, 1)
    middle = (tokens.astype(jnp.float32) + returned.astype(jnp.float32)).astype(jnp.bfloat16)
    normed_mid, inverse_mid = normalize(middle)
    second_norm = normed_mid.astype(jnp.bfloat16)
    before_act = matmul(second_norm, w_up)
    hidden = jax.nn.gelu(before_act, approximate=False).astype(jnp.bfloat16)
    after_mlp = (middle.astype(jnp.float32) + matmul(hidden, w_down)).astype(jnp.bfloat16)
    merged = merge_pairs(after_mlp)
    normed_out, inverse_out = normalize(merged)
    merged_norm = normed_out.astype(jnp.bfloat16)
    level_two = matmul(merged_norm, w_merge).astype(jnp.bfloat16)
    grad_merge = reduce_grad(merged_norm, cotangent)
    grad_merged = norm_back(normed_out, inverse_out, matmul_t(cotangent, w_merge)).astype(
        jnp.bfloat16
    )
    grad_after = split_pairs(grad_merged)
    grad_down = reduce_grad(hidden, grad_after)
    grad_before = (matmul_t(grad_after, w_down) * gelu_slope(before_act)).astype(jnp.bfloat16)
    grad_up = reduce_grad(second_norm, grad_before)
    grad_middle = (
        grad_after.astype(jnp.float32)
        + norm_back(normed_mid, inverse_mid, matmul_t(grad_before, w_up))
    ).astype(jnp.bfloat16)
    grad_attn = roll_rims(grad_middle, -1)
    grad_out = reduce_grad(attended, grad_attn)
    grad_attended = matmul_t(grad_attn, w_out).astype(jnp.bfloat16)
    grad_packed_win = window_backward(packed_win, labels, to_windows(grad_attended, WIN))
    grad_packed = from_windows(grad_packed_win, levels, lat_rows, lon_cols, WIN)
    grad_qkv = reduce_grad(rolled, grad_packed)
    grad_rolled = matmul_t(grad_packed, w_qkv).astype(jnp.bfloat16)
    grad_first = roll_rims(grad_rolled, 1)
    grad_tokens = (
        grad_middle.astype(jnp.float32)
        + norm_back(normed_in, inverse_in, grad_first.astype(jnp.float32))
    ).astype(jnp.bfloat16)
    return (level_two, grad_tokens, grad_qkv, grad_out, grad_up, grad_down, grad_merge)


def solution(mesh):
    placed = (
        P(None, "lat", "lon", None),
        P("lat", "lon"),
        P(None, "lat", "lon", None),
        P(),
        P(),
        P(),
        P(),
        P(),
    )
    return jax.shard_map(
        body,
        mesh=mesh,
        in_specs=placed,
        out_specs=(
            P(None, "lat", "lon", None),
            P(None, "lat", "lon", None),
            P(("lat", "lon"), None),
            P(("lat", "lon"), None),
            P(("lat", "lon"), None),
            P(("lat", "lon"), None),
            P(("lat", "lon"), None),
        ),
        check_vma=False,
    )
```

profile of v0, /device:TPU:0, one launch (start us, length us, event | category | flops | bytes accessed | tf_op | source)
XLA Modules:
  0.0 1617.7 jit_solution(12721735906836191881)
XLA Ops:
  10.9 5.1 collective-permute-start
  16.9 3.3 collective-permute-done
  20.3 3.8 collective-permute-start.1
  24.9 2.4 collective-permute-done.1
  27.9 3.2 convolution_convert_fusion
  36.8 6.6 fusion.143
  43.4 3.7 fusion.59
  49.2 2.3 reshape_transpose_reshape_reshape.3
  53.1 8.3 collective-permute-done.2
  62.1 8.7 collective-permute-done.3
  73.1 7.0 fusion.21
  85.5 4.7 fusion.136
  90.8 2.2 multiply_convert_fusion.1
  94.6 4.1 fusion.27
  103.0 3.0 collective-permute-done.4
  106.4 4.8 convolution_bitcast_fusion.1
  113.4 4.1 fusion.62
  117.6 4.1 fusion.144
  121.7 11.0 fusion.65
  132.7 11.4 fusion.68
  146.0 2.4 fusion.145
  148.4 3.6 fusion.79
  152.4 2.3 reshape.246
  156.6 3.3 fusion.146
  161.0 4.6 convolution_bitcast_fusion
  174.1 2.4 fusion.71
  176.7 11.6 collective-permute-done.6
  189.4 3.6 fusion.84
  193.8 4.3 collective-permute-done.7
  200.1 117.8 %all-reduce.6.cloned.1.call-done = (f32[512,1536]{1,0:T(8,128)}, f32[512,512]{1,0:T(8,128)}, f32[512,2048]{1,0:T(8,128)}) async-done(((f32[512,1536]{1,0:T(8,128)}, f32[512,512]{1,0:T(8,128)}, f32[512,2048]{1,0:T(8,128)}), (f32[512,1536]{1,0:T(8,128)}, f32[512,512]{1,0:T(8,128)}, f32[512,2048]{1,0:T(8,128)})) %all-reduce.6.cloned.1.call-update) | async-done | bytes 8388624
  322.0 641.7 %reduce-scatter.3.cloned.1.call-done = f32[16,512]{1,0:T(8,128)} async-done(((f32[2048,512]{1,0:T(8,128)}), f32[16,512]{1,0:T(8,128)}) %reduce-scatter.3.cloned.1.call-update) | async-done | bytes 32784 | tf_op jit(solution)/shard_map/reduce_scatter | solution.py:53
  963.7 647.2 %reduce-scatter.5.cloned.1.call-done = f32[16,1024]{1,0:T(8,128)} async-done(((f32[2048,1024]{1,0:T(8,128)}), f32[16,1024]{1,0:T(8,128)}) %reduce-scatter.5.cloned.1.call-update) | async-done | bytes 65552 | tf_op jit(solution)/shard_map/reduce_scatter | solution.py:53
  (151 shorter events, 54.3 us)
Async XLA Ops:
  7.2 64.2 %copy-start = (bf16[512,2048]{1,0:T(8,128)(2,1)S(1)}, bf16[512,2048]{1,0:T(8,128)(2,1)}, u32[]{:S(2)}) copy-start(bf16[512,2048]{1,0:T(8,128)(2,1)} %param.13) | copy-start | bytes 6291460
  7.2 310.6 %all-reduce.6.cloned.1.call-start = ((), (), s32[]{:S(2)}) async-start(), calls=%async_computation.4 | async-start | bytes 16777216
  10.9 9.3 collective-permute-start
  20.3 7.0 copy-start.17
  20.3 7.0 collective-permute-start.1
  34.6 8.8 copy-start.21
  36.8 6.6 copy-start.15
  47.1 23.6 %copy-start.2 = (bf16[2,12,12,512]{3,0,2,1:T(2,128)(2,1)S(1)}, bf16[2,12,12,512]{3,0,2,1:T(2,128)(2,1)}, u32[]{:S(2)}) copy-start(bf16[2,12,12,512]{3,0,2,1:T(2,128)(2,1)} %param.8) | copy-start | bytes 884740
  53.0 8.4 collective-permute-start.2
  61.5 9.3 collective-permute-start.3
  71.0 9.1 copy-start.6
  73.1 8.1 copy-start.9
  73.1 7.0 copy-start.28
  81.2 4.4 copy-start.23
  94.5 4.1 copy-start.7
  99.9 6.5 copy-start.8
  100.2 10.9 copy-start.4
  100.3 5.7 collective-permute-start.4
  106.1 5.1 copy-start.19
  106.1 5.1 copy-start.20
  106.1 5.0 collective-permute-start.5
  113.4 4.1 copy-start.16
  117.6 4.1 copy-start.22
  132.7 15.8 copy-start.12
  132.7 13.3 copy-start.14
  152.1 811.6 %reduce-scatter.3.cloned.1.call-start = ((), (), s32[]{:S(2)}) async-start(), calls=%async_computation.2 | async-start | bytes 4227072 | tf_op jit(solution)/shard_map/reduce_scatter | solution.py:53
  160.0 1450.9 %reduce-scatter.5.cloned.1.call-start = ((), (), s32[]{:S(2)}) async-start(), calls=%async_computation.3 | async-start | bytes 8454144 | tf_op jit(solution)/shard_map/reduce_scatter | solution.py:53
  176.6 11.7 collective-permute-start.6
  189.0 9.1 copy-start.11
  189.0 9.5 copy-start.5
  189.0 9.0 collective-permute-start.7
  189.4 1421.5 %copy-start.1 = (bf16[512,2048]{1,0:T(8,128)(2,1)S(1)}, bf16[512,2048]{1,0:T(8,128)(2,1)}, u32[]{:S(2)}) copy-start(bf16[512,2048]{1,0:T(8,128)(2,1)} %param.13) | copy-start | bytes 6291460
  (11 other events, 21.4 us)
Sparse Core Ops, SparseCore 0:
  152.2 165.5 all-reduce.5
  320.9 642.8 reduce-scatter.2
  966.7 644.1 reduce-scatter.4
where the time goes:
time: 1630 us; the launch traced here: 1620 us
  waiting for transfers between devices  1450 us (89%)
  matrix products  83.4 us (5%)
  local copies, waits for them, and re-layouts  41.1 us (3%)
  other arithmetic  17.7 us (1%)
    reduce_scatter x2, waiting for transfers between devices, reduce_grad(): lax.psum_scatter(lax.dot_general(flat_left, flat_right, (((0,), (0,)), ((...  1290 us
    unnamed x4, waiting for transfers between devices  118 us
    ppermute x8, waiting for transfers between devices, shifted(): return lax.ppermute(block, axis, route)  41.6 us
  transfers between devices with their start and end apart: 11, of which 10 were waited for; matrix products, arithmetic and copies ran while one was open for 3% of the time, Pallas kernels for 0%

commit v1 on v0

v1 whole, which is shorter than its diff:
```python
import functools

import jax
import jax.numpy as jnp
import numpy as np
from jax import lax
from jax.experimental import pallas as pl
from jax.experimental.pallas import tpu as pltpu
from jax.sharding import PartitionSpec as P

HEAD = 32
WIN = 12
TOKENS = 2 * WIN * WIN
MERGED = TOKENS // 4
EPS = 1e-05
LOG2E = 1.4426950408889634
GRID = ("z", "x_lo", "y", "x_hi", "core")
BF16 = jnp.bfloat16
F32 = jnp.float32

FIRST = {"z": ("z",), "y": ("y",), "x": ("x_lo", "x_hi")}
REST = {
    "z": ("x_lo", "y", "x_hi"),
    "y": ("z", "x_lo", "x_hi"),
    "x": ("z", "y"),
}
SIZES = {"z": 4, "x_lo": 2, "y": 4, "x_hi": 2}


def place_of(chunk, first):
    at = {"core": chunk % 2, "x_hi": chunk // 2 % 2, "y": chunk // 4 % 4}
    at["x_lo"], at["z"] = chunk // 16 % 2, chunk // 32
    lead = rest = 0
    for name in FIRST[first]:
        lead = lead * SIZES[name] + at[name]
    for name in REST[first]:
        rest = rest * SIZES[name] + at[name]
    return at["core"], lead, rest


def row_order(first):
    order = np.zeros((512, 512), np.float32)
    for chunk in range(128):
        core, lead, rest = place_of(chunk, first)
        for row in range(4):
            order[core * 256 + (lead * 16 + rest) * 4 + row, chunk * 4 + row] = 1.0
    return order


def token_order():
    order = np.zeros((4, TOKENS, MERGED), np.float32)
    for quad in range(4):
        for row in range(6):
            for col in range(6):
                for level in range(2):
                    position = (col % 2) * 2 + row % 2
                    patch = quad * 18 + (row // 2 * 3 + col // 2) * 2 + level
                    order[quad, position * MERGED + patch, (row * 6 + col) * 2 + level] = 1.0
    return order


def dot(left, right, left_dim=1, right_dim=0):
    return lax.dot_general(
        left, right, (((left_dim,), (right_dim,)), ((), ())), preferred_element_type=F32
    )


def normalize(wide):
    centered = wide - jnp.mean(wide, axis=-1, keepdims=True)
    inverse_std = lax.rsqrt(jnp.mean(centered * centered, axis=-1, keepdims=True) + EPS)
    return centered * inverse_std, inverse_std


def norm_back(normed, inverse_std, upstream):
    mean_grad = jnp.mean(upstream, axis=-1, keepdims=True)
    mean_cross = jnp.mean(upstream * normed, axis=-1, keepdims=True)
    return inverse_std * (upstream - mean_grad - normed * mean_cross)


def eye(size):
    rows = lax.broadcasted_iota(jnp.int32, (size, size), 0)
    cols = lax.broadcasted_iota(jnp.int32, (size, size), 1)
    return jnp.where(rows == cols, 1.0, 0.0).astype(BF16)


def forward_kernel(
    core_ref, quad0, quad1, quad2, quad3, order_ref, bias_ref, cot_ref, rows_ref, w_qkv, w_qkv_t,
    w_out, w_up, w_down, w_merge,
    level_two_ref, merge_a_keep, merge_a_send, merge_b_keep, merge_b_send, down_keep, down_send,
    up_keep, up_send, tokens_ref, packed_ref, keys_t_ref, probs_ref, attended_ref, middle_grad_ref,
    first_t_ref,
    query_t, values_t, slope_ref, hidden_ref, attended_t,
):
    even = core_ref[0] == 0
    quads = (quad0, quad1, quad2, quad3)
    tokens = sum(dot(order_ref[q], quads[q][...]) for q in range(4))
    tokens_ref[...] = tokens.astype(BF16)
    first_norm = normalize(tokens)[0].astype(BF16)
    first_t_ref[...] = dot(rows_ref[0], first_norm, 1, 1).astype(BF16)
    for part in range(12):
        packed_ref[part] = dot(first_norm, w_qkv[:, part * 128 : part * 128 + 128]).astype(BF16)
    query_t[...] = dot(w_qkv_t[:512], first_norm, 1, 1).astype(BF16)
    keys_t_ref[...] = dot(w_qkv_t[512:1024], first_norm, 1, 1).astype(BF16)
    values_t[...] = dot(w_qkv_t[1024:], first_norm, 1, 1).astype(BF16)

    head_of_row = lax.broadcasted_iota(jnp.int32, (128, TOKENS), 0) // HEAD

    def attend(group, _):
        keys = packed_ref[4 + group]
        queries = query_t[pl.ds(pl.multiple_of(group * 128, 128), 128), :]
        for head in range(4):
            masked = jnp.where(head_of_row == head, queries, jnp.zeros_like(queries))
            scores = dot(keys, masked) * (HEAD ** (-0.5) * LOG2E) + bias_ref[...]
            raised = jnp.exp2(scores - jnp.max(scores, axis=0, keepdims=True))
            inverse = 1.0 / jnp.sum(raised, axis=0, keepdims=True)
            probs = (raised * inverse).astype(BF16)
            probs_ref[group * 4 + head] = probs
            at = pl.ds(pl.multiple_of(group * 128 + head * HEAD, HEAD), HEAD)
            attended_t[at, :] = dot(values_t[at, :], probs).astype(BF16)
        return 0

    lax.fori_loop(0, 4, attend, 0)

    attended_ref[...] = attended_t[...]
    attended = dot(eye(TOKENS), attended_t[...], 1, 1).astype(BF16)
    attn_out = dot(attended, w_out[...]).astype(BF16)
    middle = (tokens + attn_out.astype(F32)).astype(BF16).astype(F32)
    normed_mid, inverse_mid = normalize(middle)
    second_norm = normed_mid.astype(BF16)
    mlp = jnp.zeros((TOKENS, 512), F32)
    for part in range(4):
        cols = slice(part * 512, part * 512 + 512)
        before = dot(second_norm, w_up[:, cols])
        cumulative = 0.5 * (1.0 + lax.erf(before * 0.7071067811865476))
        hidden = (before * cumulative).astype(BF16)
        hidden_ref[:, cols] = hidden
        slope_ref[:, cols] = (
            cumulative + before * jnp.exp(-0.5 * before * before) * 0.3989422804014327
        )
        mlp = mlp + dot(hidden, w_down[cols])
    after_mlp = (middle + mlp).astype(BF16).astype(F32)

    pieces = [after_mlp[p * MERGED : (p + 1) * MERGED] for p in range(4)]
    mean = sum(jnp.sum(v, axis=-1, keepdims=True) for v in pieces) / 2048.0
    pieces = [v - mean for v in pieces]
    inverse_out = lax.rsqrt(
        sum(jnp.sum(v * v, axis=-1, keepdims=True) for v in pieces) / 2048.0 + EPS
    )
    pieces = [v * inverse_out for v in pieces]
    merged_norm = [v.astype(BF16) for v in pieces]
    level_two_ref[...] = sum(
        dot(merged_norm[p], w_merge[p * 512 : p * 512 + 512]) for p in range(4)
    ).astype(BF16)
    cotangent = cot_ref[...]

    def store_blocks(grad, part, first, keep, send):
        narrow = grad.astype(BF16)
        for pair in range(16):
            _, lead, rest = place_of(part * 32 + pair * 2, first)
            low = narrow[pair * 32 : pair * 32 + 16]
            high = narrow[pair * 32 + 16 : pair * 32 + 32]
            keep[lead, rest] = jnp.where(even, low, high)
            send[lead, rest] = jnp.where(even, high, low)

    for part in range(4):
        grad = dot(merged_norm[part], cotangent, 0, 0)
        store_blocks(grad[:, :512], part, "y", merge_a_keep, merge_a_send)
        store_blocks(grad[:, 512:], part, "z", merge_b_keep, merge_b_send)
    upstream = [dot(cotangent, w_merge[p * 512 : p * 512 + 512], 1, 1) for p in range(4)]
    mean_grad = sum(jnp.sum(v, axis=-1, keepdims=True) for v in upstream) / 2048.0
    mean_cross = (
        sum(jnp.sum(v * u, axis=-1, keepdims=True) for v, u in zip(upstream, pieces)) / 2048.0
    )
    grad_after = jnp.concatenate(
        [inverse_out * (v - mean_grad - u * mean_cross) for v, u in zip(upstream, pieces)], axis=0
    ).astype(BF16)

    second_t = dot(rows_ref[1], second_norm, 1, 1).astype(BF16)
    back_up = jnp.zeros((TOKENS, 512), F32)
    for part in range(4):
        cols = slice(part * 512, part * 512 + 512)
        store_blocks(dot(hidden_ref[:, cols], grad_after, 0, 0), part, "x", down_keep, down_send)
        grad_before = (dot(grad_after, w_down[cols], 1, 1) * slope_ref[:, cols]).astype(BF16)
        grad_up = dot(second_t, grad_before).astype(BF16)
        up_keep[:, cols] = jnp.where(even, grad_up[:256], grad_up[256:])
        up_send[:, cols] = jnp.where(even, grad_up[256:], grad_up[:256])
        back_up = back_up + dot(grad_before, w_up[:, cols], 1, 1)
    middle_grad_ref[...] = (
        grad_after.astype(F32) + norm_back(normed_mid, inverse_mid, back_up)
    ).astype(BF16)


def backward_kernel(
    core_ref, tokens_ref, packed_ref, keys_t_ref, probs_ref, attended_ref, middle_grad_ref,
    first_t_ref, rows_ref, order_ref, w_out, w_qkv,
    late_keep, late_send, out0, out1, out2, out3,
    grad_heads, grad_heads_t, products, query_grad_t, packed_grad,
):
    even = core_ref[0] == 0
    middle_grad = middle_grad_ref[...]
    for group in range(4):
        grad_heads[group] = dot(
            middle_grad, w_out[group * 128 : group * 128 + 128], 1, 1
        ).astype(BF16)
    grad_heads_t[...] = dot(w_out[...], middle_grad, 1, 1).astype(BF16)
    products[...] = grad_heads_t[...].astype(F32) * attended_ref[...].astype(F32)

    head_of_row = lax.broadcasted_iota(jnp.int32, (128, TOKENS), 0) // HEAD
    head_of_lane = lax.broadcasted_iota(jnp.int32, (TOKENS, 128), 1) // HEAD

    def attend_back(group, _):
        queries = packed_ref[group]
        values = packed_ref[8 + group]
        upstream = grad_heads[group]
        upstream_t = grad_heads_t[pl.ds(pl.multiple_of(group * 128, 128), 128), :]
        grad_keys = jnp.zeros((TOKENS, 128), F32)
        grad_values = jnp.zeros((TOKENS, 128), F32)
        for head in range(4):
            at = pl.ds(pl.multiple_of(group * 128 + head * HEAD, HEAD), HEAD)
            masked_t = jnp.where(head_of_row == head, upstream_t, jnp.zeros_like(upstream_t))
            weights = probs_ref[group * 4 + head]
            total = jnp.sum(products[at, :], axis=0, keepdims=True)
            grad_weights = dot(values, masked_t)
            scores = (
                weights.astype(F32) * ((grad_weights - total) * HEAD ** (-0.5))
            ).astype(BF16)
            in_head = head_of_lane == head
            grad_keys += dot(scores, jnp.where(in_head, queries, jnp.zeros_like(queries)))
            grad_values += dot(weights, jnp.where(in_head, upstream, jnp.zeros_like(upstream)))
            query_grad_t[at, :] = dot(keys_t_ref[at, :], scores).astype(BF16)
        packed_grad[4 + group] = grad_keys.astype(BF16)
        packed_grad[8 + group] = grad_values.astype(BF16)
        return 0

    lax.fori_loop(0, 4, attend_back, 0)

    identity = eye(TOKENS)
    for group in range(4):
        packed_grad[group] = dot(
            identity, query_grad_t[group * 128 : group * 128 + 128, :], 1, 1
        ).astype(BF16)
    first_t = first_t_ref[...]
    back_qkv = jnp.zeros((TOKENS, 512), F32)
    for part in range(3):
        wide = jnp.concatenate([packed_grad[part * 4 + g] for g in range(4)], axis=1)
        cols = slice(part * 512, part * 512 + 512)
        grad = dot(first_t, wide).astype(BF16)
        late_keep[:, cols] = jnp.where(even, grad[:256], grad[256:])
        late_send[:, cols] = jnp.where(even, grad[256:], grad[:256])
        back_qkv = back_qkv + dot(wide, w_qkv[:, cols], 1, 1)
    attended = dot(rows_ref[0], attended_ref[...]).astype(BF16)
    grad = dot(attended, middle_grad).astype(BF16)
    late_keep[:, 1536:] = jnp.where(even, grad[:256], grad[256:])
    late_send[:, 1536:] = jnp.where(even, grad[256:], grad[:256])

    normed_in, inverse_in = normalize(tokens_ref[...].astype(F32))
    grad_first = back_qkv.astype(BF16).astype(F32)
    grad_tokens = (
        middle_grad.astype(F32) + norm_back(normed_in, inverse_in, grad_first)
    ).astype(BF16)
    for quad, out in enumerate((out0, out1, out2, out3)):
        out[...] = dot(order_ref[quad], grad_tokens).astype(BF16)


LATE, UP = "z", "y"


def call(kernel, inputs, outputs, scratch, flops):
    whole = pl.BlockSpec(memory_space=pltpu.VMEM)
    return pl.pallas_call(
        kernel,
        out_shape=[jax.ShapeDtypeStruct(shape, BF16) for shape in outputs],
        in_specs=[pl.BlockSpec(memory_space=pltpu.SMEM)] + [whole] * (len(inputs) - 1),
        out_specs=[whole] * len(outputs),
        scratch_shapes=scratch,
        compiler_params=pltpu.CompilerParams(vmem_limit_bytes=58 * 2**20),
        cost_estimate=pl.CostEstimate(
            flops=flops, bytes_accessed=25 * 2**20, transcendentals=3 * 2**20
        ),
    )(*inputs)


def window_pass(core, quads, bias, cotangent, w_qkv, w_qkv_t, w_out, w_up, w_down, w_merge):
    order = token_order()
    rows = jnp.asarray(np.stack([row_order(LATE), row_order(UP)]), BF16)
    half, wide = (4, 16, 16, 512), (256, 2048)
    by_feature, field = (512, TOKENS), (TOKENS, 512)
    outs = call(
        forward_kernel,
        [core, *quads, jnp.asarray(order, BF16), bias, cotangent, rows, w_qkv, w_qkv_t,
         w_out, w_up, w_down, w_merge],
        [(MERGED, 1024)] + [half] * 6 + [wide] * 2
        + [field, (12, TOKENS, 128), by_feature, (16, TOKENS, TOKENS), by_feature, field,
           by_feature],
        [pltpu.VMEM(by_feature, BF16), pltpu.VMEM(by_feature, BF16),
         pltpu.VMEM((TOKENS, 2048), F32), pltpu.VMEM((TOKENS, 2048), BF16),
         pltpu.VMEM(by_feature, BF16)],
        24 * 2**30,
    )
    level_two, early, kept = outs[0], outs[1:9], outs[9:]
    late_keep, late_send, *grads = call(
        backward_kernel,
        [core, *kept, rows, jnp.asarray(order.transpose(0, 2, 1), BF16), w_out, w_qkv],
        [wide] * 2 + [(MERGED, 512)] * 4,
        [pltpu.VMEM((4, TOKENS, 128), BF16), pltpu.VMEM(by_feature, BF16),
         pltpu.VMEM(by_feature, F32), pltpu.VMEM(by_feature, BF16),
         pltpu.VMEM((12, TOKENS, 128), BF16)],
        16 * 2**30,
    )
    return level_two, early, late_keep, late_send, grads


def pair_reduce(keep, send):
    arrived = lax.ppermute(send, "core", [(0, 1), (1, 0)])
    return (keep.astype(F32) + arrived.astype(F32)).astype(BF16)


def scatter_grad(keep, send, first, rows):
    blocks = pair_reduce(keep, send)
    cols = blocks.shape[-1]
    blocks = blocks.reshape(4, 16 * rows, cols)
    landed = lax.all_to_all(blocks, FIRST[first], 0, 0, tiled=True)
    blocks = jnp.sum(landed.astype(F32), axis=0).astype(BF16).reshape(16, rows, cols)
    landed = lax.all_to_all(blocks, REST[first], 0, 0, tiled=True)
    return jnp.sum(landed.astype(F32), axis=0)


def shifted_block(block, down, right):
    route = []
    for source in range(128):
        row, col = source // 16, source % 16
        route.append((source, (row + down) % 8 * 16 + (col + right) % 16))
    return lax.ppermute(block, GRID, route)


def quadrants(field):
    field = field.transpose(1, 2, 0, 3)
    rows, cols = field.shape[0] // 2, field.shape[1] // 2
    return field[:rows, :cols], field[:rows, cols:], field[rows:, :cols], field[rows:, cols:]


def roll_back(field):
    upper_left, upper_right, lower_left, lower_right = quadrants(field)
    return [
        lower_right,
        shifted_block(lower_left, 0, -1),
        shifted_block(upper_right, -1, 0),
        shifted_block(upper_left, -1, -1),
    ]


def roll_forth(corners):
    upper_left, upper_right, lower_left, lower_right = corners
    upper = jnp.concatenate(
        [shifted_block(lower_right, 1, 1), shifted_block(lower_left, 1, 0)], axis=1
    )
    lower = jnp.concatenate([shifted_block(upper_right, 0, 1), upper_left], axis=1)
    return jnp.concatenate([upper, lower], axis=0).transpose(2, 0, 1, 3)


def window_bias(window_ids):
    labels = window_ids.reshape(2, 3, 2, 2, 3, 2).transpose(5, 2, 0, 3, 1, 4)
    labels = jnp.broadcast_to(labels[..., None], (2, 2, 2, 2, 3, 3, 2)).reshape(TOKENS)
    return jnp.where(labels[:, None] == labels[None, :], 0.0, -1e30)


def body(tokens, window_ids, cotangent, w_qkv, w_out, w_up, w_down, w_merge):
    quads = [quad.reshape(MERGED, 512) for quad in roll_back(tokens)]
    cot = jnp.concatenate([quad.reshape(18, 1024) for quad in roll_back(cotangent)], axis=0)
    core = lax.axis_index("core").reshape(1)
    level_two, early, late_keep, late_send, grads = window_pass(
        core, quads, window_bias(window_ids), cot, w_qkv, w_qkv.T, w_out, w_up, w_down, w_merge
    )
    merge_a = scatter_grad(early[0], early[1], "y", 16)
    merge_b = scatter_grad(early[2], early[3], "z", 16)
    grad_down = scatter_grad(early[4], early[5], "x", 16)
    grad_up = scatter_grad(early[6], early[7], UP, 4)
    late = scatter_grad(late_keep, late_send, LATE, 4)
    grad_tokens = roll_forth([grad.reshape(6, 6, 2, 512) for grad in grads])
    corners = level_two.reshape(4, 3, 3, 2, 1024)
    level_two = roll_forth([corners[quad] for quad in range(4)])
    grad_merge = jnp.concatenate([merge_a, merge_b], axis=1)
    return (level_two, grad_tokens, late[:, :1536], late[:, 1536:], grad_up, grad_down, grad_merge)


def solution(mesh):
    cube = jax.sharding.Mesh(mesh.devices.reshape(4, 2, 4, 2, 2), GRID)
    lat, lon = GRID[:2], GRID[2:]
    field = P(None, lat, lon, None)
    share = P(GRID, None)
    return jax.shard_map(
        body,
        mesh=cube,
        in_specs=(field, P(lat, lon), field, P(), P(), P(), P(), P()),
        out_specs=(field, field, share, share, share, share, share),
        check_vma=False,
    )
```

time: 1630 us -> 229 us (0.14)
  waiting for transfers between devices: 1450 us -> 81.1 us
  matrix products: 83.4 us -> 0 us
  starting transfers between devices: 12.4 us -> 68 us
  Pallas kernels: 0 us -> 40.6 us
  local copies, waits for them, and re-layouts: 41.1 us -> 12.6 us
    reduce_scatter x2 -> x0, waiting for transfers between devices: 1290 us -> none  [reduce_grad(): lax.psum_scatter(lax.dot_general(flat_left, flat_right, (((0,), (0,)), ((...]
    unnamed x4 -> x0, waiting for transfers between devices: 118 us -> none
    dot_general x20 -> x0, matrix products: 76.8 us -> none  [the longest x5 18.8 us: reduce_grad(): lax.dot_general(flat_left, flat_right, (((0,), (0,)), ((), ())), preferre...]
    all_to_all x0 -> x10, waiting for transfers between devices: none -> 74.4 us  [the longest x5 52.6 us: scatter_grad(): landed = lax.all_to_all(blocks, FIRST[first], 0, 0, tiled=True)]
    pallas_call x0 -> x2, Pallas kernels: none -> 40.6 us  [call(): pl.pallas_call(kernel, out_shape=[jax.ShapeDtypeStruct(shape, BF16) for s...]
    all_to_all x0 -> x10, starting transfers between devices: none -> 40.2 us  [the longest x5 21.9 us: scatter_grad(): landed = lax.all_to_all(blocks, REST[first], 0, 0, tiled=True)]
    ppermute x8 -> x17, waiting for transfers between devices: 41.6 us -> 6.76 us  [the longest x12 4.56 us: shifted_block(): return lax.ppermute(block, GRID, route)]
  transfers between devices with their start and end apart: 11 -> 27, of which waited for: 10 -> 11; matrix products, arithmetic and copies ran while one was open for 3% -> 15% of each run, Pallas kernels for 0% -> 6%
where the time goes in v1:
time: 229 us; the launch traced here: 228 us
  waiting for transfers between devices  81.1 us (35%)
  starting transfers between devices  68 us (30%)
  Pallas kernels  40.6 us (18%)
  other arithmetic  24.2 us (11%)
  local copies, waits for them, and re-layouts  12.6 us (6%)
    all_to_all x5, waiting for transfers between devices, scatter_grad(): landed = lax.all_to_all(blocks, FIRST[first], 0, 0, tiled=True)  52.6 us
    pallas_call x2, Pallas kernels, call(): pl.pallas_call(kernel, out_shape=[jax.ShapeDtypeStruct(shape, BF16) for s...  40.6 us
    ppermute x12, starting transfers between devices, shifted_block(): return lax.ppermute(block, GRID, route)  24.2 us
    all_to_all x5, starting transfers between devices, scatter_grad(): landed = lax.all_to_all(blocks, REST[first], 0, 0, tiled=True)  21.9 us
    all_to_all x5, waiting for transfers between devices, scatter_grad(): landed = lax.all_to_all(blocks, REST[first], 0, 0, tiled=True)  21.8 us
    all_to_all x5, starting transfers between devices, scatter_grad(): landed = lax.all_to_all(blocks, FIRST[first], 0, 0, tiled=True)  18.3 us
    convert_element_type x5, other arithmetic, pair_reduce(): return (keep.astype(F32) + arrived.astype(F32)).astype(BF16)  12.6 us
    reduce_sum x5, other arithmetic, scatter_grad(): jnp.sum(landed.astype(F32), axis=0).astype(BF16).reshape(16, rows, cols)  5.56 us
  transfers between devices with their start and end apart: 27, of which 11 were waited for; matrix products, arithmetic and copies ran while one was open for 15% of the time, Pallas kernels for 6%

profile of v1, /device:TPU:0, one launch (start us, length us, event | category | flops | bytes accessed | tf_op | source)
XLA Modules:
  0.0 227.5 jit_solution(923381589368618664)
XLA Ops:
  1.7 8.3 %collective-permute-start.5 = (bf16[3,3,2,1024]{3,2,1,0:T(2,128)(2,1)S(1)}, bf16[3,3,2,1024]{3,2,1,0:T(2,128)(2,1)S(1)}, u32[]{:S(2)}, u32[]{:S(2)}) collective-permute-start(bf16[3,3,2,1024]{3,2,1,0:T(2,128)(2,1)S(1)} %get-tuple-element.60), channel_id=1, source_target_pairs={{0,127},{1,112},{2,113},{3,114},{4,115},{5,116},{6,117},{7,118},{8... | collective-permute-start | bytes 110600 | tf_op jit(solution)/shard_map/ppermute | solution.py:333
  10.2 2.1 collective-permute-start.3
  23.0 26.9 %shard_map.162 = (bf16[72,1024]{1,0:T(8,128)(2,1)}, bf16[4,16,16,512]{3,2,1,0:T(8,128)(2,1)}, bf16[4,16,16,512]{3,2,1,0:T(8,128)(2,1)}, bf16[4,16,16,512]{3,2,1,...) custom-call(s32[1]{0:T(128)} %bitcast.core_ref, ...), custom_call_target="tpu_custom_call" | custom-call | flops 25769803776 | bytes 26214400 | tf_op jit(solution)/shard_map/pallas_call | solution.py:270
  50.0 2.7 %collective-permute-start.13 = (bf16[256,2048]{1,0:T(8,128)(2,1)}, bf16[256,2048]{1,0:T(8,128)(2,1)S(1)}, u32[]{:S(2)}, u32[]{:S(2)}) collective-permute-start(bf16[256,2048]{1,0:T(8,128)(2,1)} %get-tuple-element.44), channel_id=1, source_target_pairs={{0,1},{1,0},{2,3},{3,2},{4,5},{5,4},{6,7},{7,6},{8,9},{9,8},{10,11... | collective-permute-start | bytes 3145736 | tf_op jit(solution)/shard_map/ppermute | solution.py:314
  53.0 2.2 collective-permute-done.13
  55.2 2.7 %add_convert_fusion.3 = bf16[256,2048]{1,0:T(8,128)(2,1)} fusion(bf16[256,2048]{1,0:T(8,128)(2,1)S(1)} %collective-permute-done.13, bf16[256,2048]{1,0:T(8,128)(2,1)} %get-tuple-element.43), kind=kLoop, calls=%fused_computation.3 | loop fusion | flops 2097152 | bytes 3145728 | tf_op jit(solution)/shard_map/convert_element_type | solution.py:315
  57.9 3.5 %all-to-all-start.2 = ((bf16[4,64,2048]{2,1,0:T(8,128)(2,1)}), bf16[4,64,2048]{2,1,0:T(8,128)(2,1)S(1)}, u32[]{:S(2)}, u32[]{:S(2)}) async-start(bf16[4,64,2048]{2,1,0:T(8,128)(2,1)} %bitcast.8), calls=%async_computation.2 | async-start | bytes 2097152 | tf_op jit(solution)/shard_map/all_to_all | solution.py:322
  63.4 13.9 %all-to-all-done.2 = bf16[4,64,2048]{2,1,0:T(8,128)(2,1)S(1)} async-done(((bf16[4,64,2048]{2,1,0:T(8,128)(2,1)}), bf16[4,64,2048]{2,1,0:T(8,128)(2,1)S(1)}, u32[]{:S(2)}, u32[]{:S(2)}) %all-to-all-start.2) | async-done | bytes 1048608 | tf_op jit(solution)/shard_map/all_to_all | solution.py:322
  77.3 3.5 %all-to-all-start.4 = ((bf16[4,256,512]{2,1,0:T(8,128)(2,1)}), bf16[4,256,512]{2,1,0:T(8,128)(2,1)S(1)}, u32[]{:S(2)}, u32[]{:S(2)}) async-start(bf16[4,256,512]{2,1,0:T(8,128)(2,1)} %bitcast.9), calls=%async_computation.4 | async-start | bytes 2097152 | tf_op jit(solution)/shard_map/all_to_all | solution.py:322
  80.8 13.7 %shard_map.163 = (bf16[256,2048]{1,0:T(8,128)(2,1)}, bf16[256,2048]{1,0:T(8,128)(2,1)}, bf16[72,512]{1,0:T(8,128)(2,1)}, bf16[72,512]{1,0:T(8,128)(2,1)}, bf16[7...) custom-call(s32[1]{0:T(128)} %bitcast.core_ref, bf16[288,512]{1,0:T(8,128)(2,1)} %get-tuple-element.30.tokens_ref, ...), custom_call_target="tpu_custom_call" | custom-call | flops 17179869184 | bytes 26214400 | tf_op jit(solution)/shard_map/pallas_call | solution.py:270
  94.6 2.6 %add_convert_fusion.1 = bf16[4,16,16,512]{3,2,1,0:T(8,128)(2,1)} fusion(bf16[4,16,16,512]{3,2,1,0:T(8,128)(2,1)} %collective-permute-done.15, bf16[4,16,16,512]{3,2,1,0:T(8,128)(2,1)S(1)} %copy-done.2), kind=kLoop, calls=%fused_computation.1 | loop fusion | flops 2097152 | bytes 3145728 | tf_op jit(solution)/shard_map/convert_element_type | solution.py:315
  97.2 3.5 %all-to-all-start.6 = ((bf16[4,256,512]{2,1,0:T(8,128)(2,1)}), bf16[4,256,512]{2,1,0:T(8,128)(2,1)S(1)}, u32[]{:S(2)}, u32[]{:S(2)}) async-start(bf16[4,256,512]{2,1,0:T(8,128)(2,1)} %bitcast.11), calls=%async_computation.6 | async-start | bytes 2097152 | tf_op jit(solution)/shard_map/all_to_all | solution.py:322
  100.7 2.9 %add_convert_fusion = bf16[4,16,16,512]{3,2,1,0:T(8,128)(2,1)} fusion(bf16[4,16,16,512]{3,2,1,0:T(8,128)(2,1)} %collective-permute-done.16, bf16[4,16,16,512]{3,2,1,0:T(8,128)(2,1)} %get-tuple-element.49), kind=kLoop, calls=%fused_computation | loop fusion | flops 2097152 | bytes 3145728 | tf_op jit(solution)/shard_map/convert_element_type | solution.py:315
  103.6 13.0 %all-to-all-done.6 = bf16[4,256,512]{2,1,0:T(8,128)(2,1)S(1)} async-done(((bf16[4,256,512]{2,1,0:T(8,128)(2,1)}), bf16[4,256,512]{2,1,0:T(8,128)(2,1)S(1)}, u32[]{:S(2)}, u32[]{:S(2)}) %all-to-all-start.6) | async-done | bytes 1048608 | tf_op jit(solution)/shard_map/all_to_all | solution.py:322
  117.7 3.5 %all-to-all-start.8 = ((bf16[4,256,512]{2,1,0:T(8,128)(2,1)}), bf16[4,256,512]{2,1,0:T(8,128)(2,1)S(1)}, u32[]{:S(2)}, u32[]{:S(2)}) async-start(bf16[4,256,512]{2,1,0:T(8,128)(2,1)} %bitcast.13), calls=%async_computation.8 | async-start | bytes 2097152 | tf_op jit(solution)/shard_map/all_to_all | solution.py:322
  121.2 2.9 %add_convert_fusion.4 = bf16[256,2048]{1,0:T(8,128)(2,1)} fusion(bf16[256,2048]{1,0:T(8,128)(2,1)} %collective-permute-done.12, bf16[256,2048]{1,0:T(8,128)(2,1)} %get-tuple-element.41), kind=kLoop, calls=%fused_computation.4 | loop fusion | flops 2097152 | bytes 3145728 | tf_op jit(solution)/shard_map/convert_element_type | solution.py:315
  124.1 12.3 %all-to-all-done.8 = bf16[4,256,512]{2,1,0:T(8,128)(2,1)S(1)} async-done(((bf16[4,256,512]{2,1,0:T(8,128)(2,1)}), bf16[4,256,512]{2,1,0:T(8,128)(2,1)S(1)}, u32[]{:S(2)}, u32[]{:S(2)}) %all-to-all-start.8) | async-done | bytes 1048608 | tf_op jit(solution)/shard_map/all_to_all | solution.py:322
  136.4 4.3 %all-to-all-start = ((bf16[4,64,2048]{2,1,0:T(8,128)(2,1)}), bf16[4,64,2048]{2,1,0:T(8,128)(2,1)}, u32[]{:S(2)}, u32[]{:S(2)}) async-start(bf16[4,64,2048]{2,1,0:T(8,128)(2,1)} %bitcast.7), calls=%async_computation | async-start | bytes 2097152 | tf_op jit(solution)/shard_map/all_to_all | solution.py:322
  141.7 13.4 %all-to-all-done = bf16[4,64,2048]{2,1,0:T(8,128)(2,1)} async-done(((bf16[4,64,2048]{2,1,0:T(8,128)(2,1)}), bf16[4,64,2048]{2,1,0:T(8,128)(2,1)}, u32[]{:S(2)}, u32[]{:S(2)}) %all-to-all-start) | async-done | bytes 1048608 | tf_op jit(solution)/shard_map/all_to_all | solution.py:322
  155.1 5.5 %all-to-all-start.3 = ((bf16[16,4,2048]{2,1,0:T(4,128)(2,1)}), bf16[16,4,2048]{2,1,0:T(4,128)(2,1)S(1)}, u32[]{:S(2)}, u32[]{:S(2)}) async-start(bf16[16,4,2048]{2,1,0:T(4,128)(2,1)} %reshape.115), calls=%async_computation.3 | async-start | bytes 524288 | tf_op jit(solution)/shard_map/all_to_all | solution.py:324
  160.5 2.2 reduce_sum.111
  162.7 6.3 %all-to-all-done.3 = bf16[16,4,2048]{2,1,0:T(4,128)(2,1)S(1)} async-done(((bf16[16,4,2048]{2,1,0:T(4,128)(2,1)}), bf16[16,4,2048]{2,1,0:T(4,128)(2,1)S(1)}, u32[]{:S(2)}, u32[]{:S(2)}) %all-to-all-start.3) | async-done | bytes 262176 | tf_op jit(solution)/shard_map/all_to_all | solution.py:324
  169.0 3.5 %all-to-all-start.7 = ((bf16[16,16,512]{2,1,0:T(8,128)(2,1)}), bf16[16,16,512]{2,1,0:T(8,128)(2,1)S(1)}, u32[]{:S(2)}, u32[]{:S(2)}) async-start(bf16[16,16,512]{2,1,0:T(8,128)(2,1)} %bitcast.12), calls=%async_computation.7 | async-start | bytes 524288 | tf_op jit(solution)/shard_map/all_to_all | solution.py:324
  175.3 3.5 %collective-permute-start.6 = (bf16[3,3,2,1024]{3,2,1,0:T(2,128)(2,1)S(1)}, bf16[3,3,2,1024]{3,2,1,0:T(2,128)(2,1)S(1)}, u32[]{:S(2)}, u32[]{:S(2)}) collective-permute-start(bf16[3,3,2,1024]{3,2,1,0:T(2,128)(2,1)S(1)} %squeeze.12), channel_id=1, source_target_pairs={{0,17},{1,18},{2,19},{3,20},{4,21},{5,22},{6,23},{7,24},{8,25},{9,... | collective-permute-start | bytes 110600 | tf_op jit(solution)/shard_map/ppermute | solution.py:333
  181.2 5.0 %all-to-all-start.1 = ((bf16[16,4,2048]{2,1,0:T(4,128)(2,1)}), bf16[16,4,2048]{2,1,0:T(4,128)(2,1)S(1)}, u32[]{:S(2)}, u32[]{:S(2)}) async-start(bf16[16,4,2048]{2,1,0:T(4,128)(2,1)} %reshape.113), calls=%async_computation.1 | async-start | bytes 524288 | tf_op jit(solution)/shard_map/all_to_all | solution.py:324
  186.6 2.0 collective-permute-start.10
  188.6 3.8 %collective-permute-start.9 = (bf16[6,6,2,512]{3,2,1,0:T(2,128)(2,1)S(1)}, bf16[6,6,2,512]{3,2,1,0:T(2,128)(2,1)S(1)}, u32[]{:S(2)}, u32[]{:S(2)}) collective-permute-start(bf16[6,6,2,512]{3,2,1,0:T(2,128)(2,1)S(1)} %reshape.108), channel_id=1, source_target_pairs={{0,17},{1,18},{2,19},{3,20},{4,21},{5,22},{6,23},{7,24},{8,25},{9,... | collective-permute-start | bytes 221192 | tf_op jit(solution)/shard_map/ppermute | solution.py:333
  194.5 3.3 %collective-permute-done.9 = bf16[6,6,2,512]{3,2,1,0:T(2,128)(2,1)S(1)} collective-permute-done((bf16[6,6,2,512]{3,2,1,0:T(2,128)(2,1)S(1)}, bf16[6,6,2,512]{3,2,1,0:T(2,128)(2,1)S(1)}, u32[]{:S(2)}, u32[]{:S(2)}) %collective-permute-start.9) | collective-permute-done | bytes 73760 | tf_op jit(solution)/shard_map/ppermute | solution.py:333
  200.7 4.1 %all-to-all-start.9 = ((bf16[16,16,512]{2,1,0:T(8,128)(2,1)}), bf16[16,16,512]{2,1,0:T(8,128)(2,1)S(1)}, u32[]{:S(2)}, u32[]{:S(2)}) async-start(bf16[16,16,512]{2,1,0:T(8,128)(2,1)} %bitcast.14), calls=%async_computation.9 | async-start | bytes 524288 | tf_op jit(solution)/shard_map/all_to_all | solution.py:324
  205.1 9.3 %all-to-all-done.9 = bf16[16,16,512]{2,1,0:T(8,128)(2,1)S(1)} async-done(((bf16[16,16,512]{2,1,0:T(8,128)(2,1)}), bf16[16,16,512]{2,1,0:T(8,128)(2,1)S(1)}, u32[]{:S(2)}, u32[]{:S(2)}) %all-to-all-start.9) | async-done | bytes 262176 | tf_op jit(solution)/shard_map/all_to_all | solution.py:324
  214.5 3.7 %all-to-all-start.5 = ((bf16[16,16,512]{2,1,0:T(8,128)(2,1)}), bf16[16,16,512]{2,1,0:T(8,128)(2,1)S(1)}, u32[]{:S(2)}, u32[]{:S(2)}) async-start(bf16[16,16,512]{2,1,0:T(8,128)(2,1)} %bitcast.10), calls=%async_computation.5 | async-start | bytes 524288 | tf_op jit(solution)/shard_map/all_to_all | solution.py:324
  220.9 6.0 %all-to-all-done.5 = bf16[16,16,512]{2,1,0:T(8,128)(2,1)S(1)} async-done(((bf16[16,16,512]{2,1,0:T(8,128)(2,1)}), bf16[16,16,512]{2,1,0:T(8,128)(2,1)S(1)}, u32[]{:S(2)}, u32[]{:S(2)}) %all-to-all-start.5) | async-done | bytes 262176 | tf_op jit(solution)/shard_map/all_to_all | solution.py:324
  (90 shorter events, 30.4 us)
Async XLA Ops:
  1.7 16.9 %collective-permute-start.5 = (bf16[3,3,2,1024]{3,2,1,0:T(2,128)(2,1)S(1)}, bf16[3,3,2,1024]{3,2,1,0:T(2,128)(2,1)S(1)}, u32[]{:S(2)}, u32[]{:S(2)}) collective-permute-start(bf16[3,3,2,1024]{3,2,1,0:T(2,128)(2,1)S(1)} %get-tuple-element.60), channel_id=1, source_target_pairs={{0,127},{1,112},{2,113},{3,114},{4,115},{5,116},{6,117},{7,118},{8... | collective-permute-start | bytes 110600 | tf_op jit(solution)/shard_map/ppermute | solution.py:333
  10.0 10.3 %collective-permute-start.4 = (bf16[3,3,2,1024]{3,2,1,0:T(2,128)(2,1)S(1)}, bf16[3,3,2,1024]{3,2,1,0:T(2,128)(2,1)S(1)}, u32[]{:S(2)}, u32[]{:S(2)}) collective-permute-start(bf16[3,3,2,1024]{3,2,1,0:T(2,128)(2,1)S(1)} %get-tuple-element.61), channel_id=1, source_target_pairs={{0,112},{1,113},{2,114},{3,115},{4,116},{5,117},{6,118},{7,119},{8... | collective-permute-start | bytes 110600 | tf_op jit(solution)/shard_map/ppermute | solution.py:333
  10.2 10.1 %collective-permute-start.3 = (bf16[3,3,2,1024]{3,2,1,0:T(2,128)(2,1)S(1)}, bf16[3,3,2,1024]{3,2,1,0:T(2,128)(2,1)S(1)}, u32[]{:S(2)}, u32[]{:S(2)}) collective-permute-start(bf16[3,3,2,1024]{3,2,1,0:T(2,128)(2,1)S(1)} %get-tuple-element.62), channel_id=1, source_target_pairs={{0,15},{1,0},{2,1},{3,2},{4,3},{5,4},{6,5},{7,6},{8,7},{9,8},{10,9... | collective-permute-start | bytes 110600 | tf_op jit(solution)/shard_map/ppermute | solution.py:333
  13.5 7.6 %collective-permute-start.2 = (bf16[6,6,2,512]{3,2,1,0:T(2,128)(2,1)S(1)}, bf16[6,6,2,512]{3,2,1,0:T(2,128)(2,1)S(1)}, u32[]{:S(2)}, u32[]{:S(2)}) collective-permute-start(bf16[6,6,2,512]{3,2,1,0:T(2,128)(2,1)S(1)} %get-tuple-element.51), channel_id=1, source_target_pairs={{0,127},{1,112},{2,113},{3,114},{4,115},{5,116},{6,117},{7,118},{8... | collective-permute-start | bytes 221192 | tf_op jit(solution)/shard_map/ppermute | solution.py:333
  13.5 8.2 %collective-permute-start.1 = (bf16[6,6,2,512]{3,2,1,0:T(2,128)(2,1)S(1)}, bf16[6,6,2,512]{3,2,1,0:T(2,128)(2,1)S(1)}, u32[]{:S(2)}, u32[]{:S(2)}) collective-permute-start(bf16[6,6,2,512]{3,2,1,0:T(2,128)(2,1)S(1)} %get-tuple-element.52), channel_id=1, source_target_pairs={{0,112},{1,113},{2,114},{3,115},{4,116},{5,117},{6,118},{7,119},{8... | collective-permute-start | bytes 221192 | tf_op jit(solution)/shard_map/ppermute | solution.py:333
  18.6 3.8 %collective-permute-start = (bf16[6,6,2,512]{3,2,1,0:T(2,128)(2,1)S(1)}, bf16[6,6,2,512]{3,2,1,0:T(2,128)(2,1)S(1)}, u32[]{:S(2)}, u32[]{:S(2)}) collective-permute-start(bf16[6,6,2,512]{3,2,1,0:T(2,128)(2,1)S(1)} %get-tuple-element.53), channel_id=1, source_target_pairs={{0,15},{1,0},{2,1},{3,2},{4,3},{5,4},{6,5},{7,6},{8,7},{9,8},{10,9... | collective-permute-start | bytes 221192 | tf_op jit(solution)/shard_map/ppermute | solution.py:333
  50.0 5.2 %collective-permute-start.13 = (bf16[256,2048]{1,0:T(8,128)(2,1)}, bf16[256,2048]{1,0:T(8,128)(2,1)S(1)}, u32[]{:S(2)}, u32[]{:S(2)}) collective-permute-start(bf16[256,2048]{1,0:T(8,128)(2,1)} %get-tuple-element.44), channel_id=1, source_target_pairs={{0,1},{1,0},{2,3},{3,2},{4,5},{5,4},{6,7},{7,6},{8,9},{9,8},{10,11... | collective-permute-start | bytes 3145736 | tf_op jit(solution)/shard_map/ppermute | solution.py:314
  52.7 9.3 %collective-permute-start.14 = (bf16[4,16,16,512]{3,2,1,0:T(8,128)(2,1)}, bf16[4,16,16,512]{3,2,1,0:T(8,128)(2,1)S(1)}, u32[]{:S(2)}, u32[]{:S(2)}) collective-permute-start(bf16[4,16,16,512]{3,2,1,0:T(8,128)(2,1)} %get-tuple-element.46), channel_id=1, source_target_pairs={{0,1},{1,0},{2,3},{3,2},{4,5},{5,4},{6,7},{7,6},{8,9},{9,8},{10,11... | collective-permute-start | bytes 3145736 | tf_op jit(solution)/shard_map/ppermute | solution.py:314
  57.9 19.4 %all-to-all-start.2 = ((bf16[4,64,2048]{2,1,0:T(8,128)(2,1)}), bf16[4,64,2048]{2,1,0:T(8,128)(2,1)S(1)}, u32[]{:S(2)}, u32[]{:S(2)}) async-start(bf16[4,64,2048]{2,1,0:T(8,128)(2,1)} %bitcast.8), calls=%async_computation.2 | async-start | bytes 2097152 | tf_op jit(solution)/shard_map/all_to_all | solution.py:322
  61.4 33.1 %collective-permute-start.15 = (bf16[4,16,16,512]{3,2,1,0:T(8,128)(2,1)}, bf16[4,16,16,512]{3,2,1,0:T(8,128)(2,1)}, u32[]{:S(2)}, u32[]{:S(2)}) collective-permute-start(bf16[4,16,16,512]{3,2,1,0:T(8,128)(2,1)} %get-tuple-element.48), channel_id=1, source_target_pairs={{0,1},{1,0},{2,3},{3,2},{4,5},{5,4},{6,7},{7,6},{8,9},{9,8},{10,11... | collective-permute-start | bytes 3145736 | tf_op jit(solution)/shard_map/ppermute | solution.py:314
  61.9 38.8 %collective-permute-start.16 = (bf16[4,16,16,512]{3,2,1,0:T(8,128)(2,1)}, bf16[4,16,16,512]{3,2,1,0:T(8,128)(2,1)}, u32[]{:S(2)}, u32[]{:S(2)}) collective-permute-start(bf16[4,16,16,512]{3,2,1,0:T(8,128)(2,1)} %get-tuple-element.50), channel_id=1, source_target_pairs={{0,1},{1,0},{2,3},{3,2},{4,5},{5,4},{6,7},{7,6},{8,9},{9,8},{10,11... | collective-permute-start | bytes 3145736 | tf_op jit(solution)/shard_map/ppermute | solution.py:314
  77.3 19.9 %all-to-all-start.4 = ((bf16[4,256,512]{2,1,0:T(8,128)(2,1)}), bf16[4,256,512]{2,1,0:T(8,128)(2,1)S(1)}, u32[]{:S(2)}, u32[]{:S(2)}) async-start(bf16[4,256,512]{2,1,0:T(8,128)(2,1)} %bitcast.9), calls=%async_computation.4 | async-start | bytes 2097152 | tf_op jit(solution)/shard_map/all_to_all | solution.py:322
  94.5 26.7 %collective-permute-start.12 = (bf16[256,2048]{1,0:T(8,128)(2,1)}, bf16[256,2048]{1,0:T(8,128)(2,1)}, u32[]{:S(2)}, u32[]{:S(2)}) collective-permute-start(bf16[256,2048]{1,0:T(8,128)(2,1)} %get-tuple-element.42), channel_id=1, source_target_pairs={{0,1},{1,0},{2,3},{3,2},{4,5},{5,4},{6,7},{7,6},{8,9},{9,8},{10,11... | collective-permute-start | bytes 3145736 | tf_op jit(solution)/shard_map/ppermute | solution.py:314
  97.2 19.5 %all-to-all-start.6 = ((bf16[4,256,512]{2,1,0:T(8,128)(2,1)}), bf16[4,256,512]{2,1,0:T(8,128)(2,1)S(1)}, u32[]{:S(2)}, u32[]{:S(2)}) async-start(bf16[4,256,512]{2,1,0:T(8,128)(2,1)} %bitcast.11), calls=%async_computation.6 | async-start | bytes 2097152 | tf_op jit(solution)/shard_map/all_to_all | solution.py:322
  117.7 18.7 %all-to-all-start.8 = ((bf16[4,256,512]{2,1,0:T(8,128)(2,1)}), bf16[4,256,512]{2,1,0:T(8,128)(2,1)S(1)}, u32[]{:S(2)}, u32[]{:S(2)}) async-start(bf16[4,256,512]{2,1,0:T(8,128)(2,1)} %bitcast.13), calls=%async_computation.8 | async-start | bytes 2097152 | tf_op jit(solution)/shard_map/all_to_all | solution.py:322
  136.4 18.7 %all-to-all-start = ((bf16[4,64,2048]{2,1,0:T(8,128)(2,1)}), bf16[4,64,2048]{2,1,0:T(8,128)(2,1)}, u32[]{:S(2)}, u32[]{:S(2)}) async-start(bf16[4,64,2048]{2,1,0:T(8,128)(2,1)} %bitcast.7), calls=%async_computation | async-start | bytes 2097152 | tf_op jit(solution)/shard_map/all_to_all | solution.py:322
  140.7 31.9 %copy-start.4 = (bf16[72,1024]{1,0:T(8,128)(2,1)S(1)}, bf16[72,1024]{1,0:T(8,128)(2,1)}, u32[]{:S(2)}) copy-start(bf16[72,1024]{1,0:T(8,128)(2,1)} %get-tuple-element.29) | copy-start | bytes 442372
  155.1 13.9 %all-to-all-start.3 = ((bf16[16,4,2048]{2,1,0:T(4,128)(2,1)}), bf16[16,4,2048]{2,1,0:T(4,128)(2,1)S(1)}, u32[]{:S(2)}, u32[]{:S(2)}) async-start(bf16[16,4,2048]{2,1,0:T(4,128)(2,1)} %reshape.115), calls=%async_computation.3 | async-start | bytes 524288 | tf_op jit(solution)/shard_map/all_to_all | solution.py:324
  162.7 23.6 %copy-start.8 = (bf16[72,512]{1,0:T(8,128)(2,1)S(1)}, bf16[72,512]{1,0:T(8,128)(2,1)}, u32[]{:S(2)}) copy-start(bf16[72,512]{1,0:T(8,128)(2,1)} %get-tuple-element.37) | copy-start | bytes 221188
  162.7 23.7 %copy-start.7 = (bf16[72,512]{1,0:T(8,128)(2,1)S(1)}, bf16[72,512]{1,0:T(8,128)(2,1)}, u32[]{:S(2)}) copy-start(bf16[72,512]{1,0:T(8,128)(2,1)} %get-tuple-element.38) | copy-start | bytes 221188
  162.7 23.7 %copy-start.6 = (bf16[72,512]{1,0:T(8,128)(2,1)S(1)}, bf16[72,512]{1,0:T(8,128)(2,1)}, u32[]{:S(2)}) copy-start(bf16[72,512]{1,0:T(8,128)(2,1)} %get-tuple-element.39) | copy-start | bytes 221188
  162.7 23.8 %copy-start.5 = (bf16[72,512]{1,0:T(8,128)(2,1)S(1)}, bf16[72,512]{1,0:T(8,128)(2,1)}, u32[]{:S(2)}) copy-start(bf16[72,512]{1,0:T(8,128)(2,1)} %get-tuple-element.40) | copy-start | bytes 221188
  169.0 12.2 %all-to-all-start.7 = ((bf16[16,16,512]{2,1,0:T(8,128)(2,1)}), bf16[16,16,512]{2,1,0:T(8,128)(2,1)S(1)}, u32[]{:S(2)}, u32[]{:S(2)}) async-start(bf16[16,16,512]{2,1,0:T(8,128)(2,1)} %bitcast.12), calls=%async_computation.7 | async-start | bytes 524288 | tf_op jit(solution)/shard_map/all_to_all | solution.py:324
  173.3 15.3 %collective-permute-start.7 = (bf16[3,3,2,1024]{3,2,1,0:T(2,128)(2,1)}, bf16[3,3,2,1024]{3,2,1,0:T(2,128)(2,1)S(1)}, u32[]{:S(2)}, u32[]{:S(2)}) collective-permute-start(bf16[3,3,2,1024]{3,2,1,0:T(2,128)(2,1)} %squeeze.13), channel_id=1, source_target_pairs={{0,16},{1,17},{2,18},{3,19},{4,20},{5,21},{6,22},{7,23},{8,24},{9,... | collective-permute-start | bytes 110600 | tf_op jit(solution)/shard_map/ppermute | solution.py:333
  175.2 17.2 %collective-permute-start.8 = (bf16[3,3,2,1024]{3,2,1,0:T(2,128)(2,1)S(1)}, bf16[3,3,2,1024]{3,2,1,0:T(2,128)(2,1)S(1)}, u32[]{:S(2)}, u32[]{:S(2)}) collective-permute-start(bf16[3,3,2,1024]{3,2,1,0:T(2,128)(2,1)S(1)} %squeeze.14), channel_id=1, source_target_pairs={{0,1},{1,2},{2,3},{3,4},{4,5},{5,6},{6,7},{7,8},{8,9},{9,10},{10,1... | collective-permute-start | bytes 110600 | tf_op jit(solution)/shard_map/ppermute | solution.py:333
  175.3 17.1 %collective-permute-start.6 = (bf16[3,3,2,1024]{3,2,1,0:T(2,128)(2,1)S(1)}, bf16[3,3,2,1024]{3,2,1,0:T(2,128)(2,1)S(1)}, u32[]{:S(2)}, u32[]{:S(2)}) collective-permute-start(bf16[3,3,2,1024]{3,2,1,0:T(2,128)(2,1)S(1)} %squeeze.12), channel_id=1, source_target_pairs={{0,17},{1,18},{2,19},{3,20},{4,21},{5,22},{6,23},{7,24},{8,25},{9,... | collective-permute-start | bytes 110600 | tf_op jit(solution)/shard_map/ppermute | solution.py:333
  181.2 19.5 %all-to-all-start.1 = ((bf16[16,4,2048]{2,1,0:T(4,128)(2,1)}), bf16[16,4,2048]{2,1,0:T(4,128)(2,1)S(1)}, u32[]{:S(2)}, u32[]{:S(2)}) async-start(bf16[16,4,2048]{2,1,0:T(4,128)(2,1)} %reshape.113), calls=%async_computation.1 | async-start | bytes 524288 | tf_op jit(solution)/shard_map/all_to_all | solution.py:324
  186.5 8.0 %collective-permute-start.11 = (bf16[6,6,2,512]{3,2,1,0:T(2,128)(2,1)S(1)}, bf16[6,6,2,512]{3,2,1,0:T(2,128)(2,1)S(1)}, u32[]{:S(2)}, u32[]{:S(2)}) collective-permute-start(bf16[6,6,2,512]{3,2,1,0:T(2,128)(2,1)S(1)} %reshape.110), channel_id=1, source_target_pairs={{0,1},{1,2},{2,3},{3,4},{4,5},{5,6},{6,7},{7,8},{8,9},{9,10},{10,1... | collective-permute-start | bytes 221192 | tf_op jit(solution)/shard_map/ppermute | solution.py:333
  186.6 7.9 %collective-permute-start.10 = (bf16[6,6,2,512]{3,2,1,0:T(2,128)(2,1)S(1)}, bf16[6,6,2,512]{3,2,1,0:T(2,128)(2,1)S(1)}, u32[]{:S(2)}, u32[]{:S(2)}) collective-permute-start(bf16[6,6,2,512]{3,2,1,0:T(2,128)(2,1)S(1)} %reshape.109), channel_id=1, source_target_pairs={{0,16},{1,17},{2,18},{3,19},{4,20},{5,21},{6,22},{7,23},{8,24},{9,... | collective-permute-start | bytes 221192 | tf_op jit(solution)/shard_map/ppermute | solution.py:333
  188.6 9.2 %collective-permute-start.9 = (bf16[6,6,2,512]{3,2,1,0:T(2,128)(2,1)S(1)}, bf16[6,6,2,512]{3,2,1,0:T(2,128)(2,1)S(1)}, u32[]{:S(2)}, u32[]{:S(2)}) collective-permute-start(bf16[6,6,2,512]{3,2,1,0:T(2,128)(2,1)S(1)} %reshape.108), channel_id=1, source_target_pairs={{0,17},{1,18},{2,19},{3,20},{4,21},{5,22},{6,23},{7,24},{8,25},{9,... | collective-permute-start | bytes 221192 | tf_op jit(solution)/shard_map/ppermute | solution.py:333
  200.7 13.7 %all-to-all-start.9 = ((bf16[16,16,512]{2,1,0:T(8,128)(2,1)}), bf16[16,16,512]{2,1,0:T(8,128)(2,1)S(1)}, u32[]{:S(2)}, u32[]{:S(2)}) async-start(bf16[16,16,512]{2,1,0:T(8,128)(2,1)} %bitcast.14), calls=%async_computation.9 | async-start | bytes 524288 | tf_op jit(solution)/shard_map/all_to_all | solution.py:324
  214.5 12.4 %all-to-all-start.5 = ((bf16[16,16,512]{2,1,0:T(8,128)(2,1)}), bf16[16,16,512]{2,1,0:T(8,128)(2,1)S(1)}, u32[]{:S(2)}, u32[]{:S(2)}) async-start(bf16[16,16,512]{2,1,0:T(8,128)(2,1)} %bitcast.10), calls=%async_computation.5 | async-start | bytes 524288 | tf_op jit(solution)/shard_map/all_to_all | solution.py:324
  (4 other events, 37.9 us)

commit v2 on v1

--- a/solution.py
+++ b/solution.py
@@ -18,33 +18,9 @@
 BF16 = jnp.bfloat16
 F32 = jnp.float32
 
-FIRST = {"z": ("z",), "y": ("y",), "x": ("x_lo", "x_hi")}
-REST = {
-    "z": ("x_lo", "y", "x_hi"),
-    "y": ("z", "x_lo", "x_hi"),
-    "x": ("z", "y"),
-}
-SIZES = {"z": 4, "x_lo": 2, "y": 4, "x_hi": 2}
-
-
-def place_of(chunk, first):
-    at = {"core": chunk % 2, "x_hi": chunk // 2 % 2, "y": chunk // 4 % 4}
-    at["x_lo"], at["z"] = chunk // 16 % 2, chunk // 32
-    lead = rest = 0
-    for name in FIRST[first]:
-        lead = lead * SIZES[name] + at[name]
-    for name in REST[first]:
-        rest = rest * SIZES[name] + at[name]
-    return at["core"], lead, rest
-
-
-def row_order(first):
-    order = np.zeros((512, 512), np.float32)
-    for chunk in range(128):
-        core, lead, rest = place_of(chunk, first)
-        for row in range(4):
-            order[core * 256 + (lead * 16 + rest) * 4 + row, chunk * 4 + row] = 1.0
-    return order
+PAIRS = ("z", "x_lo", "y", "x_hi")
+NEAR = ("y", "core")
+FAR = ("z", "x_lo", "x_hi")
 
 
 def token_order():
@@ -83,12 +59,24 @@
     return jnp.where(rows == cols, 1.0, 0.0).astype(BF16)
 
 
+def weave(even, grads, keep, send, cols):
+    tiles = [grad.reshape(64, 8, grad.shape[-1]) for grad in grads]
+    turned = [pltpu.roll(tile, 4, 1) for tile in tiles]
+    upper = lax.broadcasted_iota(jnp.int32, tiles[0].shape, 1) < 4
+    for half in range(2):
+        one, two = half * 2, half * 2 + 1
+        first = jnp.where(upper, tiles[one], turned[two])
+        second = jnp.where(upper, turned[one], tiles[two])
+        rows = slice(half * 8, half * 8 + 8)
+        keep[:, rows, cols] = jnp.where(even, first, second).astype(BF16)
+        send[:, rows, cols] = jnp.where(even, second, first).astype(BF16)
+
+
 def forward_kernel(
-    core_ref, quad0, quad1, quad2, quad3, order_ref, bias_ref, cot_ref, rows_ref, w_qkv, w_qkv_t,
+    core_ref, quad0, quad1, quad2, quad3, order_ref, bias_ref, cot_ref, w_qkv, w_qkv_t,
     w_out, w_up, w_down, w_merge,
-    level_two_ref, merge_a_keep, merge_a_send, merge_b_keep, merge_b_send, down_keep, down_send,
-    up_keep, up_send, tokens_ref, packed_ref, keys_t_ref, probs_ref, attended_ref, middle_grad_ref,
-    first_t_ref,
+    level_two_ref, merged_t_ref, keep_ref, send_ref, tokens_ref, packed_ref, keys_t_ref, probs_ref,
+    attended_ref, middle_grad_ref, first_t_ref,
     query_t, values_t, slope_ref, hidden_ref, attended_t,
 ):
     even = core_ref[0] == 0
@@ -96,7 +84,8 @@
     tokens = sum(dot(order_ref[q], quads[q][...]) for q in range(4))
     tokens_ref[...] = tokens.astype(BF16)
     first_norm = normalize(tokens)[0].astype(BF16)
-    first_t_ref[...] = dot(rows_ref[0], first_norm, 1, 1).astype(BF16)
+    by_feature = eye(512)
+    first_t_ref[...] = dot(by_feature, first_norm, 1, 1).astype(BF16)
     for part in range(12):
         packed_ref[part] = dot(first_norm, w_qkv[:, part * 128 : part * 128 + 128]).astype(BF16)
     query_t[...] = dot(w_qkv_t[:512], first_norm, 1, 1).astype(BF16)
@@ -153,19 +142,12 @@
     ).astype(BF16)
     cotangent = cot_ref[...]
 
-    def store_blocks(grad, part, first, keep, send):
-        narrow = grad.astype(BF16)
-        for pair in range(16):
-            _, lead, rest = place_of(part * 32 + pair * 2, first)
-            low = narrow[pair * 32 : pair * 32 + 16]
-            high = narrow[pair * 32 + 16 : pair * 32 + 32]
-            keep[lead, rest] = jnp.where(even, low, high)
-            send[lead, rest] = jnp.where(even, high, low)
-
     for part in range(4):
-        grad = dot(merged_norm[part], cotangent, 0, 0)
-        store_blocks(grad[:, :512], part, "y", merge_a_keep, merge_a_send)
-        store_blocks(grad[:, 512:], part, "z", merge_b_keep, merge_b_send)
+        turned = dot(by_feature, merged_norm[part], 1, 1).astype(BF16)
+        for block in range(32):
+            x_lo, y, x_hi, core = block // 16, block // 4 % 4, block // 2 % 2, block % 2
+            at = (part * 4 + x_lo * 2 + x_hi) * 16
+            merged_t_ref[y * 2 + core, at : at + 16] = turned[block * 16 : block * 16 + 16]
     upstream = [dot(cotangent, w_merge[p * 512 : p * 512 + 512], 1, 1) for p in range(4)]
     mean_grad = sum(jnp.sum(v, axis=-1, keepdims=True) for v in upstream) / 2048.0
     mean_cross = (
@@ -175,25 +157,34 @@
         [inverse_out * (v - mean_grad - u * mean_cross) for v, u in zip(upstream, pieces)], axis=0
     ).astype(BF16)
 
-    second_t = dot(rows_ref[1], second_norm, 1, 1).astype(BF16)
+    second_t = dot(by_feature, second_norm, 1, 1).astype(BF16)
     back_up = jnp.zeros((TOKENS, 512), F32)
+    grads_up = []
     for part in range(4):
         cols = slice(part * 512, part * 512 + 512)
-        store_blocks(dot(hidden_ref[:, cols], grad_after, 0, 0), part, "x", down_keep, down_send)
+        grad = dot(hidden_ref[:, cols], grad_after, 0, 0).astype(BF16)
+        for pair in range(16):
+            low = grad[pair * 32 : pair * 32 + 16]
+            high = grad[pair * 32 + 16 : pair * 32 + 32]
+            keep_ref[part * 16 + pair, :, :512] = jnp.where(even, low, high)
+            send_ref[part * 16 + pair, :, :512] = jnp.where(even, high, low)
         grad_before = (dot(grad_after, w_down[cols], 1, 1) * slope_ref[:, cols]).astype(BF16)
-        grad_up = dot(second_t, grad_before).astype(BF16)
-        up_keep[:, cols] = jnp.where(even, grad_up[:256], grad_up[256:])
-        up_send[:, cols] = jnp.where(even, grad_up[256:], grad_up[:256])
+        grads_up.append(dot(second_t, grad_before))
         back_up = back_up + dot(grad_before, w_up[:, cols], 1, 1)
-    middle_grad_ref[...] = (
+    weave(even, grads_up, keep_ref, send_ref, slice(512, 1024))
+    middle_grad = (
         grad_after.astype(F32) + norm_back(normed_mid, inverse_mid, back_up)
     ).astype(BF16)
+    middle_grad_ref[...] = middle_grad
+    grad = dot(attended_t[...], middle_grad)
+    weave(even, [grad[:, p * 128 : p * 128 + 128] for p in range(4)], keep_ref, send_ref,
+          slice(1024, 1152))
 
 
 def backward_kernel(
     core_ref, tokens_ref, packed_ref, keys_t_ref, probs_ref, attended_ref, middle_grad_ref,
-    first_t_ref, rows_ref, order_ref, w_out, w_qkv,
-    late_keep, late_send, out0, out1, out2, out3,
+    first_t_ref, order_ref, w_out, w_qkv,
+    keep_ref, send_ref, out0, out1, out2, out3,
     grad_heads, grad_heads_t, products, query_grad_t, packed_grad,
 ):
     even = core_ref[0] == 0
@@ -241,17 +232,15 @@
         ).astype(BF16)
     first_t = first_t_ref[...]
     back_qkv = jnp.zeros((TOKENS, 512), F32)
+    grads = []
     for part in range(3):
         wide = jnp.concatenate([packed_grad[part * 4 + g] for g in range(4)], axis=1)
-        cols = slice(part * 512, part * 512 + 512)
-        grad = dot(first_t, wide).astype(BF16)
-        late_keep[:, cols] = jnp.where(even, grad[:256], grad[256:])
-        late_send[:, cols] = jnp.where(even, grad[256:], grad[:256])
-        back_qkv = back_qkv + dot(wide, w_qkv[:, cols], 1, 1)
-    attended = dot(rows_ref[0], attended_ref[...]).astype(BF16)
-    grad = dot(attended, middle_grad).astype(BF16)
-    late_keep[:, 1536:] = jnp.where(even, grad[:256], grad[256:])
-    late_send[:, 1536:] = jnp.where(even, grad[256:], grad[:256])
+        grad = dot(first_t, wide)
+        grads += [grad[:, q * 128 : q * 128 + 128] for q in range(4)]
+        back_qkv = back_qkv + dot(wide, w_qkv[:, part * 512 : part * 512 + 512], 1, 1)
+    for part in range(3):
+        weave(even, [grads[q * 3 + part] for q in range(4)], keep_ref, send_ref,
+              slice(part * 128, part * 128 + 128))
 
     normed_in, inverse_in = normalize(tokens_ref[...].astype(F32))
     grad_first = back_qkv.astype(BF16).astype(F32)
@@ -262,7 +251,12 @@
         out[...] = dot(order_ref[quad], grad_tokens).astype(BF16)
 
 
-LATE, UP = "z", "y"
+def merge_kernel(merged_ref, cots_ref, grad_ref):
+    for part in range(4):
+        rows = slice(part * 64, part * 64 + 64)
+        grad = sum(dot(merged_ref[near, rows], cots_ref[near]) for near in range(8))
+        for block in range(4):
+            grad_ref[part * 4 + block] = grad[block * 16 : block * 16 + 16].astype(BF16)
 
 
 def call(kernel, inputs, outputs, scratch, flops):
@@ -270,7 +264,9 @@
     return pl.pallas_call(
         kernel,
         out_shape=[jax.ShapeDtypeStruct(shape, BF16) for shape in outputs],
-        in_specs=[pl.BlockSpec(memory_space=pltpu.SMEM)] + [whole] * (len(inputs) - 1),
+        in_specs=[
+            pl.BlockSpec(memory_space=pltpu.SMEM) if value.ndim == 1 else whole for value in inputs
+        ],
         out_specs=[whole] * len(outputs),
         scratch_shapes=scratch,
         compiler_params=pltpu.CompilerParams(vmem_limit_bytes=58 * 2**20),
@@ -282,46 +278,47 @@
 
 def window_pass(core, quads, bias, cotangent, w_qkv, w_qkv_t, w_out, w_up, w_down, w_merge):
     order = token_order()
-    rows = jnp.asarray(np.stack([row_order(LATE), row_order(UP)]), BF16)
-    half, wide = (4, 16, 16, 512), (256, 2048)
     by_feature, field = (512, TOKENS), (TOKENS, 512)
-    outs = call(
+    level_two, merged_t, keep, send, *kept = call(
         forward_kernel,
-        [core, *quads, jnp.asarray(order, BF16), bias, cotangent, rows, w_qkv, w_qkv_t,
+        [core, *quads, jnp.asarray(order, BF16), bias, cotangent, w_qkv, w_qkv_t,
          w_out, w_up, w_down, w_merge],
-        [(MERGED, 1024)] + [half] * 6 + [wide] * 2
-        + [field, (12, TOKENS, 128), by_feature, (16, TOKENS, TOKENS), by_feature, field,
-           by_feature],
+        [(MERGED, 1024), (8, 256, MERGED), (64, 16, 1152), (64, 16, 1152),
+         field, (12, TOKENS, 128), by_feature, (16, TOKENS, TOKENS), by_feature, field,
+         by_feature],
         [pltpu.VMEM(by_feature, BF16), pltpu.VMEM(by_feature, BF16),
          pltpu.VMEM((TOKENS, 2048), F32), pltpu.VMEM((TOKENS, 2048), BF16),
          pltpu.VMEM(by_feature, BF16)],
         24 * 2**30,
     )
-    level_two, early, kept = outs[0], outs[1:9], outs[9:]
     late_keep, late_send, *grads = call(
         backward_kernel,
-        [core, *kept, rows, jnp.asarray(order.transpose(0, 2, 1), BF16), w_out, w_qkv],
-        [wide] * 2 + [(MERGED, 512)] * 4,
+        [core, *kept, jnp.asarray(order.transpose(0, 2, 1), BF16), w_out, w_qkv],
+        [(64, 16, 384)] * 2 + [(MERGED, 512)] * 4,
         [pltpu.VMEM((4, TOKENS, 128), BF16), pltpu.VMEM(by_feature, BF16),
          pltpu.VMEM(by_feature, F32), pltpu.VMEM(by_feature, BF16),
          pltpu.VMEM((12, TOKENS, 128), BF16)],
         16 * 2**30,
     )
-    return level_two, early, late_keep, late_send, grads
-
-
-def pair_reduce(keep, send):
+    return level_two, merged_t, keep, send, late_keep, late_send, grads
+
+
+def scatter_grad(keep, send):
     arrived = lax.ppermute(send, "core", [(0, 1), (1, 0)])
-    return (keep.astype(F32) + arrived.astype(F32)).astype(BF16)
-
-
-def scatter_grad(keep, send, first, rows):
-    blocks = pair_reduce(keep, send)
-    cols = blocks.shape[-1]
-    blocks = blocks.reshape(4, 16 * rows, cols)
-    landed = lax.all_to_all(blocks, FIRST[first], 0, 0, tiled=True)
-    blocks = jnp.sum(landed.astype(F32), axis=0).astype(BF16).reshape(16, rows, cols)
-    landed = lax.all_to_all(blocks, REST[first], 0, 0, tiled=True)
+    blocks = (keep.astype(F32) + arrived.astype(F32)).astype(BF16)
+    landed = lax.all_to_all(blocks, PAIRS, 0, 0, tiled=True)
+    return jnp.sum(landed.astype(F32), axis=0)
+
+
+def unweave(share):
+    cols = share.shape[-1]
+    return share.reshape(4, 4, cols).transpose(1, 0, 2).reshape(4, 4 * cols)
+
+
+def scatter_merge(merged_t, cotangents):
+    merged = lax.all_to_all(merged_t, NEAR, 0, 0, tiled=True)
+    grad, = call(merge_kernel, [merged, cotangents], [(16, 16, 1024)], [], 2**29)
+    landed = lax.all_to_all(grad, FAR, 0, 0, tiled=True)
     return jnp.sum(landed.astype(F32), axis=0)
 
 
@@ -336,7 +333,8 @@
 def quadrants(field):
     field = field.transpose(1, 2, 0, 3)
     rows, cols = field.shape[0] // 2, field.shape[1] // 2
-    return field[:rows, :cols], field[:rows, cols:], field[rows:, :cols], field[rows:, cols:]
+    corners = field[:rows, :cols], field[:rows, cols:], field[rows:, :cols], field[rows:, cols:]
+    return [corner.reshape(-1, field.shape[-1]) for corner in corners]
 
 
 def roll_back(field):
@@ -349,12 +347,17 @@
     ]
 
 
-def roll_forth(corners):
+def roll_forth(corners, side):
     upper_left, upper_right, lower_left, lower_right = corners
-    upper = jnp.concatenate(
-        [shifted_block(lower_right, 1, 1), shifted_block(lower_left, 1, 0)], axis=1
-    )
-    lower = jnp.concatenate([shifted_block(upper_right, 0, 1), upper_left], axis=1)
+    moved = [
+        shifted_block(lower_right, 1, 1),
+        shifted_block(lower_left, 1, 0),
+        shifted_block(upper_right, 0, 1),
+        upper_left,
+    ]
+    moved = [corner.reshape(side, side, 2, corner.shape[-1]) for corner in moved]
+    upper = jnp.concatenate(moved[:2], axis=1)
+    lower = jnp.concatenate(moved[2:], axis=1)
     return jnp.concatenate([upper, lower], axis=0).transpose(2, 0, 1, 3)
 
 
@@ -365,22 +368,21 @@
 
 
 def body(tokens, window_ids, cotangent, w_qkv, w_out, w_up, w_down, w_merge):
-    quads = [quad.reshape(MERGED, 512) for quad in roll_back(tokens)]
-    cot = jnp.concatenate([quad.reshape(18, 1024) for quad in roll_back(cotangent)], axis=0)
+    quads = roll_back(tokens)
+    cot = jnp.concatenate(roll_back(cotangent), axis=0)
+    cotangents = lax.all_gather(cot, NEAR)
     core = lax.axis_index("core").reshape(1)
-    level_two, early, late_keep, late_send, grads = window_pass(
+    level_two, merged_t, keep, send, late_keep, late_send, grads = window_pass(
         core, quads, window_bias(window_ids), cot, w_qkv, w_qkv.T, w_out, w_up, w_down, w_merge
     )
-    merge_a = scatter_grad(early[0], early[1], "y", 16)
-    merge_b = scatter_grad(early[2], early[3], "z", 16)
-    grad_down = scatter_grad(early[4], early[5], "x", 16)
-    grad_up = scatter_grad(early[6], early[7], UP, 4)
-    late = scatter_grad(late_keep, late_send, LATE, 4)
-    grad_tokens = roll_forth([grad.reshape(6, 6, 2, 512) for grad in grads])
-    corners = level_two.reshape(4, 3, 3, 2, 1024)
-    level_two = roll_forth([corners[quad] for quad in range(4)])
-    grad_merge = jnp.concatenate([merge_a, merge_b], axis=1)
-    return (level_two, grad_tokens, late[:, :1536], late[:, 1536:], grad_up, grad_down, grad_merge)
+    grad_merge = scatter_merge(merged_t, cotangents)
+    share = scatter_grad(keep, send)
+    grad_qkv = unweave(scatter_grad(late_keep, late_send))
+    grad_down, grad_up = share[:, :512], unweave(share[:, 512:1024])
+    grad_out = unweave(share[:, 1024:])
+    grad_tokens = roll_forth(grads, 6)
+    level_two = roll_forth([level_two[quad * 18 : quad * 18 + 18] for quad in range(4)], 3)
+    return (level_two, grad_tokens, grad_qkv, grad_out, grad_up, grad_down, grad_merge)
 
 
 def solution(mesh):

time: 229 us -> 179 us (0.78)
  waiting for transfers between devices: 81.1 us -> 50.8 us
  starting transfers between devices: 68 us -> 40.9 us
  between operations: 1 us -> 14.3 us
  other arithmetic: 24.2 us -> 11.8 us
  local copies, waits for them, and re-layouts: 12.6 us -> 16.2 us
    all_to_all x10 -> x4, waiting for transfers between devices: 74.4 us -> 22 us  [the longest x2 10.6 us: scatter_grad(): landed = lax.all_to_all(blocks, PAIRS, 0, 0, tiled=True)]
    ppermute x12, waiting for transfers between devices: 4.56 us -> 28.8 us  [shifted_block(): return lax.ppermute(block, GRID, route)]
    all_to_all x10 -> x4, starting transfers between devices: 40.2 us -> 20.2 us  [the longest x2 12.6 us: scatter_grad(): landed = lax.all_to_all(blocks, PAIRS, 0, 0, tiled=True)]
    convert_element_type x5 -> x2, other arithmetic: 12.6 us -> 5.91 us  [scatter_grad(): blocks = (keep.astype(F32) + arrived.astype(F32)).astype(BF16)]
    ppermute x12, starting transfers between devices: 24.2 us -> 19.7 us  [shifted_block(): return lax.ppermute(block, GRID, route)]
    reduce_sum x5 -> x1, other arithmetic: 5.56 us -> 1.75 us  [scatter_merge(): return jnp.sum(landed.astype(F32), axis=0)]
    ppermute x5 -> x2, starting transfers between devices: 3.65 us -> 0.95 us  [scatter_grad(): arrived = lax.ppermute(send, 'core', [(0, 1), (1, 0)])]
    pallas_call x2 -> x3, Pallas kernels: 40.6 us -> 42.7 us  [call(): pl.pallas_call(kernel, out_shape=[jax.ShapeDtypeStruct(shape, BF16) for s...]
  transfers between devices with their start and end apart: 27 -> 19, of which waited for: 11 -> 6; matrix products, arithmetic and copies ran while one was open for 15% -> 14% of each run, Pallas kernels for 6% -> 24%
where the time goes in v2:
time: 179 us; the launch traced here: 177 us
  waiting for transfers between devices  50.8 us (28%)
  Pallas kernels  42.7 us (24%)
  starting transfers between devices  40.9 us (23%)
  local copies, waits for them, and re-layouts  16.2 us (9%)
  between operations  14.3 us (8%)
  other arithmetic  11.8 us (7%)
    pallas_call x3, Pallas kernels, call(): pl.pallas_call(kernel, out_shape=[jax.ShapeDtypeStruct(shape, BF16) for s...  42.7 us
    ppermute x12, waiting for transfers between devices, shifted_block(): return lax.ppermute(block, GRID, route)  28.8 us
    ppermute x12, starting transfers between devices, shifted_block(): return lax.ppermute(block, GRID, route)  19.7 us
    all_to_all x2, starting transfers between devices, scatter_grad(): landed = lax.all_to_all(blocks, PAIRS, 0, 0, tiled=True)  12.6 us
    all_to_all x2, waiting for transfers between devices, scatter_grad(): landed = lax.all_to_all(blocks, PAIRS, 0, 0, tiled=True)  10.6 us
    convert_element_type x2, other arithmetic, scatter_grad(): blocks = (keep.astype(F32) + arrived.astype(F32)).astype(BF16)  5.91 us
    all_to_all x1, waiting for transfers between devices, scatter_merge(): landed = lax.all_to_all(grad, FAR, 0, 0, tiled=True)  5.87 us
    all_to_all x1, waiting for transfers between devices, scatter_merge(): merged = lax.all_to_all(merged_t, NEAR, 0, 0, tiled=True)  5.56 us
  transfers between devices with their start and end apart: 19, of which 6 were waited for; matrix products, arithmetic and copies ran while one was open for 14% of the time, Pallas kernels for 24%

profile of v2, /device:TPU:0, one launch (start us, length us, event | category | flops | bytes accessed | tf_op | source)
XLA Modules:
  0.0 176.7 jit_solution(9413383251736061223)
XLA Ops:
  7.2 1.0 fusion.2
  8.3 5.1 %collective-permute-start.3 = (bf16[18,1024]{1,0:T(8,128)(2,1)S(1)}, bf16[18,1024]{1,0:T(8,128)(2,1)S(1)}, u32[]{:S(2)}, u32[]{:S(2)}) collective-permute-start(bf16[18,1024]{1,0:T(8,128)(2,1)S(1)} %reshape.96), channel_id=1, source_target_pairs={{0,15},{1,0},{2,1},{3,2},{4,3},{5,4},{6,5},{7,6},{8,7},{9,8},{10,9... | collective-permute-start | bytes 110600 | tf_op jit(solution)/shard_map/ppermute | solution.py:330
  13.4 4.1 %collective-permute-start.4 = (bf16[18,1024]{1,0:T(8,128)(2,1)S(1)}, bf16[18,1024]{1,0:T(8,128)(2,1)S(1)}, u32[]{:S(2)}, u32[]{:S(2)}) collective-permute-start(bf16[18,1024]{1,0:T(8,128)(2,1)S(1)} %reshape.97), channel_id=1, source_target_pairs={{0,112},{1,113},{2,114},{3,115},{4,116},{5,117},{6,118},{7,119},{8... | collective-permute-start | bytes 110600 | tf_op jit(solution)/shard_map/ppermute | solution.py:330
  18.0 1.2 fusion
  19.2 1.5 collective-permute-start
  20.7 1.3 collective-permute-start.1
  25.0 1.6 copy.26
  27.4 3.0 %collective-permute-done.2.quad3 = bf16[72,512]{1,0:T(8,128)(2,1)S(1)} collective-permute-done((bf16[72,512]{1,0:T(8,128)(2,1)S(1)}, bf16[72,512]{1,0:T(8,128)(2,1)S(1)}, u32[]{:S(2)}, u32[]{:S(2)}) %collective-permute-start.2) | collective-permute-done | bytes 73760 | tf_op jit(solution)/shard_map/ppermute | solution.py:330
  31.0 26.6 %shard_map.153 = (bf16[72,1024]{1,0:T(8,128)(2,1)}, bf16[8,256,72]{2,1,0:T(8,128)(2,1)}, bf16[64,16,1152]{2,1,0:T(8,128)(2,1)}, bf16[64,16,1152]{2,1,0:T(8,128)(...) custom-call(s32[1]{0:T(128)} %bitcast.core_ref, ...), custom_call_target="tpu_custom_call" | custom-call | flops 25769803776 | bytes 26214400 | tf_op jit(solution)/shard_map/pallas_call | solution.py:264
  57.6 0.9 collective-permute-start.13
  58.5 12.5 %shard_map.154 = (bf16[64,16,384]{2,1,0:T(8,128)(2,1)}, bf16[64,16,384]{2,1,0:T(8,128)(2,1)}, bf16[72,512]{1,0:T(8,128)(2,1)}, bf16[72,512]{1,0:T(8,128)(2,1)}, ...) custom-call(s32[1]{0:T(128)} %bitcast.core_ref, bf16[288,512]{1,0:T(8,128)(2,1)} %get-tuple-element.25.tokens_ref, ...), custom_call_target="tpu_custom_call" | custom-call | flops 17179869184 | bytes 26214400 | tf_op jit(solution)/shard_map/pallas_call | solution.py:264
  71.1 0.9 copy.29
  72.0 3.4 %all-to-all-start.2 = ((bf16[8,256,72]{1,2,0:T(8,128)(2,1)}), bf16[8,256,72]{1,2,0:T(8,128)(2,1)S(1)}, u32[]{:S(2)}, u32[]{:S(2)}) async-start(bf16[8,256,72]{1,2,0:T(8,128)(2,1)} %copy.29), calls=%async_computation.2 | async-start | bytes 589824 | tf_op jit(solution)/shard_map/all_to_all | solution.py:319
  75.4 2.2 %add_convert_fusion.1 = bf16[64,16,384]{2,1,0:T(8,128)(2,1)} fusion(bf16[64,16,384]{2,1,0:T(8,128)(2,1)S(1)} %collective-permute-done.12, bf16[64,16,384]{2,1,0:T(8,128)(2,1)} %get-tuple-element.36), kind=kLoop, calls=%fused_computation.3 | loop fusion | flops 1572864 | bytes 2359296 | tf_op jit(solution)/shard_map/convert_element_type | solution.py:308
  77.7 5.6 %all-to-all-done.2 = bf16[8,256,72]{1,2,0:T(8,128)(2,1)S(1)} async-done(((bf16[8,256,72]{1,2,0:T(8,128)(2,1)}), bf16[8,256,72]{1,2,0:T(8,128)(2,1)S(1)}, u32[]{:S(2)}, u32[]{:S(2)}) %all-to-all-start.2) | async-done | bytes 294944 | tf_op jit(solution)/shard_map/all_to_all | solution.py:319
  83.2 6.8 %all-to-all-start = ((bf16[64,16,384]{2,1,0:T(8,128)(2,1)}), bf16[64,16,384]{2,1,0:T(8,128)(2,1)S(1)}, u32[]{:S(2)}, u32[]{:S(2)}) async-start(bf16[64,16,384]{2,1,0:T(8,128)(2,1)} %add_convert_fusion.1), calls=%async_computation | async-start | bytes 1572864 | tf_op jit(solution)/shard_map/all_to_all | solution.py:309
  90.0 1.0 copy.30.merged_ref
  91.1 3.6 %shard_map.155 = bf16[16,16,1024]{2,1,0:T(8,128)(2,1)} custom-call(bf16[8,256,72]{2,1,0:T(8,128)(2,1)} %copy.30.merged_ref, bf16[8,72,1024]{2,1,0:T(8,128)(2,1)} %bitcast.28), custom_call_target="tpu_custom_call" | custom-call | flops 536870912 | bytes 26214400 | tf_op jit(solution)/shard_map/pallas_call | solution.py:264
  94.7 10.6 %all-to-all-done = bf16[64,16,384]{2,1,0:T(8,128)(2,1)S(1)} async-done(((bf16[64,16,384]{2,1,0:T(8,128)(2,1)}), bf16[64,16,384]{2,1,0:T(8,128)(2,1)S(1)}, u32[]{:S(2)}, u32[]{:S(2)}) %all-to-all-start) | async-done | bytes 786464 | tf_op jit(solution)/shard_map/all_to_all | solution.py:309
  105.3 4.2 %all-to-all-start.3 = ((bf16[16,16,1024]{2,1,0:T(8,128)(2,1)}), bf16[16,16,1024]{2,1,0:T(8,128)(2,1)}, u32[]{:S(2)}, u32[]{:S(2)}) async-start(bf16[16,16,1024]{2,1,0:T(8,128)(2,1)} %shard_map.155), calls=%async_computation.3 | async-start | bytes 1048576 | tf_op jit(solution)/shard_map/all_to_all | solution.py:321
  109.5 3.7 %add_convert_fusion = bf16[64,16,1152]{2,1,0:T(8,128)(2,1)} fusion(bf16[64,16,1152]{2,1,0:T(8,128)(2,1)} %collective-permute-done.13, bf16[64,16,1152]{2,1,0:T(8,128)(2,1)S(1)} %copy-done), kind=kLoop, calls=%fused_computation.1 | loop fusion | flops 4718592 | bytes 7077888 | tf_op jit(solution)/shard_map/convert_element_type | solution.py:308
  113.2 5.9 %all-to-all-done.3 = bf16[16,16,1024]{2,1,0:T(8,128)(2,1)} async-done(((bf16[16,16,1024]{2,1,0:T(8,128)(2,1)}), bf16[16,16,1024]{2,1,0:T(8,128)(2,1)}, u32[]{:S(2)}, u32[]{:S(2)}) %all-to-all-start.3) | async-done | bytes 524320 | tf_op jit(solution)/shard_map/all_to_all | solution.py:321
  119.1 5.8 %all-to-all-start.1 = ((bf16[64,16,1152]{2,1,0:T(8,128)(2,1)}), bf16[64,16,1152]{2,1,0:T(8,128)(2,1)S(1)}, u32[]{:S(2)}, u32[]{:S(2)}) async-start(bf16[64,16,1152]{2,1,0:T(8,128)(2,1)} %add_convert_fusion), calls=%async_computation.1 | async-start | bytes 4718592 | tf_op jit(solution)/shard_map/all_to_all | solution.py:309
  125.5 1.6 collective-permute-start.7
  127.1 3.5 %collective-permute-start.6 = (bf16[18,1024]{1,0:T(8,128)(2,1)S(1)}, bf16[18,1024]{1,0:T(8,128)(2,1)}, u32[]{:S(2)}, u32[]{:S(2)}) collective-permute-start(bf16[18,1024]{1,0:T(8,128)(2,1)S(1)} %get-tuple-element.45), channel_id=1, source_target_pairs={{0,17},{1,18},{2,19},{3,20},{4,21},{5,22},{6,23},{7,24},{8,25},{9,... | collective-permute-start | bytes 110600 | tf_op jit(solution)/shard_map/ppermute | solution.py:330
  130.7 2.1 %collective-permute-start.10 = (bf16[72,512]{1,0:T(8,128)(2,1)}, bf16[72,512]{1,0:T(8,128)(2,1)S(1)}, u32[]{:S(2)}, u32[]{:S(2)}) collective-permute-start(bf16[72,512]{1,0:T(8,128)(2,1)} %get-tuple-element.33), channel_id=1, source_target_pairs={{0,16},{1,17},{2,18},{3,19},{4,20},{5,21},{6,22},{7,23},{8,24},{9,... | collective-permute-start | bytes 221192 | tf_op jit(solution)/shard_map/ppermute | solution.py:330
  132.9 22.4 %collective-permute-done.7 = bf16[18,1024]{1,0:T(8,128)(2,1)} collective-permute-done((bf16[18,1024]{1,0:T(8,128)(2,1)}, bf16[18,1024]{1,0:T(8,128)(2,1)}, u32[]{:S(2)}, u32[]{:S(2)}) %collective-permute-start.7) | collective-permute-done | bytes 36896 | tf_op jit(solution)/shard_map/ppermute | solution.py:330
  158.7 0.9 reshape.103
  159.7 3.4 %collective-permute-done.11 = bf16[72,512]{1,0:T(8,128)(2,1)} collective-permute-done((bf16[72,512]{1,0:T(8,128)(2,1)}, bf16[72,512]{1,0:T(8,128)(2,1)}, u32[]{:S(2)}, u32[]{:S(2)}) %collective-permute-start.11) | collective-permute-done | bytes 73760 | tf_op jit(solution)/shard_map/ppermute | solution.py:330
  163.1 0.9 reshape.105
  164.0 1.1 maximum_bitcast_fusion
  165.9 1.8 convert_reduce_fusion.2
  (65 shorter events, 12.1 us)
Async XLA Ops:
  7.2 17.8 %copy-start.1 = (bf16[512,1536]{1,0:T(8,128)(2,1)S(1)}, bf16[512,1536]{1,0:T(8,128)(2,1)}, u32[]{:S(2)}) copy-start(bf16[512,1536]{1,0:T(8,128)(2,1)} %w_qkv.3) | copy-start | bytes 4718596
  7.2 83.9 %all-gather.3.cloned.1.call-start = ((), (), s32[]{:S(2)}) async-start(), calls=%async_computation.4 | async-start | bytes 1327104 | tf_op jit(solution)/shard_map/all_gather | solution.py:373
  8.3 18.3 %collective-permute-start.3 = (bf16[18,1024]{1,0:T(8,128)(2,1)S(1)}, bf16[18,1024]{1,0:T(8,128)(2,1)S(1)}, u32[]{:S(2)}, u32[]{:S(2)}) collective-permute-start(bf16[18,1024]{1,0:T(8,128)(2,1)S(1)} %reshape.96), channel_id=1, source_target_pairs={{0,15},{1,0},{2,1},{3,2},{4,3},{5,4},{6,5},{7,6},{8,7},{9,8},{10,9... | collective-permute-start | bytes 110600 | tf_op jit(solution)/shard_map/ppermute | solution.py:330
  13.4 13.2 %collective-permute-start.4 = (bf16[18,1024]{1,0:T(8,128)(2,1)S(1)}, bf16[18,1024]{1,0:T(8,128)(2,1)S(1)}, u32[]{:S(2)}, u32[]{:S(2)}) collective-permute-start(bf16[18,1024]{1,0:T(8,128)(2,1)S(1)} %reshape.97), channel_id=1, source_target_pairs={{0,112},{1,113},{2,114},{3,115},{4,116},{5,117},{6,118},{7,119},{8... | collective-permute-start | bytes 110600 | tf_op jit(solution)/shard_map/ppermute | solution.py:330
  17.5 9.1 %collective-permute-start.5 = (bf16[18,1024]{1,0:T(8,128)(2,1)S(1)}, bf16[18,1024]{1,0:T(8,128)(2,1)S(1)}, u32[]{:S(2)}, u32[]{:S(2)}) collective-permute-start(bf16[18,1024]{1,0:T(8,128)(2,1)S(1)} %reshape.98), channel_id=1, source_target_pairs={{0,127},{1,112},{2,113},{3,114},{4,115},{5,116},{6,117},{7,118},{8... | collective-permute-start | bytes 110600 | tf_op jit(solution)/shard_map/ppermute | solution.py:330
  19.2 8.2 %collective-permute-start = (bf16[72,512]{1,0:T(8,128)(2,1)S(1)}, bf16[72,512]{1,0:T(8,128)(2,1)S(1)}, u32[]{:S(2)}, u32[]{:S(2)}) collective-permute-start(bf16[72,512]{1,0:T(8,128)(2,1)S(1)} %reshape.91), channel_id=1, source_target_pairs={{0,15},{1,0},{2,1},{3,2},{4,3},{5,4},{6,5},{7,6},{8,7},{9,8},{10,9... | collective-permute-start | bytes 221192 | tf_op jit(solution)/shard_map/ppermute | solution.py:330
  20.7 6.7 %collective-permute-start.1 = (bf16[72,512]{1,0:T(8,128)(2,1)S(1)}, bf16[72,512]{1,0:T(8,128)(2,1)S(1)}, u32[]{:S(2)}, u32[]{:S(2)}) collective-permute-start(bf16[72,512]{1,0:T(8,128)(2,1)S(1)} %reshape.92), channel_id=1, source_target_pairs={{0,112},{1,113},{2,114},{3,115},{4,116},{5,117},{6,118},{7,119},{8... | collective-permute-start | bytes 221192 | tf_op jit(solution)/shard_map/ppermute | solution.py:330
  26.6 3.8 %collective-permute-start.2 = (bf16[72,512]{1,0:T(8,128)(2,1)S(1)}, bf16[72,512]{1,0:T(8,128)(2,1)S(1)}, u32[]{:S(2)}, u32[]{:S(2)}) collective-permute-start(bf16[72,512]{1,0:T(8,128)(2,1)S(1)} %reshape.93), channel_id=1, source_target_pairs={{0,127},{1,112},{2,113},{3,114},{4,115},{5,116},{6,117},{7,118},{8... | collective-permute-start | bytes 221192 | tf_op jit(solution)/shard_map/ppermute | solution.py:330
  27.4 3.0 %copy-start.5 = (bf16[72,512]{1,0:T(8,128)(2,1)}, bf16[72,512]{1,0:T(8,128)(2,1)S(1)}, u32[]{:S(2)}) copy-start(bf16[72,512]{1,0:T(8,128)(2,1)S(1)} %collective-permute-done.quad1) | copy-start | bytes 221188
  27.4 3.0 %copy-start.6 = (bf16[72,512]{1,0:T(8,128)(2,1)}, bf16[72,512]{1,0:T(8,128)(2,1)S(1)}, u32[]{:S(2)}) copy-start(bf16[72,512]{1,0:T(8,128)(2,1)S(1)} %collective-permute-done.1.quad2) | copy-start | bytes 221188
  30.4 0.6 copy-start.7
  57.6 51.9 %collective-permute-start.13 = (bf16[64,16,1152]{2,1,0:T(8,128)(2,1)}, bf16[64,16,1152]{2,1,0:T(8,128)(2,1)}, u32[]{:S(2)}, u32[]{:S(2)}) collective-permute-start(bf16[64,16,1152]{2,1,0:T(8,128)(2,1)} %get-tuple-element.39), channel_id=1, source_target_pairs={{0,1},{1,0},{2,3},{3,2},{4,5},{5,4},{6,7},{7,6},{8,9},{9,8},{10,11... | collective-permute-start | bytes 7077896 | tf_op jit(solution)/shard_map/ppermute | solution.py:307
  58.5 12.6 %copy-start.2 = (bf16[8,256,72]{2,1,0:T(8,128)(2,1)S(1)}, bf16[8,256,72]{2,1,0:T(8,128)(2,1)}, u32[]{:S(2)}) copy-start(bf16[8,256,72]{2,1,0:T(8,128)(2,1)} %get-tuple-element.40) | copy-start | bytes 884740
  71.0 4.4 %collective-permute-start.12 = (bf16[64,16,384]{2,1,0:T(8,128)(2,1)}, bf16[64,16,384]{2,1,0:T(8,128)(2,1)S(1)}, u32[]{:S(2)}, u32[]{:S(2)}) collective-permute-start(bf16[64,16,384]{2,1,0:T(8,128)(2,1)} %get-tuple-element.37), channel_id=1, source_target_pairs={{0,1},{1,0},{2,3},{3,2},{4,5},{5,4},{6,7},{7,6},{8,9},{9,8},{10,11... | collective-permute-start | bytes 2359304 | tf_op jit(solution)/shard_map/ppermute | solution.py:307
  72.0 11.2 %all-to-all-start.2 = ((bf16[8,256,72]{1,2,0:T(8,128)(2,1)}), bf16[8,256,72]{1,2,0:T(8,128)(2,1)S(1)}, u32[]{:S(2)}, u32[]{:S(2)}) async-start(bf16[8,256,72]{1,2,0:T(8,128)(2,1)} %copy.29), calls=%async_computation.2 | async-start | bytes 589824 | tf_op jit(solution)/shard_map/all_to_all | solution.py:319
  83.2 22.0 %all-to-all-start = ((bf16[64,16,384]{2,1,0:T(8,128)(2,1)}), bf16[64,16,384]{2,1,0:T(8,128)(2,1)S(1)}, u32[]{:S(2)}, u32[]{:S(2)}) async-start(bf16[64,16,384]{2,1,0:T(8,128)(2,1)} %add_convert_fusion.1), calls=%async_computation | async-start | bytes 1572864 | tf_op jit(solution)/shard_map/all_to_all | solution.py:309
  91.1 18.5 %copy-start = (bf16[64,16,1152]{2,1,0:T(8,128)(2,1)S(1)}, bf16[64,16,1152]{2,1,0:T(8,128)(2,1)}, u32[]{:S(2)}) copy-start(bf16[64,16,1152]{2,1,0:T(8,128)(2,1)} %get-tuple-element.38) | copy-start | bytes 7077892
  105.3 13.8 %all-to-all-start.3 = ((bf16[16,16,1024]{2,1,0:T(8,128)(2,1)}), bf16[16,16,1024]{2,1,0:T(8,128)(2,1)}, u32[]{:S(2)}, u32[]{:S(2)}) async-start(bf16[16,16,1024]{2,1,0:T(8,128)(2,1)} %shard_map.155), calls=%async_computation.3 | async-start | bytes 1048576 | tf_op jit(solution)/shard_map/all_to_all | solution.py:321
  113.2 11.7 %copy-start.3 = (bf16[72,1024]{1,0:T(8,128)(2,1)S(1)}, bf16[72,1024]{1,0:T(8,128)(2,1)}, u32[]{:S(2)}) copy-start(bf16[72,1024]{1,0:T(8,128)(2,1)} %get-tuple-element.24) | copy-start | bytes 442372
  113.2 19.6 %copy-start.4 = (bf16[72,512]{1,0:T(8,128)(2,1)S(1)}, bf16[72,512]{1,0:T(8,128)(2,1)}, u32[]{:S(2)}) copy-start(bf16[72,512]{1,0:T(8,128)(2,1)} %get-tuple-element.35) | copy-start | bytes 221188
  119.1 48.6 %all-to-all-start.1 = ((bf16[64,16,1152]{2,1,0:T(8,128)(2,1)}), bf16[64,16,1152]{2,1,0:T(8,128)(2,1)S(1)}, u32[]{:S(2)}, u32[]{:S(2)}) async-start(bf16[64,16,1152]{2,1,0:T(8,128)(2,1)} %add_convert_fusion), calls=%async_computation.1 | async-start | bytes 4718592 | tf_op jit(solution)/shard_map/all_to_all | solution.py:309
  125.5 29.8 %collective-permute-start.7 = (bf16[18,1024]{1,0:T(8,128)(2,1)}, bf16[18,1024]{1,0:T(8,128)(2,1)}, u32[]{:S(2)}, u32[]{:S(2)}) collective-permute-start(bf16[18,1024]{1,0:T(8,128)(2,1)} %get-tuple-element.48), channel_id=1, source_target_pairs={{0,16},{1,17},{2,18},{3,19},{4,20},{5,21},{6,22},{7,23},{8,24},{9,... | collective-permute-start | bytes 110600 | tf_op jit(solution)/shard_map/ppermute | solution.py:330
  127.1 29.1 %collective-permute-start.8 = (bf16[18,1024]{1,0:T(8,128)(2,1)}, bf16[18,1024]{1,0:T(8,128)(2,1)}, u32[]{:S(2)}, u32[]{:S(2)}) collective-permute-start(bf16[18,1024]{1,0:T(8,128)(2,1)} %get-tuple-element.47), channel_id=1, source_target_pairs={{0,1},{1,2},{2,3},{3,4},{4,5},{5,6},{6,7},{7,8},{8,9},{9,10},{10,1... | collective-permute-start | bytes 110600 | tf_op jit(solution)/shard_map/ppermute | solution.py:330
  127.1 29.9 %collective-permute-start.6 = (bf16[18,1024]{1,0:T(8,128)(2,1)S(1)}, bf16[18,1024]{1,0:T(8,128)(2,1)}, u32[]{:S(2)}, u32[]{:S(2)}) collective-permute-start(bf16[18,1024]{1,0:T(8,128)(2,1)S(1)} %get-tuple-element.45), channel_id=1, source_target_pairs={{0,17},{1,18},{2,19},{3,20},{4,21},{5,22},{6,23},{7,24},{8,25},{9,... | collective-permute-start | bytes 110600 | tf_op jit(solution)/shard_map/ppermute | solution.py:330
  130.7 28.1 %collective-permute-start.9 = (bf16[72,512]{1,0:T(8,128)(2,1)}, bf16[72,512]{1,0:T(8,128)(2,1)}, u32[]{:S(2)}, u32[]{:S(2)}) collective-permute-start(bf16[72,512]{1,0:T(8,128)(2,1)} %get-tuple-element.32), channel_id=1, source_target_pairs={{0,17},{1,18},{2,19},{3,20},{4,21},{5,22},{6,23},{7,24},{8,25},{9,... | collective-permute-start | bytes 221192 | tf_op jit(solution)/shard_map/ppermute | solution.py:330
  130.7 28.9 %collective-permute-start.10 = (bf16[72,512]{1,0:T(8,128)(2,1)}, bf16[72,512]{1,0:T(8,128)(2,1)S(1)}, u32[]{:S(2)}, u32[]{:S(2)}) collective-permute-start(bf16[72,512]{1,0:T(8,128)(2,1)} %get-tuple-element.33), channel_id=1, source_target_pairs={{0,16},{1,17},{2,18},{3,19},{4,20},{5,21},{6,22},{7,23},{8,24},{9,... | collective-permute-start | bytes 221192 | tf_op jit(solution)/shard_map/ppermute | solution.py:330
  155.4 7.7 %collective-permute-start.11 = (bf16[72,512]{1,0:T(8,128)(2,1)}, bf16[72,512]{1,0:T(8,128)(2,1)}, u32[]{:S(2)}, u32[]{:S(2)}) collective-permute-start(bf16[72,512]{1,0:T(8,128)(2,1)} %get-tuple-element.34), channel_id=1, source_target_pairs={{0,1},{1,2},{2,3},{3,4},{4,5},{5,6},{6,7},{7,8},{8,9},{9,10},{10,1... | collective-permute-start | bytes 221192 | tf_op jit(solution)/shard_map/ppermute | solution.py:330
Sparse Core Ops, SparseCore 0:
  27.5 21.4 all-gather.2

commit v3 on v2

--- a/solution.py
+++ b/solution.py
@@ -72,20 +72,49 @@
         send[:, rows, cols] = jnp.where(even, second, first).astype(BF16)
 
 
+def load(pairs, sems):
+    copies = [pltpu.make_async_copy(*pair, sems.at[at]) for at, pair in enumerate(pairs)]
+    for copy in copies:
+        copy.start()
+    return copies
+
+
+def merge_norm(after_mlp):
+    pieces = [after_mlp[p * MERGED : (p + 1) * MERGED] for p in range(4)]
+    mean = sum(jnp.sum(v, axis=-1, keepdims=True) for v in pieces) / 2048.0
+    pieces = [v - mean for v in pieces]
+    inverse_out = lax.rsqrt(
+        sum(jnp.sum(v * v, axis=-1, keepdims=True) for v in pieces) / 2048.0 + EPS
+    )
+    return [v * inverse_out for v in pieces], inverse_out
+
+
+def near_order():
+    source = lax.broadcasted_iota(jnp.int32, (512, 512), 0)
+    target = lax.broadcasted_iota(jnp.int32, (512, 512), 1)
+    block = source // 16
+    near = block // 4 % 4 * 2 + block % 2
+    far = block // 16 * 2 + block // 2 % 2
+    return jnp.where(target == near * 64 + far * 16 + source % 16, 1.0, 0.0).astype(BF16)
+
+
 def forward_kernel(
-    core_ref, quad0, quad1, quad2, quad3, order_ref, bias_ref, cot_ref, w_qkv, w_qkv_t,
-    w_out, w_up, w_down, w_merge,
-    level_two_ref, merged_t_ref, keep_ref, send_ref, tokens_ref, packed_ref, keys_t_ref, probs_ref,
-    attended_ref, middle_grad_ref, first_t_ref,
-    query_t, values_t, slope_ref, hidden_ref, attended_t,
+    quad0, quad1, quad2, quad3, order_ref, bias_ref, w_qkv, w_qkv_t,
+    w_out_hbm, w_up_hbm, w_down_hbm, w_merge_hbm,
+    level_two_ref, merged_ref, tokens_ref, packed_ref, keys_t_ref, attended_ref, first_t_ref,
+    middle_ref, after_mlp_ref, probs_hbm, hidden_hbm, slope_hbm,
+    query_t, values_t, slope_ref, hidden_ref, probs_ref, w_out, w_up, w_down, w_merge,
+    in_sems, out_sems,
 ):
-    even = core_ref[0] == 0
+    weights = load(
+        [(w_out_hbm, w_out), (w_up_hbm, w_up), (w_down_hbm, w_down), (w_merge_hbm, w_merge)],
+        in_sems,
+    )
     quads = (quad0, quad1, quad2, quad3)
     tokens = sum(dot(order_ref[q], quads[q][...]) for q in range(4))
     tokens_ref[...] = tokens.astype(BF16)
     first_norm = normalize(tokens)[0].astype(BF16)
-    by_feature = eye(512)
-    first_t_ref[...] = dot(by_feature, first_norm, 1, 1).astype(BF16)
+    first_t_ref[...] = dot(eye(512), first_norm, 1, 1).astype(BF16)
     for part in range(12):
         packed_ref[part] = dot(first_norm, w_qkv[:, part * 128 : part * 128 + 128]).astype(BF16)
     query_t[...] = dot(w_qkv_t[:512], first_norm, 1, 1).astype(BF16)
@@ -105,18 +134,22 @@
             probs = (raised * inverse).astype(BF16)
             probs_ref[group * 4 + head] = probs
             at = pl.ds(pl.multiple_of(group * 128 + head * HEAD, HEAD), HEAD)
-            attended_t[at, :] = dot(values_t[at, :], probs).astype(BF16)
+            attended_ref[at, :] = dot(values_t[at, :], probs).astype(BF16)
         return 0
 
     lax.fori_loop(0, 4, attend, 0)
-
-    attended_ref[...] = attended_t[...]
-    attended = dot(eye(TOKENS), attended_t[...], 1, 1).astype(BF16)
+    saves = load([(probs_ref, probs_hbm)], out_sems.at[pl.ds(0, 1)])
+
+    attended = dot(eye(TOKENS), attended_ref[...], 1, 1).astype(BF16)
+    weights[0].wait()
     attn_out = dot(attended, w_out[...]).astype(BF16)
-    middle = (tokens + attn_out.astype(F32)).astype(BF16).astype(F32)
-    normed_mid, inverse_mid = normalize(middle)
-    second_norm = normed_mid.astype(BF16)
+    narrow_middle = (tokens + attn_out.astype(F32)).astype(BF16)
+    middle_ref[...] = narrow_middle
+    middle = narrow_middle.astype(F32)
+    second_norm = normalize(middle)[0].astype(BF16)
     mlp = jnp.zeros((TOKENS, 512), F32)
+    weights[1].wait()
+    weights[2].wait()
     for part in range(4):
         cols = slice(part * 512, part * 512 + 512)
         before = dot(second_norm, w_up[:, cols])
@@ -125,29 +158,42 @@
         hidden_ref[:, cols] = hidden
         slope_ref[:, cols] = (
             cumulative + before * jnp.exp(-0.5 * before * before) * 0.3989422804014327
-        )
+        ).astype(BF16)
         mlp = mlp + dot(hidden, w_down[cols])
-    after_mlp = (middle + mlp).astype(BF16).astype(F32)
-
-    pieces = [after_mlp[p * MERGED : (p + 1) * MERGED] for p in range(4)]
-    mean = sum(jnp.sum(v, axis=-1, keepdims=True) for v in pieces) / 2048.0
-    pieces = [v - mean for v in pieces]
-    inverse_out = lax.rsqrt(
-        sum(jnp.sum(v * v, axis=-1, keepdims=True) for v in pieces) / 2048.0 + EPS
-    )
-    pieces = [v * inverse_out for v in pieces]
-    merged_norm = [v.astype(BF16) for v in pieces]
+    saves += load([(hidden_ref, hidden_hbm), (slope_ref, slope_hbm)], out_sems.at[pl.ds(1, 2)])
+    after_mlp = (middle + mlp).astype(BF16)
+    after_mlp_ref[...] = after_mlp
+    merged_norm = [v.astype(BF16) for v in merge_norm(after_mlp.astype(F32))[0]]
+    order = near_order()
+    spread = [dot(v, order) for v in merged_norm]
+    for near in range(8):
+        at = slice(near * 64, near * 64 + 64)
+        merged_ref[near] = jnp.concatenate([v[:, at] for v in spread], axis=1).astype(BF16)
+    weights[3].wait()
     level_two_ref[...] = sum(
         dot(merged_norm[p], w_merge[p * 512 : p * 512 + 512]) for p in range(4)
     ).astype(BF16)
+    for save in saves:
+        save.wait()
+
+
+def middle_kernel(
+    core_ref, cot_ref, middle_ref, after_mlp_ref, attended_ref,
+    w_merge_hbm, hidden_hbm, w_down_hbm, slope_hbm, w_up_hbm,
+    keep_ref, send_ref, middle_grad_ref,
+    w_merge, hidden_ref, w_down, slope_ref, w_up, sems,
+):
+    loads = load(
+        [(w_merge_hbm, w_merge), (hidden_hbm, hidden_ref), (w_down_hbm, w_down),
+         (slope_hbm, slope_ref), (w_up_hbm, w_up)],
+        sems,
+    )
+    even = core_ref[0] == 0
     cotangent = cot_ref[...]
-
-    for part in range(4):
-        turned = dot(by_feature, merged_norm[part], 1, 1).astype(BF16)
-        for block in range(32):
-            x_lo, y, x_hi, core = block // 16, block // 4 % 4, block // 2 % 2, block % 2
-            at = (part * 4 + x_lo * 2 + x_hi) * 16
-            merged_t_ref[y * 2 + core, at : at + 16] = turned[block * 16 : block * 16 + 16]
+    pieces, inverse_out = merge_norm(after_mlp_ref[...].astype(F32))
+    normed_mid, inverse_mid = normalize(middle_ref[...].astype(F32))
+    second_t = dot(eye(512), normed_mid.astype(BF16), 1, 1).astype(BF16)
+    loads[0].wait()
     upstream = [dot(cotangent, w_merge[p * 512 : p * 512 + 512], 1, 1) for p in range(4)]
     mean_grad = sum(jnp.sum(v, axis=-1, keepdims=True) for v in upstream) / 2048.0
     mean_cross = (
@@ -157,9 +203,10 @@
         [inverse_out * (v - mean_grad - u * mean_cross) for v, u in zip(upstream, pieces)], axis=0
     ).astype(BF16)
 
-    second_t = dot(by_feature, second_norm, 1, 1).astype(BF16)
     back_up = jnp.zeros((TOKENS, 512), F32)
     grads_up = []
+    for copy in loads[1:]:
+        copy.wait()
     for part in range(4):
         cols = slice(part * 512, part * 512 + 512)
         grad = dot(hidden_ref[:, cols], grad_after, 0, 0).astype(BF16)
@@ -168,7 +215,9 @@
             high = grad[pair * 32 + 16 : pair * 32 + 32]
             keep_ref[part * 16 + pair, :, :512] = jnp.where(even, low, high)
             send_ref[part * 16 + pair, :, :512] = jnp.where(even, high, low)
-        grad_before = (dot(grad_after, w_down[cols], 1, 1) * slope_ref[:, cols]).astype(BF16)
+        grad_before = (
+            dot(grad_after, w_down[cols], 1, 1) * slope_ref[:, cols].astype(F32)
+        ).astype(BF16)
         grads_up.append(dot(second_t, grad_before))
         back_up = back_up + dot(grad_before, w_up[:, cols], 1, 1)
     weave(even, grads_up, keep_ref, send_ref, slice(512, 1024))
@@ -176,17 +225,22 @@
         grad_after.astype(F32) + norm_back(normed_mid, inverse_mid, back_up)
     ).astype(BF16)
     middle_grad_ref[...] = middle_grad
-    grad = dot(attended_t[...], middle_grad)
+    grad = dot(attended_ref[...], middle_grad)
     weave(even, [grad[:, p * 128 : p * 128 + 128] for p in range(4)], keep_ref, send_ref,
           slice(1024, 1152))
 
 
 def backward_kernel(
-    core_ref, tokens_ref, packed_ref, keys_t_ref, probs_ref, attended_ref, middle_grad_ref,
-    first_t_ref, order_ref, w_out, w_qkv,
+    core_ref, tokens_ref, packed_ref, keys_t_ref, attended_ref, middle_grad_ref,
+    first_t_ref, order_ref, w_out, probs_hbm, w_qkv_hbm,
     keep_ref, send_ref, out0, out1, out2, out3,
-    grad_heads, grad_heads_t, products, query_grad_t, packed_grad,
+    grad_heads, grad_heads_t, products, query_grad_t, packed_grad, probs_ref, w_qkv, sems,
 ):
+    loads = load(
+        [(probs_hbm.at[pl.ds(g * 4, 4)], probs_ref.at[pl.ds(g * 4, 4)]) for g in range(4)]
+        + [(w_qkv_hbm, w_qkv)],
+        sems,
+    )
     even = core_ref[0] == 0
     middle_grad = middle_grad_ref[...]
     for group in range(4):
@@ -199,15 +253,16 @@
     head_of_row = lax.broadcasted_iota(jnp.int32, (128, TOKENS), 0) // HEAD
     head_of_lane = lax.broadcasted_iota(jnp.int32, (TOKENS, 128), 1) // HEAD
 
-    def attend_back(group, _):
+    def attend_back(group):
+        loads[group].wait()
         queries = packed_ref[group]
         values = packed_ref[8 + group]
         upstream = grad_heads[group]
-        upstream_t = grad_heads_t[pl.ds(pl.multiple_of(group * 128, 128), 128), :]
+        upstream_t = grad_heads_t[slice(group * 128, group * 128 + 128), :]
         grad_keys = jnp.zeros((TOKENS, 128), F32)
         grad_values = jnp.zeros((TOKENS, 128), F32)
         for head in range(4):
-            at = pl.ds(pl.multiple_of(group * 128 + head * HEAD, HEAD), HEAD)
+            at = slice(group * 128 + head * HEAD, group * 128 + head * HEAD + HEAD)
             masked_t = jnp.where(head_of_row == head, upstream_t, jnp.zeros_like(upstream_t))
             weights = probs_ref[group * 4 + head]
             total = jnp.sum(products[at, :], axis=0, keepdims=True)
@@ -221,9 +276,9 @@
             query_grad_t[at, :] = dot(keys_t_ref[at, :], scores).astype(BF16)
         packed_grad[4 + group] = grad_keys.astype(BF16)
         packed_grad[8 + group] = grad_values.astype(BF16)
-        return 0
-
-    lax.fori_loop(0, 4, attend_back, 0)
+
+    for group in range(4):
+        attend_back(group)
 
     identity = eye(TOKENS)
     for group in range(4):
@@ -231,6 +286,7 @@
             identity, query_grad_t[group * 128 : group * 128 + 128, :], 1, 1
         ).astype(BF16)
     first_t = first_t_ref[...]
+    loads[4].wait()
     back_qkv = jnp.zeros((TOKENS, 512), F32)
     grads = []
     for part in range(3):
@@ -252,74 +308,66 @@
 
 
 def merge_kernel(merged_ref, cots_ref, grad_ref):
-    for part in range(4):
-        rows = slice(part * 64, part * 64 + 64)
-        grad = sum(dot(merged_ref[near, rows], cots_ref[near]) for near in range(8))
-        for block in range(4):
-            grad_ref[part * 4 + block] = grad[block * 16 : block * 16 + 16].astype(BF16)
-
-
-def call(kernel, inputs, outputs, scratch, flops):
-    whole = pl.BlockSpec(memory_space=pltpu.VMEM)
+    grad = dot(merged_ref[...], cots_ref[...], 0, 0)
+    for block in range(16):
+        grad_ref[block] = grad[block * 16 : block * 16 + 16].astype(BF16)
+
+
+def call(kernel, inputs, held, outputs, saved, scratch, micros):
+    whole, there = pl.BlockSpec(memory_space=pltpu.VMEM), pl.BlockSpec(memory_space=pl.ANY)
+    specs = [whole if at < held else there for at in range(len(inputs))]
+    if inputs[0].ndim == 1:
+        specs[0] = pl.BlockSpec(memory_space=pltpu.SMEM)
     return pl.pallas_call(
         kernel,
         out_shape=[jax.ShapeDtypeStruct(shape, BF16) for shape in outputs],
-        in_specs=[
-            pl.BlockSpec(memory_space=pltpu.SMEM) if value.ndim == 1 else whole for value in inputs
-        ],
-        out_specs=[whole] * len(outputs),
+        in_specs=specs,
+        out_specs=[whole if at < saved else there for at in range(len(outputs))],
         scratch_shapes=scratch,
-        compiler_params=pltpu.CompilerParams(vmem_limit_bytes=58 * 2**20),
+        compiler_params=pltpu.CompilerParams(vmem_limit_bytes=56 * 2**20),
         cost_estimate=pl.CostEstimate(
-            flops=flops, bytes_accessed=25 * 2**20, transcendentals=3 * 2**20
+            flops=micros * 10**9, bytes_accessed=micros * 10**6, transcendentals=0
         ),
     )(*inputs)
 
 
-def window_pass(core, quads, bias, cotangent, w_qkv, w_qkv_t, w_out, w_up, w_down, w_merge):
-    order = token_order()
-    by_feature, field = (512, TOKENS), (TOKENS, 512)
-    level_two, merged_t, keep, send, *kept = call(
-        forward_kernel,
-        [core, *quads, jnp.asarray(order, BF16), bias, cotangent, w_qkv, w_qkv_t,
-         w_out, w_up, w_down, w_merge],
-        [(MERGED, 1024), (8, 256, MERGED), (64, 16, 1152), (64, 16, 1152),
-         field, (12, TOKENS, 128), by_feature, (16, TOKENS, TOKENS), by_feature, field,
-         by_feature],
-        [pltpu.VMEM(by_feature, BF16), pltpu.VMEM(by_feature, BF16),
-         pltpu.VMEM((TOKENS, 2048), F32), pltpu.VMEM((TOKENS, 2048), BF16),
-         pltpu.VMEM(by_feature, BF16)],
-        24 * 2**30,
-    )
-    late_keep, late_send, *grads = call(
-        backward_kernel,
-        [core, *kept, jnp.asarray(order.transpose(0, 2, 1), BF16), w_out, w_qkv],
-        [(64, 16, 384)] * 2 + [(MERGED, 512)] * 4,
-        [pltpu.VMEM((4, TOKENS, 128), BF16), pltpu.VMEM(by_feature, BF16),
-         pltpu.VMEM(by_feature, F32), pltpu.VMEM(by_feature, BF16),
-         pltpu.VMEM((12, TOKENS, 128), BF16)],
-        16 * 2**30,
-    )
-    return level_two, merged_t, keep, send, late_keep, late_send, grads
-
-
-def scatter_grad(keep, send):
+def vmem(*shape):
+    return pltpu.VMEM(shape, BF16)
+
+
+def add_kernel(keep_ref, arrived_ref, blocks_ref):
+    blocks_ref[...] = (keep_ref[...].astype(F32) + arrived_ref[...].astype(F32)).astype(BF16)
+
+
+def add_into_kernel(keep_ref, arrived_ref, _, blocks_ref):
+    add_kernel(keep_ref, arrived_ref, blocks_ref)
+
+
+def pair_sum(keep, send, blocks, place):
     arrived = lax.ppermute(send, "core", [(0, 1), (1, 0)])
-    blocks = (keep.astype(F32) + arrived.astype(F32)).astype(BF16)
-    landed = lax.all_to_all(blocks, PAIRS, 0, 0, tiled=True)
-    return jnp.sum(landed.astype(F32), axis=0)
+    tile = (16, 16, keep.shape[-1])
+    taken = pl.BlockSpec(tile, lambda step: (step, 0, 0))
+    inputs, specs, aliases = [keep, arrived], [taken, taken], {}
+    if blocks is not None:
+        inputs, specs = inputs + [blocks], specs + [pl.BlockSpec(memory_space=pl.ANY)]
+        aliases = {2: 0}
+    return pl.pallas_call(
+        add_kernel if blocks is None else add_into_kernel,
+        grid=(4,),
+        out_shape=jax.ShapeDtypeStruct((64, 16, 1536), BF16),
+        in_specs=specs,
+        out_specs=pl.BlockSpec(tile, lambda step: (step, 0, place)),
+        input_output_aliases=aliases,
+        compiler_params=pltpu.CompilerParams(vmem_limit_bytes=16 * 2**20),
+        cost_estimate=pl.CostEstimate(
+            flops=keep.size, bytes_accessed=6 * keep.size, transcendentals=0
+        ),
+    )(*inputs)
 
 
 def unweave(share):
     cols = share.shape[-1]
     return share.reshape(4, 4, cols).transpose(1, 0, 2).reshape(4, 4 * cols)
-
-
-def scatter_merge(merged_t, cotangents):
-    merged = lax.all_to_all(merged_t, NEAR, 0, 0, tiled=True)
-    grad, = call(merge_kernel, [merged, cotangents], [(16, 16, 1024)], [], 2**29)
-    landed = lax.all_to_all(grad, FAR, 0, 0, tiled=True)
-    return jnp.sum(landed.astype(F32), axis=0)
 
 
 def shifted_block(block, down, right):
@@ -347,7 +395,7 @@
     ]
 
 
-def roll_forth(corners, side):
+def roll_forth(corners):
     upper_left, upper_right, lower_left, lower_right = corners
     moved = [
         shifted_block(lower_right, 1, 1),
@@ -355,7 +403,6 @@
         shifted_block(upper_right, 0, 1),
         upper_left,
     ]
-    moved = [corner.reshape(side, side, 2, corner.shape[-1]) for corner in moved]
     upper = jnp.concatenate(moved[:2], axis=1)
     lower = jnp.concatenate(moved[2:], axis=1)
     return jnp.concatenate([upper, lower], axis=0).transpose(2, 0, 1, 3)
@@ -368,20 +415,60 @@
 
 
 def body(tokens, window_ids, cotangent, w_qkv, w_out, w_up, w_down, w_merge):
+    order = token_order()
+    by_feature, field, hidden_shape = (512, TOKENS), (TOKENS, 512), (TOKENS, 2048)
+    all_probs = (16, TOKENS, TOKENS)
+    core = lax.axis_index("core").reshape(1)
     quads = roll_back(tokens)
     cot = jnp.concatenate(roll_back(cotangent), axis=0)
-    cotangents = lax.all_gather(cot, NEAR)
-    core = lax.axis_index("core").reshape(1)
-    level_two, merged_t, keep, send, late_keep, late_send, grads = window_pass(
-        core, quads, window_bias(window_ids), cot, w_qkv, w_qkv.T, w_out, w_up, w_down, w_merge
-    )
-    grad_merge = scatter_merge(merged_t, cotangents)
-    share = scatter_grad(keep, send)
-    grad_qkv = unweave(scatter_grad(late_keep, late_send))
+    cotangents = lax.all_gather(cot, NEAR, tiled=True)
+
+    (level_two, merged, tokens_in, packed, keys_t, attended, first_t, middle, after_mlp, probs,
+     hidden, slope) = call(
+        forward_kernel,
+        [*quads, jnp.asarray(order, BF16), window_bias(window_ids), w_qkv, w_qkv.T,
+         w_out, w_up, w_down, w_merge], 8,
+        [(MERGED, 1024), (8, MERGED, 256), field, (12, TOKENS, 128), by_feature, by_feature,
+         by_feature, field, field, all_probs, hidden_shape, hidden_shape], 9,
+        [vmem(*by_feature), vmem(*by_feature), vmem(*hidden_shape), vmem(*hidden_shape),
+         vmem(*all_probs), vmem(*w_out.shape), vmem(*w_up.shape), vmem(*w_down.shape),
+         vmem(*w_merge.shape), pltpu.SemaphoreType.DMA((4,)), pltpu.SemaphoreType.DMA((3,))],
+        15,
+    )
+    keep, send, middle_grad = call(
+        middle_kernel,
+        [core, cot, middle, after_mlp, attended, w_merge, hidden, w_down, slope, w_up], 5,
+        [(64, 16, 1152), (64, 16, 1152), field], 3,
+        [vmem(*w_merge.shape), vmem(*hidden_shape), vmem(*w_down.shape), vmem(*hidden_shape),
+         vmem(*w_up.shape), pltpu.SemaphoreType.DMA((5,))],
+        12,
+    )
+    merged = lax.all_to_all(merged, NEAR, 0, 0, tiled=True).reshape(8 * MERGED, 256)
+    merge_part, = call(merge_kernel, [merged, cotangents], 2, [(16, 16, 1024)], 1, [], 3)
+    merge_part, middle_grad = lax.optimization_barrier((merge_part, middle_grad))
+    late_keep, late_send, *grads = call(
+        backward_kernel,
+        [core, tokens_in, packed, keys_t, attended, middle_grad, first_t,
+         jnp.asarray(order.transpose(0, 2, 1), BF16), w_out, probs, w_qkv], 9,
+        [(64, 16, 384)] * 2 + [(MERGED, 512)] * 4, 6,
+        [vmem(4, TOKENS, 128), vmem(*by_feature), pltpu.VMEM(by_feature, F32), vmem(*by_feature),
+         vmem(12, TOKENS, 128), vmem(*all_probs), vmem(*w_qkv.shape),
+         pltpu.SemaphoreType.DMA((5,))],
+        12,
+    )
+    merge_landed = lax.all_to_all(merge_part, FAR, 0, 0, tiled=True)
+    grad_merge = jnp.sum(merge_landed.astype(F32), axis=0)
+    level_two = level_two.reshape(4, 3, 3, 2, 1024)
+    level_two = roll_forth([level_two[quad] for quad in range(4)])
+
+    blocks = pair_sum(keep, send, None, 0)
+    blocks = pair_sum(late_keep, late_send, blocks, 3)
+    blocks, grad_merge, level_two = lax.optimization_barrier((blocks, grad_merge, level_two))
+    landed = lax.all_to_all(blocks, PAIRS, 0, 0, tiled=True)
+    share = jnp.sum(landed.astype(F32), axis=0)
     grad_down, grad_up = share[:, :512], unweave(share[:, 512:1024])
-    grad_out = unweave(share[:, 1024:])
-    grad_tokens = roll_forth(grads, 6)
-    level_two = roll_forth([level_two[quad * 18 : quad * 18 + 18] for quad in range(4)], 3)
+    grad_out, grad_qkv = unweave(share[:, 1024:1152]), unweave(share[:, 1152:])
+    grad_tokens = roll_forth([grad.reshape(6, 6, 2, 512) for grad in grads])
     return (level_two, grad_tokens, grad_qkv, grad_out, grad_up, grad_down, grad_merge)
 
 

time: 179 us -> 177 us (0.989)
  blocking collectives: 0 us -> 11 us
  Pallas kernels: 42.7 us -> 52.2 us
  other arithmetic: 11.8 us -> 5.81 us
  starting transfers between devices: 40.9 us -> 35 us
  local copies, waits for them, and re-layouts: 16.2 us -> 11.4 us
  waiting for transfers between devices: 50.8 us -> 46.6 us
    all_to_all x4 -> x2, waiting for transfers between devices: 22 us -> 0.01 us  [the longest x1 0.01 us: body(): merge_landed = lax.all_to_all(merge_part, FAR, 0, 0, tiled=True)]
    ppermute x12, waiting for transfers between devices: 28.8 us -> 46.5 us  [shifted_block(): return lax.ppermute(block, GRID, route)]
    all_to_all x0 -> x1, blocking collectives: none -> 11 us  [body(): lax.all_to_all(merged, NEAR, 0, 0, tiled=True).reshape(8 * MERGED, 256)]
    all_to_all x4 -> x2, starting transfers between devices: 20.2 us -> 9.78 us  [the longest x1 5.01 us: body(): landed = lax.all_to_all(blocks, PAIRS, 0, 0, tiled=True)]
    pallas_call x0 -> x2, Pallas kernels: none -> 7.65 us  [pair_sum(): pl.pallas_call(add_kernel if blocks is None else add_into_kernel, grid=(4...]
    convert_element_type x2 -> x0, other arithmetic: 5.91 us -> none  [scatter_grad(): blocks = (keep.astype(F32) + arrived.astype(F32)).astype(BF16)]
    ppermute x12, starting transfers between devices: 19.7 us -> 22.8 us  [shifted_block(): return lax.ppermute(block, GRID, route)]
    reshape x8 -> x4, local copies, waits for them, and re-layouts: 4.39 us -> 2.01 us  [body(): grad_tokens = roll_forth([grad.reshape(6, 6, 2, 512) for grad in grads])]
  transfers between devices with their start and end apart: 19 -> 17, of which waited for: 6 -> 5; matrix products, arithmetic and copies ran while one was open for 14% -> 7% of each run, Pallas kernels for 24% -> 28%
where the time goes in v3:
time: 177 us; the launch traced here: 176 us
  Pallas kernels  52.2 us (29%)
  waiting for transfers between devices  46.6 us (26%)
  starting transfers between devices  35 us (20%)
  between operations  14.2 us (8%)
  local copies, waits for them, and re-layouts  11.4 us (6%)
  blocking collectives  11 us (6%)
  other arithmetic  5.81 us (3%)
    ppermute x12, waiting for transfers between devices, shifted_block(): return lax.ppermute(block, GRID, route)  46.5 us
    pallas_call x4, Pallas kernels, call(): pl.pallas_call(kernel, out_shape=[jax.ShapeDtypeStruct(shape, BF16) for s...  44.6 us
    ppermute x12, starting transfers between devices, shifted_block(): return lax.ppermute(block, GRID, route)  22.8 us
    all_to_all x1, blocking collectives, body(): lax.all_to_all(merged, NEAR, 0, 0, tiled=True).reshape(8 * MERGED, 256)  11 us
    pallas_call x2, Pallas kernels, pair_sum(): pl.pallas_call(add_kernel if blocks is None else add_into_kernel, grid=(4...  7.65 us
    all_to_all x1, starting transfers between devices, body(): landed = lax.all_to_all(blocks, PAIRS, 0, 0, tiled=True)  5.01 us
    all_to_all x1, starting transfers between devices, body(): merge_landed = lax.all_to_all(merge_part, FAR, 0, 0, tiled=True)  4.76 us
  transfers between devices with their start and end apart: 17, of which 5 were waited for; matrix products, arithmetic and copies ran while one was open for 7% of the time, Pallas kernels for 28%

profile of v3, /device:TPU:0, one launch (start us, length us, event | category | flops | bytes accessed | tf_op | source)
XLA Modules:
  0.0 176.2 jit_solution(7371569572341721037)
XLA Ops:
  7.2 1.3 fusion
  8.6 5.1 %collective-permute-start = (bf16[72,512]{1,0:T(8,128)(2,1)S(1)}, bf16[72,512]{1,0:T(8,128)(2,1)S(1)}, u32[]{:S(2)}, u32[]{:S(2)}) collective-permute-start(bf16[72,512]{1,0:T(8,128)(2,1)S(1)} %reshape.91), channel_id=1, source_target_pairs={{0,15},{1,0},{2,1},{3,2},{4,3},{5,4},{6,5},{7,6},{8,7},{9,8},{10,9... | collective-permute-start | bytes 221192 | tf_op jit(solution)/shard_map/ppermute | solution.py:378
  13.7 4.1 %collective-permute-start.1 = (bf16[72,512]{1,0:T(8,128)(2,1)S(1)}, bf16[72,512]{1,0:T(8,128)(2,1)S(1)}, u32[]{:S(2)}, u32[]{:S(2)}) collective-permute-start(bf16[72,512]{1,0:T(8,128)(2,1)S(1)} %reshape.92), channel_id=1, source_target_pairs={{0,112},{1,113},{2,114},{3,115},{4,116},{5,117},{6,118},{7,119},{8... | collective-permute-start | bytes 221192 | tf_op jit(solution)/shard_map/ppermute | solution.py:378
  17.8 0.9 fusion.2
  18.8 1.1 collective-permute-start.3
  20.4 0.9 collective-permute-start.5
  21.3 0.8 reshape.94
  22.6 0.9 compare_select_fusion.bias_ref
  24.2 1.6 copy.24
  25.9 1.1 collective-permute-start.2
  27.8 2.1 %collective-permute-done.2.quad3 = bf16[72,512]{1,0:T(8,128)(2,1)S(1)} collective-permute-done((bf16[72,512]{1,0:T(8,128)(2,1)S(1)}, bf16[72,512]{1,0:T(8,128)(2,1)S(1)}, u32[]{:S(2)}, u32[]{:S(2)}) %collective-permute-start.2) | collective-permute-done | bytes 73760 | tf_op jit(solution)/shard_map/ppermute | solution.py:378
  30.6 17.5 %shard_map.153 = (bf16[72,1024]{1,0:T(8,128)(2,1)}, bf16[8,72,256]{2,1,0:T(8,128)(2,1)}, bf16[288,512]{1,0:T(8,128)(2,1)}, bf16[12,288,128]{2,1,0:T(8,128)(2,1)}...) custom-call(bf16[72,512]{1,0:T(8,128)(2,1)} %reshape.90.quad0, ...), custom_call_target="tpu_custom_call" | custom-call | flops 15000000512 | bytes 15000000 | tf_op jit(solution)/shard_map/pallas_call | solution.py:321
  48.0 12.7 %shard_map.155 = (bf16[64,16,1152]{2,1,0:T(8,128)(2,1)}, bf16[64,16,1152]{2,1,0:T(8,128)(2,1)}, bf16[288,512]{1,0:T(8,128)(2,1)}) custom-call(s32[1]{0:T(128)} %bitcast.core_ref, bf16[72,1024]{1,0:T(8,128)(2,1)} %pad_maximum_fusion.cot_ref, bf16[288,512]{1,0:T(8,128)(2,1)} %get-tuple-element.38.middle_ref, bf16[288,512]{1,0:T(8,128)(2,1)} %get-tuple-element.39.after_mlp_ref, ...), custom_call_target="tpu_custom_call" | custom-call | flops 12000000000 | bytes 12000000 | tf_op jit(solution)/shard_map/pallas_call | solution.py:321
  60.7 2.3 %collective-permute-start.7 = (bf16[64,16,1152]{2,1,0:T(8,128)(2,1)}, bf16[64,16,1152]{2,1,0:T(8,128)(2,1)}, u32[]{:S(2)}, u32[]{:S(2)}) collective-permute-start(bf16[64,16,1152]{2,1,0:T(8,128)(2,1)} %get-tuple-element.49), channel_id=1, source_target_pairs={{0,1},{1,0},{2,3},{3,2},{4,5},{5,4},{6,7},{7,6},{8,9},{9,8},{10,11... | collective-permute-start | bytes 7077896 | tf_op jit(solution)/shard_map/ppermute | solution.py:347
  63.1 11.0 %all_to_all.15 = bf16[8,72,256]{2,1,0:T(8,128)(2,1)} all-to-all(bf16[8,72,256]{2,1,0:T(8,128)(2,1)S(1)} %copy-done.3), channel_id=1, replica_groups=mesh['z'=4,'x_lo'=2,'y'=4,'x_hi'=2,'core'=2] {'y','core'}, dimensions={0} | all-to-all | bytes 589824 | tf_op jit(solution)/shard_map/all_to_all | solution.py:446
  74.0 2.8 %shard_map.154 = bf16[16,16,1024]{2,1,0:T(8,128)(2,1)} custom-call(bf16[576,256]{1,0:T(8,128)(2,1)} %bitcast.23, bf16[576,1024]{1,0:T(8,128)(2,1)} %all-gather.2.cloned.1.call-done.cots_ref), custom_call_target="tpu_custom_call" | custom-call | flops 3000000000 | bytes 3000000 | tf_op jit(solution)/shard_map/pallas_call | solution.py:321
  76.8 11.7 %shard_map.156 = (bf16[64,16,384]{2,1,0:T(8,128)(2,1)}, bf16[64,16,384]{2,1,0:T(8,128)(2,1)}, bf16[72,512]{1,0:T(8,128)(2,1)}, bf16[72,512]{1,0:T(8,128)(2,1)}, ...) custom-call(s32[1]{0:T(128)} %bitcast.core_ref, bf16[288,512]{1,0:T(8,128)(2,1)} %get-tuple-element.33.tokens_ref, ...), custom_call_target="tpu_custom_call" | custom-call | flops 12000000000 | bytes 12000000 | tf_op jit(solution)/shard_map/pallas_call | solution.py:321
  88.6 4.8 %all-to-all-start.1 = ((bf16[16,16,1024]{2,1,0:T(8,128)(2,1)}), bf16[16,16,1024]{2,1,0:T(8,128)(2,1)}, u32[]{:S(2)}, u32[]{:S(2)}) async-start(bf16[16,16,1024]{2,1,0:T(8,128)(2,1)} %shard_map.154), calls=%async_computation.1 | async-start | bytes 1048576 | tf_op jit(solution)/shard_map/all_to_all | solution.py:459
  93.7 3.5 %collective-permute-start.8 = (bf16[3,3,2,1024]{3,2,1,0:T(2,128)(2,1)S(1)}, bf16[3,3,2,1024]{3,2,1,0:T(2,128)(2,1)S(1)}, u32[]{:S(2)}, u32[]{:S(2)}) collective-permute-start(bf16[3,3,2,1024]{3,2,1,0:T(2,128)(2,1)S(1)} %squeeze.12), channel_id=1, source_target_pairs={{0,17},{1,18},{2,19},{3,20},{4,21},{5,22},{6,23},{7,24},{8,25},{9,... | collective-permute-start | bytes 110600 | tf_op jit(solution)/shard_map/ppermute | solution.py:378
  97.3 2.4 %collective-permute-start.9 = (bf16[3,3,2,1024]{3,2,1,0:T(2,128)(2,1)S(1)}, bf16[3,3,2,1024]{3,2,1,0:T(2,128)(2,1)S(1)}, u32[]{:S(2)}, u32[]{:S(2)}) collective-permute-start(bf16[3,3,2,1024]{3,2,1,0:T(2,128)(2,1)S(1)} %squeeze.13), channel_id=1, source_target_pairs={{0,16},{1,17},{2,18},{3,19},{4,20},{5,21},{6,22},{7,23},{8,24},{9,... | collective-permute-start | bytes 110600 | tf_op jit(solution)/shard_map/ppermute | solution.py:378
  99.7 4.3 %collective-permute-done.10 = bf16[3,3,2,1024]{3,2,1,0:T(2,128)(2,1)S(1)} collective-permute-done((bf16[3,3,2,1024]{3,2,1,0:T(2,128)(2,1)S(1)}, bf16[3,3,2,1024]{3,2,1,0:T(2,128)(2,1)S(1)}, u32[]{:S(2)}, u32[]{:S(2)}) %collective-permute-start.10) | collective-permute-done | bytes 36896 | tf_op jit(solution)/shard_map/ppermute | solution.py:378
  104.0 2.5 %collective-permute-done.8 = bf16[3,3,2,1024]{3,2,1,0:T(2,128)(2,1)S(1)} collective-permute-done((bf16[3,3,2,1024]{3,2,1,0:T(2,128)(2,1)S(1)}, bf16[3,3,2,1024]{3,2,1,0:T(2,128)(2,1)S(1)}, u32[]{:S(2)}, u32[]{:S(2)}) %collective-permute-start.8) | collective-permute-done | bytes 36896 | tf_op jit(solution)/shard_map/ppermute | solution.py:378
  106.5 0.9 maximum_bitcast_fusion.1
  107.4 4.2 %shard_map.157._ = bf16[64,16,1536]{2,1,0:T(8,128)(2,1)} custom-call(bf16[64,16,1152]{2,1,0:T(8,128)(2,1)S(1)} %copy-done, bf16[64,16,1152]{2,1,0:T(8,128)(2,1)} %collective-permute-done.7.arrived_ref), custom_call_target="tpu_custom_call" | custom-call | flops 1179648 | bytes 7077888 | tf_op jit(solution)/shard_map/pallas_call | solution.py:354
  111.6 1.8 convert_reduce_fusion.1
  113.4 3.4 %shard_map.158 = bf16[64,16,1536]{2,1,0:T(8,128)(2,1)} custom-call(bf16[64,16,384]{2,1,0:T(8,128)(2,1)S(1)} %copy-done.1, bf16[64,16,384]{2,1,0:T(8,128)(2,1)} %collective-permute-done.6.arrived_ref, bf16[64,16,1536]{2,1,0:T(8,128)(2,1)} %shard_map.157._), custom_call_target="tpu_custom_call", output_to_operand_aliasing={{}: (2, {})} | custom-call | flops 393216 | bytes 2359296 | tf_op jit(solution)/shard_map/pallas_call | solution.py:354
  116.8 5.0 %all-to-all-start.2 = ((bf16[64,16,1536]{2,1,0:T(8,128)(2,1)}), bf16[64,16,1536]{2,1,0:T(8,128)(2,1)S(1)}, u32[]{:S(2)}, u32[]{:S(2)}) async-start(bf16[64,16,1536]{2,1,0:T(8,128)(2,1)} %shard_map.158), calls=%async_computation.2 | async-start | bytes 6291456 | tf_op jit(solution)/shard_map/all_to_all | solution.py:467
  123.2 1.5 collective-permute-start.12
  125.4 2.2 %collective-permute-start.13 = (bf16[6,6,2,512]{3,2,1,0:T(2,128)(2,1)}, bf16[6,6,2,512]{3,2,1,0:T(2,128)(2,1)S(1)}, u32[]{:S(2)}, u32[]{:S(2)}) collective-permute-start(bf16[6,6,2,512]{3,2,1,0:T(2,128)(2,1)} %reshape.102), channel_id=1, source_target_pairs={{0,1},{1,2},{2,3},{3,4},{4,5},{5,6},{6,7},{7,8},{8,9},{9,10},{10,1... | collective-permute-start | bytes 221192 | tf_op jit(solution)/shard_map/ppermute | solution.py:378
  127.6 36.4 %collective-permute-done.11 = bf16[6,6,2,512]{3,2,1,0:T(2,128)(2,1)S(1)} collective-permute-done((bf16[6,6,2,512]{3,2,1,0:T(2,128)(2,1)}, bf16[6,6,2,512]{3,2,1,0:T(2,128)(2,1)S(1)}, u32[]{:S(2)}, u32[]{:S(2)}) %collective-permute-start.11) | collective-permute-done | bytes 73760 | tf_op jit(solution)/shard_map/ppermute | solution.py:378
  164.1 1.2 collective-permute-done.12
  165.2 1.1 maximum_bitcast_fusion
  (69 shorter events, 8.9 us)
Async XLA Ops:
  7.2 17.1 %copy-start.2 = (bf16[512,1536]{1,0:T(8,128)(2,1)S(1)}, bf16[512,1536]{1,0:T(8,128)(2,1)}, u32[]{:S(2)}) copy-start(bf16[512,1536]{1,0:T(8,128)(2,1)} %w_qkv_hbm.1) | copy-start | bytes 4718596
  7.2 66.8 %all-gather.2.cloned.1.call-start = ((), (), s32[]{:S(2)}) async-start(), calls=%async_computation.3 | async-start | bytes 1327104 | tf_op jit(solution)/shard_map/all_gather | solution.py:424
  8.6 19.2 %collective-permute-start = (bf16[72,512]{1,0:T(8,128)(2,1)S(1)}, bf16[72,512]{1,0:T(8,128)(2,1)S(1)}, u32[]{:S(2)}, u32[]{:S(2)}) collective-permute-start(bf16[72,512]{1,0:T(8,128)(2,1)S(1)} %reshape.91), channel_id=1, source_target_pairs={{0,15},{1,0},{2,1},{3,2},{4,3},{5,4},{6,5},{7,6},{8,7},{9,8},{10,9... | collective-permute-start | bytes 221192 | tf_op jit(solution)/shard_map/ppermute | solution.py:378
  13.7 14.1 %collective-permute-start.1 = (bf16[72,512]{1,0:T(8,128)(2,1)S(1)}, bf16[72,512]{1,0:T(8,128)(2,1)S(1)}, u32[]{:S(2)}, u32[]{:S(2)}) collective-permute-start(bf16[72,512]{1,0:T(8,128)(2,1)S(1)} %reshape.92), channel_id=1, source_target_pairs={{0,112},{1,113},{2,114},{3,115},{4,116},{5,117},{6,118},{7,119},{8... | collective-permute-start | bytes 221192 | tf_op jit(solution)/shard_map/ppermute | solution.py:378
  18.8 7.1 %collective-permute-start.3 = (bf16[18,1024]{1,0:T(8,128)(2,1)S(1)}, bf16[18,1024]{1,0:T(8,128)(2,1)S(1)}, u32[]{:S(2)}, u32[]{:S(2)}) collective-permute-start(bf16[18,1024]{1,0:T(8,128)(2,1)S(1)} %reshape.97), channel_id=1, source_target_pairs={{0,15},{1,0},{2,1},{3,2},{4,3},{5,4},{6,5},{7,6},{8,7},{9,8},{10,9... | collective-permute-start | bytes 110600 | tf_op jit(solution)/shard_map/ppermute | solution.py:378
  19.9 7.2 %collective-permute-start.4 = (bf16[18,1024]{1,0:T(8,128)(2,1)S(1)}, bf16[18,1024]{1,0:T(8,128)(2,1)S(1)}, u32[]{:S(2)}, u32[]{:S(2)}) collective-permute-start(bf16[18,1024]{1,0:T(8,128)(2,1)S(1)} %reshape.98), channel_id=1, source_target_pairs={{0,112},{1,113},{2,114},{3,115},{4,116},{5,117},{6,118},{7,119},{8... | collective-permute-start | bytes 110600 | tf_op jit(solution)/shard_map/ppermute | solution.py:378
  20.4 6.6 %collective-permute-start.5 = (bf16[18,1024]{1,0:T(8,128)(2,1)S(1)}, bf16[18,1024]{1,0:T(8,128)(2,1)S(1)}, u32[]{:S(2)}, u32[]{:S(2)}) collective-permute-start(bf16[18,1024]{1,0:T(8,128)(2,1)S(1)} %reshape.99), channel_id=1, source_target_pairs={{0,127},{1,112},{2,113},{3,114},{4,115},{5,116},{6,117},{7,118},{8... | collective-permute-start | bytes 110600 | tf_op jit(solution)/shard_map/ppermute | solution.py:378
  25.9 4.0 %collective-permute-start.2 = (bf16[72,512]{1,0:T(8,128)(2,1)S(1)}, bf16[72,512]{1,0:T(8,128)(2,1)S(1)}, u32[]{:S(2)}, u32[]{:S(2)}) collective-permute-start(bf16[72,512]{1,0:T(8,128)(2,1)S(1)} %reshape.93), channel_id=1, source_target_pairs={{0,127},{1,112},{2,113},{3,114},{4,115},{5,116},{6,117},{7,118},{8... | collective-permute-start | bytes 221192 | tf_op jit(solution)/shard_map/ppermute | solution.py:378
  27.8 2.2 %copy-start.9 = (bf16[72,512]{1,0:T(8,128)(2,1)}, bf16[72,512]{1,0:T(8,128)(2,1)S(1)}, u32[]{:S(2)}) copy-start(bf16[72,512]{1,0:T(8,128)(2,1)S(1)} %collective-permute-done.quad1) | copy-start | bytes 221188
  27.8 2.2 %copy-start.10 = (bf16[72,512]{1,0:T(8,128)(2,1)}, bf16[72,512]{1,0:T(8,128)(2,1)S(1)}, u32[]{:S(2)}) copy-start(bf16[72,512]{1,0:T(8,128)(2,1)S(1)} %collective-permute-done.1.quad2) | copy-start | bytes 221188
  29.9 0.6 copy-start.11
  48.0 15.0 %copy-start.3 = (bf16[8,72,256]{2,1,0:T(8,128)(2,1)S(1)}, bf16[8,72,256]{2,1,0:T(8,128)(2,1)}, u32[]{:S(2)}) copy-start(bf16[8,72,256]{2,1,0:T(8,128)(2,1)} %get-tuple-element.37) | copy-start | bytes 884740
  60.7 46.7 %collective-permute-start.7 = (bf16[64,16,1152]{2,1,0:T(8,128)(2,1)}, bf16[64,16,1152]{2,1,0:T(8,128)(2,1)}, u32[]{:S(2)}, u32[]{:S(2)}) collective-permute-start(bf16[64,16,1152]{2,1,0:T(8,128)(2,1)} %get-tuple-element.49), channel_id=1, source_target_pairs={{0,1},{1,0},{2,3},{3,2},{4,5},{5,4},{6,7},{7,6},{8,9},{9,8},{10,11... | collective-permute-start | bytes 7077896 | tf_op jit(solution)/shard_map/ppermute | solution.py:347
  76.8 16.5 %copy-start.4 = (bf16[72,1024]{1,0:T(8,128)(2,1)S(1)}, bf16[72,1024]{1,0:T(8,128)(2,1)}, u32[]{:S(2)}) copy-start(bf16[72,1024]{1,0:T(8,128)(2,1)} %get-tuple-element.51) | copy-start | bytes 442372
  76.8 30.6 %copy-start = (bf16[64,16,1152]{2,1,0:T(8,128)(2,1)S(1)}, bf16[64,16,1152]{2,1,0:T(8,128)(2,1)}, u32[]{:S(2)}) copy-start(bf16[64,16,1152]{2,1,0:T(8,128)(2,1)} %get-tuple-element.48.keep_ref) | copy-start | bytes 7077892
  88.5 24.9 %collective-permute-start.6 = (bf16[64,16,384]{2,1,0:T(8,128)(2,1)}, bf16[64,16,384]{2,1,0:T(8,128)(2,1)}, u32[]{:S(2)}, u32[]{:S(2)}) collective-permute-start(bf16[64,16,384]{2,1,0:T(8,128)(2,1)} %get-tuple-element.47), channel_id=1, source_target_pairs={{0,1},{1,0},{2,3},{3,2},{4,5},{5,4},{6,7},{7,6},{8,9},{9,8},{10,11... | collective-permute-start | bytes 2359304 | tf_op jit(solution)/shard_map/ppermute | solution.py:347
  88.6 23.1 %all-to-all-start.1 = ((bf16[16,16,1024]{2,1,0:T(8,128)(2,1)}), bf16[16,16,1024]{2,1,0:T(8,128)(2,1)}, u32[]{:S(2)}, u32[]{:S(2)}) async-start(bf16[16,16,1024]{2,1,0:T(8,128)(2,1)} %shard_map.154), calls=%async_computation.1 | async-start | bytes 1048576 | tf_op jit(solution)/shard_map/all_to_all | solution.py:459
  93.4 10.6 %collective-permute-start.10 = (bf16[3,3,2,1024]{3,2,1,0:T(2,128)(2,1)S(1)}, bf16[3,3,2,1024]{3,2,1,0:T(2,128)(2,1)S(1)}, u32[]{:S(2)}, u32[]{:S(2)}) collective-permute-start(bf16[3,3,2,1024]{3,2,1,0:T(2,128)(2,1)S(1)} %squeeze.14), channel_id=1, source_target_pairs={{0,1},{1,2},{2,3},{3,4},{4,5},{5,6},{6,7},{7,8},{8,9},{9,10},{10,1... | collective-permute-start | bytes 110600 | tf_op jit(solution)/shard_map/ppermute | solution.py:378
  93.7 12.8 %collective-permute-start.8 = (bf16[3,3,2,1024]{3,2,1,0:T(2,128)(2,1)S(1)}, bf16[3,3,2,1024]{3,2,1,0:T(2,128)(2,1)S(1)}, u32[]{:S(2)}, u32[]{:S(2)}) collective-permute-start(bf16[3,3,2,1024]{3,2,1,0:T(2,128)(2,1)S(1)} %squeeze.12), channel_id=1, source_target_pairs={{0,17},{1,18},{2,19},{3,20},{4,21},{5,22},{6,23},{7,24},{8,25},{9,... | collective-permute-start | bytes 110600 | tf_op jit(solution)/shard_map/ppermute | solution.py:378
  97.3 9.3 %collective-permute-start.9 = (bf16[3,3,2,1024]{3,2,1,0:T(2,128)(2,1)S(1)}, bf16[3,3,2,1024]{3,2,1,0:T(2,128)(2,1)S(1)}, u32[]{:S(2)}, u32[]{:S(2)}) collective-permute-start(bf16[3,3,2,1024]{3,2,1,0:T(2,128)(2,1)S(1)} %squeeze.13), channel_id=1, source_target_pairs={{0,16},{1,17},{2,18},{3,19},{4,20},{5,21},{6,22},{7,23},{8,24},{9,... | collective-permute-start | bytes 110600 | tf_op jit(solution)/shard_map/ppermute | solution.py:378
  107.4 6.0 %copy-start.1 = (bf16[64,16,384]{2,1,0:T(8,128)(2,1)S(1)}, bf16[64,16,384]{2,1,0:T(8,128)(2,1)}, u32[]{:S(2)}) copy-start(bf16[64,16,384]{2,1,0:T(8,128)(2,1)} %get-tuple-element.46.keep_ref) | copy-start | bytes 2359300
  116.8 5.0 %copy-start.8 = (bf16[72,512]{1,0:T(8,128)(2,1)S(1)}, bf16[72,512]{1,0:T(8,128)(2,1)}, u32[]{:S(2)}) copy-start(bf16[72,512]{1,0:T(8,128)(2,1)} %get-tuple-element.53) | copy-start | bytes 221188
  116.8 5.8 %copy-start.7 = (bf16[72,512]{1,0:T(8,128)(2,1)S(1)}, bf16[72,512]{1,0:T(8,128)(2,1)}, u32[]{:S(2)}) copy-start(bf16[72,512]{1,0:T(8,128)(2,1)} %get-tuple-element.54) | copy-start | bytes 221188
  116.8 7.9 %copy-start.6 = (bf16[72,512]{1,0:T(8,128)(2,1)S(1)}, bf16[72,512]{1,0:T(8,128)(2,1)}, u32[]{:S(2)}) copy-start(bf16[72,512]{1,0:T(8,128)(2,1)} %get-tuple-element.55) | copy-start | bytes 221188
  116.8 10.8 %copy-start.5 = (bf16[72,512]{1,0:T(8,128)(2,1)S(1)}, bf16[72,512]{1,0:T(8,128)(2,1)}, u32[]{:S(2)}) copy-start(bf16[72,512]{1,0:T(8,128)(2,1)} %get-tuple-element.56) | copy-start | bytes 221188
  116.8 49.6 %all-to-all-start.2 = ((bf16[64,16,1536]{2,1,0:T(8,128)(2,1)}), bf16[64,16,1536]{2,1,0:T(8,128)(2,1)S(1)}, u32[]{:S(2)}, u32[]{:S(2)}) async-start(bf16[64,16,1536]{2,1,0:T(8,128)(2,1)} %shard_map.158), calls=%async_computation.2 | async-start | bytes 6291456 | tf_op jit(solution)/shard_map/all_to_all | solution.py:467
  122.5 41.6 %collective-permute-start.11 = (bf16[6,6,2,512]{3,2,1,0:T(2,128)(2,1)}, bf16[6,6,2,512]{3,2,1,0:T(2,128)(2,1)S(1)}, u32[]{:S(2)}, u32[]{:S(2)}) collective-permute-start(bf16[6,6,2,512]{3,2,1,0:T(2,128)(2,1)} %reshape.100), channel_id=1, source_target_pairs={{0,17},{1,18},{2,19},{3,20},{4,21},{5,22},{6,23},{7,24},{8,25},{9,... | collective-permute-start | bytes 221192 | tf_op jit(solution)/shard_map/ppermute | solution.py:378
  123.2 42.0 %collective-permute-start.12 = (bf16[6,6,2,512]{3,2,1,0:T(2,128)(2,1)}, bf16[6,6,2,512]{3,2,1,0:T(2,128)(2,1)S(1)}, u32[]{:S(2)}, u32[]{:S(2)}) collective-permute-start(bf16[6,6,2,512]{3,2,1,0:T(2,128)(2,1)} %reshape.101), channel_id=1, source_target_pairs={{0,16},{1,17},{2,18},{3,19},{4,20},{5,21},{6,22},{7,23},{8,24},{9,... | collective-permute-start | bytes 221192 | tf_op jit(solution)/shard_map/ppermute | solution.py:378
  125.4 39.8 %collective-permute-start.13 = (bf16[6,6,2,512]{3,2,1,0:T(2,128)(2,1)}, bf16[6,6,2,512]{3,2,1,0:T(2,128)(2,1)S(1)}, u32[]{:S(2)}, u32[]{:S(2)}) collective-permute-start(bf16[6,6,2,512]{3,2,1,0:T(2,128)(2,1)} %reshape.102), channel_id=1, source_target_pairs={{0,1},{1,2},{2,3},{3,4},{4,5},{5,6},{6,7},{7,8},{8,9},{9,10},{10,1... | collective-permute-start | bytes 221192 | tf_op jit(solution)/shard_map/ppermute | solution.py:378
Sparse Core Ops, SparseCore 0:
  27.9 20.9 all-gather.1

commit v4 on v3

--- a/solution.py
+++ b/solution.py
@@ -20,11 +20,13 @@
 
 PAIRS = ("z", "x_lo", "y", "x_hi")
 NEAR = ("y", "core")
-FAR = ("z", "x_lo", "x_hi")
+
+
+PACKED = MERGED + 36
 
 
 def token_order():
-    order = np.zeros((4, TOKENS, MERGED), np.float32)
+    order = np.zeros((4, TOKENS, PACKED), np.float32)
     for quad in range(4):
         for row in range(6):
             for col in range(6):
@@ -32,6 +34,15 @@
                     position = (col % 2) * 2 + row % 2
                     patch = quad * 18 + (row // 2 * 3 + col // 2) * 2 + level
                     order[quad, position * MERGED + patch, (row * 6 + col) * 2 + level] = 1.0
+    return order
+
+
+def cotangent_order():
+    order = np.zeros((4, 2 * MERGED, PACKED), np.float32)
+    for quad in range(4):
+        for half in range(2):
+            for patch in range(18):
+                order[quad, half * MERGED + quad * 18 + patch, MERGED + half * 18 + patch] = 1.0
     return order
 
 
@@ -72,6 +83,18 @@
         send[:, rows, cols] = jnp.where(even, second, first).astype(BF16)
 
 
+def weave_all(grads):
+    tiles = [grad.reshape(32, 8, grad.shape[-1]) for grad in grads]
+    turned = [pltpu.roll(tile, 4, 1) for tile in tiles]
+    upper = lax.broadcasted_iota(jnp.int32, tiles[0].shape, 1) < 4
+    halves = []
+    for one, two in ((0, 1), (2, 3)):
+        first = jnp.where(upper, tiles[one], turned[two])
+        second = jnp.where(upper, turned[one], tiles[two])
+        halves.append(jnp.stack([first, second], axis=1))
+    return jnp.stack(halves, axis=2).reshape(64, 16, grads[0].shape[-1]).astype(BF16)
+
+
 def load(pairs, sems):
     copies = [pltpu.make_async_copy(*pair, sems.at[at]) for at, pair in enumerate(pairs)]
     for copy in copies:
@@ -92,16 +115,15 @@
 def near_order():
     source = lax.broadcasted_iota(jnp.int32, (512, 512), 0)
     target = lax.broadcasted_iota(jnp.int32, (512, 512), 1)
-    block = source // 16
-    near = block // 4 % 4 * 2 + block % 2
-    far = block // 16 * 2 + block // 2 % 2
-    return jnp.where(target == near * 64 + far * 16 + source % 16, 1.0, 0.0).astype(BF16)
+    near = source // 4 % 4 * 2 + source // 16 % 2
+    place = near * 64 + source // 32 * 4 + source % 4
+    return jnp.where(target == place, 1.0, 0.0).astype(BF16)
 
 
 def forward_kernel(
-    quad0, quad1, quad2, quad3, order_ref, bias_ref, w_qkv, w_qkv_t,
+    quad0, quad1, quad2, quad3, order_ref, cot_order_ref, bias_ref, w_qkv, w_qkv_t,
     w_out_hbm, w_up_hbm, w_down_hbm, w_merge_hbm,
-    level_two_ref, merged_ref, tokens_ref, packed_ref, keys_t_ref, attended_ref, first_t_ref,
+    cot_ref, level_two_ref, merged_ref, tokens_ref, packed_ref, keys_t_ref, attended_ref, first_t_ref,
     middle_ref, after_mlp_ref, probs_hbm, hidden_hbm, slope_hbm,
     query_t, values_t, slope_ref, hidden_ref, probs_ref, w_out, w_up, w_down, w_merge,
     in_sems, out_sems,
@@ -113,6 +135,9 @@
     quads = (quad0, quad1, quad2, quad3)
     tokens = sum(dot(order_ref[q], quads[q][...]) for q in range(4))
     tokens_ref[...] = tokens.astype(BF16)
+    halves = sum(dot(cot_order_ref[q], quads[q][...]) for q in range(4))
+    cot_ref[:, :512] = halves[:MERGED].astype(BF16)
+    cot_ref[:, 512:] = halves[MERGED:].astype(BF16)
     first_norm = normalize(tokens)[0].astype(BF16)
     first_t_ref[...] = dot(eye(512), first_norm, 1, 1).astype(BF16)
     for part in range(12):
@@ -307,24 +332,76 @@
         out[...] = dot(order_ref[quad], grad_tokens).astype(BF16)
 
 
-def merge_kernel(merged_ref, cots_ref, grad_ref):
+def assemble_kernel(
+    merged_ref, cots_ref, keep_hbm, arrived_hbm, blocks_hbm, keep_ref, arrived_ref, merge_ref,
+    keep_sems, arrived_sems, out_sems,
+):
+    parts = [pl.ds(p * 16, 16) for p in range(4)]
+    keeps = load([(keep_hbm.at[p], keep_ref.at[p]) for p in parts], keep_sems)
+    arrivals = load([(arrived_hbm.at[p], arrived_ref.at[p]) for p in parts], arrived_sems)
     grad = dot(merged_ref[...], cots_ref[...], 0, 0)
-    for block in range(16):
-        grad_ref[block] = grad[block * 16 : block * 16 + 16].astype(BF16)
-
-
-def call(kernel, inputs, held, outputs, saved, scratch, micros):
+    merge_ref[...] = weave_all([grad[:, q * 256 : q * 256 + 256] for q in range(4)])
+    saves = load(
+        [(merge_ref, blocks_hbm.at[:, :, pl.ds(1536, 256)])], out_sems.at[pl.ds(4, 1)]
+    )
+    for part, rows in enumerate(parts):
+        keeps[part].wait()
+        arrivals[part].wait()
+        total = keep_ref[rows].astype(F32) + arrived_ref[rows].astype(F32)
+        keep_ref[rows] = total.astype(BF16)
+        saves += load(
+            [(keep_ref.at[rows], blocks_hbm.at[rows, :, pl.ds(0, 1152)])],
+            out_sems.at[pl.ds(part, 1)],
+        )
+    for save in saves:
+        save.wait()
+
+
+def late_kernel(keep_ref, arrived_ref, _, blocks_hbm, total_ref, sem):
+    total = keep_ref[...].astype(F32) + arrived_ref[...].astype(F32)
+    total_ref[...] = total.astype(BF16)
+    save, = load([(total_ref, blocks_hbm.at[:, :, pl.ds(1152, 384)])], sem)
+    save.wait()
+
+
+def share_kernel(landed_hbm, qkv_ref, out_ref, up_ref, down_ref, merge_ref, landed_ref, sems):
+    loads = load(
+        [(landed_hbm.at[pl.ds(p * 16, 16)], landed_ref.at[pl.ds(p * 16, 16)]) for p in range(4)],
+        sems,
+    )
+    shared = jnp.zeros((16, 1536), F32)
+    merge = [jnp.zeros((16, 256), F32) for _ in range(4)]
+    for part in range(4):
+        loads[part].wait()
+        for chip in range(part * 16, part * 16 + 16):
+            y = chip // 2 % 4
+            shared = shared + landed_ref[chip, :, :1536].astype(F32)
+            merge[y] = merge[y] + landed_ref[chip, :, 1536:].astype(F32)
+    down_ref[...] = shared[:, :512]
+    for block in range(4):
+        rows = shared[block * 4 : block * 4 + 4]
+        up_ref[:, block * 512 : block * 512 + 512] = rows[:, 512:1024]
+        out_ref[:, block * 128 : block * 128 + 128] = rows[:, 1024:1152]
+        qkv_ref[:, block * 384 : block * 384 + 384] = rows[:, 1152:]
+        for y in range(4):
+            merge_ref[y * 4 : y * 4 + 4, block * 256 : block * 256 + 256] = merge[y][
+                block * 4 : block * 4 + 4
+            ]
+
+
+def call(kernel, inputs, held, outputs, saved, scratch, micros, kind=BF16, aliases=()):
     whole, there = pl.BlockSpec(memory_space=pltpu.VMEM), pl.BlockSpec(memory_space=pl.ANY)
     specs = [whole if at < held else there for at in range(len(inputs))]
     if inputs[0].ndim == 1:
         specs[0] = pl.BlockSpec(memory_space=pltpu.SMEM)
     return pl.pallas_call(
         kernel,
-        out_shape=[jax.ShapeDtypeStruct(shape, BF16) for shape in outputs],
+        out_shape=[jax.ShapeDtypeStruct(shape, kind) for shape in outputs],
         in_specs=specs,
         out_specs=[whole if at < saved else there for at in range(len(outputs))],
         scratch_shapes=scratch,
-        compiler_params=pltpu.CompilerParams(vmem_limit_bytes=56 * 2**20),
+        input_output_aliases=dict(aliases),
+        compiler_params=pltpu.CompilerParams(vmem_limit_bytes=(56 if micros > 9 else 24) * 2**20),
         cost_estimate=pl.CostEstimate(
             flops=micros * 10**9, bytes_accessed=micros * 10**6, transcendentals=0
         ),
@@ -335,39 +412,12 @@
     return pltpu.VMEM(shape, BF16)
 
 
-def add_kernel(keep_ref, arrived_ref, blocks_ref):
-    blocks_ref[...] = (keep_ref[...].astype(F32) + arrived_ref[...].astype(F32)).astype(BF16)
-
-
-def add_into_kernel(keep_ref, arrived_ref, _, blocks_ref):
-    add_kernel(keep_ref, arrived_ref, blocks_ref)
-
-
-def pair_sum(keep, send, blocks, place):
-    arrived = lax.ppermute(send, "core", [(0, 1), (1, 0)])
-    tile = (16, 16, keep.shape[-1])
-    taken = pl.BlockSpec(tile, lambda step: (step, 0, 0))
-    inputs, specs, aliases = [keep, arrived], [taken, taken], {}
-    if blocks is not None:
-        inputs, specs = inputs + [blocks], specs + [pl.BlockSpec(memory_space=pl.ANY)]
-        aliases = {2: 0}
-    return pl.pallas_call(
-        add_kernel if blocks is None else add_into_kernel,
-        grid=(4,),
-        out_shape=jax.ShapeDtypeStruct((64, 16, 1536), BF16),
-        in_specs=specs,
-        out_specs=pl.BlockSpec(tile, lambda step: (step, 0, place)),
-        input_output_aliases=aliases,
-        compiler_params=pltpu.CompilerParams(vmem_limit_bytes=16 * 2**20),
-        cost_estimate=pl.CostEstimate(
-            flops=keep.size, bytes_accessed=6 * keep.size, transcendentals=0
-        ),
-    )(*inputs)
-
-
-def unweave(share):
-    cols = share.shape[-1]
-    return share.reshape(4, 4, cols).transpose(1, 0, 2).reshape(4, 4 * cols)
+def dmas(count):
+    return pltpu.SemaphoreType.DMA((count,))
+
+
+def from_pair(send):
+    return lax.ppermute(send, "core", [(0, 1), (1, 0)])
 
 
 def shifted_block(block, down, right):
@@ -385,8 +435,12 @@
     return [corner.reshape(-1, field.shape[-1]) for corner in corners]
 
 
-def roll_back(field):
-    upper_left, upper_right, lower_left, lower_right = quadrants(field)
+def roll_back(tokens, cotangent):
+    corners = [
+        jnp.concatenate([corner, cot[:, :512], cot[:, 512:]], axis=0)
+        for corner, cot in zip(quadrants(tokens), quadrants(cotangent))
+    ]
+    upper_left, upper_right, lower_left, lower_right = corners
     return [
         lower_right,
         shifted_block(lower_left, 0, -1),
@@ -419,55 +473,58 @@
     by_feature, field, hidden_shape = (512, TOKENS), (TOKENS, 512), (TOKENS, 2048)
     all_probs = (16, TOKENS, TOKENS)
     core = lax.axis_index("core").reshape(1)
-    quads = roll_back(tokens)
-    cot = jnp.concatenate(roll_back(cotangent), axis=0)
-    cotangents = lax.all_gather(cot, NEAR, tiled=True)
-
-    (level_two, merged, tokens_in, packed, keys_t, attended, first_t, middle, after_mlp, probs,
+    quads = roll_back(tokens, cotangent)
+
+    (cot, level_two, merged, tokens_in, packed, keys_t, attended, first_t, middle, after_mlp, probs,
      hidden, slope) = call(
         forward_kernel,
-        [*quads, jnp.asarray(order, BF16), window_bias(window_ids), w_qkv, w_qkv.T,
-         w_out, w_up, w_down, w_merge], 8,
-        [(MERGED, 1024), (8, MERGED, 256), field, (12, TOKENS, 128), by_feature, by_feature,
-         by_feature, field, field, all_probs, hidden_shape, hidden_shape], 9,
+        [*quads, jnp.asarray(order, BF16), jnp.asarray(cotangent_order(), BF16),
+         window_bias(window_ids), w_qkv, w_qkv.T, w_out, w_up, w_down, w_merge], 9,
+        [(MERGED, 1024), (MERGED, 1024), (8, MERGED, 256), field, (12, TOKENS, 128), by_feature, by_feature,
+         by_feature, field, field, all_probs, hidden_shape, hidden_shape], 10,
         [vmem(*by_feature), vmem(*by_feature), vmem(*hidden_shape), vmem(*hidden_shape),
          vmem(*all_probs), vmem(*w_out.shape), vmem(*w_up.shape), vmem(*w_down.shape),
-         vmem(*w_merge.shape), pltpu.SemaphoreType.DMA((4,)), pltpu.SemaphoreType.DMA((3,))],
+         vmem(*w_merge.shape), dmas(4), dmas(3)],
         15,
     )
+    cotangents = lax.all_gather(cot, NEAR, tiled=True)
+    merged = lax.all_to_all(merged, NEAR, 0, 0, tiled=True).reshape(8 * MERGED, 256)
     keep, send, middle_grad = call(
         middle_kernel,
         [core, cot, middle, after_mlp, attended, w_merge, hidden, w_down, slope, w_up], 5,
         [(64, 16, 1152), (64, 16, 1152), field], 3,
         [vmem(*w_merge.shape), vmem(*hidden_shape), vmem(*w_down.shape), vmem(*hidden_shape),
-         vmem(*w_up.shape), pltpu.SemaphoreType.DMA((5,))],
+         vmem(*w_up.shape), dmas(5)],
         12,
     )
-    merged = lax.all_to_all(merged, NEAR, 0, 0, tiled=True).reshape(8 * MERGED, 256)
-    merge_part, = call(merge_kernel, [merged, cotangents], 2, [(16, 16, 1024)], 1, [], 3)
-    merge_part, middle_grad = lax.optimization_barrier((merge_part, middle_grad))
     late_keep, late_send, *grads = call(
         backward_kernel,
         [core, tokens_in, packed, keys_t, attended, middle_grad, first_t,
-         jnp.asarray(order.transpose(0, 2, 1), BF16), w_out, probs, w_qkv], 9,
+         jnp.asarray(order[:, :, :MERGED].transpose(0, 2, 1), BF16), w_out, probs, w_qkv], 9,
         [(64, 16, 384)] * 2 + [(MERGED, 512)] * 4, 6,
         [vmem(4, TOKENS, 128), vmem(*by_feature), pltpu.VMEM(by_feature, F32), vmem(*by_feature),
          vmem(12, TOKENS, 128), vmem(*all_probs), vmem(*w_qkv.shape),
-         pltpu.SemaphoreType.DMA((5,))],
+         dmas(5)],
         12,
     )
-    merge_landed = lax.all_to_all(merge_part, FAR, 0, 0, tiled=True)
-    grad_merge = jnp.sum(merge_landed.astype(F32), axis=0)
+    blocks, = call(
+        assemble_kernel, [merged, cotangents, keep, from_pair(send)], 2,
+        [(64, 16, 1792)], 0,
+        [vmem(64, 16, 1152), vmem(64, 16, 1152), vmem(64, 16, 256), dmas(4), dmas(4), dmas(5)],
+        4,
+    )
+    blocks, = call(
+        late_kernel, [late_keep, from_pair(late_send), blocks], 2, [blocks.shape], 0,
+        [vmem(64, 16, 384), dmas(1)], 2, aliases={2: 0},
+    )
+    landed = lax.all_to_all(blocks, PAIRS, 0, 0, tiled=True)
+    grad_qkv, grad_out, grad_up, grad_down, grad_merge = call(
+        share_kernel, [landed], 0,
+        [(4, 1536), (4, 512), (4, 2048), (16, 512), (16, 1024)], 5,
+        [vmem(*blocks.shape), dmas(4)], 3, kind=F32,
+    )
     level_two = level_two.reshape(4, 3, 3, 2, 1024)
     level_two = roll_forth([level_two[quad] for quad in range(4)])
-
-    blocks = pair_sum(keep, send, None, 0)
-    blocks = pair_sum(late_keep, late_send, blocks, 3)
-    blocks, grad_merge, level_two = lax.optimization_barrier((blocks, grad_merge, level_two))
-    landed = lax.all_to_all(blocks, PAIRS, 0, 0, tiled=True)
-    share = jnp.sum(landed.astype(F32), axis=0)
-    grad_down, grad_up = share[:, :512], unweave(share[:, 512:1024])
-    grad_out, grad_qkv = unweave(share[:, 1024:1152]), unweave(share[:, 1152:])
     grad_tokens = roll_forth([grad.reshape(6, 6, 2, 512) for grad in grads])
     return (level_two, grad_tokens, grad_qkv, grad_out, grad_up, grad_down, grad_merge)
 

time: 177 us -> 162 us (0.915)
  starting transfers between devices: 35 us -> 26.4 us
  Pallas kernels: 52.2 us -> 47.6 us
  other arithmetic: 5.81 us -> 3.61 us
    ppermute x12 -> x9, starting transfers between devices: 22.8 us -> 16 us  [shifted_block(): return lax.ppermute(block, GRID, route)]
    all_to_all x1 -> x0, starting transfers between devices: 4.76 us -> none  [body(): merge_landed = lax.all_to_all(merge_part, FAR, 0, 0, tiled=True)]
    unnamed x25 -> x31, local copies, waits for them, and re-layouts: 2.31 us -> 7.07 us
    pallas_call x6, Pallas kernels: 52.2 us -> 47.6 us  [call(): pl.pallas_call(kernel, out_shape=[jax.ShapeDtypeStruct(shape, kind) for s...]
    all_to_all x1, starting transfers between devices: 5.01 us -> 8.82 us  [body(): landed = lax.all_to_all(blocks, PAIRS, 0, 0, tiled=True)]
    reduce_sum x2 -> x0, other arithmetic: 2.2 us -> none  [the longest x1 1.75 us: body(): grad_merge = jnp.sum(merge_landed.astype(F32), axis=0)]
    slice x4, local copies, waits for them, and re-layouts: 2.15 us -> 0.02 us  [roll_back(): cot[:, :512]]
    reshape x4, local copies, waits for them, and re-layouts: 2.01 us -> 0.14 us  [body(): grad_tokens = roll_forth([grad.reshape(6, 6, 2, 512) for grad in grads])]
  transfers between devices with their start and end apart: 17 -> 13, of which waited for: 5 -> 6; matrix products, arithmetic and copies ran while one was open for 7% -> 4% of each run, Pallas kernels for 28% -> 9%
where the time goes in v4:
time: 162 us; the launch traced here: 161 us
  waiting for transfers between devices  48 us (30%)
  Pallas kernels  47.6 us (29%)
  starting transfers between devices  26.4 us (16%)
  between operations  14.4 us (9%)
  blocking collectives  10.8 us (7%)
  local copies, waits for them, and re-layouts  10.5 us (6%)
  other arithmetic  3.61 us (2%)
    pallas_call x6, Pallas kernels, call(): pl.pallas_call(kernel, out_shape=[jax.ShapeDtypeStruct(shape, kind) for s...  47.6 us
    ppermute x9, waiting for transfers between devices, shifted_block(): return lax.ppermute(block, GRID, route)  46.7 us
    ppermute x9, starting transfers between devices, shifted_block(): return lax.ppermute(block, GRID, route)  16 us
    all_to_all x1, blocking collectives, body(): lax.all_to_all(merged, NEAR, 0, 0, tiled=True).reshape(8 * MERGED, 256)  10.8 us
    all_to_all x1, starting transfers between devices, body(): landed = lax.all_to_all(blocks, PAIRS, 0, 0, tiled=True)  8.82 us
    unnamed x31, local copies, waits for them, and re-layouts  7.07 us
  transfers between devices with their start and end apart: 13, of which 6 were waited for; matrix products, arithmetic and copies ran while one was open for 4% of the time, Pallas kernels for 9%

profile of v4, /device:TPU:0, one launch (start us, length us, event | category | flops | bytes accessed | tf_op | source)
XLA Modules:
  0.0 161.3 jit_solution(15537396168400589303)
XLA Ops:
  7.2 1.0 fusion.2
  8.3 1.2 fusion
  9.6 5.1 %collective-permute-start = (bf16[108,512]{1,0:T(8,128)(2,1)S(1)}, bf16[108,512]{1,0:T(8,128)(2,1)S(1)}, u32[]{:S(2)}, u32[]{:S(2)}) collective-permute-start(bf16[108,512]{1,0:T(8,128)(2,1)S(1)} %pad_maximum_fusion.1), channel_id=1, source_target_pairs={{0,15},{1,0},{2,1},{3,2},{4,3},{5,4},{6,5},{7,6},{8,7},{9,8},{10,9... | collective-permute-start | bytes 331784 | tf_op jit(solution)/shard_map/ppermute | solution.py:428
  14.8 4.1 %collective-permute-start.1 = (bf16[108,512]{1,0:T(8,128)(2,1)S(1)}, bf16[108,512]{1,0:T(8,128)(2,1)S(1)}, u32[]{:S(2)}, u32[]{:S(2)}) collective-permute-start(bf16[108,512]{1,0:T(8,128)(2,1)S(1)} %pad_maximum_fusion.2), channel_id=1, source_target_pairs={{0,112},{1,113},{2,114},{3,115},{4,116},{5,117},{6,118},{7,119},{8... | collective-permute-start | bytes 331784 | tf_op jit(solution)/shard_map/ppermute | solution.py:428
  19.0 0.4 collective-permute-start.2
  19.6 0.3 copy.21
  20.2 0.9 compare_select_fusion.bias_ref
  21.1 1.6 copy.22
  22.7 0.7 pad_maximum_fusion.quad0
  23.4 0.6 copy-done.12
  24.1 17.7 %shard_map.162 = (bf16[72,1024]{1,0:T(8,128)(2,1)}, bf16[72,1024]{1,0:T(8,128)(2,1)}, bf16[8,72,256]{2,1,0:T(8,128)(2,1)}, bf16[288,512]{1,0:T(8,128)(2,1)}, bf1...) custom-call(bf16[108,512]{1,0:T(8,128)(2,1)} %pad_maximum_fusion.qua, ...), custom_call_target="tpu_custom_call" | custom-call | flops 15000000512 | bytes 15000000 | tf_op jit(solution)/shard_map/pallas_call | solution.py:397
  41.8 12.7 %shard_map.163 = (bf16[64,16,1152]{2,1,0:T(8,128)(2,1)}, bf16[64,16,1152]{2,1,0:T(8,128)(2,1)}, bf16[288,512]{1,0:T(8,128)(2,1)}) custom-call(s32[1]{0:T(128)} %bitcast.5.core_ref, bf16[72,1024]{1,0:T(8,128)(2,1)} %get-tuple-element.39.cot_ref, bf16[288,512]{1,0:T(8,128)(2,1)} %get-tuple-element.40.middle_ref, ...), custom_call_target="tpu_custom_call" | custom-call | flops 12000000000 | bytes 12000000 | tf_op jit(solution)/shard_map/pallas_call | solution.py:397
  54.5 1.5 collective-permute-start.10
  56.0 11.6 %shard_map.164 = (bf16[64,16,384]{2,1,0:T(8,128)(2,1)}, bf16[64,16,384]{2,1,0:T(8,128)(2,1)}, bf16[72,512]{1,0:T(8,128)(2,1)}, bf16[72,512]{1,0:T(8,128)(2,1)}, ...) custom-call(s32[1]{0:T(128)} %bitcast.5.core_ref, bf16[288,512]{1,0:T(8,128)(2,1)} %get-tuple-element.35.tokens_ref, ...), custom_call_target="tpu_custom_call" | custom-call | flops 12000000000 | bytes 12000000 | tf_op jit(solution)/shard_map/pallas_call | solution.py:397
  67.7 10.8 %all_to_all.10 = bf16[8,72,256]{2,1,0:T(8,128)(2,1)S(1)} all-to-all(bf16[8,72,256]{2,1,0:T(8,128)(2,1)S(1)} %copy-done.5), channel_id=1, replica_groups=mesh['z'=4,'x_lo'=2,'y'=4,'x_hi'=2,'core'=2] {'y','core'}, dimensions={0} | all-to-all | bytes 589824 | tf_op jit(solution)/shard_map/all_to_all | solution.py:491
  78.5 1.3 all-gather.2.cloned.1.call-done.cots_ref
  79.8 1.3 copy-done.2
  81.1 1.7 %copy-done.3 = bf16[64,16,1152]{2,1,0:T(8,128)(2,1)S(1)} copy-done((bf16[64,16,1152]{2,1,0:T(8,128)(2,1)S(1)}, bf16[64,16,1152]{2,1,0:T(8,128)(2,1)}, u32[]{:S(2)}) %copy-start.3) | copy-done | bytes 2359320
  82.7 2.5 %shard_map.165._ = bf16[64,16,1792]{2,1,0:T(8,128)(2,1)S(1)} custom-call(bf16[576,256]{1,0:T(8,128)(2,1)S(1)} %bitcast.10, bf16[576,1024]{1,0:T(8,128)(2,1)S(1)} %copy-done.2, bf16[64,16,1152]{2,1,0:T(8,128)(2,1)S(1)} %copy-done.3, bf16[64,16,1152]{2,1,0:T(8,128)(2,1)S(1)} %collective-permute-done.10.arrived_hbm), custom_call_target="tpu_custom_call" | custom-call | flops 4000000000 | bytes 4000000 | tf_op jit(solution)/shard_map/pallas_call | solution.py:397
  85.5 1.8 %copy-done = bf16[64,16,1792]{2,1,0:T(8,128)(2,1)} copy-done((bf16[64,16,1792]{2,1,0:T(8,128)(2,1)}, bf16[64,16,1792]{2,1,0:T(8,128)(2,1)S(1)}, u32[]{:S(2)}) %copy-start) | copy-done | bytes 3670040
  87.3 8.8 %all-to-all-start.1 = ((bf16[64,16,1792]{2,1,0:T(8,128)(2,1)}), bf16[64,16,1792]{2,1,0:T(8,128)(2,1)}, u32[]{:S(2)}, u32[]{:S(2)}) async-start(bf16[64,16,1792]{2,1,0:T(8,128)(2,1)} %copy-done), calls=%async_computation.1 | async-start | bytes 7340032 | tf_op jit(solution)/shard_map/all_to_all | solution.py:520
  96.4 1.6 collective-permute-start.4
  98.0 3.9 %collective-permute-start.3 = (bf16[3,3,2,1024]{3,2,1,0:T(2,128)(2,1)S(1)}, bf16[3,3,2,1024]{3,2,1,0:T(2,128)(2,1)S(1)}, u32[]{:S(2)}, u32[]{:S(2)}) collective-permute-start(bf16[3,3,2,1024]{3,2,1,0:T(2,128)(2,1)S(1)} %squeeze.12), channel_id=1, source_target_pairs={{0,17},{1,18},{2,19},{3,20},{4,21},{5,22},{6,23},{7,24},{8,25},{9,... | collective-permute-start | bytes 110600 | tf_op jit(solution)/shard_map/ppermute | solution.py:428
  102.2 0.7 collective-permute-start.7
  102.9 38.4 %collective-permute-done.5 = bf16[3,3,2,1024]{3,2,1,0:T(2,128)(2,1)S(1)} collective-permute-done((bf16[3,3,2,1024]{3,2,1,0:T(2,128)(2,1)S(1)}, bf16[3,3,2,1024]{3,2,1,0:T(2,128)(2,1)S(1)}, u32[]{:S(2)}, u32[]{:S(2)}) %collective-permute-start.5) | collective-permute-done | bytes 36896 | tf_op jit(solution)/shard_map/ppermute | solution.py:428
  141.3 1.4 collective-permute-done.4
  142.7 2.1 %collective-permute-done.3 = bf16[3,3,2,1024]{3,2,1,0:T(2,128)(2,1)S(1)} collective-permute-done((bf16[3,3,2,1024]{3,2,1,0:T(2,128)(2,1)S(1)}, bf16[3,3,2,1024]{3,2,1,0:T(2,128)(2,1)S(1)}, u32[]{:S(2)}, u32[]{:S(2)}) %collective-permute-start.3) | collective-permute-done | bytes 36896 | tf_op jit(solution)/shard_map/ppermute | solution.py:428
  144.8 0.9 maximum_bitcast_fusion.1
  145.7 0.8 collective-permute-done.7
  146.4 4.0 %collective-permute-done.6 = bf16[6,6,2,512]{3,2,1,0:T(2,128)(2,1)S(1)} collective-permute-done((bf16[6,6,2,512]{3,2,1,0:T(2,128)(2,1)S(1)}, bf16[6,6,2,512]{3,2,1,0:T(2,128)(2,1)S(1)}, u32[]{:S(2)}, u32[]{:S(2)}) %collective-permute-start.6) | collective-permute-done | bytes 73760 | tf_op jit(solution)/shard_map/ppermute | solution.py:428
  150.5 1.1 maximum_bitcast_fusion
  151.6 2.8 %shard_map.167 = (f32[4,1536]{1,0:T(4,128)}, f32[4,512]{1,0:T(4,128)}, f32[4,2048]{1,0:T(4,128)}, f32[16,512]{1,0:T(8,128)}, f32[16,1024]{1,0:T(8,128)}) custom-call(bf16[64,16,1792]{2,1,0:T(8,128)(2,1)} %all-to-all-done.1.landed_hbm), custom_call_target="tpu_custom_call" | custom-call | flops 3000000000 | bytes 3000000 | tf_op jit(solution)/shard_map/pallas_call | solution.py:397
  (67 shorter events, 1.6 us)
Async XLA Ops:
  7.2 12.3 %copy-start.11 = (s32[12,12]{1,0:T(8,128)S(1)}, s32[12,12]{1,0:T(8,128)}, u32[]{:S(2)}) copy-start(s32[12,12]{1,0:T(8,128)} %param.12) | copy-start | bytes 1732
  7.2 13.9 %copy-start.4 = (bf16[512,1536]{1,0:T(8,128)(2,1)S(1)}, bf16[512,1536]{1,0:T(8,128)(2,1)}, u32[]{:S(2)}) copy-start(bf16[512,1536]{1,0:T(8,128)(2,1)} %w_qkv_hbm.1) | copy-start | bytes 4718596
  7.2 72.6 %all-gather.2.cloned.1.call-start = ((), (), s32[]{:S(2)}) async-start(), calls=%async_computation.2 | async-start | bytes 1327104 | tf_op jit(solution)/shard_map/all_gather | solution.py:490
  9.6 13.8 %collective-permute-start = (bf16[108,512]{1,0:T(8,128)(2,1)S(1)}, bf16[108,512]{1,0:T(8,128)(2,1)S(1)}, u32[]{:S(2)}, u32[]{:S(2)}) collective-permute-start(bf16[108,512]{1,0:T(8,128)(2,1)S(1)} %pad_maximum_fusion.1), channel_id=1, source_target_pairs={{0,15},{1,0},{2,1},{3,2},{4,3},{5,4},{6,5},{7,6},{8,7},{9,8},{10,9... | collective-permute-start | bytes 331784 | tf_op jit(solution)/shard_map/ppermute | solution.py:428
  14.8 8.6 %collective-permute-start.1 = (bf16[108,512]{1,0:T(8,128)(2,1)S(1)}, bf16[108,512]{1,0:T(8,128)(2,1)S(1)}, u32[]{:S(2)}, u32[]{:S(2)}) collective-permute-start(bf16[108,512]{1,0:T(8,128)(2,1)S(1)} %pad_maximum_fusion.2), channel_id=1, source_target_pairs={{0,112},{1,113},{2,114},{3,115},{4,116},{5,117},{6,118},{7,119},{8... | collective-permute-start | bytes 331784 | tf_op jit(solution)/shard_map/ppermute | solution.py:428
  19.0 4.4 %collective-permute-start.2 = (bf16[108,512]{1,0:T(8,128)(2,1)S(1)}, bf16[108,512]{1,0:T(8,128)(2,1)S(1)}, u32[]{:S(2)}, u32[]{:S(2)}) collective-permute-start(bf16[108,512]{1,0:T(8,128)(2,1)S(1)} %pad_maximum_fusion.3), channel_id=1, source_target_pairs={{0,127},{1,112},{2,113},{3,114},{4,115},{5,116},{6,117},{7,118},{8... | collective-permute-start | bytes 331784 | tf_op jit(solution)/shard_map/ppermute | solution.py:428
  23.3 0.6 copy-start.12
  23.4 0.7 copy-start.13
  23.4 0.7 copy-start.14
  54.5 25.3 %collective-permute-start.10 = (bf16[64,16,1152]{2,1,0:T(8,128)(2,1)}, bf16[64,16,1152]{2,1,0:T(8,128)(2,1)S(1)}, u32[]{:S(2)}, u32[]{:S(2)}) collective-permute-start(bf16[64,16,1152]{2,1,0:T(8,128)(2,1)} %get-tuple-element.55), channel_id=1, source_target_pairs={{0,1},{1,0},{2,3},{3,2},{4,5},{5,4},{6,7},{7,6},{8,9},{9,8},{10,11... | collective-permute-start | bytes 7077896 | tf_op jit(solution)/shard_map/ppermute | solution.py:420
  56.0 11.7 %copy-start.5 = (bf16[8,72,256]{2,1,0:T(8,128)(2,1)S(1)}, bf16[8,72,256]{2,1,0:T(8,128)(2,1)}, u32[]{:S(2)}) copy-start(bf16[8,72,256]{2,1,0:T(8,128)(2,1)} %get-tuple-element.53) | copy-start | bytes 884740
  67.6 17.6 %collective-permute-start.9 = (bf16[64,16,384]{2,1,0:T(8,128)(2,1)}, bf16[64,16,384]{2,1,0:T(8,128)(2,1)S(1)}, u32[]{:S(2)}, u32[]{:S(2)}) collective-permute-start(bf16[64,16,384]{2,1,0:T(8,128)(2,1)} %get-tuple-element.52), channel_id=1, source_target_pairs={{0,1},{1,0},{2,3},{3,2},{4,5},{5,4},{6,7},{7,6},{8,9},{9,8},{10,11... | collective-permute-start | bytes 2359304 | tf_op jit(solution)/shard_map/ppermute | solution.py:420
  79.8 1.3 copy-start.2
  81.1 1.7 %copy-start.3 = (bf16[64,16,1152]{2,1,0:T(8,128)(2,1)S(1)}, bf16[64,16,1152]{2,1,0:T(8,128)(2,1)}, u32[]{:S(2)}) copy-start(bf16[64,16,1152]{2,1,0:T(8,128)(2,1)} %get-tuple-element.54.keep_hbm) | copy-start | bytes 7077892
  82.7 2.5 %copy-start.1 = (bf16[64,16,384]{2,1,0:T(8,128)(2,1)S(1)}, bf16[64,16,384]{2,1,0:T(8,128)(2,1)}, u32[]{:S(2)}) copy-start(bf16[64,16,384]{2,1,0:T(8,128)(2,1)} %get-tuple-element.51.keep_ref) | copy-start | bytes 2359300
  85.5 1.8 %copy-start = (bf16[64,16,1792]{2,1,0:T(8,128)(2,1)}, bf16[64,16,1792]{2,1,0:T(8,128)(2,1)S(1)}, u32[]{:S(2)}) copy-start(bf16[64,16,1792]{2,1,0:T(8,128)(2,1)S(1)} %shard_map.166) | copy-start | bytes 11010052
  87.3 8.9 %copy-start.6 = (bf16[72,1024]{1,0:T(8,128)(2,1)S(1)}, bf16[72,1024]{1,0:T(8,128)(2,1)}, u32[]{:S(2)}) copy-start(bf16[72,1024]{1,0:T(8,128)(2,1)} %get-tuple-element.34) | copy-start | bytes 442372
  87.3 14.6 %copy-start.10 = (bf16[72,512]{1,0:T(8,128)(2,1)S(1)}, bf16[72,512]{1,0:T(8,128)(2,1)}, u32[]{:S(2)}) copy-start(bf16[72,512]{1,0:T(8,128)(2,1)} %get-tuple-element.50) | copy-start | bytes 221188
  87.3 14.6 %copy-start.9 = (bf16[72,512]{1,0:T(8,128)(2,1)S(1)}, bf16[72,512]{1,0:T(8,128)(2,1)}, u32[]{:S(2)}) copy-start(bf16[72,512]{1,0:T(8,128)(2,1)} %get-tuple-element.49) | copy-start | bytes 221188
  87.3 14.8 %copy-start.8 = (bf16[72,512]{1,0:T(8,128)(2,1)S(1)}, bf16[72,512]{1,0:T(8,128)(2,1)}, u32[]{:S(2)}) copy-start(bf16[72,512]{1,0:T(8,128)(2,1)} %get-tuple-element.48) | copy-start | bytes 221188
  87.3 15.5 %copy-start.7 = (bf16[72,512]{1,0:T(8,128)(2,1)S(1)}, bf16[72,512]{1,0:T(8,128)(2,1)}, u32[]{:S(2)}) copy-start(bf16[72,512]{1,0:T(8,128)(2,1)} %get-tuple-element.47) | copy-start | bytes 221188
  87.3 64.3 %all-to-all-start.1 = ((bf16[64,16,1792]{2,1,0:T(8,128)(2,1)}), bf16[64,16,1792]{2,1,0:T(8,128)(2,1)}, u32[]{:S(2)}, u32[]{:S(2)}) async-start(bf16[64,16,1792]{2,1,0:T(8,128)(2,1)} %copy-done), calls=%async_computation.1 | async-start | bytes 7340032 | tf_op jit(solution)/shard_map/all_to_all | solution.py:520
  96.3 45.0 %collective-permute-start.5 = (bf16[3,3,2,1024]{3,2,1,0:T(2,128)(2,1)S(1)}, bf16[3,3,2,1024]{3,2,1,0:T(2,128)(2,1)S(1)}, u32[]{:S(2)}, u32[]{:S(2)}) collective-permute-start(bf16[3,3,2,1024]{3,2,1,0:T(2,128)(2,1)S(1)} %squeeze.14), channel_id=1, source_target_pairs={{0,1},{1,2},{2,3},{3,4},{4,5},{5,6},{6,7},{7,8},{8,9},{9,10},{10,1... | collective-permute-start | bytes 110600 | tf_op jit(solution)/shard_map/ppermute | solution.py:428
  96.4 46.3 %collective-permute-start.4 = (bf16[3,3,2,1024]{3,2,1,0:T(2,128)(2,1)S(1)}, bf16[3,3,2,1024]{3,2,1,0:T(2,128)(2,1)S(1)}, u32[]{:S(2)}, u32[]{:S(2)}) collective-permute-start(bf16[3,3,2,1024]{3,2,1,0:T(2,128)(2,1)S(1)} %squeeze.13), channel_id=1, source_target_pairs={{0,16},{1,17},{2,18},{3,19},{4,20},{5,21},{6,22},{7,23},{8,24},{9,... | collective-permute-start | bytes 110600 | tf_op jit(solution)/shard_map/ppermute | solution.py:428
  98.0 46.8 %collective-permute-start.3 = (bf16[3,3,2,1024]{3,2,1,0:T(2,128)(2,1)S(1)}, bf16[3,3,2,1024]{3,2,1,0:T(2,128)(2,1)S(1)}, u32[]{:S(2)}, u32[]{:S(2)}) collective-permute-start(bf16[3,3,2,1024]{3,2,1,0:T(2,128)(2,1)S(1)} %squeeze.12), channel_id=1, source_target_pairs={{0,17},{1,18},{2,19},{3,20},{4,21},{5,22},{6,23},{7,24},{8,25},{9,... | collective-permute-start | bytes 110600 | tf_op jit(solution)/shard_map/ppermute | solution.py:428
  102.0 43.6 %collective-permute-start.8 = (bf16[6,6,2,512]{3,2,1,0:T(2,128)(2,1)S(1)}, bf16[6,6,2,512]{3,2,1,0:T(2,128)(2,1)S(1)}, u32[]{:S(2)}, u32[]{:S(2)}) collective-permute-start(bf16[6,6,2,512]{3,2,1,0:T(2,128)(2,1)S(1)} %reshape.83), channel_id=1, source_target_pairs={{0,1},{1,2},{2,3},{3,4},{4,5},{5,6},{6,7},{7,8},{8,9},{9,10},{10,1... | collective-permute-start | bytes 221192 | tf_op jit(solution)/shard_map/ppermute | solution.py:428
  102.2 44.3 %collective-permute-start.7 = (bf16[6,6,2,512]{3,2,1,0:T(2,128)(2,1)S(1)}, bf16[6,6,2,512]{3,2,1,0:T(2,128)(2,1)S(1)}, u32[]{:S(2)}, u32[]{:S(2)}) collective-permute-start(bf16[6,6,2,512]{3,2,1,0:T(2,128)(2,1)S(1)} %reshape.82), channel_id=1, source_target_pairs={{0,16},{1,17},{2,18},{3,19},{4,20},{5,21},{6,22},{7,23},{8,24},{9,... | collective-permute-start | bytes 221192 | tf_op jit(solution)/shard_map/ppermute | solution.py:428
  141.2 9.2 %collective-permute-start.6 = (bf16[6,6,2,512]{3,2,1,0:T(2,128)(2,1)S(1)}, bf16[6,6,2,512]{3,2,1,0:T(2,128)(2,1)S(1)}, u32[]{:S(2)}, u32[]{:S(2)}) collective-permute-start(bf16[6,6,2,512]{3,2,1,0:T(2,128)(2,1)S(1)} %reshape.81), channel_id=1, source_target_pairs={{0,17},{1,18},{2,19},{3,20},{4,21},{5,22},{6,23},{7,24},{8,25},{9,... | collective-permute-start | bytes 221192 | tf_op jit(solution)/shard_map/ppermute | solution.py:428
Sparse Core Ops, SparseCore 0:
  56.1 23.5 all-gather.1

commit v5 on v4

--- a/solution.py
+++ b/solution.py
@@ -19,7 +19,6 @@
 F32 = jnp.float32
 
 PAIRS = ("z", "x_lo", "y", "x_hi")
-NEAR = ("y", "core")
 
 
 PACKED = MERGED + 36
@@ -70,29 +69,15 @@
     return jnp.where(rows == cols, 1.0, 0.0).astype(BF16)
 
 
-def weave(even, grads, keep, send, cols):
+def weave(grads, slots, cols):
     tiles = [grad.reshape(64, 8, grad.shape[-1]) for grad in grads]
     turned = [pltpu.roll(tile, 4, 1) for tile in tiles]
     upper = lax.broadcasted_iota(jnp.int32, tiles[0].shape, 1) < 4
     for half in range(2):
         one, two = half * 2, half * 2 + 1
-        first = jnp.where(upper, tiles[one], turned[two])
-        second = jnp.where(upper, turned[one], tiles[two])
         rows = slice(half * 8, half * 8 + 8)
-        keep[:, rows, cols] = jnp.where(even, first, second).astype(BF16)
-        send[:, rows, cols] = jnp.where(even, second, first).astype(BF16)
-
-
-def weave_all(grads):
-    tiles = [grad.reshape(32, 8, grad.shape[-1]) for grad in grads]
-    turned = [pltpu.roll(tile, 4, 1) for tile in tiles]
-    upper = lax.broadcasted_iota(jnp.int32, tiles[0].shape, 1) < 4
-    halves = []
-    for one, two in ((0, 1), (2, 3)):
-        first = jnp.where(upper, tiles[one], turned[two])
-        second = jnp.where(upper, turned[one], tiles[two])
-        halves.append(jnp.stack([first, second], axis=1))
-    return jnp.stack(halves, axis=2).reshape(64, 16, grads[0].shape[-1]).astype(BF16)
+        slots[0, :, rows, cols] = jnp.where(upper, tiles[one], turned[two]).astype(BF16)
+        slots[1, :, rows, cols] = jnp.where(upper, turned[one], tiles[two]).astype(BF16)
 
 
 def load(pairs, sems):
@@ -115,15 +100,24 @@
 def near_order():
     source = lax.broadcasted_iota(jnp.int32, (512, 512), 0)
     target = lax.broadcasted_iota(jnp.int32, (512, 512), 1)
-    near = source // 4 % 4 * 2 + source // 16 % 2
-    place = near * 64 + source // 32 * 4 + source % 4
+    place = source // 4 % 4 * 128 + source // 16 * 4 + source % 4
     return jnp.where(target == place, 1.0, 0.0).astype(BF16)
 
 
+def gelu_parts(values):
+    density = jnp.exp2(values * values * (-0.5 * LOG2E))
+    inverse = 1.0 / (1.0 + jnp.abs(values) * (0.3275911 * 0.7071067811865476))
+    series = 0.5 * 1.061405429
+    for term in (-1.453152027, 1.421413741, -0.284496736, 0.254829592):
+        series = series * inverse + 0.5 * term
+    tail = series * inverse * density
+    return jnp.where(values < 0.0, tail, 1.0 - tail), density
+
+
 def forward_kernel(
-    quad0, quad1, quad2, quad3, order_ref, cot_order_ref, bias_ref, w_qkv, w_qkv_t,
+    where_ref, quad0, quad1, quad2, quad3, order_ref, cot_order_ref, bias_ref, w_qkv, w_qkv_t,
     w_out_hbm, w_up_hbm, w_down_hbm, w_merge_hbm,
-    cot_ref, level_two_ref, merged_ref, tokens_ref, packed_ref, keys_t_ref, attended_ref, first_t_ref,
+    cot_ref, level_two_ref, near0, near1, near2, near3, tokens_ref, packed_ref, keys_t_ref, attended_ref, first_t_ref,
     middle_ref, after_mlp_ref, probs_hbm, hidden_hbm, slope_hbm,
     query_t, values_t, slope_ref, hidden_ref, probs_ref, w_out, w_up, w_down, w_merge,
     in_sems, out_sems,
@@ -142,7 +136,8 @@
     first_t_ref[...] = dot(eye(512), first_norm, 1, 1).astype(BF16)
     for part in range(12):
         packed_ref[part] = dot(first_norm, w_qkv[:, part * 128 : part * 128 + 128]).astype(BF16)
-    query_t[...] = dot(w_qkv_t[:512], first_norm, 1, 1).astype(BF16)
+    queries = dot(w_qkv_t[:512], first_norm, 1, 1)
+    query_t[...] = (queries * (HEAD ** (-0.5) * LOG2E)).astype(BF16)
     keys_t_ref[...] = dot(w_qkv_t[512:1024], first_norm, 1, 1).astype(BF16)
     values_t[...] = dot(w_qkv_t[1024:], first_norm, 1, 1).astype(BF16)
 
@@ -153,7 +148,7 @@
         queries = query_t[pl.ds(pl.multiple_of(group * 128, 128), 128), :]
         for head in range(4):
             masked = jnp.where(head_of_row == head, queries, jnp.zeros_like(queries))
-            scores = dot(keys, masked) * (HEAD ** (-0.5) * LOG2E) + bias_ref[...]
+            scores = dot(keys, masked) + bias_ref[...]
             raised = jnp.exp2(scores - jnp.max(scores, axis=0, keepdims=True))
             inverse = 1.0 / jnp.sum(raised, axis=0, keepdims=True)
             probs = (raised * inverse).astype(BF16)
@@ -178,12 +173,10 @@
     for part in range(4):
         cols = slice(part * 512, part * 512 + 512)
         before = dot(second_norm, w_up[:, cols])
-        cumulative = 0.5 * (1.0 + lax.erf(before * 0.7071067811865476))
+        cumulative, density = gelu_parts(before)
         hidden = (before * cumulative).astype(BF16)
         hidden_ref[:, cols] = hidden
-        slope_ref[:, cols] = (
-            cumulative + before * jnp.exp(-0.5 * before * before) * 0.3989422804014327
-        ).astype(BF16)
+        slope_ref[:, cols] = (cumulative + before * density * 0.3989422804014327).astype(BF16)
         mlp = mlp + dot(hidden, w_down[cols])
     saves += load([(hidden_ref, hidden_hbm), (slope_ref, slope_hbm)], out_sems.at[pl.ds(1, 2)])
     after_mlp = (middle + mlp).astype(BF16)
@@ -191,9 +184,16 @@
     merged_norm = [v.astype(BF16) for v in merge_norm(after_mlp.astype(F32))[0]]
     order = near_order()
     spread = [dot(v, order) for v in merged_norm]
-    for near in range(8):
-        at = slice(near * 64, near * 64 + 64)
-        merged_ref[near] = jnp.concatenate([v[:, at] for v in spread], axis=1).astype(BF16)
+    blocks = [
+        jnp.concatenate([v[:, at * 128 : at * 128 + 128] for v in spread], axis=1).astype(BF16)
+        for at in range(4)
+    ]
+    y = where_ref[1]
+    for step, near in enumerate((near0, near1, near2, near3)):
+        block = blocks[step]
+        for own in range(1, 4):
+            block = jnp.where(y == own, blocks[(own + step) % 4], block)
+        near[...] = block
     weights[3].wait()
     level_two_ref[...] = sum(
         dot(merged_norm[p], w_merge[p * 512 : p * 512 + 512]) for p in range(4)
@@ -203,17 +203,17 @@
 
 
 def middle_kernel(
-    core_ref, cot_ref, middle_ref, after_mlp_ref, attended_ref,
+    where_ref, cot_ref, middle_ref, after_mlp_ref, attended_ref,
     w_merge_hbm, hidden_hbm, w_down_hbm, slope_hbm, w_up_hbm,
-    keep_ref, send_ref, middle_grad_ref,
-    w_merge, hidden_ref, w_down, slope_ref, w_up, sems,
+    middle_grad_ref, keep_hbm, send_hbm,
+    w_merge, hidden_ref, w_down, slope_ref, w_up, slots, sems, out_sems,
 ):
     loads = load(
         [(w_merge_hbm, w_merge), (hidden_hbm, hidden_ref), (w_down_hbm, w_down),
          (slope_hbm, slope_ref), (w_up_hbm, w_up)],
         sems,
     )
-    even = core_ref[0] == 0
+    core = where_ref[0]
     cotangent = cot_ref[...]
     pieces, inverse_out = merge_norm(after_mlp_ref[...].astype(F32))
     normed_mid, inverse_mid = normalize(middle_ref[...].astype(F32))
@@ -228,45 +228,63 @@
         [inverse_out * (v - mean_grad - u * mean_cross) for v, u in zip(upstream, pieces)], axis=0
     ).astype(BF16)
 
+    def save(cols, at):
+        return load(
+            [(slots.at[core, :, :, cols], keep_hbm.at[:, :, cols]),
+             (slots.at[1 - core, :, :, cols], send_hbm.at[:, :, cols])],
+            out_sems.at[pl.ds(at, 2)],
+        )
+
+    loads[1].wait()
+    for part in range(4):
+        grad = dot(hidden_ref[:, part * 512 : part * 512 + 512], grad_after, 0, 0).astype(BF16)
+        for block in range(32):
+            slots[block % 2, part * 16 + block // 2, :, :512] = grad[block * 16 : block * 16 + 16]
+    saves = save(pl.ds(0, 512), 0)
     back_up = jnp.zeros((TOKENS, 512), F32)
     grads_up = []
-    for copy in loads[1:]:
+    for copy in loads[2:]:
         copy.wait()
     for part in range(4):
         cols = slice(part * 512, part * 512 + 512)
-        grad = dot(hidden_ref[:, cols], grad_after, 0, 0).astype(BF16)
-        for pair in range(16):
-            low = grad[pair * 32 : pair * 32 + 16]
-            high = grad[pair * 32 + 16 : pair * 32 + 32]
-            keep_ref[part * 16 + pair, :, :512] = jnp.where(even, low, high)
-            send_ref[part * 16 + pair, :, :512] = jnp.where(even, high, low)
         grad_before = (
             dot(grad_after, w_down[cols], 1, 1) * slope_ref[:, cols].astype(F32)
         ).astype(BF16)
         grads_up.append(dot(second_t, grad_before))
         back_up = back_up + dot(grad_before, w_up[:, cols], 1, 1)
-    weave(even, grads_up, keep_ref, send_ref, slice(512, 1024))
+    weave(grads_up, slots, slice(512, 1024))
     middle_grad = (
         grad_after.astype(F32) + norm_back(normed_mid, inverse_mid, back_up)
     ).astype(BF16)
     middle_grad_ref[...] = middle_grad
     grad = dot(attended_ref[...], middle_grad)
-    weave(even, [grad[:, p * 128 : p * 128 + 128] for p in range(4)], keep_ref, send_ref,
-          slice(1024, 1152))
+    weave([grad[:, p * 128 : p * 128 + 128] for p in range(4)], slots, slice(1024, 1152))
+    saves += save(pl.ds(512, 640), 2)
+    for copy in saves:
+        copy.wait()
 
 
 def backward_kernel(
-    core_ref, tokens_ref, packed_ref, keys_t_ref, attended_ref, middle_grad_ref,
-    first_t_ref, order_ref, w_out, probs_hbm, w_qkv_hbm,
-    keep_ref, send_ref, out0, out1, out2, out3,
-    grad_heads, grad_heads_t, products, query_grad_t, packed_grad, probs_ref, w_qkv, sems,
+    where_ref, tokens_ref, packed_ref, keys_t_ref, attended_ref, middle_grad_ref,
+    first_t_ref, order_ref, level_order_ref, level_two_ref, near0, near1, near2, near3, cots_ref,
+    w_out, probs_hbm, w_qkv_hbm,
+    out0, out1, out2, out3, keep_hbm, send_hbm,
+    grad_heads, grad_heads_t, products, query_grad_t, packed_grad, probs_ref, w_qkv, slots, sems,
+    out_sems,
 ):
     loads = load(
         [(probs_hbm.at[pl.ds(g * 4, 4)], probs_ref.at[pl.ds(g * 4, 4)]) for g in range(4)]
         + [(w_qkv_hbm, w_qkv)],
         sems,
     )
-    even = core_ref[0] == 0
+    core, y = where_ref[0], where_ref[1]
+
+    near = [near0[...], near1[...], near2[...], near3[...]]
+    near = jnp.concatenate([v.astype(F32) for v in near], axis=0).astype(BF16)
+    cots = [cots_ref[lax.rem(y + 4 - step, 4)].astype(F32) for step in range(4)]
+    grad = dot(near, jnp.concatenate(cots, axis=0).astype(BF16), 0, 0)
+    weave([grad[:, q * 256 : q * 256 + 256] for q in range(4)], slots, slice(384, 640))
+
     middle_grad = middle_grad_ref[...]
     for group in range(4):
         grad_heads[group] = dot(
@@ -320,8 +338,8 @@
         grads += [grad[:, q * 128 : q * 128 + 128] for q in range(4)]
         back_qkv = back_qkv + dot(wide, w_qkv[:, part * 512 : part * 512 + 512], 1, 1)
     for part in range(3):
-        weave(even, [grads[q * 3 + part] for q in range(4)], keep_ref, send_ref,
-              slice(part * 128, part * 128 + 128))
+        weave([grads[q * 3 + part] for q in range(4)], slots, slice(part * 128, part * 128 + 128))
+    saves = load([(slots.at[core], keep_hbm), (slots.at[1 - core], send_hbm)], out_sems)
 
     normed_in, inverse_in = normalize(tokens_ref[...].astype(F32))
     grad_first = back_qkv.astype(BF16).astype(F32)
@@ -329,39 +347,32 @@
         middle_grad.astype(F32) + norm_back(normed_in, inverse_in, grad_first)
     ).astype(BF16)
     for quad, out in enumerate((out0, out1, out2, out3)):
-        out[...] = dot(order_ref[quad], grad_tokens).astype(BF16)
-
-
-def assemble_kernel(
-    merged_ref, cots_ref, keep_hbm, arrived_hbm, blocks_hbm, keep_ref, arrived_ref, merge_ref,
-    keep_sems, arrived_sems, out_sems,
-):
+        rows = dot(order_ref[quad], grad_tokens)
+        for half in range(2):
+            level_two = level_two_ref[:, half * 512 : half * 512 + 512]
+            rows = rows + dot(level_order_ref[half * 4 + quad], level_two)
+        out[...] = rows.astype(BF16)
+    for copy in saves:
+        copy.wait()
+
+
+def pair_kernel(keep_hbm, arrived_hbm, *refs, place):
+    blocks_hbm, keep_ref, arrived_ref, keep_sems, arrived_sems, out_sems = refs[-6:]
+    cols = pl.ds(place, keep_hbm.shape[-1])
     parts = [pl.ds(p * 16, 16) for p in range(4)]
     keeps = load([(keep_hbm.at[p], keep_ref.at[p]) for p in parts], keep_sems)
     arrivals = load([(arrived_hbm.at[p], arrived_ref.at[p]) for p in parts], arrived_sems)
-    grad = dot(merged_ref[...], cots_ref[...], 0, 0)
-    merge_ref[...] = weave_all([grad[:, q * 256 : q * 256 + 256] for q in range(4)])
-    saves = load(
-        [(merge_ref, blocks_hbm.at[:, :, pl.ds(1536, 256)])], out_sems.at[pl.ds(4, 1)]
-    )
+    saves = []
     for part, rows in enumerate(parts):
         keeps[part].wait()
         arrivals[part].wait()
         total = keep_ref[rows].astype(F32) + arrived_ref[rows].astype(F32)
         keep_ref[rows] = total.astype(BF16)
         saves += load(
-            [(keep_ref.at[rows], blocks_hbm.at[rows, :, pl.ds(0, 1152)])],
-            out_sems.at[pl.ds(part, 1)],
+            [(keep_ref.at[rows], blocks_hbm.at[rows, :, cols])], out_sems.at[pl.ds(part, 1)]
         )
     for save in saves:
         save.wait()
-
-
-def late_kernel(keep_ref, arrived_ref, _, blocks_hbm, total_ref, sem):
-    total = keep_ref[...].astype(F32) + arrived_ref[...].astype(F32)
-    total_ref[...] = total.astype(BF16)
-    save, = load([(total_ref, blocks_hbm.at[:, :, pl.ds(1152, 384)])], sem)
-    save.wait()
 
 
 def share_kernel(landed_hbm, qkv_ref, out_ref, up_ref, down_ref, merge_ref, landed_ref, sems):
@@ -390,8 +401,10 @@
 
 
 def call(kernel, inputs, held, outputs, saved, scratch, micros, kind=BF16, aliases=()):
-    whole, there = pl.BlockSpec(memory_space=pltpu.VMEM), pl.BlockSpec(memory_space=pl.ANY)
+    whole, there = pl.BlockSpec(memory_space=pltpu.VMEM), pl.BlockSpec(memory_space=pltpu.HBM)
     specs = [whole if at < held else there for at in range(len(inputs))]
+    if held == 0 and len(inputs) > 1:
+        specs[1] = pl.BlockSpec(memory_space=pl.ANY)
     if inputs[0].ndim == 1:
         specs[0] = pl.BlockSpec(memory_space=pltpu.SMEM)
     return pl.pallas_call(
@@ -401,7 +414,7 @@
         out_specs=[whole if at < saved else there for at in range(len(outputs))],
         scratch_shapes=scratch,
         input_output_aliases=dict(aliases),
-        compiler_params=pltpu.CompilerParams(vmem_limit_bytes=(56 if micros > 9 else 24) * 2**20),
+        compiler_params=pltpu.CompilerParams(vmem_limit_bytes=56 * 2**20),
         cost_estimate=pl.CostEstimate(
             flops=micros * 10**9, bytes_accessed=micros * 10**6, transcendentals=0
         ),
@@ -449,16 +462,19 @@
     ]
 
 
-def roll_forth(corners):
+def send_forth(corners):
     upper_left, upper_right, lower_left, lower_right = corners
-    moved = [
+    return [
         shifted_block(lower_right, 1, 1),
         shifted_block(lower_left, 1, 0),
         shifted_block(upper_right, 0, 1),
         upper_left,
     ]
-    upper = jnp.concatenate(moved[:2], axis=1)
-    lower = jnp.concatenate(moved[2:], axis=1)
+
+
+def from_corners(corners):
+    upper = jnp.concatenate(corners[:2], axis=1)
+    lower = jnp.concatenate(corners[2:], axis=1)
     return jnp.concatenate([upper, lower], axis=0).transpose(2, 0, 1, 3)
 
 
@@ -469,63 +485,71 @@
 
 
 def body(tokens, window_ids, cotangent, w_qkv, w_out, w_up, w_down, w_merge):
-    order = token_order()
+    order, cot_order = token_order(), cotangent_order()
+    level_order = np.concatenate([cot_order[:, :MERGED], cot_order[:, MERGED:]]).transpose(0, 2, 1)
     by_feature, field, hidden_shape = (512, TOKENS), (TOKENS, 512), (TOKENS, 2048)
-    all_probs = (16, TOKENS, TOKENS)
-    core = lax.axis_index("core").reshape(1)
+    all_probs, near_shape, corner = (16, TOKENS, TOKENS), (MERGED, 512), (PACKED, 512)
+    where = jnp.stack([lax.axis_index("core"), lax.axis_index("y")])
     quads = roll_back(tokens, cotangent)
 
-    (cot, level_two, merged, tokens_in, packed, keys_t, attended, first_t, middle, after_mlp, probs,
-     hidden, slope) = call(
+    (cot, level_two, near0, near1, near2, near3, tokens_in, packed, keys_t, attended, first_t,
+     middle, after_mlp, probs, hidden, slope) = call(
         forward_kernel,
-        [*quads, jnp.asarray(order, BF16), jnp.asarray(cotangent_order(), BF16),
-         window_bias(window_ids), w_qkv, w_qkv.T, w_out, w_up, w_down, w_merge], 9,
-        [(MERGED, 1024), (MERGED, 1024), (8, MERGED, 256), field, (12, TOKENS, 128), by_feature, by_feature,
-         by_feature, field, field, all_probs, hidden_shape, hidden_shape], 10,
+        [where, *quads, jnp.asarray(order, BF16), jnp.asarray(cot_order, BF16),
+         window_bias(window_ids), w_qkv, w_qkv.T, w_out, w_up, w_down, w_merge], 10,
+        [(MERGED, 1024), (MERGED, 1024)] + [near_shape] * 4 + [field, (12, TOKENS, 128),
+         by_feature, by_feature, by_feature, field, field, all_probs, hidden_shape, hidden_shape],
+        13,
         [vmem(*by_feature), vmem(*by_feature), vmem(*hidden_shape), vmem(*hidden_shape),
          vmem(*all_probs), vmem(*w_out.shape), vmem(*w_up.shape), vmem(*w_down.shape),
          vmem(*w_merge.shape), dmas(4), dmas(3)],
         15,
     )
-    cotangents = lax.all_gather(cot, NEAR, tiled=True)
-    merged = lax.all_to_all(merged, NEAR, 0, 0, tiled=True).reshape(8 * MERGED, 256)
-    keep, send, middle_grad = call(
+    cotangents = lax.all_gather(cot, "y")
+    near = [near0]
+    for step, block in ((1, near1), (2, near2), (3, near3)):
+        near.append(lax.ppermute(block, "y", [(i, (i + step) % 4) for i in range(4)]))
+    middle_grad, keep, send = call(
         middle_kernel,
-        [core, cot, middle, after_mlp, attended, w_merge, hidden, w_down, slope, w_up], 5,
-        [(64, 16, 1152), (64, 16, 1152), field], 3,
+        [where, cot, middle, after_mlp, attended, w_merge, hidden, w_down, slope, w_up], 5,
+        [field, (64, 16, 1152), (64, 16, 1152)], 1,
         [vmem(*w_merge.shape), vmem(*hidden_shape), vmem(*w_down.shape), vmem(*hidden_shape),
-         vmem(*w_up.shape), dmas(5)],
+         vmem(*w_up.shape), vmem(2, 64, 16, 1152), dmas(5), dmas(4)],
         12,
     )
-    late_keep, late_send, *grads = call(
+    *corners, late_keep, late_send = call(
         backward_kernel,
-        [core, tokens_in, packed, keys_t, attended, middle_grad, first_t,
-         jnp.asarray(order[:, :, :MERGED].transpose(0, 2, 1), BF16), w_out, probs, w_qkv], 9,
-        [(64, 16, 384)] * 2 + [(MERGED, 512)] * 4, 6,
+        [where, tokens_in, packed, keys_t, attended, middle_grad, first_t,
+         jnp.asarray(order.transpose(0, 2, 1), BF16), jnp.asarray(level_order, BF16), level_two,
+         *near, cotangents, w_out, probs, w_qkv], 16,
+        [corner] * 4 + [(64, 16, 640)] * 2, 4,
         [vmem(4, TOKENS, 128), vmem(*by_feature), pltpu.VMEM(by_feature, F32), vmem(*by_feature),
-         vmem(12, TOKENS, 128), vmem(*all_probs), vmem(*w_qkv.shape),
-         dmas(5)],
+         vmem(12, TOKENS, 128), vmem(*all_probs), vmem(*w_qkv.shape), vmem(2, 64, 16, 640),
+         dmas(5), dmas(2)],
         12,
     )
-    blocks, = call(
-        assemble_kernel, [merged, cotangents, keep, from_pair(send)], 2,
-        [(64, 16, 1792)], 0,
-        [vmem(64, 16, 1152), vmem(64, 16, 1152), vmem(64, 16, 256), dmas(4), dmas(4), dmas(5)],
-        4,
-    )
-    blocks, = call(
-        late_kernel, [late_keep, from_pair(late_send), blocks], 2, [blocks.shape], 0,
-        [vmem(64, 16, 384), dmas(1)], 2, aliases={2: 0},
-    )
+    blocks = None
+    for kept, sent, place in ((keep, send, 0), (late_keep, late_send, 1152)):
+        blocks, = call(
+            functools.partial(pair_kernel, place=place),
+            [kept, from_pair(sent)] + ([] if blocks is None else [blocks]), 0,
+            [(64, 16, 1792)], 0,
+            [vmem(*kept.shape), vmem(*kept.shape), dmas(4), dmas(4), dmas(4)],
+            2, aliases={} if blocks is None else {2: 0},
+        )
+    corners = send_forth(corners)
+    blocks, *corners = lax.optimization_barrier((blocks, *corners))
     landed = lax.all_to_all(blocks, PAIRS, 0, 0, tiled=True)
     grad_qkv, grad_out, grad_up, grad_down, grad_merge = call(
         share_kernel, [landed], 0,
         [(4, 1536), (4, 512), (4, 2048), (16, 512), (16, 1024)], 5,
         [vmem(*blocks.shape), dmas(4)], 3, kind=F32,
     )
-    level_two = level_two.reshape(4, 3, 3, 2, 1024)
-    level_two = roll_forth([level_two[quad] for quad in range(4)])
-    grad_tokens = roll_forth([grad.reshape(6, 6, 2, 512) for grad in grads])
+    grad_tokens = from_corners([c[:MERGED].reshape(6, 6, 2, 512) for c in corners])
+    halves = [(c[MERGED : MERGED + 18], c[MERGED + 18 :]) for c in corners]
+    level_two = from_corners(
+        [jnp.concatenate(pair, axis=1).reshape(3, 3, 2, 1024) for pair in halves]
+    )
     return (level_two, grad_tokens, grad_qkv, grad_out, grad_up, grad_down, grad_merge)
 
 

time: 162 us -> 154 us (0.951); the launches traced: 161 us -> 152 us
  between operations: 14.4 us -> 1.21 us
  Pallas kernels: 47.6 us -> 52.8 us
  blocking collectives: 10.8 us -> 14.1 us
  waiting for transfers between devices: 48 us -> 45.6 us
    ppermute x9 -> x6, waiting for transfers between devices: 46.7 us -> 0.98 us  [shifted_block(): return lax.ppermute(block, GRID, route)]
    all_to_all x1, waiting for transfers between devices: 0.01 us -> 44.6 us  [body(): landed = lax.all_to_all(blocks, PAIRS, 0, 0, tiled=True)]
    all_gather x0 -> x1, blocking collectives: none -> 14.1 us  [body(): cotangents = lax.all_gather(cot, 'y')]
    all_to_all x1 -> x0, blocking collectives: 10.8 us -> none  [body(): lax.all_to_all(merged, NEAR, 0, 0, tiled=True).reshape(8 * MERGED, 256)]
    pallas_call x6, Pallas kernels: 47.6 us -> 52.8 us  [call(): pl.pallas_call(kernel, out_shape=[jax.ShapeDtypeStruct(shape, kind) for s...]
    ppermute x9 -> x6, starting transfers between devices: 16 us -> 11 us  [shifted_block(): return lax.ppermute(block, GRID, route)]
    ppermute x0 -> x3, starting transfers between devices: none -> 3.33 us  [body(): lax.ppermute(block, 'y', [(i, (i + step) % 4) for i in range(4)])]
    unnamed x31 -> x25, local copies, waits for them, and re-layouts: 7.07 us -> 5.47 us
  transfers between devices with their start and end apart: 13 -> 12, of which waited for: 6 -> 3; matrix products, arithmetic and copies ran while one was open for 4% -> 5% of each run, Pallas kernels for 9% -> 21%
where the time goes in v5:
time: 154 us; the launch traced here: 152 us
  Pallas kernels  52.8 us (34%)
  waiting for transfers between devices  45.6 us (30%)
  starting transfers between devices  24.8 us (16%)
  blocking collectives  14.1 us (9%)
  local copies, waits for them, and re-layouts  8.93 us (6%)
  other arithmetic  4.21 us (3%)
    pallas_call x6, Pallas kernels, call(): pl.pallas_call(kernel, out_shape=[jax.ShapeDtypeStruct(shape, kind) for s...  52.8 us
    all_to_all x1, waiting for transfers between devices, body(): landed = lax.all_to_all(blocks, PAIRS, 0, 0, tiled=True)  44.6 us
    all_gather x1, blocking collectives, body(): cotangents = lax.all_gather(cot, 'y')  14.1 us
    ppermute x6, starting transfers between devices, shifted_block(): return lax.ppermute(block, GRID, route)  11 us
    all_to_all x1, starting transfers between devices, body(): landed = lax.all_to_all(blocks, PAIRS, 0, 0, tiled=True)  9.79 us
    unnamed x25, local copies, waits for them, and re-layouts  5.47 us
    ppermute x3, starting transfers between devices, body(): lax.ppermute(block, 'y', [(i, (i + step) % 4) for i in range(4)])  3.33 us
  transfers between devices with their start and end apart: 12, of which 3 were waited for; matrix products, arithmetic and copies ran while one was open for 5% of the time, Pallas kernels for 21%

profile of v5, /device:TPU:0, one launch (start us, length us, event | category | flops | bytes accessed | tf_op | source)
XLA Modules:
  0.0 151.7 jit_solution(16744663634670504611)
XLA Ops:
  0.7 1.0 fusion.1
  1.7 1.2 fusion
  3.0 5.1 %collective-permute-start = (bf16[108,512]{1,0:T(8,128)(2,1)S(1)}, bf16[108,512]{1,0:T(8,128)(2,1)S(1)}, u32[]{:S(2)}, u32[]{:S(2)}) collective-permute-start(bf16[108,512]{1,0:T(8,128)(2,1)S(1)} %pad_maximum_fusion.1), channel_id=1, source_target_pairs={{0,15},{1,0},{2,1},{3,2},{4,3},{5,4},{6,5},{7,6},{8,7},{9,8},{10,9... | collective-permute-start | bytes 331784 | tf_op jit(solution)/shard_map/ppermute | solution.py:441
  8.2 4.1 %collective-permute-start.1 = (bf16[108,512]{1,0:T(8,128)(2,1)S(1)}, bf16[108,512]{1,0:T(8,128)(2,1)S(1)}, u32[]{:S(2)}, u32[]{:S(2)}) collective-permute-start(bf16[108,512]{1,0:T(8,128)(2,1)S(1)} %pad_maximum_fusion.2), channel_id=1, source_target_pairs={{0,112},{1,113},{2,114},{3,115},{4,116},{5,117},{6,118},{7,119},{8... | collective-permute-start | bytes 331784 | tf_op jit(solution)/shard_map/ppermute | solution.py:441
  12.4 0.4 collective-permute-start.2
  13.0 0.3 copy.22
  13.6 0.9 compare_select_fusion.bias_ref
  14.5 1.6 %copy.23 = bf16[512,1536]{0,1:T(8,128)(2,1)} copy(bf16[512,1536]{1,0:T(8,128)(2,1)S(1)} %copy-done.1) | data formatting | bytes 3145728 | tf_op args[3]
  16.1 0.7 pad_maximum_fusion.quad0
  16.8 0.6 pad_add_fusion.where_ref
  17.4 0.6 copy-done.6
  18.1 18.4 %shard_map.171 = (bf16[72,1024]{1,0:T(8,128)(2,1)}, bf16[72,1024]{1,0:T(8,128)(2,1)}, bf16[72,512]{1,0:T(8,128)(2,1)}, bf16[72,512]{1,0:T(8,128)(2,1)}, bf16[72,...) custom-call(s32[2]{0:T(128)} %pad_add_fusion.where_ref, ...), custom_call_target="tpu_custom_call" | custom-call | flops 15000000512 | bytes 15000000 | tf_op jit(solution)/shard_map/pallas_call | solution.py:410
  36.5 2.2 %collective-permute-start.4 = (bf16[72,512]{1,0:T(8,128)(2,1)}, bf16[72,512]{1,0:T(8,128)(2,1)S(1)}, u32[]{:S(2)}, u32[]{:S(2)}) collective-permute-start(bf16[72,512]{1,0:T(8,128)(2,1)} %get-tuple-element.56), channel_id=1, source_target_pairs={{0,8},{4,12},{8,0},{12,4},{1,9},{5,13},{9,1},{13,5},{2,10},{6,14},... | collective-permute-start | bytes 221192 | tf_op jit(solution)/shard_map/ppermute | solution.py:511
  38.7 1.0 collective-permute-start.5
  39.8 12.3 %shard_map.172 = (bf16[288,512]{1,0:T(8,128)(2,1)}, bf16[64,16,1152]{2,1,0:T(8,128)(2,1)}, bf16[64,16,1152]{2,1,0:T(8,128)(2,1)}) custom-call(s32[2]{0:T(128)} %pad_add_fusion.where_ref, bf16[72,1024]{1,0:T(8,128)(2,1)} %get-tuple-element.46.cot_ref, bf16[288,512]{1,0:T(8,128)(2,1)} %get-tuple-element.47.middle_ref, ...), custom_call_target="tpu_custom_call" | custom-call | flops 12000000000 | bytes 12000000 | tf_op jit(solution)/shard_map/pallas_call | solution.py:410
  52.1 0.7 collective-permute-start.7
  52.8 14.1 %all-gather = bf16[288,1024]{1,0:T(8,128)(2,1)} all-gather(bf16[72,1024]{1,0:T(8,128)(2,1)S(1)} %copy-done.3), channel_id=2, replica_groups=mesh['z'=4,'x_lo'=2,'y'=4,'x_hi'=2,'core'=2] {'y'}, dimensions={0}, use_global_device_ids=true | all-gather | bytes 737280 | tf_op jit(solution)/shard_map/all_gather | solution.py:508
  66.9 0.6 copy-done.9
  67.6 13.2 %shard_map.173 = (bf16[108,512]{1,0:T(8,128)(2,1)}, bf16[108,512]{1,0:T(8,128)(2,1)}, bf16[108,512]{1,0:T(8,128)(2,1)}, bf16[108,512]{1,0:T(8,128)(2,1)}, bf16[6...) custom-call(s32[2]{0:T(128)} %pad_add_fusion.where_ref, bf16[288,512]{1,0:T(8,128)(2,1)} %get-tuple-element.42.tokens_ref, ...), custom_call_target="tpu_custom_call" | custom-call | flops 12000000000 | bytes 12000000 | tf_op jit(solution)/shard_map/pallas_call | solution.py:410
  80.9 0.7 collective-permute-start.8
  81.7 0.6 collective-permute-start.10
  82.3 1.4 copy-done
  83.7 3.5 %shard_map.174.refs_0_ = bf16[64,16,1792]{2,1,0:T(8,128)(2,1)} custom-call(bf16[64,16,1152]{2,1,0:T(8,128)(2,1)} %get-tuple-element.61.keep_hbm, bf16[64,16,1152]{2,1,0:T(8,128)(2,1)} %copy-done), custom_call_target="tpu_custom_call" | custom-call | flops 2000000000 | bytes 2000000 | tf_op jit(solution)/shard_map/pallas_call | solution.py:410
  87.2 1.1 copy-done.2
  88.2 2.6 %shard_map.175 = bf16[64,16,1792]{2,1,0:T(8,128)(2,1)} custom-call(bf16[64,16,640]{2,1,0:T(8,128)(2,1)} %get-tuple-element.59.keep_hbm, bf16[64,16,640]{2,1,0:T(8,128)(2,1)} %copy-done.2, bf16[64,16,1792]{2,1,0:T(8,128)(2,1)} %shard_map.174.refs_0_), custom_call_target="tpu_custom_call", output_to_operand_aliasing={{}: (2, {})} | custom-call | flops 2000000000 | bytes 2000000 | tf_op jit(solution)/shard_map/pallas_call | solution.py:410
  90.8 0.6 collective-permute-done.8
  91.5 0.4 collective-permute-done.9
  91.8 9.8 %all-to-all-start = ((bf16[64,16,1792]{2,1,0:T(8,128)(2,1)}), bf16[64,16,1792]{2,1,0:T(8,128)(2,1)}, u32[]{:S(2)}, u32[]{:S(2)}) async-start(bf16[64,16,1792]{2,1,0:T(8,128)(2,1)} %shard_map.175), calls=%async_computation | async-start | bytes 7340032 | tf_op jit(solution)/shard_map/all_to_all | solution.py:542
  102.1 0.9 maximum_bitcast_fusion.1
  103.0 1.1 maximum_bitcast_fusion
  104.1 44.6 %all-to-all-done.landed_hbm = bf16[64,16,1792]{2,1,0:T(8,128)(2,1)} async-done(((bf16[64,16,1792]{2,1,0:T(8,128)(2,1)}), bf16[64,16,1792]{2,1,0:T(8,128)(2,1)}, u32[]{:S(2)}, u32[]{:S(2)}) %all-to-all-start) | async-done | bytes 3670048 | tf_op jit(solution)/shard_map/all_to_all | solution.py:542
  148.7 2.8 %shard_map.176 = (f32[4,1536]{1,0:T(4,128)}, f32[4,512]{1,0:T(4,128)}, f32[4,2048]{1,0:T(4,128)}, f32[16,512]{1,0:T(8,128)}, f32[16,1024]{1,0:T(8,128)}) custom-call(bf16[64,16,1792]{2,1,0:T(8,128)(2,1)} %all-to-all-done.landed_hbm), custom_call_target="tpu_custom_call" | custom-call | flops 3000000000 | bytes 3000000 | tf_op jit(solution)/shard_map/pallas_call | solution.py:410
  (68 shorter events, 1.4 us)
Async XLA Ops:
  0.6 12.3 %copy-start.5 = (s32[12,12]{1,0:T(8,128)S(1)}, s32[12,12]{1,0:T(8,128)}, u32[]{:S(2)}) copy-start(s32[12,12]{1,0:T(8,128)} %param.13) | copy-start | bytes 1732
  0.6 13.9 %copy-start.1 = (bf16[512,1536]{1,0:T(8,128)(2,1)S(1)}, bf16[512,1536]{1,0:T(8,128)(2,1)}, u32[]{:S(2)}) copy-start(bf16[512,1536]{1,0:T(8,128)(2,1)} %w_qkv_hbm.1) | copy-start | bytes 4718596
  3.0 14.3 %collective-permute-start = (bf16[108,512]{1,0:T(8,128)(2,1)S(1)}, bf16[108,512]{1,0:T(8,128)(2,1)S(1)}, u32[]{:S(2)}, u32[]{:S(2)}) collective-permute-start(bf16[108,512]{1,0:T(8,128)(2,1)S(1)} %pad_maximum_fusion.1), channel_id=1, source_target_pairs={{0,15},{1,0},{2,1},{3,2},{4,3},{5,4},{6,5},{7,6},{8,7},{9,8},{10,9... | collective-permute-start | bytes 331784 | tf_op jit(solution)/shard_map/ppermute | solution.py:441
  8.2 9.2 %collective-permute-start.1 = (bf16[108,512]{1,0:T(8,128)(2,1)S(1)}, bf16[108,512]{1,0:T(8,128)(2,1)S(1)}, u32[]{:S(2)}, u32[]{:S(2)}) collective-permute-start(bf16[108,512]{1,0:T(8,128)(2,1)S(1)} %pad_maximum_fusion.2), channel_id=1, source_target_pairs={{0,112},{1,113},{2,114},{3,115},{4,116},{5,117},{6,118},{7,119},{8... | collective-permute-start | bytes 331784 | tf_op jit(solution)/shard_map/ppermute | solution.py:441
  12.4 5.0 %collective-permute-start.2 = (bf16[108,512]{1,0:T(8,128)(2,1)S(1)}, bf16[108,512]{1,0:T(8,128)(2,1)S(1)}, u32[]{:S(2)}, u32[]{:S(2)}) collective-permute-start(bf16[108,512]{1,0:T(8,128)(2,1)S(1)} %pad_maximum_fusion.3), channel_id=1, source_target_pairs={{0,127},{1,112},{2,113},{3,114},{4,115},{5,116},{6,117},{7,118},{8... | collective-permute-start | bytes 331784 | tf_op jit(solution)/shard_map/ppermute | solution.py:441
  17.4 0.6 copy-start.6
  17.4 0.7 copy-start.7
  17.4 0.7 copy-start.8
  36.4 30.5 %collective-permute-start.3 = (bf16[72,512]{1,0:T(8,128)(2,1)}, bf16[72,512]{1,0:T(8,128)(2,1)S(1)}, u32[]{:S(2)}, u32[]{:S(2)}) collective-permute-start(bf16[72,512]{1,0:T(8,128)(2,1)} %get-tuple-element.55), channel_id=1, source_target_pairs={{0,4},{4,8},{8,12},{12,0},{1,5},{5,9},{9,13},{13,1},{2,6},{6,10},{... | collective-permute-start | bytes 221192 | tf_op jit(solution)/shard_map/ppermute | solution.py:511
  36.5 30.4 %collective-permute-start.4 = (bf16[72,512]{1,0:T(8,128)(2,1)}, bf16[72,512]{1,0:T(8,128)(2,1)S(1)}, u32[]{:S(2)}, u32[]{:S(2)}) collective-permute-start(bf16[72,512]{1,0:T(8,128)(2,1)} %get-tuple-element.56), channel_id=1, source_target_pairs={{0,8},{4,12},{8,0},{12,4},{1,9},{5,13},{9,1},{13,5},{2,10},{6,14},... | collective-permute-start | bytes 221192 | tf_op jit(solution)/shard_map/ppermute | solution.py:511
  38.7 28.2 %collective-permute-start.5 = (bf16[72,512]{1,0:T(8,128)(2,1)}, bf16[72,512]{1,0:T(8,128)(2,1)S(1)}, u32[]{:S(2)}, u32[]{:S(2)}) collective-permute-start(bf16[72,512]{1,0:T(8,128)(2,1)} %get-tuple-element.57), channel_id=1, source_target_pairs={{0,12},{4,0},{8,4},{12,8},{1,13},{5,1},{9,5},{13,9},{2,14},{6,2},{... | collective-permute-start | bytes 221192 | tf_op jit(solution)/shard_map/ppermute | solution.py:511
  39.8 13.0 %copy-start.3 = (bf16[72,1024]{1,0:T(8,128)(2,1)S(1)}, bf16[72,1024]{1,0:T(8,128)(2,1)}, u32[]{:S(2)}) copy-start(bf16[72,1024]{1,0:T(8,128)(2,1)} %get-tuple-element.46.cot_ref) | copy-start | bytes 442372
  52.1 30.1 %collective-permute-start.7 = (bf16[64,16,1152]{2,1,0:T(8,128)(2,1)}, bf16[64,16,1152]{2,1,0:T(8,128)(2,1)S(1)}, u32[]{:S(2)}, u32[]{:S(2)}) collective-permute-start(bf16[64,16,1152]{2,1,0:T(8,128)(2,1)} %get-tuple-element.62), channel_id=1, source_target_pairs={{0,1},{1,0},{2,3},{3,2},{4,5},{5,4},{6,7},{7,6},{8,9},{9,8},{10,11... | collective-permute-start | bytes 7077896 | tf_op jit(solution)/shard_map/ppermute | solution.py:433
  66.9 0.6 copy-start.9
  66.9 0.7 copy-start.10
  66.9 0.7 copy-start.11
  80.8 6.3 %collective-permute-start.6 = (bf16[64,16,640]{2,1,0:T(8,128)(2,1)}, bf16[64,16,640]{2,1,0:T(8,128)(2,1)S(1)}, u32[]{:S(2)}, u32[]{:S(2)}) collective-permute-start(bf16[64,16,640]{2,1,0:T(8,128)(2,1)} %get-tuple-element.60), channel_id=1, source_target_pairs={{0,1},{1,0},{2,3},{3,2},{4,5},{5,4},{6,7},{7,6},{8,9},{9,8},{10,11... | collective-permute-start | bytes 3932168 | tf_op jit(solution)/shard_map/ppermute | solution.py:433
  80.9 10.5 %collective-permute-start.8 = (bf16[108,512]{1,0:T(8,128)(2,1)}, bf16[108,512]{1,0:T(8,128)(2,1)S(1)}, u32[]{:S(2)}, u32[]{:S(2)}) collective-permute-start(bf16[108,512]{1,0:T(8,128)(2,1)} %get-tuple-element.63), channel_id=1, source_target_pairs={{0,17},{1,18},{2,19},{3,20},{4,21},{5,22},{6,23},{7,24},{8,25},{9,... | collective-permute-start | bytes 331784 | tf_op jit(solution)/shard_map/ppermute | solution.py:441
  81.6 10.2 %collective-permute-start.9 = (bf16[108,512]{1,0:T(8,128)(2,1)}, bf16[108,512]{1,0:T(8,128)(2,1)S(1)}, u32[]{:S(2)}, u32[]{:S(2)}) collective-permute-start(bf16[108,512]{1,0:T(8,128)(2,1)} %get-tuple-element.64), channel_id=1, source_target_pairs={{0,16},{1,17},{2,18},{3,19},{4,20},{5,21},{6,22},{7,23},{8,24},{9,... | collective-permute-start | bytes 331784 | tf_op jit(solution)/shard_map/ppermute | solution.py:441
  81.7 10.1 %collective-permute-start.10 = (bf16[108,512]{1,0:T(8,128)(2,1)}, bf16[108,512]{1,0:T(8,128)(2,1)S(1)}, u32[]{:S(2)}, u32[]{:S(2)}) collective-permute-start(bf16[108,512]{1,0:T(8,128)(2,1)} %get-tuple-element.65), channel_id=1, source_target_pairs={{0,1},{1,2},{2,3},{3,4},{4,5},{5,6},{6,7},{7,8},{8,9},{9,10},{10,1... | collective-permute-start | bytes 331784 | tf_op jit(solution)/shard_map/ppermute | solution.py:441
  82.3 1.4 copy-start
  87.2 1.1 copy-start.2
  91.8 9.8 %copy-start.4 = (bf16[108,512]{1,0:T(8,128)(2,1)S(1)}, bf16[108,512]{1,0:T(8,128)(2,1)}, u32[]{:S(2)}) copy-start(bf16[108,512]{1,0:T(8,128)(2,1)} %get-tuple-element.70) | copy-start | bytes 331780
  91.8 56.9 %all-to-all-start = ((bf16[64,16,1792]{2,1,0:T(8,128)(2,1)}), bf16[64,16,1792]{2,1,0:T(8,128)(2,1)}, u32[]{:S(2)}, u32[]{:S(2)}) async-start(bf16[64,16,1792]{2,1,0:T(8,128)(2,1)} %shard_map.175), calls=%async_computation | async-start | bytes 7340032 | tf_op jit(solution)/shard_map/all_to_all | solution.py:542

commit v6 on v5

--- a/solution.py
+++ b/solution.py
@@ -14,6 +14,7 @@
 MERGED = TOKENS // 4
 EPS = 1e-05
 LOG2E = 1.4426950408889634
+QUERY_SCALE = HEAD ** (-0.5) * LOG2E
 GRID = ("z", "x_lo", "y", "x_hi", "core")
 BF16 = jnp.bfloat16
 F32 = jnp.float32
@@ -36,6 +37,19 @@
     return order
 
 
+def window_places():
+    places = np.zeros((2, TOKENS, WIN), np.float32)
+    for row in range(WIN):
+        for col in range(WIN):
+            position = (col % 2) * 2 + row % 2
+            quad = row // 6 * 2 + col // 6
+            patch = quad * 18 + (row % 6 // 2 * 3 + col % 6 // 2) * 2
+            for level in range(2):
+                places[0, position * MERGED + patch + level, row] = 1.0
+                places[1, position * MERGED + patch + level, col] = 1.0
+    return places
+
+
 def cotangent_order():
     order = np.zeros((4, 2 * MERGED, PACKED), np.float32)
     for quad in range(4):
@@ -64,8 +78,8 @@
 
 
 def eye(size):
-    rows = lax.broadcasted_iota(jnp.int32, (size, size), 0)
-    cols = lax.broadcasted_iota(jnp.int32, (size, size), 1)
+    rows = lax.broadcasted_iota(jnp.int32, (size, 1), 0)
+    cols = lax.broadcasted_iota(jnp.int32, (1, size), 1)
     return jnp.where(rows == cols, 1.0, 0.0).astype(BF16)
 
 
@@ -98,9 +112,9 @@
 
 
 def near_order():
-    source = lax.broadcasted_iota(jnp.int32, (512, 512), 0)
-    target = lax.broadcasted_iota(jnp.int32, (512, 512), 1)
-    place = source // 4 % 4 * 128 + source // 16 * 4 + source % 4
+    source = lax.broadcasted_iota(jnp.int32, (512, 1), 0)
+    target = lax.broadcasted_iota(jnp.int32, (1, 512), 1)
+    place = ((source >> 2) & 3) * 128 + (source >> 4) * 4 + (source & 3)
     return jnp.where(target == place, 1.0, 0.0).astype(BF16)
 
 
@@ -115,33 +129,43 @@
 
 
 def forward_kernel(
-    where_ref, quad0, quad1, quad2, quad3, order_ref, cot_order_ref, bias_ref, w_qkv, w_qkv_t,
-    w_out_hbm, w_up_hbm, w_down_hbm, w_merge_hbm,
-    cot_ref, level_two_ref, near0, near1, near2, near3, tokens_ref, packed_ref, keys_t_ref, attended_ref, first_t_ref,
-    middle_ref, after_mlp_ref, probs_hbm, hidden_hbm, slope_hbm,
-    query_t, values_t, slope_ref, hidden_ref, probs_ref, w_out, w_up, w_down, w_merge,
-    in_sems, out_sems,
+    where_ref, order_ref, cot_order_ref, ids_ref, places_ref, cols_t_ref, w_qkv,
+    quad0_hbm, quad1_hbm, quad2_hbm, quad3_hbm, w_out_hbm, w_up_hbm, w_down_hbm, w_merge_hbm,
+    cot_ref, level_two_ref, near0, near1, near2, near3, tokens_ref, packed_ref, keys_t_ref,
+    attended_ref, first_t_ref, middle_ref, after_mlp_ref, probs_hbm, hidden_hbm, slope_hbm,
+    quads_ref, bias_ref, query_t, values_t, slope_ref, hidden_ref, probs_ref, w_out, w_up, w_down,
+    w_merge, quad_sems, in_sems, out_sems,
 ):
+    quads = (quad0_hbm, quad1_hbm, quad2_hbm, quad3_hbm)
+    quads = load([(quads[q], quads_ref.at[q]) for q in range(4)], quad_sems)
     weights = load(
         [(w_out_hbm, w_out), (w_up_hbm, w_up), (w_down_hbm, w_down), (w_merge_hbm, w_merge)],
         in_sems,
     )
-    quads = (quad0, quad1, quad2, quad3)
-    tokens = sum(dot(order_ref[q], quads[q][...]) for q in range(4))
+    ids = ids_ref[...].astype(F32).astype(BF16)
+    by_row = dot(places_ref[0], ids) * places_ref[1].astype(F32)
+    by_col = dot(ids, places_ref[0], 0, 1) * cols_t_ref[...]
+    alike = jnp.sum(by_row, axis=1, keepdims=True) == jnp.sum(by_col, axis=0, keepdims=True)
+    bias_ref[...] = jnp.where(alike, 0.0, -1e30)
+    for quad in quads:
+        quad.wait()
+    tokens = sum(dot(order_ref[q], quads_ref[q]) for q in range(4))
     tokens_ref[...] = tokens.astype(BF16)
-    halves = sum(dot(cot_order_ref[q], quads[q][...]) for q in range(4))
-    cot_ref[:, :512] = halves[:MERGED].astype(BF16)
-    cot_ref[:, 512:] = halves[MERGED:].astype(BF16)
+    halves = sum(dot(cot_order_ref[q], quads_ref[q]) for q in range(4))
+    cotangent = jnp.concatenate([halves[:MERGED], halves[MERGED:]], axis=1).astype(BF16)
+    cot_ref[...] = cotangent
     first_norm = normalize(tokens)[0].astype(BF16)
     first_t_ref[...] = dot(eye(512), first_norm, 1, 1).astype(BF16)
+    by_lane = eye(128)
     for part in range(12):
-        packed_ref[part] = dot(first_norm, w_qkv[:, part * 128 : part * 128 + 128]).astype(BF16)
-    queries = dot(w_qkv_t[:512], first_norm, 1, 1)
-    query_t[...] = (queries * (HEAD ** (-0.5) * LOG2E)).astype(BF16)
-    keys_t_ref[...] = dot(w_qkv_t[512:1024], first_norm, 1, 1).astype(BF16)
-    values_t[...] = dot(w_qkv_t[1024:], first_norm, 1, 1).astype(BF16)
-
-    head_of_row = lax.broadcasted_iota(jnp.int32, (128, TOKENS), 0) // HEAD
+        grid = dot(first_norm, w_qkv[:, part * 128 : part * 128 + 128])
+        grid = (grid * QUERY_SCALE if part < 4 else grid).astype(BF16)
+        packed_ref[part] = grid
+        turned = (query_t, keys_t_ref, values_t)[part // 4]
+        rows = slice(part % 4 * 128, part % 4 * 128 + 128)
+        turned[rows, :] = dot(by_lane, grid, 1, 1).astype(BF16)
+
+    head_of_row = lax.broadcasted_iota(jnp.int32, (128, TOKENS), 0) >> 5
 
     def attend(group, _):
         keys = packed_ref[4 + group]
@@ -188,12 +212,13 @@
         jnp.concatenate([v[:, at * 128 : at * 128 + 128] for v in spread], axis=1).astype(BF16)
         for at in range(4)
     ]
-    y = where_ref[1]
+    y = where_ref[0] >> 1
     for step, near in enumerate((near0, near1, near2, near3)):
         block = blocks[step]
         for own in range(1, 4):
             block = jnp.where(y == own, blocks[(own + step) % 4], block)
-        near[...] = block
+        near[:, :512] = block
+        near[:, 512:] = cotangent
     weights[3].wait()
     level_two_ref[...] = sum(
         dot(merged_norm[p], w_merge[p * 512 : p * 512 + 512]) for p in range(4)
@@ -213,7 +238,7 @@
          (slope_hbm, slope_ref), (w_up_hbm, w_up)],
         sems,
     )
-    core = where_ref[0]
+    core = where_ref[0] & 1
     cotangent = cot_ref[...]
     pieces, inverse_out = merge_norm(after_mlp_ref[...].astype(F32))
     normed_mid, inverse_mid = normalize(middle_ref[...].astype(F32))
@@ -266,25 +291,20 @@
 
 def backward_kernel(
     where_ref, tokens_ref, packed_ref, keys_t_ref, attended_ref, middle_grad_ref,
-    first_t_ref, order_ref, level_order_ref, level_two_ref, near0, near1, near2, near3, cots_ref,
-    w_out, probs_hbm, w_qkv_hbm,
+    first_t_ref, order_ref, level_order_ref, level_two_ref, w_out,
+    near0_hbm, near1_hbm, near2_hbm, near3_hbm, probs_hbm, w_qkv_hbm,
     out0, out1, out2, out3, keep_hbm, send_hbm,
-    grad_heads, grad_heads_t, products, query_grad_t, packed_grad, probs_ref, w_qkv, slots, sems,
-    out_sems,
+    grad_heads, grad_heads_t, products, query_grad_t, packed_grad, probs_ref, w_qkv, near_ref,
+    slots, near_sems, sems, out_sems,
 ):
     loads = load(
         [(probs_hbm.at[pl.ds(g * 4, 4)], probs_ref.at[pl.ds(g * 4, 4)]) for g in range(4)]
         + [(w_qkv_hbm, w_qkv)],
         sems,
     )
-    core, y = where_ref[0], where_ref[1]
-
-    near = [near0[...], near1[...], near2[...], near3[...]]
-    near = jnp.concatenate([v.astype(F32) for v in near], axis=0).astype(BF16)
-    cots = [cots_ref[lax.rem(y + 4 - step, 4)].astype(F32) for step in range(4)]
-    grad = dot(near, jnp.concatenate(cots, axis=0).astype(BF16), 0, 0)
-    weave([grad[:, q * 256 : q * 256 + 256] for q in range(4)], slots, slice(384, 640))
-
+    nears = (near0_hbm, near1_hbm, near2_hbm, near3_hbm)
+    nears = load([(nears[step], near_ref.at[step]) for step in range(4)], near_sems)
+    core = where_ref[0] & 1
     middle_grad = middle_grad_ref[...]
     for group in range(4):
         grad_heads[group] = dot(
@@ -293,8 +313,8 @@
     grad_heads_t[...] = dot(w_out[...], middle_grad, 1, 1).astype(BF16)
     products[...] = grad_heads_t[...].astype(F32) * attended_ref[...].astype(F32)
 
-    head_of_row = lax.broadcasted_iota(jnp.int32, (128, TOKENS), 0) // HEAD
-    head_of_lane = lax.broadcasted_iota(jnp.int32, (TOKENS, 128), 1) // HEAD
+    head_of_row = lax.broadcasted_iota(jnp.int32, (128, TOKENS), 0) >> 5
+    head_of_lane = lax.broadcasted_iota(jnp.int32, (TOKENS, 128), 1) >> 5
 
     def attend_back(group):
         loads[group].wait()
@@ -310,18 +330,22 @@
             weights = probs_ref[group * 4 + head]
             total = jnp.sum(products[at, :], axis=0, keepdims=True)
             grad_weights = dot(values, masked_t)
-            scores = (
-                weights.astype(F32) * ((grad_weights - total) * HEAD ** (-0.5))
-            ).astype(BF16)
+            scores = (weights.astype(F32) * ((grad_weights - total) * (1 / LOG2E))).astype(BF16)
             in_head = head_of_lane == head
             grad_keys += dot(scores, jnp.where(in_head, queries, jnp.zeros_like(queries)))
             grad_values += dot(weights, jnp.where(in_head, upstream, jnp.zeros_like(upstream)))
-            query_grad_t[at, :] = dot(keys_t_ref[at, :], scores).astype(BF16)
+            query_grad_t[at, :] = (dot(keys_t_ref[at, :], scores) * QUERY_SCALE).astype(BF16)
         packed_grad[4 + group] = grad_keys.astype(BF16)
         packed_grad[8 + group] = grad_values.astype(BF16)
 
     for group in range(4):
         attend_back(group)
+
+    for copy in nears:
+        copy.wait()
+    near = jnp.concatenate([near_ref[step].astype(F32) for step in range(4)], axis=0).astype(BF16)
+    grad = dot(near[:, :512], near[:, 512:], 0, 0)
+    weave([grad[:, q * 256 : q * 256 + 256] for q in range(4)], slots, slice(384, 640))
 
     identity = eye(TOKENS)
     for group in range(4):
@@ -400,11 +424,11 @@
             ]
 
 
-def call(kernel, inputs, held, outputs, saved, scratch, micros, kind=BF16, aliases=()):
+def call(kernel, inputs, held, outputs, saved, scratch, micros, kind=BF16, free=(), aliases=()):
     whole, there = pl.BlockSpec(memory_space=pltpu.VMEM), pl.BlockSpec(memory_space=pltpu.HBM)
     specs = [whole if at < held else there for at in range(len(inputs))]
-    if held == 0 and len(inputs) > 1:
-        specs[1] = pl.BlockSpec(memory_space=pl.ANY)
+    for at in free:
+        specs[at] = pl.BlockSpec(memory_space=pl.ANY)
     if inputs[0].ndim == 1:
         specs[0] = pl.BlockSpec(memory_space=pltpu.SMEM)
     return pl.pallas_call(
@@ -414,7 +438,7 @@
         out_specs=[whole if at < saved else there for at in range(len(outputs))],
         scratch_shapes=scratch,
         input_output_aliases=dict(aliases),
-        compiler_params=pltpu.CompilerParams(vmem_limit_bytes=56 * 2**20),
+        compiler_params=pltpu.CompilerParams(vmem_limit_bytes=(40 if micros > 9 else 14) * 2**20),
         cost_estimate=pl.CostEstimate(
             flops=micros * 10**9, bytes_accessed=micros * 10**6, transcendentals=0
         ),
@@ -478,34 +502,29 @@
     return jnp.concatenate([upper, lower], axis=0).transpose(2, 0, 1, 3)
 
 
-def window_bias(window_ids):
-    labels = window_ids.reshape(2, 3, 2, 2, 3, 2).transpose(5, 2, 0, 3, 1, 4)
-    labels = jnp.broadcast_to(labels[..., None], (2, 2, 2, 2, 3, 3, 2)).reshape(TOKENS)
-    return jnp.where(labels[:, None] == labels[None, :], 0.0, -1e30)
-
-
 def body(tokens, window_ids, cotangent, w_qkv, w_out, w_up, w_down, w_merge):
     order, cot_order = token_order(), cotangent_order()
     level_order = np.concatenate([cot_order[:, :MERGED], cot_order[:, MERGED:]]).transpose(0, 2, 1)
     by_feature, field, hidden_shape = (512, TOKENS), (TOKENS, 512), (TOKENS, 2048)
-    all_probs, near_shape, corner = (16, TOKENS, TOKENS), (MERGED, 512), (PACKED, 512)
-    where = jnp.stack([lax.axis_index("core"), lax.axis_index("y")])
+    all_probs, near_shape, corner = (16, TOKENS, TOKENS), (MERGED, 1536), (PACKED, 512)
+    places = window_places()
+    where = lax.axis_index(("y", "core")).reshape(1)
     quads = roll_back(tokens, cotangent)
 
     (cot, level_two, near0, near1, near2, near3, tokens_in, packed, keys_t, attended, first_t,
      middle, after_mlp, probs, hidden, slope) = call(
         forward_kernel,
-        [where, *quads, jnp.asarray(order, BF16), jnp.asarray(cot_order, BF16),
-         window_bias(window_ids), w_qkv, w_qkv.T, w_out, w_up, w_down, w_merge], 10,
+        [where, jnp.asarray(order, BF16), jnp.asarray(cot_order, BF16), window_ids,
+         jnp.asarray(places, BF16), jnp.asarray(places[1].T, F32), w_qkv, *quads,
+         w_out, w_up, w_down, w_merge], 7,
         [(MERGED, 1024), (MERGED, 1024)] + [near_shape] * 4 + [field, (12, TOKENS, 128),
          by_feature, by_feature, by_feature, field, field, all_probs, hidden_shape, hidden_shape],
         13,
-        [vmem(*by_feature), vmem(*by_feature), vmem(*hidden_shape), vmem(*hidden_shape),
-         vmem(*all_probs), vmem(*w_out.shape), vmem(*w_up.shape), vmem(*w_down.shape),
-         vmem(*w_merge.shape), dmas(4), dmas(3)],
-        15,
-    )
-    cotangents = lax.all_gather(cot, "y")
+        [vmem(4, *corner), pltpu.VMEM((TOKENS, TOKENS), F32), vmem(*by_feature), vmem(*by_feature),
+         vmem(*hidden_shape), vmem(*hidden_shape), vmem(*all_probs), vmem(*w_out.shape),
+         vmem(*w_up.shape), vmem(*w_down.shape), vmem(*w_merge.shape), dmas(4), dmas(4), dmas(3)],
+        15, free=range(7, 11),
+    )
     near = [near0]
     for step, block in ((1, near1), (2, near2), (3, near3)):
         near.append(lax.ppermute(block, "y", [(i, (i + step) % 4) for i in range(4)]))
@@ -521,12 +540,12 @@
         backward_kernel,
         [where, tokens_in, packed, keys_t, attended, middle_grad, first_t,
          jnp.asarray(order.transpose(0, 2, 1), BF16), jnp.asarray(level_order, BF16), level_two,
-         *near, cotangents, w_out, probs, w_qkv], 16,
+         w_out, *near, probs, w_qkv], 11,
         [corner] * 4 + [(64, 16, 640)] * 2, 4,
         [vmem(4, TOKENS, 128), vmem(*by_feature), pltpu.VMEM(by_feature, F32), vmem(*by_feature),
-         vmem(12, TOKENS, 128), vmem(*all_probs), vmem(*w_qkv.shape), vmem(2, 64, 16, 640),
-         dmas(5), dmas(2)],
-        12,
+         vmem(12, TOKENS, 128), vmem(*all_probs), vmem(*w_qkv.shape), vmem(4, *near_shape),
+         vmem(2, 64, 16, 640), dmas(4), dmas(5), dmas(2)],
+        12, free=range(12, 15),
     )
     blocks = None
     for kept, sent, place in ((keep, send, 0), (late_keep, late_send, 1152)):
@@ -535,7 +554,7 @@
             [kept, from_pair(sent)] + ([] if blocks is None else [blocks]), 0,
             [(64, 16, 1792)], 0,
             [vmem(*kept.shape), vmem(*kept.shape), dmas(4), dmas(4), dmas(4)],
-            2, aliases={} if blocks is None else {2: 0},
+            2, free=(1,), aliases={} if blocks is None else {2: 0},
         )
     corners = send_forth(corners)
     blocks, *corners = lax.optimization_barrier((blocks, *corners))

time: 154 us -> 153 us (level)
  blocking collectives: 14.1 us -> 0 us
  waiting for transfers between devices: 45.6 us -> 58.2 us
  local copies, waits for them, and re-layouts: 8.93 us -> 18 us
  Pallas kernels: 52.8 us -> 45.5 us
  starting transfers between devices: 24.8 us -> 20.5 us
  other arithmetic: 4.21 us -> 7.16 us
    all_gather x1 -> x0, blocking collectives: 14.1 us -> none  [body(): cotangents = lax.all_gather(cot, 'y')]
    pallas_call x6, Pallas kernels: 52.8 us -> 45.5 us  [call(): pl.pallas_call(kernel, out_shape=[jax.ShapeDtypeStruct(shape, kind) for s...]
    all_to_all x1, waiting for transfers between devices: 44.6 us -> 51.4 us  [body(): landed = lax.all_to_all(blocks, PAIRS, 0, 0, tiled=True)]
    concatenate x4, other arithmetic: 0.7 us -> 5.11 us  [roll_back(): jnp.concatenate([corner, cot[:, :512], cot[:, 512:]], axis=0)]
    all_to_all x1, starting transfers between devices: 9.79 us -> 6.17 us  [body(): landed = lax.all_to_all(blocks, PAIRS, 0, 0, tiled=True)]
    ppermute x6, waiting for transfers between devices: 0.98 us -> 4.59 us  [shifted_block(): return lax.ppermute(block, GRID, route)]
    slice x4, local copies, waits for them, and re-layouts: 0.02 us -> 3.21 us  [roll_back(): cot[:, :512]]
    unnamed x25 -> x32, local copies, waits for them, and re-layouts: 5.47 us -> 8.64 us
  transfers between devices with their start and end apart: 12 -> 12, of which waited for: 3 -> 6; matrix products, arithmetic and copies ran while one was open for 5% -> 8% of each run, Pallas kernels for 21% -> 16%
where the time goes in v6:
time: 153 us; the launch traced here: 151 us
  waiting for transfers between devices  58.2 us (38%)
  Pallas kernels  45.5 us (30%)
  starting transfers between devices  20.5 us (13%)
  local copies, waits for them, and re-layouts  18 us (12%)
  other arithmetic  7.16 us (5%)
    all_to_all x1, waiting for transfers between devices, body(): landed = lax.all_to_all(blocks, PAIRS, 0, 0, tiled=True)  51.4 us
    pallas_call x6, Pallas kernels, call(): pl.pallas_call(kernel, out_shape=[jax.ShapeDtypeStruct(shape, kind) for s...  45.5 us
    ppermute x6, starting transfers between devices, shifted_block(): return lax.ppermute(block, GRID, route)  10.2 us
    unnamed x32, local copies, waits for them, and re-layouts  8.64 us
    all_to_all x1, starting transfers between devices, body(): landed = lax.all_to_all(blocks, PAIRS, 0, 0, tiled=True)  6.17 us
    concatenate x4, other arithmetic, roll_back(): jnp.concatenate([corner, cot[:, :512], cot[:, 512:]], axis=0)  5.11 us
    ppermute x6, waiting for transfers between devices, shifted_block(): return lax.ppermute(block, GRID, route)  4.59 us
    ppermute x3, starting transfers between devices, body(): lax.ppermute(block, 'y', [(i, (i + step) % 4) for i in range(4)])  3.26 us
  transfers between devices with their start and end apart: 12, of which 6 were waited for; matrix products, arithmetic and copies ran while one was open for 8% of the time, Pallas kernels for 16%

profile of v6, /device:TPU:0, one launch (start us, length us, event | category | flops | bytes accessed | tf_op | source)
XLA Modules:
  0.0 150.5 jit_solution(3402916311519738307)
XLA Ops:
  0.7 1.7 %fusion.1 = (bf16[3,3,2,1024]{3,2,1,0:T(2,128)(2,1)}, bf16[3,3,2,1024]{3,2,1,0:T(2,128)(2,1)S(1)}, bf16[3,3,2,1024]{3,2,1,0:T(2,128)(2,1)S(1)}, bf16[3,3,2,1024]{3,2,1,0:T(2,128)(2,1)}) fusion(bf16[6,6,2,1024]{3,2,1,0:T(2,128)(2,1)} %bitcast.8), kind=kLoop, calls=%fused_computation.11 | loop fusion | bytes 294912 | tf_op jit(solution)/shard_map/slice | solution.py:471
  3.0 1.2 fusion
  4.3 1.4 pad_maximum_fusion.1
  5.7 5.0 %collective-permute-start = (bf16[108,512]{1,0:T(8,128)(2,1)}, bf16[108,512]{1,0:T(8,128)(2,1)S(1)}, u32[]{:S(2)}, u32[]{:S(2)}) collective-permute-start(bf16[108,512]{1,0:T(8,128)(2,1)} %pad_maximum_fusion.1), channel_id=1, source_target_pairs={{0,15},{1,0},{2,1},{3,2},{4,3},{5,4},{6,5},{7,6},{8,7},{9,8},{10,9... | collective-permute-start | bytes 331784 | tf_op jit(solution)/shard_map/ppermute | solution.py:465
  11.3 1.4 pad_maximum_fusion.2
  12.7 4.1 %collective-permute-start.1 = (bf16[108,512]{1,0:T(8,128)(2,1)}, bf16[108,512]{1,0:T(8,128)(2,1)S(1)}, u32[]{:S(2)}, u32[]{:S(2)}) collective-permute-start(bf16[108,512]{1,0:T(8,128)(2,1)} %pad_maximum_fusion.2), channel_id=1, source_target_pairs={{0,112},{1,113},{2,114},{3,115},{4,116},{5,117},{6,118},{7,119},{8... | collective-permute-start | bytes 331784 | tf_op jit(solution)/shard_map/ppermute | solution.py:465
  16.8 0.8 reshape.73
  18.3 1.4 pad_maximum_fusion.3
  20.0 1.4 reshape.67
  21.4 1.4 fusion.9
  23.5 0.9 pad_maximum_fusion.quad0_hbm
  24.5 1.6 %copy-done.2 = bf16[2048,512]{1,0:T(8,128)(2,1)S(1)} copy-done((bf16[2048,512]{1,0:T(8,128)(2,1)S(1)}, bf16[2048,512]{1,0:T(8,128)(2,1)}, u32[]{:S(2)}) %copy-start.2) | copy-done | bytes 2097176
  26.1 1.4 copy-done.3
  27.5 0.9 copy-done.11
  28.4 18.2 %shard_map.189 = (bf16[72,1024]{1,0:T(8,128)(2,1)S(1)}, bf16[72,1024]{1,0:T(8,128)(2,1)S(1)}, bf16[72,1536]{1,0:T(8,128)(2,1)S(1)}, bf16[72,1536]{1,0:T(8,128)(2...) custom-call(s32[1]{0:T(128)} %bitcast.where_ref, ...), custom_call_target="tpu_custom_call" | custom-call | flops 15000000512 | bytes 15000000 | tf_op jit(solution)/shard_map/pallas_call | solution.py:434
  46.6 0.9 copy-done.14
  47.5 2.2 %collective-permute-start.4 = (bf16[72,1536]{1,0:T(8,128)(2,1)S(1)}, bf16[72,1536]{1,0:T(8,128)(2,1)S(1)}, u32[]{:S(2)}, u32[]{:S(2)}) collective-permute-start(bf16[72,1536]{1,0:T(8,128)(2,1)S(1)} %get-tuple-element.56), channel_id=1, source_target_pairs={{0,8},{4,12},{8,0},{12,4},{1,9},{5,13},{9,1},{13,5},{2,10},{6,14},... | collective-permute-start | bytes 663560 | tf_op jit(solution)/shard_map/ppermute | solution.py:530
  49.7 1.1 collective-permute-start.5
  50.7 9.3 %shard_map.190 = (bf16[288,512]{1,0:T(8,128)(2,1)S(1)}, bf16[64,16,1152]{2,1,0:T(8,128)(2,1)S(1)}, bf16[64,16,1152]{2,1,0:T(8,128)(2,1)S(1)}) custom-call(s32[1]{0:T(128)} %bitcast.where_ref, bf16[72,1024]{1,0:T(8,128)(2,1)S(1)} %get-tuple-element.46.cot_ref, bf16[288,512]{1,0:T(8,128)(2,1)S(1)} %get-tuple-element.47.middle_ref, ...), custom_call_target="tpu_custom_call" | custom-call | flops 12000000000 | bytes 12000000 | tf_op jit(solution)/shard_map/pallas_call | solution.py:434
  60.7 0.8 collective-permute-done.3.near1_hbm
  61.5 1.0 collective-permute-done.5.near3_hbm
  62.6 2.0 %copy-done.13 = bf16[16,288,288]{2,1,0:T(8,128)(2,1)S(1)} copy-done((bf16[16,288,288]{2,1,0:T(8,128)(2,1)S(1)}, bf16[16,288,288]{2,1,0:T(8,128)(2,1)}, u32[]{:S(2)}) %copy-start.13) | copy-done | bytes 2654232
  64.6 12.0 %shard_map.191 = (bf16[108,512]{1,0:T(8,128)(2,1)S(1)}, bf16[108,512]{1,0:T(8,128)(2,1)S(1)}, bf16[108,512]{1,0:T(8,128)(2,1)S(1)}, bf16[108,512]{1,0:T(8,128)(2...) custom-call(s32[1]{0:T(128)} %bitcast.where_ref, ...), custom_call_target="tpu_custom_call" | custom-call | flops 12000000000 | bytes 12000000 | tf_op jit(solution)/shard_map/pallas_call | solution.py:434
  77.5 1.8 %shard_map.192.refs_0_ = bf16[64,16,1792]{2,1,0:T(8,128)(2,1)S(1)} custom-call(bf16[64,16,1152]{2,1,0:T(8,128)(2,1)S(1)} %get-tuple-element.61.keep_hbm, bf16[64,16,1152]{2,1,0:T(8,128)(2,1)S(1)} %collective-permute-done.7.arrived_hbm), custom_call_target="tpu_custom_call" | custom-call | flops 2000000000 | bytes 2000000 | tf_op jit(solution)/shard_map/pallas_call | solution.py:434
  79.7 1.4 shard_map.193
  81.1 1.8 %copy-done = bf16[64,16,1792]{2,1,0:T(8,128)(2,1)} copy-done((bf16[64,16,1792]{2,1,0:T(8,128)(2,1)}, bf16[64,16,1792]{2,1,0:T(8,128)(2,1)S(1)}, u32[]{:S(2)}) %copy-start) | copy-done | bytes 3670040
  82.9 4.1 %collective-permute-done.8 = bf16[108,512]{1,0:T(8,128)(2,1)S(1)} collective-permute-done((bf16[108,512]{1,0:T(8,128)(2,1)S(1)}, bf16[108,512]{1,0:T(8,128)(2,1)S(1)}, u32[]{:S(2)}, u32[]{:S(2)}) %collective-permute-start.8) | collective-permute-done | bytes 110624 | tf_op jit(solution)/shard_map/ppermute | solution.py:465
  87.5 6.2 %all-to-all-start = ((bf16[64,16,1792]{2,1,0:T(8,128)(2,1)}), bf16[64,16,1792]{2,1,0:T(8,128)(2,1)}, u32[]{:S(2)}, u32[]{:S(2)}) async-start(bf16[64,16,1792]{2,1,0:T(8,128)(2,1)} %copy-done), calls=%async_computation | async-start | bytes 7340032 | tf_op jit(solution)/shard_map/all_to_all | solution.py:561
  94.1 0.9 maximum_bitcast_fusion.1
  95.0 1.1 maximum_bitcast_fusion
  96.1 51.4 %all-to-all-done.landed_hbm = bf16[64,16,1792]{2,1,0:T(8,128)(2,1)} async-done(((bf16[64,16,1792]{2,1,0:T(8,128)(2,1)}), bf16[64,16,1792]{2,1,0:T(8,128)(2,1)}, u32[]{:S(2)}, u32[]{:S(2)}) %all-to-all-start) | async-done | bytes 3670048 | tf_op jit(solution)/shard_map/all_to_all | solution.py:561
  147.6 2.8 %shard_map.194 = (f32[4,1536]{1,0:T(4,128)}, f32[4,512]{1,0:T(4,128)}, f32[4,2048]{1,0:T(4,128)}, f32[16,512]{1,0:T(8,128)}, f32[16,1024]{1,0:T(8,128)}) custom-call(bf16[64,16,1792]{2,1,0:T(8,128)(2,1)} %all-to-all-done.landed_hbm), custom_call_target="tpu_custom_call" | custom-call | flops 3000000000 | bytes 3000000 | tf_op jit(solution)/shard_map/pallas_call | solution.py:434
  (68 shorter events, 5.8 us)
Async XLA Ops:
  0.6 23.8 %copy-start.12 = (f32[12,288]{1,0:T(8,128)S(1)}, f32[12,288]{1,0:T(8,128)}, u32[]{:S(2)}) copy-start(f32[12,288]{1,0:T(8,128)} %constant.26.clone.cols_t_ref) | copy-start | bytes 41476
  0.6 23.8 %copy-start.10 = (bf16[2,288,12]{2,1,0:T(8,128)(2,1)S(1)}, bf16[2,288,12]{2,1,0:T(8,128)(2,1)}, u32[]{:S(2)}) copy-start(bf16[2,288,12]{2,1,0:T(8,128)(2,1)} %constant.25.clone.places_ref) | copy-start | bytes 41476
  0.7 23.8 %copy-start.8 = (bf16[4,288,108]{2,1,0:T(8,128)(2,1)S(1)}, bf16[4,288,108]{2,1,0:T(8,128)(2,1)}, u32[]{:S(2)}) copy-start(bf16[4,288,108]{2,1,0:T(8,128)(2,1)} %constant.23.clone.order_ref) | copy-start | bytes 746500
  0.7 23.8 %copy-start.1 = (bf16[512,2048]{1,0:T(8,128)(2,1)S(1)}, bf16[512,2048]{1,0:T(8,128)(2,1)}, u32[]{:S(2)}) copy-start(bf16[512,2048]{1,0:T(8,128)(2,1)} %w_up_hbm.3) | copy-start | bytes 6291460
  0.7 23.8 %copy-start.5 = (bf16[512,512]{1,0:T(8,128)(2,1)S(1)}, bf16[512,512]{1,0:T(8,128)(2,1)}, u32[]{:S(2)}) copy-start(bf16[512,512]{1,0:T(8,128)(2,1)} %w_out.1) | copy-start | bytes 1572868
  0.7 23.8 %copy-start.6 = (s32[12,12]{1,0:T(8,128)S(1)}, s32[12,12]{1,0:T(8,128)}, u32[]{:S(2)}) copy-start(s32[12,12]{1,0:T(8,128)} %ids_ref.1) | copy-start | bytes 1732
  5.7 18.7 %collective-permute-start = (bf16[108,512]{1,0:T(8,128)(2,1)}, bf16[108,512]{1,0:T(8,128)(2,1)S(1)}, u32[]{:S(2)}, u32[]{:S(2)}) collective-permute-start(bf16[108,512]{1,0:T(8,128)(2,1)} %pad_maximum_fusion.1), channel_id=1, source_target_pairs={{0,15},{1,0},{2,1},{3,2},{4,3},{5,4},{6,5},{7,6},{8,7},{9,8},{10,9... | collective-permute-start | bytes 331784 | tf_op jit(solution)/shard_map/ppermute | solution.py:465
  12.7 11.7 %collective-permute-start.1 = (bf16[108,512]{1,0:T(8,128)(2,1)}, bf16[108,512]{1,0:T(8,128)(2,1)S(1)}, u32[]{:S(2)}, u32[]{:S(2)}) collective-permute-start(bf16[108,512]{1,0:T(8,128)(2,1)} %pad_maximum_fusion.2), channel_id=1, source_target_pairs={{0,112},{1,113},{2,114},{3,115},{4,116},{5,117},{6,118},{7,119},{8... | collective-permute-start | bytes 331784 | tf_op jit(solution)/shard_map/ppermute | solution.py:465
  19.7 4.7 %collective-permute-start.2 = (bf16[108,512]{1,0:T(8,128)(2,1)}, bf16[108,512]{1,0:T(8,128)(2,1)S(1)}, u32[]{:S(2)}, u32[]{:S(2)}) collective-permute-start(bf16[108,512]{1,0:T(8,128)(2,1)} %pad_maximum_fusion.3), channel_id=1, source_target_pairs={{0,127},{1,112},{2,113},{3,114},{4,115},{5,116},{6,117},{7,118},{8... | collective-permute-start | bytes 331784 | tf_op jit(solution)/shard_map/ppermute | solution.py:465
  24.5 1.6 %copy-start.2 = (bf16[2048,512]{1,0:T(8,128)(2,1)S(1)}, bf16[2048,512]{1,0:T(8,128)(2,1)}, u32[]{:S(2)}) copy-start(bf16[2048,512]{1,0:T(8,128)(2,1)} %w_down_hbm.3) | copy-start | bytes 6291460
  26.1 1.4 copy-start.3
  27.5 0.9 copy-start.11
  46.5 0.9 copy-start.14
  47.5 14.0 %collective-permute-start.3 = (bf16[72,1536]{1,0:T(8,128)(2,1)S(1)}, bf16[72,1536]{1,0:T(8,128)(2,1)S(1)}, u32[]{:S(2)}, u32[]{:S(2)}) collective-permute-start(bf16[72,1536]{1,0:T(8,128)(2,1)S(1)} %get-tuple-element.55), channel_id=1, source_target_pairs={{0,4},{4,8},{8,12},{12,0},{1,5},{5,9},{9,13},{13,1},{2,6},{6,10},{... | collective-permute-start | bytes 663560 | tf_op jit(solution)/shard_map/ppermute | solution.py:530
  47.5 14.0 %collective-permute-start.4 = (bf16[72,1536]{1,0:T(8,128)(2,1)S(1)}, bf16[72,1536]{1,0:T(8,128)(2,1)S(1)}, u32[]{:S(2)}, u32[]{:S(2)}) collective-permute-start(bf16[72,1536]{1,0:T(8,128)(2,1)S(1)} %get-tuple-element.56), channel_id=1, source_target_pairs={{0,8},{4,12},{8,0},{12,4},{1,9},{5,13},{9,1},{13,5},{2,10},{6,14},... | collective-permute-start | bytes 663560 | tf_op jit(solution)/shard_map/ppermute | solution.py:530
  49.7 12.9 %collective-permute-start.5 = (bf16[72,1536]{1,0:T(8,128)(2,1)S(1)}, bf16[72,1536]{1,0:T(8,128)(2,1)S(1)}, u32[]{:S(2)}, u32[]{:S(2)}) collective-permute-start(bf16[72,1536]{1,0:T(8,128)(2,1)S(1)} %get-tuple-element.57), channel_id=1, source_target_pairs={{0,12},{4,0},{8,4},{12,8},{1,13},{5,1},{9,5},{13,9},{2,14},{6,2},{... | collective-permute-start | bytes 663560 | tf_op jit(solution)/shard_map/ppermute | solution.py:530
  50.7 11.8 %copy-start.4 = (bf16[512,1536]{1,0:T(8,128)(2,1)S(1)}, bf16[512,1536]{1,0:T(8,128)(2,1)}, u32[]{:S(2)}) copy-start(bf16[512,1536]{1,0:T(8,128)(2,1)} %w_qkv_hbm.1) | copy-start | bytes 4718596
  50.7 11.8 %copy-start.7 = (bf16[4,108,288]{2,1,0:T(8,128)(2,1)S(1)}, bf16[4,108,288]{2,1,0:T(8,128)(2,1)}, u32[]{:S(2)}) copy-start(bf16[4,108,288]{2,1,0:T(8,128)(2,1)} %constant.27.clone.order_ref) | copy-start | bytes 746500
  50.7 11.8 %copy-start.9 = (bf16[8,108,72]{2,1,0:T(8,128)(2,1)S(1)}, bf16[8,108,72]{2,1,0:T(8,128)(2,1)}, u32[]{:S(2)}) copy-start(bf16[8,108,72]{2,1,0:T(8,128)(2,1)} %constant.28.clone.level_order_ref) | copy-start | bytes 373252
  50.7 11.8 %copy-start.15 = (bf16[12,288,128]{2,1,0:T(8,128)(2,1)S(1)}, bf16[12,288,128]{2,1,0:T(8,128)(2,1)}, u32[]{:S(2)}) copy-start(bf16[12,288,128]{2,1,0:T(8,128)(2,1)} %copy-done.14) | copy-start | bytes 2654212
  60.0 17.5 %collective-permute-start.7 = (bf16[64,16,1152]{2,1,0:T(8,128)(2,1)S(1)}, bf16[64,16,1152]{2,1,0:T(8,128)(2,1)S(1)}, u32[]{:S(2)}, u32[]{:S(2)}) collective-permute-start(bf16[64,16,1152]{2,1,0:T(8,128)(2,1)S(1)} %get-tuple-element.62), channel_id=1, source_target_pairs={{0,1},{1,0},{2,3},{3,2},{4,5},{5,4},{6,7},{7,6},{8,9},{9,8},{10,11... | collective-permute-start | bytes 7077896 | tf_op jit(solution)/shard_map/ppermute | solution.py:457
  62.6 2.0 %copy-start.13 = (bf16[16,288,288]{2,1,0:T(8,128)(2,1)S(1)}, bf16[16,288,288]{2,1,0:T(8,128)(2,1)}, u32[]{:S(2)}) copy-start(bf16[16,288,288]{2,1,0:T(8,128)(2,1)} %get-tuple-element.58.probs_hbm) | copy-start | bytes 7962628
  76.6 3.1 %collective-permute-start.6 = (bf16[64,16,640]{2,1,0:T(8,128)(2,1)S(1)}, bf16[64,16,640]{2,1,0:T(8,128)(2,1)S(1)}, u32[]{:S(2)}, u32[]{:S(2)}) collective-permute-start(bf16[64,16,640]{2,1,0:T(8,128)(2,1)S(1)} %get-tuple-element.60), channel_id=1, source_target_pairs={{0,1},{1,0},{2,3},{3,2},{4,5},{5,4},{6,7},{7,6},{8,9},{9,8},{10,11... | collective-permute-start | bytes 3932168 | tf_op jit(solution)/shard_map/ppermute | solution.py:457
  76.7 10.3 %collective-permute-start.8 = (bf16[108,512]{1,0:T(8,128)(2,1)S(1)}, bf16[108,512]{1,0:T(8,128)(2,1)S(1)}, u32[]{:S(2)}, u32[]{:S(2)}) collective-permute-start(bf16[108,512]{1,0:T(8,128)(2,1)S(1)} %get-tuple-element.63), channel_id=1, source_target_pairs={{0,17},{1,18},{2,19},{3,20},{4,21},{5,22},{6,23},{7,24},{8,25},{9,... | collective-permute-start | bytes 331784 | tf_op jit(solution)/shard_map/ppermute | solution.py:465
  77.4 10.1 %collective-permute-start.9 = (bf16[108,512]{1,0:T(8,128)(2,1)S(1)}, bf16[108,512]{1,0:T(8,128)(2,1)S(1)}, u32[]{:S(2)}, u32[]{:S(2)}) collective-permute-start(bf16[108,512]{1,0:T(8,128)(2,1)S(1)} %get-tuple-element.64), channel_id=1, source_target_pairs={{0,16},{1,17},{2,18},{3,19},{4,20},{5,21},{6,22},{7,23},{8,24},{9,... | collective-permute-start | bytes 331784 | tf_op jit(solution)/shard_map/ppermute | solution.py:465
  77.5 10.0 %collective-permute-start.10 = (bf16[108,512]{1,0:T(8,128)(2,1)S(1)}, bf16[108,512]{1,0:T(8,128)(2,1)S(1)}, u32[]{:S(2)}, u32[]{:S(2)}) collective-permute-start(bf16[108,512]{1,0:T(8,128)(2,1)S(1)} %get-tuple-element.65), channel_id=1, source_target_pairs={{0,1},{1,2},{2,3},{3,4},{4,5},{5,6},{6,7},{7,8},{8,9},{9,10},{10,1... | collective-permute-start | bytes 331784 | tf_op jit(solution)/shard_map/ppermute | solution.py:465
  81.1 1.8 %copy-start = (bf16[64,16,1792]{2,1,0:T(8,128)(2,1)}, bf16[64,16,1792]{2,1,0:T(8,128)(2,1)S(1)}, u32[]{:S(2)}) copy-start(bf16[64,16,1792]{2,1,0:T(8,128)(2,1)S(1)} %shard_map.193) | copy-start | bytes 11010052
  87.5 60.1 %all-to-all-start = ((bf16[64,16,1792]{2,1,0:T(8,128)(2,1)}), bf16[64,16,1792]{2,1,0:T(8,128)(2,1)}, u32[]{:S(2)}, u32[]{:S(2)}) async-start(bf16[64,16,1792]{2,1,0:T(8,128)(2,1)} %copy-done), calls=%async_computation | async-start | bytes 7340032 | tf_op jit(solution)/shard_map/all_to_all | solution.py:561

commit v7 on v6

--- a/solution.py
+++ b/solution.py
@@ -131,10 +131,10 @@
 def forward_kernel(
     where_ref, order_ref, cot_order_ref, ids_ref, places_ref, cols_t_ref, w_qkv,
     quad0_hbm, quad1_hbm, quad2_hbm, quad3_hbm, w_out_hbm, w_up_hbm, w_down_hbm, w_merge_hbm,
-    cot_ref, level_two_ref, near0, near1, near2, near3, tokens_ref, packed_ref, keys_t_ref,
-    attended_ref, first_t_ref, middle_ref, after_mlp_ref, probs_hbm, hidden_hbm, slope_hbm,
+    level_two_ref, near0, near1, near2, near3, tokens_ref, packed_ref, keys_t_ref,
+    attended_ref, first_t_ref, middle_ref, grad_after_ref, probs_hbm, slope_hbm, keep_hbm, send_hbm,
     quads_ref, bias_ref, query_t, values_t, slope_ref, hidden_ref, probs_ref, w_out, w_up, w_down,
-    w_merge, quad_sems, in_sems, out_sems,
+    w_merge, slots, quad_sems, in_sems, out_sems,
 ):
     quads = (quad0_hbm, quad1_hbm, quad2_hbm, quad3_hbm)
     quads = load([(quads[q], quads_ref.at[q]) for q in range(4)], quad_sems)
@@ -153,35 +153,36 @@
     tokens_ref[...] = tokens.astype(BF16)
     halves = sum(dot(cot_order_ref[q], quads_ref[q]) for q in range(4))
     cotangent = jnp.concatenate([halves[:MERGED], halves[MERGED:]], axis=1).astype(BF16)
-    cot_ref[...] = cotangent
     first_norm = normalize(tokens)[0].astype(BF16)
     first_t_ref[...] = dot(eye(512), first_norm, 1, 1).astype(BF16)
     by_lane = eye(128)
-    for part in range(12):
-        grid = dot(first_norm, w_qkv[:, part * 128 : part * 128 + 128])
-        grid = (grid * QUERY_SCALE if part < 4 else grid).astype(BF16)
-        packed_ref[part] = grid
-        turned = (query_t, keys_t_ref, values_t)[part // 4]
-        rows = slice(part % 4 * 128, part % 4 * 128 + 128)
-        turned[rows, :] = dot(by_lane, grid, 1, 1).astype(BF16)
+    for part in range(3):
+        wide = dot(first_norm, w_qkv[:, part * 512 : part * 512 + 512])
+        wide = (wide * QUERY_SCALE if part == 0 else wide).astype(BF16)
+        for group in range(4):
+            grid = wide[:, group * 128 : group * 128 + 128]
+            packed_ref[part * 4 + group] = grid
+            turned = (query_t, keys_t_ref, values_t)[part]
+            turned[group * 128 : group * 128 + 128, :] = dot(by_lane, grid, 1, 1).astype(BF16)
 
     head_of_row = lax.broadcasted_iota(jnp.int32, (128, TOKENS), 0) >> 5
 
-    def attend(group, _):
-        keys = packed_ref[4 + group]
-        queries = query_t[pl.ds(pl.multiple_of(group * 128, 128), 128), :]
-        for head in range(4):
-            masked = jnp.where(head_of_row == head, queries, jnp.zeros_like(queries))
-            scores = dot(keys, masked) + bias_ref[...]
-            raised = jnp.exp2(scores - jnp.max(scores, axis=0, keepdims=True))
-            inverse = 1.0 / jnp.sum(raised, axis=0, keepdims=True)
-            probs = (raised * inverse).astype(BF16)
-            probs_ref[group * 4 + head] = probs
-            at = pl.ds(pl.multiple_of(group * 128 + head * HEAD, HEAD), HEAD)
-            attended_ref[at, :] = dot(values_t[at, :], probs).astype(BF16)
-        return 0
-
-    lax.fori_loop(0, 4, attend, 0)
+    def scores_of(head):
+        queries = query_t[head // 4 * 128 : head // 4 * 128 + 128, :]
+        masked = jnp.where(head_of_row == head % 4, queries, jnp.zeros_like(queries))
+        return dot(packed_ref[4 + head // 4], masked)
+
+    ahead = scores_of(0)
+    for head in range(16):
+        scores = ahead + bias_ref[...]
+        if head < 15:
+            ahead = scores_of(head + 1)
+        raised = jnp.exp2(scores - jnp.max(scores, axis=0, keepdims=True))
+        inverse = 1.0 / jnp.sum(raised, axis=0, keepdims=True)
+        probs = (raised * inverse).astype(BF16)
+        probs_ref[head] = probs
+        at = slice(head * HEAD, head * HEAD + HEAD)
+        attended_ref[at, :] = dot(values_t[at, :], probs).astype(BF16)
     saves = load([(probs_ref, probs_hbm)], out_sems.at[pl.ds(0, 1)])
 
     attended = dot(eye(TOKENS), attended_ref[...], 1, 1).astype(BF16)
@@ -194,18 +195,21 @@
     mlp = jnp.zeros((TOKENS, 512), F32)
     weights[1].wait()
     weights[2].wait()
+    ahead = dot(second_norm, w_up[:, :512])
     for part in range(4):
         cols = slice(part * 512, part * 512 + 512)
-        before = dot(second_norm, w_up[:, cols])
+        before = ahead
+        if part < 3:
+            ahead = dot(second_norm, w_up[:, part * 512 + 512 : part * 512 + 1024])
         cumulative, density = gelu_parts(before)
         hidden = (before * cumulative).astype(BF16)
         hidden_ref[:, cols] = hidden
         slope_ref[:, cols] = (cumulative + before * density * 0.3989422804014327).astype(BF16)
         mlp = mlp + dot(hidden, w_down[cols])
-    saves += load([(hidden_ref, hidden_hbm), (slope_ref, slope_hbm)], out_sems.at[pl.ds(1, 2)])
+    saves += load([(slope_ref, slope_hbm)], out_sems.at[pl.ds(1, 1)])
     after_mlp = (middle + mlp).astype(BF16)
-    after_mlp_ref[...] = after_mlp
-    merged_norm = [v.astype(BF16) for v in merge_norm(after_mlp.astype(F32))[0]]
+    pieces, inverse_out = merge_norm(after_mlp.astype(F32))
+    merged_norm = [v.astype(BF16) for v in pieces]
     order = near_order()
     spread = [dot(v, order) for v in merged_norm]
     blocks = [
@@ -219,31 +223,11 @@
             block = jnp.where(y == own, blocks[(own + step) % 4], block)
         near[:, :512] = block
         near[:, 512:] = cotangent
+
     weights[3].wait()
     level_two_ref[...] = sum(
         dot(merged_norm[p], w_merge[p * 512 : p * 512 + 512]) for p in range(4)
     ).astype(BF16)
-    for save in saves:
-        save.wait()
-
-
-def middle_kernel(
-    where_ref, cot_ref, middle_ref, after_mlp_ref, attended_ref,
-    w_merge_hbm, hidden_hbm, w_down_hbm, slope_hbm, w_up_hbm,
-    middle_grad_ref, keep_hbm, send_hbm,
-    w_merge, hidden_ref, w_down, slope_ref, w_up, slots, sems, out_sems,
-):
-    loads = load(
-        [(w_merge_hbm, w_merge), (hidden_hbm, hidden_ref), (w_down_hbm, w_down),
-         (slope_hbm, slope_ref), (w_up_hbm, w_up)],
-        sems,
-    )
-    core = where_ref[0] & 1
-    cotangent = cot_ref[...]
-    pieces, inverse_out = merge_norm(after_mlp_ref[...].astype(F32))
-    normed_mid, inverse_mid = normalize(middle_ref[...].astype(F32))
-    second_t = dot(eye(512), normed_mid.astype(BF16), 1, 1).astype(BF16)
-    loads[0].wait()
     upstream = [dot(cotangent, w_merge[p * 512 : p * 512 + 512], 1, 1) for p in range(4)]
     mean_grad = sum(jnp.sum(v, axis=-1, keepdims=True) for v in upstream) / 2048.0
     mean_cross = (
@@ -252,6 +236,29 @@
     grad_after = jnp.concatenate(
         [inverse_out * (v - mean_grad - u * mean_cross) for v, u in zip(upstream, pieces)], axis=0
     ).astype(BF16)
+    grad_after_ref[...] = grad_after
+    core = where_ref[0] & 1
+    for part in range(4):
+        grad = dot(hidden_ref[:, part * 512 : part * 512 + 512], grad_after, 0, 0).astype(BF16)
+        for block in range(32):
+            slots[block % 2, part * 16 + block // 2] = grad[block * 16 : block * 16 + 16]
+    saves += load(
+        [(slots.at[core], keep_hbm), (slots.at[1 - core], send_hbm)], out_sems.at[pl.ds(2, 2)]
+    )
+    for save in saves:
+        save.wait()
+
+
+def middle_kernel(
+    where_ref, grad_after_ref, middle_ref, attended_ref, w_down_hbm, slope_hbm, w_up_hbm,
+    middle_grad_ref, keep_hbm, send_hbm,
+    w_down, slope_ref, w_up, slots, sems, out_sems,
+):
+    loads = load([(w_down_hbm, w_down), (slope_hbm, slope_ref), (w_up_hbm, w_up)], sems)
+    core = where_ref[0] & 1
+    grad_after = grad_after_ref[...]
+    normed_mid, inverse_mid = normalize(middle_ref[...].astype(F32))
+    second_t = dot(eye(512), normed_mid.astype(BF16), 1, 1).astype(BF16)
 
     def save(cols, at):
         return load(
@@ -260,15 +267,9 @@
             out_sems.at[pl.ds(at, 2)],
         )
 
-    loads[1].wait()
-    for part in range(4):
-        grad = dot(hidden_ref[:, part * 512 : part * 512 + 512], grad_after, 0, 0).astype(BF16)
-        for block in range(32):
-            slots[block % 2, part * 16 + block // 2, :, :512] = grad[block * 16 : block * 16 + 16]
-    saves = save(pl.ds(0, 512), 0)
     back_up = jnp.zeros((TOKENS, 512), F32)
     grads_up = []
-    for copy in loads[2:]:
+    for copy in loads:
         copy.wait()
     for part in range(4):
         cols = slice(part * 512, part * 512 + 512)
@@ -277,14 +278,15 @@
         ).astype(BF16)
         grads_up.append(dot(second_t, grad_before))
         back_up = back_up + dot(grad_before, w_up[:, cols], 1, 1)
-    weave(grads_up, slots, slice(512, 1024))
+    weave(grads_up, slots, slice(0, 512))
+    saves = save(pl.ds(0, 512), 0)
     middle_grad = (
         grad_after.astype(F32) + norm_back(normed_mid, inverse_mid, back_up)
     ).astype(BF16)
     middle_grad_ref[...] = middle_grad
     grad = dot(attended_ref[...], middle_grad)
-    weave([grad[:, p * 128 : p * 128 + 128] for p in range(4)], slots, slice(1024, 1152))
-    saves += save(pl.ds(512, 640), 2)
+    weave([grad[:, p * 128 : p * 128 + 128] for p in range(4)], slots, slice(512, 640))
+    saves += save(pl.ds(512, 128), 2)
     for copy in saves:
         copy.wait()
 
@@ -306,10 +308,9 @@
     nears = load([(nears[step], near_ref.at[step]) for step in range(4)], near_sems)
     core = where_ref[0] & 1
     middle_grad = middle_grad_ref[...]
+    wide = dot(middle_grad, w_out[...], 1, 1).astype(BF16)
     for group in range(4):
-        grad_heads[group] = dot(
-            middle_grad, w_out[group * 128 : group * 128 + 128], 1, 1
-        ).astype(BF16)
+        grad_heads[group] = wide[:, group * 128 : group * 128 + 128]
     grad_heads_t[...] = dot(w_out[...], middle_grad, 1, 1).astype(BF16)
     products[...] = grad_heads_t[...].astype(F32) * attended_ref[...].astype(F32)
 
@@ -399,25 +400,31 @@
         save.wait()
 
 
-def share_kernel(landed_hbm, qkv_ref, out_ref, up_ref, down_ref, merge_ref, landed_ref, sems):
-    loads = load(
-        [(landed_hbm.at[pl.ds(p * 16, 16)], landed_ref.at[pl.ds(p * 16, 16)]) for p in range(4)],
-        sems,
-    )
-    shared = jnp.zeros((16, 1536), F32)
+def arrive(landed_hbm, landed_ref, sems):
+    parts = [pl.ds(p * 16, 16) for p in range(4)]
+    loads = load([(landed_hbm.at[p], landed_ref.at[p]) for p in parts], sems)
+    for chip in range(64):
+        if chip % 16 == 0:
+            loads[chip // 16].wait()
+        yield chip, landed_ref[chip].astype(F32)
+
+
+def down_kernel(landed_hbm, down_ref, landed_ref, sems):
+    down_ref[...] = sum(block for _, block in arrive(landed_hbm, landed_ref, sems))
+
+
+def share_kernel(landed_hbm, qkv_ref, out_ref, up_ref, merge_ref, landed_ref, sems):
+    shared = jnp.zeros((16, 1024), F32)
     merge = [jnp.zeros((16, 256), F32) for _ in range(4)]
-    for part in range(4):
-        loads[part].wait()
-        for chip in range(part * 16, part * 16 + 16):
-            y = chip // 2 % 4
-            shared = shared + landed_ref[chip, :, :1536].astype(F32)
-            merge[y] = merge[y] + landed_ref[chip, :, 1536:].astype(F32)
-    down_ref[...] = shared[:, :512]
+    for chip, block in arrive(landed_hbm, landed_ref, sems):
+        y = chip // 2 % 4
+        shared = shared + block[:, :1024]
+        merge[y] = merge[y] + block[:, 1024:]
     for block in range(4):
         rows = shared[block * 4 : block * 4 + 4]
-        up_ref[:, block * 512 : block * 512 + 512] = rows[:, 512:1024]
-        out_ref[:, block * 128 : block * 128 + 128] = rows[:, 1024:1152]
-        qkv_ref[:, block * 384 : block * 384 + 384] = rows[:, 1152:]
+        up_ref[:, block * 512 : block * 512 + 512] = rows[:, :512]
+        out_ref[:, block * 128 : block * 128 + 128] = rows[:, 512:640]
+        qkv_ref[:, block * 384 : block * 384 + 384] = rows[:, 640:]
         for y in range(4):
             merge_ref[y * 4 : y * 4 + 4, block * 256 : block * 256 + 256] = merge[y][
                 block * 4 : block * 4 + 4
@@ -438,7 +445,7 @@
         out_specs=[whole if at < saved else there for at in range(len(outputs))],
         scratch_shapes=scratch,
         input_output_aliases=dict(aliases),
-        compiler_params=pltpu.CompilerParams(vmem_limit_bytes=(40 if micros > 9 else 14) * 2**20),
+        compiler_params=pltpu.CompilerParams(vmem_limit_bytes=(56 if micros > 5 else 14) * 2**20),
         cost_estimate=pl.CostEstimate(
             flops=micros * 10**9, bytes_accessed=micros * 10**6, transcendentals=0
         ),
@@ -453,8 +460,15 @@
     return pltpu.SemaphoreType.DMA((count,))
 
 
-def from_pair(send):
-    return lax.ppermute(send, "core", [(0, 1), (1, 0)])
+def pair_sum(keep, send, width, place, blocks=None):
+    arrived = lax.ppermute(send, "core", [(0, 1), (1, 0)])
+    blocks, = call(
+        functools.partial(pair_kernel, place=place),
+        [keep, arrived] + ([] if blocks is None else [blocks]), 0, [(64, 16, width)], 0,
+        [vmem(*keep.shape), vmem(*keep.shape), dmas(4), dmas(4), dmas(4)],
+        2, free=(1,), aliases={} if blocks is None else {2: 0},
+    )
+    return blocks
 
 
 def shifted_block(block, down, right):
@@ -511,30 +525,36 @@
     where = lax.axis_index(("y", "core")).reshape(1)
     quads = roll_back(tokens, cotangent)
 
-    (cot, level_two, near0, near1, near2, near3, tokens_in, packed, keys_t, attended, first_t,
-     middle, after_mlp, probs, hidden, slope) = call(
+    (level_two, near0, near1, near2, near3, tokens_in, packed, keys_t, attended, first_t,
+     middle, grad_after, probs, slope, down_keep, down_send) = call(
         forward_kernel,
         [where, jnp.asarray(order, BF16), jnp.asarray(cot_order, BF16), window_ids,
          jnp.asarray(places, BF16), jnp.asarray(places[1].T, F32), w_qkv, *quads,
          w_out, w_up, w_down, w_merge], 7,
-        [(MERGED, 1024), (MERGED, 1024)] + [near_shape] * 4 + [field, (12, TOKENS, 128),
-         by_feature, by_feature, by_feature, field, field, all_probs, hidden_shape, hidden_shape],
-        13,
+        [(MERGED, 1024)] + [near_shape] * 4 + [field, (12, TOKENS, 128), by_feature, by_feature,
+         by_feature, field, field, all_probs, hidden_shape, (64, 16, 512), (64, 16, 512)], 12,
         [vmem(4, *corner), pltpu.VMEM((TOKENS, TOKENS), F32), vmem(*by_feature), vmem(*by_feature),
          vmem(*hidden_shape), vmem(*hidden_shape), vmem(*all_probs), vmem(*w_out.shape),
-         vmem(*w_up.shape), vmem(*w_down.shape), vmem(*w_merge.shape), dmas(4), dmas(4), dmas(3)],
-        15, free=range(7, 11),
+         vmem(*w_up.shape), vmem(*w_down.shape), vmem(*w_merge.shape), vmem(2, 64, 16, 512),
+         dmas(4), dmas(4), dmas(4)],
+        20, free=range(7, 11),
     )
     near = [near0]
     for step, block in ((1, near1), (2, near2), (3, near3)):
         near.append(lax.ppermute(block, "y", [(i, (i + step) % 4) for i in range(4)]))
     middle_grad, keep, send = call(
         middle_kernel,
-        [where, cot, middle, after_mlp, attended, w_merge, hidden, w_down, slope, w_up], 5,
-        [field, (64, 16, 1152), (64, 16, 1152)], 1,
-        [vmem(*w_merge.shape), vmem(*hidden_shape), vmem(*w_down.shape), vmem(*hidden_shape),
-         vmem(*w_up.shape), vmem(2, 64, 16, 1152), dmas(5), dmas(4)],
-        12,
+        [where, grad_after, middle, attended, w_down, slope, w_up], 4,
+        [field, (64, 16, 640), (64, 16, 640)], 1,
+        [vmem(*w_down.shape), vmem(*hidden_shape), vmem(*w_up.shape), vmem(2, 64, 16, 640),
+         dmas(3), dmas(4)],
+        7,
+    )
+    down_blocks = pair_sum(down_keep, down_send, 512, 0)
+    middle_grad, down_blocks = lax.optimization_barrier((middle_grad, down_blocks))
+    landed = lax.all_to_all(down_blocks, PAIRS, 0, 0, tiled=True)
+    grad_down, = call(
+        down_kernel, [landed], 0, [(16, 512)], 1, [vmem(64, 16, 512), dmas(4)], 1, kind=F32
     )
     *corners, late_keep, late_send = call(
         backward_kernel,
@@ -547,21 +567,14 @@
          vmem(2, 64, 16, 640), dmas(4), dmas(5), dmas(2)],
         12, free=range(12, 15),
     )
-    blocks = None
-    for kept, sent, place in ((keep, send, 0), (late_keep, late_send, 1152)):
-        blocks, = call(
-            functools.partial(pair_kernel, place=place),
-            [kept, from_pair(sent)] + ([] if blocks is None else [blocks]), 0,
-            [(64, 16, 1792)], 0,
-            [vmem(*kept.shape), vmem(*kept.shape), dmas(4), dmas(4), dmas(4)],
-            2, free=(1,), aliases={} if blocks is None else {2: 0},
-        )
+    blocks = pair_sum(keep, send, 1280, 0)
+    late_keep, grad_down = lax.optimization_barrier((late_keep, grad_down))
+    blocks = pair_sum(late_keep, late_send, 1280, 640, blocks)
     corners = send_forth(corners)
     blocks, *corners = lax.optimization_barrier((blocks, *corners))
     landed = lax.all_to_all(blocks, PAIRS, 0, 0, tiled=True)
-    grad_qkv, grad_out, grad_up, grad_down, grad_merge = call(
-        share_kernel, [landed], 0,
-        [(4, 1536), (4, 512), (4, 2048), (16, 512), (16, 1024)], 5,
+    grad_qkv, grad_out, grad_up, grad_merge = call(
+        share_kernel, [landed], 0, [(4, 1536), (4, 512), (4, 2048), (16, 1024)], 4,
         [vmem(*blocks.shape), dmas(4)], 3, kind=F32,
     )
     grad_tokens = from_corners([c[:MERGED].reshape(6, 6, 2, 512) for c in corners])

time: 153 us -> 144 us (0.941); the launches traced: 151 us -> 144 us
  local copies, waits for them, and re-layouts: 18 us -> 5.36 us
  starting transfers between devices: 20.5 us -> 31 us
  waiting for transfers between devices: 58.2 us -> 47.9 us
  Pallas kernels: 45.5 us -> 55.3 us
  other arithmetic: 7.16 us -> 2.75 us
    all_to_all x1, waiting for transfers between devices: 51.4 us -> 29.8 us  [body(): landed = lax.all_to_all(blocks, PAIRS, 0, 0, tiled=True)]
    all_to_all x0 -> x1, waiting for transfers between devices: none -> 14.7 us  [body(): landed = lax.all_to_all(down_blocks, PAIRS, 0, 0, tiled=True)]
    pallas_call x6 -> x8, Pallas kernels: 45.5 us -> 55.3 us  [call(): pl.pallas_call(kernel, out_shape=[jax.ShapeDtypeStruct(shape, kind) for s...]
    all_to_all x0 -> x1, starting transfers between devices: none -> 8.46 us  [body(): landed = lax.all_to_all(down_blocks, PAIRS, 0, 0, tiled=True)]
    unnamed x32 -> x26, local copies, waits for them, and re-layouts: 8.64 us -> 2.68 us
    concatenate x4, other arithmetic: 5.11 us -> 0.71 us  [roll_back(): jnp.concatenate([corner, cot[:, :512], cot[:, 512:]], axis=0)]
    slice x4, local copies, waits for them, and re-layouts: 3.21 us -> 0.02 us  [roll_back(): cot[:, :512]]
    ppermute x6, starting transfers between devices: 10.2 us -> 13.4 us  [shifted_block(): return lax.ppermute(block, GRID, route)]
  transfers between devices with their start and end apart: 12 -> 14, of which waited for: 6 -> 5; matrix products, arithmetic and copies ran while one was open for 8% -> 2% of each run, Pallas kernels for 16% -> 21%
where the time goes in v7:
time: 144 us
  Pallas kernels  55.3 us (38%)
  waiting for transfers between devices  47.9 us (33%)
  starting transfers between devices  31 us (22%)
  local copies, waits for them, and re-layouts  5.36 us (4%)
  other arithmetic  2.75 us (2%)
    pallas_call x8, Pallas kernels, call(): pl.pallas_call(kernel, out_shape=[jax.ShapeDtypeStruct(shape, kind) for s...  55.3 us
    all_to_all x1, waiting for transfers between devices, body(): landed = lax.all_to_all(blocks, PAIRS, 0, 0, tiled=True)  29.8 us
    all_to_all x1, waiting for transfers between devices, body(): landed = lax.all_to_all(down_blocks, PAIRS, 0, 0, tiled=True)  14.7 us
    ppermute x6, starting transfers between devices, shifted_block(): return lax.ppermute(block, GRID, route)  13.4 us
    all_to_all x1, starting transfers between devices, body(): landed = lax.all_to_all(down_blocks, PAIRS, 0, 0, tiled=True)  8.46 us
    all_to_all x1, starting transfers between devices, body(): landed = lax.all_to_all(blocks, PAIRS, 0, 0, tiled=True)  4.86 us
    ppermute x3, starting transfers between devices, body(): lax.ppermute(block, 'y', [(i, (i + step) % 4) for i in range(4)])  3.71 us
    ppermute x6, waiting for transfers between devices, shifted_block(): return lax.ppermute(block, GRID, route)  3.1 us
  transfers between devices with their start and end apart: 14, of which 5 were waited for; matrix products, arithmetic and copies ran while one was open for 2% of the time, Pallas kernels for 21%

profile of v7, /device:TPU:0, one launch (start us, length us, event | category | flops | bytes accessed | tf_op | source)
XLA Modules:
  0.0 143.6 jit_solution(15930535371034007521)
XLA Ops:
  0.6 0.9 fusion.1
  1.6 1.2 fusion
  2.9 5.1 %collective-permute-start = (bf16[108,512]{1,0:T(8,128)(2,1)S(1)}, bf16[108,512]{1,0:T(8,128)(2,1)S(1)}, u32[]{:S(2)}, u32[]{:S(2)}) collective-permute-start(bf16[108,512]{1,0:T(8,128)(2,1)S(1)} %pad_maximum_fusion.1), channel_id=1, source_target_pairs={{0,15},{1,0},{2,1},{3,2},{4,3},{5,4},{6,5},{7,6},{8,7},{9,8},{10,9... | collective-permute-start | bytes 331784 | tf_op jit(solution)/shard_map/ppermute | solution.py:479
  8.0 4.1 %collective-permute-start.1 = (bf16[108,512]{1,0:T(8,128)(2,1)S(1)}, bf16[108,512]{1,0:T(8,128)(2,1)S(1)}, u32[]{:S(2)}, u32[]{:S(2)}) collective-permute-start(bf16[108,512]{1,0:T(8,128)(2,1)S(1)} %pad_maximum_fusion.2), channel_id=1, source_target_pairs={{0,112},{1,113},{2,114},{3,115},{4,116},{5,117},{6,118},{7,119},{8... | collective-permute-start | bytes 331784 | tf_op jit(solution)/shard_map/ppermute | solution.py:479
  12.3 0.4 collective-permute-start.2
  12.8 0.7 pad_maximum_fusion.quad0_hbm
  13.5 1.2 collective-permute-done.1.quad2_hbm
  14.7 1.9 %collective-permute-done.2.quad3_hbm = bf16[108,512]{1,0:T(8,128)(2,1)S(1)} collective-permute-done((bf16[108,512]{1,0:T(8,128)(2,1)S(1)}, bf16[108,512]{1,0:T(8,128)(2,1)S(1)}, u32[]{:S(2)}, u32[]{:S(2)}) %collective-permute-start.2) | collective-permute-done | bytes 110624 | tf_op jit(solution)/shard_map/ppermute | solution.py:479
  16.6 0.6 copy-done.9
  17.2 23.5 %shard_map.189 = (bf16[72,1024]{1,0:T(8,128)(2,1)}, bf16[72,1536]{1,0:T(8,128)(2,1)}, bf16[72,1536]{1,0:T(8,128)(2,1)}, bf16[72,1536]{1,0:T(8,128)(2,1)}, bf16[7...) custom-call(s32[1]{0:T(128)} %bitcast.where_ref, ...), custom_call_target="tpu_custom_call" | custom-call | flops 20000000000 | bytes 20000000 | tf_op jit(solution)/shard_map/pallas_call | solution.py:441
  40.8 2.5 %collective-permute-start.5 = (bf16[72,1536]{1,0:T(8,128)(2,1)}, bf16[72,1536]{1,0:T(8,128)(2,1)S(1)}, u32[]{:S(2)}, u32[]{:S(2)}) collective-permute-start(bf16[72,1536]{1,0:T(8,128)(2,1)} %get-tuple-element.60), channel_id=1, source_target_pairs={{0,8},{4,12},{8,0},{12,4},{1,9},{5,13},{9,1},{13,5},{2,10},{6,14},... | collective-permute-start | bytes 663560 | tf_op jit(solution)/shard_map/ppermute | solution.py:544
  43.3 1.2 collective-permute-start.6
  44.5 9.2 %shard_map.190 = (bf16[288,512]{1,0:T(8,128)(2,1)}, bf16[64,16,640]{2,1,0:T(8,128)(2,1)}, bf16[64,16,640]{2,1,0:T(8,128)(2,1)}) custom-call(s32[1]{0:T(128)} %bitcast.where_ref, bf16[288,512]{1,0:T(8,128)(2,1)} %get-tuple-element.49.grad_after_ref, bf16[288,512]{1,0:T(8,128)(2,1)} %get-tuple-element.50.middle_ref, ...), custom_call_target="tpu_custom_call" | custom-call | flops 7000000000 | bytes 7000000 | tf_op jit(solution)/shard_map/pallas_call | solution.py:441
  53.8 1.3 shard_map.191
  55.1 0.3 collective-permute-done.6.near3_hbm
  55.4 0.4 copy-done.4
  56.1 13.5 %shard_map.192 = (bf16[108,512]{1,0:T(8,128)(2,1)}, bf16[108,512]{1,0:T(8,128)(2,1)}, bf16[108,512]{1,0:T(8,128)(2,1)}, bf16[108,512]{1,0:T(8,128)(2,1)}, bf16[6...) custom-call(s32[1]{0:T(128)} %bitcast.where_ref, bf16[288,512]{1,0:T(8,128)(2,1)} %get-tuple-element.45.tokens_ref, ...), custom_call_target="tpu_custom_call" | custom-call | flops 12000000000 | bytes 12000000 | tf_op jit(solution)/shard_map/pallas_call | solution.py:441
  69.6 0.4 collective-permute-start.7
  70.0 8.5 %all-to-all-start = ((bf16[64,16,512]{2,1,0:T(8,128)(2,1)}), bf16[64,16,512]{2,1,0:T(8,128)(2,1)}, u32[]{:S(2)}, u32[]{:S(2)}) async-start(bf16[64,16,512]{2,1,0:T(8,128)(2,1)} %shard_map.191), calls=%async_computation | async-start | bytes 2097152 | tf_op jit(solution)/shard_map/all_to_all | solution.py:555
  78.5 0.8 collective-permute-start.9
  79.3 1.5 %collective-permute-start.10 = (bf16[108,512]{1,0:T(8,128)(2,1)S(1)}, bf16[108,512]{1,0:T(8,128)(2,1)S(1)}, u32[]{:S(2)}, u32[]{:S(2)}) collective-permute-start(bf16[108,512]{1,0:T(8,128)(2,1)S(1)} %copy-done.11), channel_id=1, source_target_pairs={{0,16},{1,17},{2,18},{3,19},{4,20},{5,21},{6,22},{7,23},{8,24},{9,... | collective-permute-start | bytes 331784 | tf_op jit(solution)/shard_map/ppermute | solution.py:479
  80.7 1.5 %collective-permute-start.11 = (bf16[108,512]{1,0:T(8,128)(2,1)S(1)}, bf16[108,512]{1,0:T(8,128)(2,1)S(1)}, u32[]{:S(2)}, u32[]{:S(2)}) collective-permute-start(bf16[108,512]{1,0:T(8,128)(2,1)S(1)} %copy-done.10), channel_id=1, source_target_pairs={{0,1},{1,2},{2,3},{3,4},{4,5},{5,6},{6,7},{7,8},{8,9},{9,10},{10,1... | collective-permute-start | bytes 331784 | tf_op jit(solution)/shard_map/ppermute | solution.py:479
  82.3 1.3 copy-done.1
  83.6 2.1 %shard_map.194.refs_0_ = bf16[64,16,1280]{2,1,0:T(8,128)(2,1)} custom-call(bf16[64,16,640]{2,1,0:T(8,128)(2,1)S(1)} %copy-done.1, bf16[64,16,640]{2,1,0:T(8,128)(2,1)S(1)} %collective-permute-done.8.arrived_hbm), custom_call_target="tpu_custom_call" | custom-call | flops 2000000000 | bytes 2000000 | tf_op jit(solution)/shard_map/pallas_call | solution.py:441
  85.7 14.7 %all-to-all-done.landed_hbm = bf16[64,16,512]{2,1,0:T(8,128)(2,1)} async-done(((bf16[64,16,512]{2,1,0:T(8,128)(2,1)}), bf16[64,16,512]{2,1,0:T(8,128)(2,1)}, u32[]{:S(2)}, u32[]{:S(2)}) %all-to-all-start) | async-done | bytes 1048608 | tf_op jit(solution)/shard_map/all_to_all | solution.py:555
  100.3 1.9 %shard_map.193 = f32[16,512]{1,0:T(8,128)} custom-call(bf16[64,16,512]{2,1,0:T(8,128)(2,1)} %all-to-all-done.landed_hbm), custom_call_target="tpu_custom_call" | custom-call | flops 1000000000 | bytes 1000000 | tf_op jit(solution)/shard_map/pallas_call | solution.py:441
  102.2 2.1 %shard_map.195 = bf16[64,16,1280]{2,1,0:T(8,128)(2,1)} custom-call(bf16[64,16,640]{2,1,0:T(8,128)(2,1)S(1)} %copy-done, bf16[64,16,640]{2,1,0:T(8,128)(2,1)S(1)} %collective-permute-done.7.arrived_hbm, bf16[64,16,1280]{2,1,0:T(8,128)(2,1)} %shard_map.194.refs_0_), custom_call_target="tpu_custom_call", output_to_operand_aliasing={{}: (2, {})} | custom-call | flops 2000000000 | bytes 2000000 | tf_op jit(solution)/shard_map/pallas_call | solution.py:441
  104.4 4.9 %all-to-all-start.1 = ((bf16[64,16,1280]{2,1,0:T(8,128)(2,1)}), bf16[64,16,1280]{2,1,0:T(8,128)(2,1)S(1)}, u32[]{:S(2)}, u32[]{:S(2)}) async-start(bf16[64,16,1280]{2,1,0:T(8,128)(2,1)} %shard_map.195), calls=%async_computation.1 | async-start | bytes 5242880 | tf_op jit(solution)/shard_map/all_to_all | solution.py:575
  109.8 0.9 maximum_bitcast_fusion.1
  110.6 1.1 maximum_bitcast_fusion
  111.8 29.8 %all-to-all-done.1.landed_hbm = bf16[64,16,1280]{2,1,0:T(8,128)(2,1)S(1)} async-done(((bf16[64,16,1280]{2,1,0:T(8,128)(2,1)}), bf16[64,16,1280]{2,1,0:T(8,128)(2,1)S(1)}, u32[]{:S(2)}, u32[]{:S(2)}) %all-to-all-start.1) | async-done | bytes 2621472 | tf_op jit(solution)/shard_map/all_to_all | solution.py:575
  141.6 1.8 %shard_map.196 = (f32[4,1536]{1,0:T(4,128)}, f32[4,512]{1,0:T(4,128)}, f32[4,2048]{1,0:T(4,128)}, f32[16,1024]{1,0:T(8,128)}) custom-call(bf16[64,16,1280]{2,1,0:T(8,128)(2,1)S(1)} %all-to-all-done.1.landed_hbm), custom_call_target="tpu_custom_call" | custom-call | flops 3000000000 | bytes 3000000 | tf_op jit(solution)/shard_map/pallas_call | solution.py:441
  (68 shorter events, 1.2 us)
Async XLA Ops:
  2.9 10.6 %collective-permute-start = (bf16[108,512]{1,0:T(8,128)(2,1)S(1)}, bf16[108,512]{1,0:T(8,128)(2,1)S(1)}, u32[]{:S(2)}, u32[]{:S(2)}) collective-permute-start(bf16[108,512]{1,0:T(8,128)(2,1)S(1)} %pad_maximum_fusion.1), channel_id=1, source_target_pairs={{0,15},{1,0},{2,1},{3,2},{4,3},{5,4},{6,5},{7,6},{8,7},{9,8},{10,9... | collective-permute-start | bytes 331784 | tf_op jit(solution)/shard_map/ppermute | solution.py:479
  8.0 6.6 %collective-permute-start.1 = (bf16[108,512]{1,0:T(8,128)(2,1)S(1)}, bf16[108,512]{1,0:T(8,128)(2,1)S(1)}, u32[]{:S(2)}, u32[]{:S(2)}) collective-permute-start(bf16[108,512]{1,0:T(8,128)(2,1)S(1)} %pad_maximum_fusion.2), channel_id=1, source_target_pairs={{0,112},{1,113},{2,114},{3,115},{4,116},{5,117},{6,118},{7,119},{8... | collective-permute-start | bytes 331784 | tf_op jit(solution)/shard_map/ppermute | solution.py:479
  12.3 4.3 %collective-permute-start.2 = (bf16[108,512]{1,0:T(8,128)(2,1)S(1)}, bf16[108,512]{1,0:T(8,128)(2,1)S(1)}, u32[]{:S(2)}, u32[]{:S(2)}) collective-permute-start(bf16[108,512]{1,0:T(8,128)(2,1)S(1)} %pad_maximum_fusion.3), channel_id=1, source_target_pairs={{0,127},{1,112},{2,113},{3,114},{4,115},{5,116},{6,117},{7,118},{8... | collective-permute-start | bytes 331784 | tf_op jit(solution)/shard_map/ppermute | solution.py:479
  13.5 3.1 %copy-start.7 = (bf16[108,512]{1,0:T(8,128)(2,1)}, bf16[108,512]{1,0:T(8,128)(2,1)S(1)}, u32[]{:S(2)}) copy-start(bf16[108,512]{1,0:T(8,128)(2,1)S(1)} %collective-permute-done.quad1_hbm) | copy-start | bytes 331780
  14.7 1.9 %copy-start.8 = (bf16[108,512]{1,0:T(8,128)(2,1)}, bf16[108,512]{1,0:T(8,128)(2,1)S(1)}, u32[]{:S(2)}) copy-start(bf16[108,512]{1,0:T(8,128)(2,1)S(1)} %collective-permute-done.1.quad2_hbm) | copy-start | bytes 331780
  16.6 0.6 copy-start.9
  40.7 13.1 %collective-permute-start.3 = (bf16[64,16,512]{2,1,0:T(8,128)(2,1)}, bf16[64,16,512]{2,1,0:T(8,128)(2,1)S(1)}, u32[]{:S(2)}, u32[]{:S(2)}) collective-permute-start(bf16[64,16,512]{2,1,0:T(8,128)(2,1)} %get-tuple-element.54), channel_id=1, source_target_pairs={{0,1},{1,0},{2,3},{3,2},{4,5},{5,4},{6,7},{7,6},{8,9},{9,8},{10,11... | collective-permute-start | bytes 3145736 | tf_op jit(solution)/shard_map/ppermute | solution.py:464
  40.8 14.3 %collective-permute-start.4 = (bf16[72,1536]{1,0:T(8,128)(2,1)}, bf16[72,1536]{1,0:T(8,128)(2,1)S(1)}, u32[]{:S(2)}, u32[]{:S(2)}) collective-permute-start(bf16[72,1536]{1,0:T(8,128)(2,1)} %get-tuple-element.59), channel_id=1, source_target_pairs={{0,4},{4,8},{8,12},{12,0},{1,5},{5,9},{9,13},{13,1},{2,6},{6,10},{... | collective-permute-start | bytes 663560 | tf_op jit(solution)/shard_map/ppermute | solution.py:544
  40.8 14.3 %collective-permute-start.5 = (bf16[72,1536]{1,0:T(8,128)(2,1)}, bf16[72,1536]{1,0:T(8,128)(2,1)S(1)}, u32[]{:S(2)}, u32[]{:S(2)}) collective-permute-start(bf16[72,1536]{1,0:T(8,128)(2,1)} %get-tuple-element.60), channel_id=1, source_target_pairs={{0,8},{4,12},{8,0},{12,4},{1,9},{5,13},{9,1},{13,5},{2,10},{6,14},... | collective-permute-start | bytes 663560 | tf_op jit(solution)/shard_map/ppermute | solution.py:544
  43.3 12.1 %collective-permute-start.6 = (bf16[72,1536]{1,0:T(8,128)(2,1)}, bf16[72,1536]{1,0:T(8,128)(2,1)S(1)}, u32[]{:S(2)}, u32[]{:S(2)}) collective-permute-start(bf16[72,1536]{1,0:T(8,128)(2,1)} %get-tuple-element.61), channel_id=1, source_target_pairs={{0,12},{4,0},{8,4},{12,8},{1,13},{5,1},{9,5},{13,9},{2,14},{6,2},{... | collective-permute-start | bytes 663560 | tf_op jit(solution)/shard_map/ppermute | solution.py:544
  44.5 9.3 %copy-start.2 = (bf16[64,16,512]{2,1,0:T(8,128)(2,1)S(1)}, bf16[64,16,512]{2,1,0:T(8,128)(2,1)}, u32[]{:S(2)}) copy-start(bf16[64,16,512]{2,1,0:T(8,128)(2,1)} %get-tuple-element.53.keep_hbm) | copy-start | bytes 3145732
  53.6 28.6 %collective-permute-start.8 = (bf16[64,16,640]{2,1,0:T(8,128)(2,1)}, bf16[64,16,640]{2,1,0:T(8,128)(2,1)S(1)}, u32[]{:S(2)}, u32[]{:S(2)}) collective-permute-start(bf16[64,16,640]{2,1,0:T(8,128)(2,1)} %get-tuple-element.68), channel_id=1, source_target_pairs={{0,1},{1,0},{2,3},{3,2},{4,5},{5,4},{6,7},{7,6},{8,9},{9,8},{10,11... | collective-permute-start | bytes 3932168 | tf_op jit(solution)/shard_map/ppermute | solution.py:464
  55.1 0.7 copy-start.4
  55.1 0.8 copy-start.5
  55.4 0.7 copy-start.6
  69.6 8.9 %copy-start.12 = (bf16[108,512]{1,0:T(8,128)(2,1)S(1)}, bf16[108,512]{1,0:T(8,128)(2,1)}, u32[]{:S(2)}) copy-start(bf16[108,512]{1,0:T(8,128)(2,1)} %get-tuple-element.69) | copy-start | bytes 331780
  69.6 9.7 %copy-start.11 = (bf16[108,512]{1,0:T(8,128)(2,1)S(1)}, bf16[108,512]{1,0:T(8,128)(2,1)}, u32[]{:S(2)}) copy-start(bf16[108,512]{1,0:T(8,128)(2,1)} %get-tuple-element.70) | copy-start | bytes 331780
  69.6 11.2 %copy-start.10 = (bf16[108,512]{1,0:T(8,128)(2,1)S(1)}, bf16[108,512]{1,0:T(8,128)(2,1)}, u32[]{:S(2)}) copy-start(bf16[108,512]{1,0:T(8,128)(2,1)} %get-tuple-element.71) | copy-start | bytes 331780
  69.6 32.6 %collective-permute-start.7 = (bf16[64,16,640]{2,1,0:T(8,128)(2,1)}, bf16[64,16,640]{2,1,0:T(8,128)(2,1)S(1)}, u32[]{:S(2)}, u32[]{:S(2)}) collective-permute-start(bf16[64,16,640]{2,1,0:T(8,128)(2,1)} %get-tuple-element.66), channel_id=1, source_target_pairs={{0,1},{1,0},{2,3},{3,2},{4,5},{5,4},{6,7},{7,6},{8,9},{9,8},{10,11... | collective-permute-start | bytes 3932168 | tf_op jit(solution)/shard_map/ppermute | solution.py:464
  70.0 30.3 %all-to-all-start = ((bf16[64,16,512]{2,1,0:T(8,128)(2,1)}), bf16[64,16,512]{2,1,0:T(8,128)(2,1)}, u32[]{:S(2)}, u32[]{:S(2)}) async-start(bf16[64,16,512]{2,1,0:T(8,128)(2,1)} %shard_map.191), calls=%async_computation | async-start | bytes 2097152 | tf_op jit(solution)/shard_map/all_to_all | solution.py:555
  78.5 25.9 %collective-permute-start.9 = (bf16[108,512]{1,0:T(8,128)(2,1)S(1)}, bf16[108,512]{1,0:T(8,128)(2,1)S(1)}, u32[]{:S(2)}, u32[]{:S(2)}) collective-permute-start(bf16[108,512]{1,0:T(8,128)(2,1)S(1)} %copy-done.12), channel_id=1, source_target_pairs={{0,17},{1,18},{2,19},{3,20},{4,21},{5,22},{6,23},{7,24},{8,25},{9,... | collective-permute-start | bytes 331784 | tf_op jit(solution)/shard_map/ppermute | solution.py:479
  79.3 25.1 %collective-permute-start.10 = (bf16[108,512]{1,0:T(8,128)(2,1)S(1)}, bf16[108,512]{1,0:T(8,128)(2,1)S(1)}, u32[]{:S(2)}, u32[]{:S(2)}) collective-permute-start(bf16[108,512]{1,0:T(8,128)(2,1)S(1)} %copy-done.11), channel_id=1, source_target_pairs={{0,16},{1,17},{2,18},{3,19},{4,20},{5,21},{6,22},{7,23},{8,24},{9,... | collective-permute-start | bytes 331784 | tf_op jit(solution)/shard_map/ppermute | solution.py:479
  80.7 23.7 %collective-permute-start.11 = (bf16[108,512]{1,0:T(8,128)(2,1)S(1)}, bf16[108,512]{1,0:T(8,128)(2,1)S(1)}, u32[]{:S(2)}, u32[]{:S(2)}) collective-permute-start(bf16[108,512]{1,0:T(8,128)(2,1)S(1)} %copy-done.10), channel_id=1, source_target_pairs={{0,1},{1,2},{2,3},{3,4},{4,5},{5,6},{6,7},{7,8},{8,9},{9,10},{10,1... | collective-permute-start | bytes 331784 | tf_op jit(solution)/shard_map/ppermute | solution.py:479
  82.3 1.3 copy-start.1
  85.7 16.6 %copy-start = (bf16[64,16,640]{2,1,0:T(8,128)(2,1)S(1)}, bf16[64,16,640]{2,1,0:T(8,128)(2,1)}, u32[]{:S(2)}) copy-start(bf16[64,16,640]{2,1,0:T(8,128)(2,1)} %get-tuple-element.65.keep_hbm) | copy-start | bytes 3932164
  104.4 5.1 %copy-start.3 = (bf16[108,512]{1,0:T(8,128)(2,1)S(1)}, bf16[108,512]{1,0:T(8,128)(2,1)}, u32[]{:S(2)}) copy-start(bf16[108,512]{1,0:T(8,128)(2,1)} %get-tuple-element.76) | copy-start | bytes 331780
  104.4 37.2 %all-to-all-start.1 = ((bf16[64,16,1280]{2,1,0:T(8,128)(2,1)}), bf16[64,16,1280]{2,1,0:T(8,128)(2,1)S(1)}, u32[]{:S(2)}, u32[]{:S(2)}) async-start(bf16[64,16,1280]{2,1,0:T(8,128)(2,1)} %shard_map.195), calls=%async_computation.1 | async-start | bytes 5242880 | tf_op jit(solution)/shard_map/all_to_all | solution.py:575

commit v8 on v7

--- a/solution.py
+++ b/solution.py
@@ -431,7 +431,8 @@
             ]
 
 
-def call(kernel, inputs, held, outputs, saved, scratch, micros, kind=BF16, free=(), aliases=()):
+def call(kernel, inputs, held, outputs, saved, scratch, micros, kind=BF16, free=(), aliases=(),
+         weight=1):
     whole, there = pl.BlockSpec(memory_space=pltpu.VMEM), pl.BlockSpec(memory_space=pltpu.HBM)
     specs = [whole if at < held else there for at in range(len(inputs))]
     for at in free:
@@ -447,7 +448,7 @@
         input_output_aliases=dict(aliases),
         compiler_params=pltpu.CompilerParams(vmem_limit_bytes=(56 if micros > 5 else 14) * 2**20),
         cost_estimate=pl.CostEstimate(
-            flops=micros * 10**9, bytes_accessed=micros * 10**6, transcendentals=0
+            flops=weight * micros * 10**9, bytes_accessed=micros * 10**6, transcendentals=0
         ),
     )(*inputs)
 
@@ -554,7 +555,8 @@
     middle_grad, down_blocks = lax.optimization_barrier((middle_grad, down_blocks))
     landed = lax.all_to_all(down_blocks, PAIRS, 0, 0, tiled=True)
     grad_down, = call(
-        down_kernel, [landed], 0, [(16, 512)], 1, [vmem(64, 16, 512), dmas(4)], 1, kind=F32
+        down_kernel, [landed], 0, [(16, 512)], 1, [vmem(64, 16, 512), dmas(4)], 1, kind=F32,
+        weight=60,
     )
     *corners, late_keep, late_send = call(
         backward_kernel,

time: 144 us -> 137 us (0.951)
  waiting for transfers between devices: 47.9 us -> 36.5 us
  starting transfers between devices: 31 us -> 36.1 us
    all_to_all x1, waiting for transfers between devices: 14.7 us -> 0.01 us  [body(): landed = lax.all_to_all(down_blocks, PAIRS, 0, 0, tiled=True)]
    all_to_all x1, starting transfers between devices: 4.86 us -> 8.42 us  [body(): landed = lax.all_to_all(blocks, PAIRS, 0, 0, tiled=True)]
    all_to_all x1, waiting for transfers between devices: 29.8 us -> 32.8 us  [body(): landed = lax.all_to_all(blocks, PAIRS, 0, 0, tiled=True)]
    ppermute x3, starting transfers between devices: 0.58 us -> 2.03 us  [pair_sum(): arrived = lax.ppermute(send, 'core', [(0, 1), (1, 0)])]
  transfers between devices with their start and end apart: 14 -> 14, of which waited for: 5 -> 4; matrix products, arithmetic and copies ran while one was open for 2% -> 2% of each run, Pallas kernels for 21% -> 22%
where the time goes in v8:
time: 137 us; the launch traced here: 136 us
  Pallas kernels  55.6 us (41%)
  waiting for transfers between devices  36.5 us (27%)
  starting transfers between devices  36.1 us (26%)
  local copies, waits for them, and re-layouts  4.16 us (3%)
  other arithmetic  2.74 us (2%)
    pallas_call x8, Pallas kernels, call(): pl.pallas_call(kernel, out_shape=[jax.ShapeDtypeStruct(shape, kind) for s...  55.6 us
    all_to_all x1, waiting for transfers between devices, body(): landed = lax.all_to_all(blocks, PAIRS, 0, 0, tiled=True)  32.8 us
    ppermute x6, starting transfers between devices, shifted_block(): return lax.ppermute(block, GRID, route)  13.2 us
    all_to_all x1, starting transfers between devices, body(): landed = lax.all_to_all(down_blocks, PAIRS, 0, 0, tiled=True)  8.71 us
    all_to_all x1, starting transfers between devices, body(): landed = lax.all_to_all(blocks, PAIRS, 0, 0, tiled=True)  8.42 us
    ppermute x3, starting transfers between devices, body(): lax.ppermute(block, 'y', [(i, (i + step) % 4) for i in range(4)])  3.74 us
    ppermute x6, waiting for transfers between devices, shifted_block(): return lax.ppermute(block, GRID, route)  3.7 us
  transfers between devices with their start and end apart: 14, of which 4 were waited for; matrix products, arithmetic and copies ran while one was open for 2% of the time, Pallas kernels for 22%

profile of v8, /device:TPU:0, one launch (start us, length us, event | category | flops | bytes accessed | tf_op | source)
XLA Modules:
  0.0 136.4 jit_solution(5988536076531937653)
XLA Ops:
  0.6 0.9 fusion.1
  1.6 1.2 fusion
  2.9 5.1 %collective-permute-start = (bf16[108,512]{1,0:T(8,128)(2,1)S(1)}, bf16[108,512]{1,0:T(8,128)(2,1)S(1)}, u32[]{:S(2)}, u32[]{:S(2)}) collective-permute-start(bf16[108,512]{1,0:T(8,128)(2,1)S(1)} %pad_maximum_fusion.1), channel_id=1, source_target_pairs={{0,15},{1,0},{2,1},{3,2},{4,3},{5,4},{6,5},{7,6},{8,7},{9,8},{10,9... | collective-permute-start | bytes 331784 | tf_op jit(solution)/shard_map/ppermute | solution.py:480
  8.0 4.1 %collective-permute-start.1 = (bf16[108,512]{1,0:T(8,128)(2,1)S(1)}, bf16[108,512]{1,0:T(8,128)(2,1)S(1)}, u32[]{:S(2)}, u32[]{:S(2)}) collective-permute-start(bf16[108,512]{1,0:T(8,128)(2,1)S(1)} %pad_maximum_fusion.2), channel_id=1, source_target_pairs={{0,112},{1,113},{2,114},{3,115},{4,116},{5,117},{6,118},{7,119},{8... | collective-permute-start | bytes 331784 | tf_op jit(solution)/shard_map/ppermute | solution.py:480
  12.3 0.4 collective-permute-start.2
  12.8 0.7 pad_maximum_fusion.quad0_hbm
  13.5 1.2 collective-permute-done.1.quad2_hbm
  14.7 1.9 %collective-permute-done.2.quad3_hbm = bf16[108,512]{1,0:T(8,128)(2,1)S(1)} collective-permute-done((bf16[108,512]{1,0:T(8,128)(2,1)S(1)}, bf16[108,512]{1,0:T(8,128)(2,1)S(1)}, u32[]{:S(2)}, u32[]{:S(2)}) %collective-permute-start.2) | collective-permute-done | bytes 110624 | tf_op jit(solution)/shard_map/ppermute | solution.py:480
  16.6 0.6 copy-done.9
  17.2 23.5 %shard_map.189 = (bf16[72,1024]{1,0:T(8,128)(2,1)}, bf16[72,1536]{1,0:T(8,128)(2,1)}, bf16[72,1536]{1,0:T(8,128)(2,1)}, bf16[72,1536]{1,0:T(8,128)(2,1)}, bf16[7...) custom-call(s32[1]{0:T(128)} %bitcast.where_ref, ...), custom_call_target="tpu_custom_call" | custom-call | flops 20000000000 | bytes 20000000 | tf_op jit(solution)/shard_map/pallas_call | solution.py:442
  40.7 0.1 collective-permute-start.3
  40.9 2.5 %collective-permute-start.5 = (bf16[72,1536]{1,0:T(8,128)(2,1)}, bf16[72,1536]{1,0:T(8,128)(2,1)S(1)}, u32[]{:S(2)}, u32[]{:S(2)}) collective-permute-start(bf16[72,1536]{1,0:T(8,128)(2,1)} %get-tuple-element.60), channel_id=1, source_target_pairs={{0,8},{4,12},{8,0},{12,4},{1,9},{5,13},{9,1},{13,5},{2,10},{6,14},... | collective-permute-start | bytes 663560 | tf_op jit(solution)/shard_map/ppermute | solution.py:545
  43.4 1.2 collective-permute-start.6
  44.5 9.2 %shard_map.190 = (bf16[288,512]{1,0:T(8,128)(2,1)}, bf16[64,16,640]{2,1,0:T(8,128)(2,1)}, bf16[64,16,640]{2,1,0:T(8,128)(2,1)}) custom-call(s32[1]{0:T(128)} %bitcast.where_ref, bf16[288,512]{1,0:T(8,128)(2,1)} %get-tuple-element.49.grad_after_ref, bf16[288,512]{1,0:T(8,128)(2,1)} %get-tuple-element.50.middle_ref, ...), custom_call_target="tpu_custom_call" | custom-call | flops 7000000000 | bytes 7000000 | tf_op jit(solution)/shard_map/pallas_call | solution.py:442
  53.8 1.3 shard_map.191
  55.1 8.7 %all-to-all-start = ((bf16[64,16,512]{2,1,0:T(8,128)(2,1)}), bf16[64,16,512]{2,1,0:T(8,128)(2,1)}, u32[]{:S(2)}, u32[]{:S(2)}) async-start(bf16[64,16,512]{2,1,0:T(8,128)(2,1)} %shard_map.191), calls=%async_computation | async-start | bytes 2097152 | tf_op jit(solution)/shard_map/all_to_all | solution.py:556
  63.9 0.6 copy-done.4
  64.5 0.1 copy-done.5
  64.7 13.6 %shard_map.192 = (bf16[108,512]{1,0:T(8,128)(2,1)}, bf16[108,512]{1,0:T(8,128)(2,1)}, bf16[108,512]{1,0:T(8,128)(2,1)}, bf16[108,512]{1,0:T(8,128)(2,1)}, bf16[6...) custom-call(s32[1]{0:T(128)} %bitcast.where_ref, bf16[288,512]{1,0:T(8,128)(2,1)} %get-tuple-element.45.tokens_ref, ...), custom_call_target="tpu_custom_call" | custom-call | flops 12000000000 | bytes 12000000 | tf_op jit(solution)/shard_map/pallas_call | solution.py:442
  78.3 0.9 collective-permute-start.9
  79.2 1.5 %collective-permute-start.10 = (bf16[108,512]{1,0:T(8,128)(2,1)}, bf16[108,512]{1,0:T(8,128)(2,1)S(1)}, u32[]{:S(2)}, u32[]{:S(2)}) collective-permute-start(bf16[108,512]{1,0:T(8,128)(2,1)} %get-tuple-element.70), channel_id=1, source_target_pairs={{0,16},{1,17},{2,18},{3,19},{4,20},{5,21},{6,22},{7,23},{8,24},{9,... | collective-permute-start | bytes 331784 | tf_op jit(solution)/shard_map/ppermute | solution.py:480
  80.7 1.2 collective-permute-start.11
  81.9 1.9 %collective-permute-start.7 = (bf16[64,16,640]{2,1,0:T(8,128)(2,1)}, bf16[64,16,640]{2,1,0:T(8,128)(2,1)S(1)}, u32[]{:S(2)}, u32[]{:S(2)}) collective-permute-start(bf16[64,16,640]{2,1,0:T(8,128)(2,1)} %get-tuple-element.66), channel_id=1, source_target_pairs={{0,1},{1,0},{2,3},{3,2},{4,5},{5,4},{6,7},{7,6},{8,9},{9,8},{10,11... | collective-permute-start | bytes 3932168 | tf_op jit(solution)/shard_map/ppermute | solution.py:465
  83.8 2.1 %shard_map.194.refs_0_ = bf16[64,16,1280]{2,1,0:T(8,128)(2,1)} custom-call(bf16[64,16,640]{2,1,0:T(8,128)(2,1)S(1)} %copy-done.1, bf16[64,16,640]{2,1,0:T(8,128)(2,1)S(1)} %collective-permute-done.8.arrived_hbm), custom_call_target="tpu_custom_call" | custom-call | flops 2000000000 | bytes 2000000 | tf_op jit(solution)/shard_map/pallas_call | solution.py:442
  85.9 2.0 %shard_map.193 = f32[16,512]{1,0:T(8,128)} custom-call(bf16[64,16,512]{2,1,0:T(8,128)(2,1)} %all-to-all-done.landed_hbm), custom_call_target="tpu_custom_call" | custom-call | flops 60000002048 | bytes 1000000 | tf_op jit(solution)/shard_map/pallas_call | solution.py:442
  87.9 2.1 %shard_map.195 = bf16[64,16,1280]{2,1,0:T(8,128)(2,1)} custom-call(bf16[64,16,640]{2,1,0:T(8,128)(2,1)S(1)} %copy-done, bf16[64,16,640]{2,1,0:T(8,128)(2,1)S(1)} %collective-permute-done.7.arrived_hbm, bf16[64,16,1280]{2,1,0:T(8,128)(2,1)} %shard_map.194.refs_0_), custom_call_target="tpu_custom_call", output_to_operand_aliasing={{}: (2, {})} | custom-call | flops 2000000000 | bytes 2000000 | tf_op jit(solution)/shard_map/pallas_call | solution.py:442
  90.1 0.6 collective-permute-done.11
  90.7 8.4 %all-to-all-start.1 = ((bf16[64,16,1280]{2,1,0:T(8,128)(2,1)}), bf16[64,16,1280]{2,1,0:T(8,128)(2,1)S(1)}, u32[]{:S(2)}, u32[]{:S(2)}) async-start(bf16[64,16,1280]{2,1,0:T(8,128)(2,1)} %shard_map.195), calls=%async_computation.1 | async-start | bytes 5242880 | tf_op jit(solution)/shard_map/all_to_all | solution.py:577
  99.6 0.9 maximum_bitcast_fusion.1
  100.5 1.1 maximum_bitcast_fusion
  101.6 32.8 %all-to-all-done.1.landed_hbm = bf16[64,16,1280]{2,1,0:T(8,128)(2,1)S(1)} async-done(((bf16[64,16,1280]{2,1,0:T(8,128)(2,1)}), bf16[64,16,1280]{2,1,0:T(8,128)(2,1)S(1)}, u32[]{:S(2)}, u32[]{:S(2)}) %all-to-all-start.1) | async-done | bytes 2621472 | tf_op jit(solution)/shard_map/all_to_all | solution.py:577
  134.3 1.8 %shard_map.196 = (f32[4,1536]{1,0:T(4,128)}, f32[4,512]{1,0:T(4,128)}, f32[4,2048]{1,0:T(4,128)}, f32[16,1024]{1,0:T(8,128)}) custom-call(bf16[64,16,1280]{2,1,0:T(8,128)(2,1)S(1)} %all-to-all-done.1.landed_hbm), custom_call_target="tpu_custom_call" | custom-call | flops 3000000000 | bytes 3000000 | tf_op jit(solution)/shard_map/pallas_call | solution.py:442
  (62 shorter events, 0.9 us)
Async XLA Ops:
  2.9 10.6 %collective-permute-start = (bf16[108,512]{1,0:T(8,128)(2,1)S(1)}, bf16[108,512]{1,0:T(8,128)(2,1)S(1)}, u32[]{:S(2)}, u32[]{:S(2)}) collective-permute-start(bf16[108,512]{1,0:T(8,128)(2,1)S(1)} %pad_maximum_fusion.1), channel_id=1, source_target_pairs={{0,15},{1,0},{2,1},{3,2},{4,3},{5,4},{6,5},{7,6},{8,7},{9,8},{10,9... | collective-permute-start | bytes 331784 | tf_op jit(solution)/shard_map/ppermute | solution.py:480
  8.0 6.6 %collective-permute-start.1 = (bf16[108,512]{1,0:T(8,128)(2,1)S(1)}, bf16[108,512]{1,0:T(8,128)(2,1)S(1)}, u32[]{:S(2)}, u32[]{:S(2)}) collective-permute-start(bf16[108,512]{1,0:T(8,128)(2,1)S(1)} %pad_maximum_fusion.2), channel_id=1, source_target_pairs={{0,112},{1,113},{2,114},{3,115},{4,116},{5,117},{6,118},{7,119},{8... | collective-permute-start | bytes 331784 | tf_op jit(solution)/shard_map/ppermute | solution.py:480
  12.3 4.3 %collective-permute-start.2 = (bf16[108,512]{1,0:T(8,128)(2,1)S(1)}, bf16[108,512]{1,0:T(8,128)(2,1)S(1)}, u32[]{:S(2)}, u32[]{:S(2)}) collective-permute-start(bf16[108,512]{1,0:T(8,128)(2,1)S(1)} %pad_maximum_fusion.3), channel_id=1, source_target_pairs={{0,127},{1,112},{2,113},{3,114},{4,115},{5,116},{6,117},{7,118},{8... | collective-permute-start | bytes 331784 | tf_op jit(solution)/shard_map/ppermute | solution.py:480
  13.5 3.1 %copy-start.7 = (bf16[108,512]{1,0:T(8,128)(2,1)}, bf16[108,512]{1,0:T(8,128)(2,1)S(1)}, u32[]{:S(2)}) copy-start(bf16[108,512]{1,0:T(8,128)(2,1)S(1)} %collective-permute-done.quad1_hbm) | copy-start | bytes 331780
  14.7 1.9 %copy-start.8 = (bf16[108,512]{1,0:T(8,128)(2,1)}, bf16[108,512]{1,0:T(8,128)(2,1)S(1)}, u32[]{:S(2)}) copy-start(bf16[108,512]{1,0:T(8,128)(2,1)S(1)} %collective-permute-done.1.quad2_hbm) | copy-start | bytes 331780
  16.6 0.6 copy-start.9
  40.7 13.1 %collective-permute-start.3 = (bf16[64,16,512]{2,1,0:T(8,128)(2,1)}, bf16[64,16,512]{2,1,0:T(8,128)(2,1)S(1)}, u32[]{:S(2)}, u32[]{:S(2)}) collective-permute-start(bf16[64,16,512]{2,1,0:T(8,128)(2,1)} %get-tuple-element.54), channel_id=1, source_target_pairs={{0,1},{1,0},{2,3},{3,2},{4,5},{5,4},{6,7},{7,6},{8,9},{9,8},{10,11... | collective-permute-start | bytes 3145736 | tf_op jit(solution)/shard_map/ppermute | solution.py:465
  40.8 23.1 %collective-permute-start.4 = (bf16[72,1536]{1,0:T(8,128)(2,1)}, bf16[72,1536]{1,0:T(8,128)(2,1)S(1)}, u32[]{:S(2)}, u32[]{:S(2)}) collective-permute-start(bf16[72,1536]{1,0:T(8,128)(2,1)} %get-tuple-element.59), channel_id=1, source_target_pairs={{0,4},{4,8},{8,12},{12,0},{1,5},{5,9},{9,13},{13,1},{2,6},{6,10},{... | collective-permute-start | bytes 663560 | tf_op jit(solution)/shard_map/ppermute | solution.py:545
  40.9 23.0 %collective-permute-start.5 = (bf16[72,1536]{1,0:T(8,128)(2,1)}, bf16[72,1536]{1,0:T(8,128)(2,1)S(1)}, u32[]{:S(2)}, u32[]{:S(2)}) collective-permute-start(bf16[72,1536]{1,0:T(8,128)(2,1)} %get-tuple-element.60), channel_id=1, source_target_pairs={{0,8},{4,12},{8,0},{12,4},{1,9},{5,13},{9,1},{13,5},{2,10},{6,14},... | collective-permute-start | bytes 663560 | tf_op jit(solution)/shard_map/ppermute | solution.py:545
  43.4 20.5 %collective-permute-start.6 = (bf16[72,1536]{1,0:T(8,128)(2,1)}, bf16[72,1536]{1,0:T(8,128)(2,1)S(1)}, u32[]{:S(2)}, u32[]{:S(2)}) collective-permute-start(bf16[72,1536]{1,0:T(8,128)(2,1)} %get-tuple-element.61), channel_id=1, source_target_pairs={{0,12},{4,0},{8,4},{12,8},{1,13},{5,1},{9,5},{13,9},{2,14},{6,2},{... | collective-permute-start | bytes 663560 | tf_op jit(solution)/shard_map/ppermute | solution.py:545
  44.5 9.3 %copy-start.2 = (bf16[64,16,512]{2,1,0:T(8,128)(2,1)S(1)}, bf16[64,16,512]{2,1,0:T(8,128)(2,1)}, u32[]{:S(2)}) copy-start(bf16[64,16,512]{2,1,0:T(8,128)(2,1)} %get-tuple-element.53.keep_hbm) | copy-start | bytes 3145732
  53.7 30.1 %collective-permute-start.8 = (bf16[64,16,640]{2,1,0:T(8,128)(2,1)}, bf16[64,16,640]{2,1,0:T(8,128)(2,1)S(1)}, u32[]{:S(2)}, u32[]{:S(2)}) collective-permute-start(bf16[64,16,640]{2,1,0:T(8,128)(2,1)} %get-tuple-element.68), channel_id=1, source_target_pairs={{0,1},{1,0},{2,3},{3,2},{4,5},{5,4},{6,7},{7,6},{8,9},{9,8},{10,11... | collective-permute-start | bytes 3932168 | tf_op jit(solution)/shard_map/ppermute | solution.py:465
  55.1 30.8 %all-to-all-start = ((bf16[64,16,512]{2,1,0:T(8,128)(2,1)}), bf16[64,16,512]{2,1,0:T(8,128)(2,1)}, u32[]{:S(2)}, u32[]{:S(2)}) async-start(bf16[64,16,512]{2,1,0:T(8,128)(2,1)} %shard_map.191), calls=%async_computation | async-start | bytes 2097152 | tf_op jit(solution)/shard_map/all_to_all | solution.py:556
  63.9 0.7 copy-start.4
  63.9 0.8 copy-start.5
  63.9 0.8 copy-start.6
  64.7 19.1 %copy-start.1 = (bf16[64,16,640]{2,1,0:T(8,128)(2,1)S(1)}, bf16[64,16,640]{2,1,0:T(8,128)(2,1)}, u32[]{:S(2)}) copy-start(bf16[64,16,640]{2,1,0:T(8,128)(2,1)} %get-tuple-element.67.keep_hbm) | copy-start | bytes 3932164
  78.3 11.7 %collective-permute-start.9 = (bf16[108,512]{1,0:T(8,128)(2,1)}, bf16[108,512]{1,0:T(8,128)(2,1)S(1)}, u32[]{:S(2)}, u32[]{:S(2)}) collective-permute-start(bf16[108,512]{1,0:T(8,128)(2,1)} %get-tuple-element.69), channel_id=1, source_target_pairs={{0,17},{1,18},{2,19},{3,20},{4,21},{5,22},{6,23},{7,24},{8,25},{9,... | collective-permute-start | bytes 331784 | tf_op jit(solution)/shard_map/ppermute | solution.py:480
  79.2 10.9 %collective-permute-start.10 = (bf16[108,512]{1,0:T(8,128)(2,1)}, bf16[108,512]{1,0:T(8,128)(2,1)S(1)}, u32[]{:S(2)}, u32[]{:S(2)}) collective-permute-start(bf16[108,512]{1,0:T(8,128)(2,1)} %get-tuple-element.70), channel_id=1, source_target_pairs={{0,16},{1,17},{2,18},{3,19},{4,20},{5,21},{6,22},{7,23},{8,24},{9,... | collective-permute-start | bytes 331784 | tf_op jit(solution)/shard_map/ppermute | solution.py:480
  80.7 10.0 %collective-permute-start.11 = (bf16[108,512]{1,0:T(8,128)(2,1)}, bf16[108,512]{1,0:T(8,128)(2,1)S(1)}, u32[]{:S(2)}, u32[]{:S(2)}) collective-permute-start(bf16[108,512]{1,0:T(8,128)(2,1)} %get-tuple-element.71), channel_id=1, source_target_pairs={{0,1},{1,2},{2,3},{3,4},{4,5},{5,6},{6,7},{7,8},{8,9},{9,10},{10,1... | collective-permute-start | bytes 331784 | tf_op jit(solution)/shard_map/ppermute | solution.py:480
  81.9 6.0 %collective-permute-start.7 = (bf16[64,16,640]{2,1,0:T(8,128)(2,1)}, bf16[64,16,640]{2,1,0:T(8,128)(2,1)S(1)}, u32[]{:S(2)}, u32[]{:S(2)}) collective-permute-start(bf16[64,16,640]{2,1,0:T(8,128)(2,1)} %get-tuple-element.66), channel_id=1, source_target_pairs={{0,1},{1,0},{2,3},{3,2},{4,5},{5,4},{6,7},{7,6},{8,9},{9,8},{10,11... | collective-permute-start | bytes 3932168 | tf_op jit(solution)/shard_map/ppermute | solution.py:465
  85.9 2.0 %copy-start = (bf16[64,16,640]{2,1,0:T(8,128)(2,1)S(1)}, bf16[64,16,640]{2,1,0:T(8,128)(2,1)}, u32[]{:S(2)}) copy-start(bf16[64,16,640]{2,1,0:T(8,128)(2,1)} %get-tuple-element.65.keep_hbm) | copy-start | bytes 3932164
  90.7 8.7 %copy-start.3 = (bf16[108,512]{1,0:T(8,128)(2,1)S(1)}, bf16[108,512]{1,0:T(8,128)(2,1)}, u32[]{:S(2)}) copy-start(bf16[108,512]{1,0:T(8,128)(2,1)} %get-tuple-element.76) | copy-start | bytes 331780
  90.7 43.7 %all-to-all-start.1 = ((bf16[64,16,1280]{2,1,0:T(8,128)(2,1)}), bf16[64,16,1280]{2,1,0:T(8,128)(2,1)S(1)}, u32[]{:S(2)}, u32[]{:S(2)}) async-start(bf16[64,16,1280]{2,1,0:T(8,128)(2,1)} %shard_map.195), calls=%async_computation.1 | async-start | bytes 5242880 | tf_op jit(solution)/shard_map/all_to_all | solution.py:577

commit v9 on v8

--- a/solution.py
+++ b/solution.py
@@ -216,7 +216,7 @@
         jnp.concatenate([v[:, at * 128 : at * 128 + 128] for v in spread], axis=1).astype(BF16)
         for at in range(4)
     ]
-    y = where_ref[0] >> 1
+    y = (where_ref[0] >> 1) & 3
     for step, near in enumerate((near0, near1, near2, near3)):
         block = blocks[step]
         for own in range(1, 4):
@@ -240,8 +240,12 @@
     core = where_ref[0] & 1
     for part in range(4):
         grad = dot(hidden_ref[:, part * 512 : part * 512 + 512], grad_after, 0, 0).astype(BF16)
-        for block in range(32):
-            slots[block % 2, part * 16 + block // 2] = grad[block * 16 : block * 16 + 16]
+        grad = grad.reshape(16, 2, 16, 512)
+        for unit in range(4):
+            for parity in range(2):
+                slots[parity, unit, part * 16 : part * 16 + 16] = grad[
+                    :, parity, :, unit * 128 : unit * 128 + 128
+                ]
     saves += load(
         [(slots.at[core], keep_hbm), (slots.at[1 - core], send_hbm)], out_sems.at[pl.ds(2, 2)]
     )
@@ -260,10 +264,10 @@
     normed_mid, inverse_mid = normalize(middle_ref[...].astype(F32))
     second_t = dot(eye(512), normed_mid.astype(BF16), 1, 1).astype(BF16)
 
-    def save(cols, at):
+    def save(units, at):
         return load(
-            [(slots.at[core, :, :, cols], keep_hbm.at[:, :, cols]),
-             (slots.at[1 - core, :, :, cols], send_hbm.at[:, :, cols])],
+            [(slots.at[core, units], keep_hbm.at[units]),
+             (slots.at[1 - core, units], send_hbm.at[units])],
             out_sems.at[pl.ds(at, 2)],
         )
 
@@ -278,15 +282,18 @@
         ).astype(BF16)
         grads_up.append(dot(second_t, grad_before))
         back_up = back_up + dot(grad_before, w_up[:, cols], 1, 1)
-    weave(grads_up, slots, slice(0, 512))
-    saves = save(pl.ds(0, 512), 0)
+    for unit in range(4):
+        cols = slice(unit * 128, unit * 128 + 128)
+        weave([grad[:, cols] for grad in grads_up], slots.at[:, unit], slice(0, 128))
+    saves = save(pl.ds(0, 4), 0)
     middle_grad = (
         grad_after.astype(F32) + norm_back(normed_mid, inverse_mid, back_up)
     ).astype(BF16)
     middle_grad_ref[...] = middle_grad
     grad = dot(attended_ref[...], middle_grad)
-    weave([grad[:, p * 128 : p * 128 + 128] for p in range(4)], slots, slice(512, 640))
-    saves += save(pl.ds(512, 128), 2)
+    columns = [grad[:, p * 128 : p * 128 + 128] for p in range(4)]
+    weave(columns, slots.at[:, 4], slice(0, 128))
+    saves += save(pl.ds(4, 1), 2)
     for copy in saves:
         copy.wait()
 
@@ -400,35 +407,56 @@
         save.wait()
 
 
-def arrive(landed_hbm, landed_ref, sems):
+def ring_kernel(where_ref, keep_hbm, arrived_hbm, *refs, shift):
+    *outs, keep_ref, arrived_ref, keep_sems, arrived_sems = refs
+    me = (where_ref[0] >> shift) & 3
+    units = [(me + step) & 3 for step in range(4)] + list(range(4, len(outs)))
+    keeps = [(keep_hbm.at[unit], keep_ref.at[at]) for at, unit in enumerate(units)]
+    arrivals = [(arrived_hbm.at[unit], arrived_ref.at[at]) for at, unit in enumerate(units)]
+    copies = list(zip(load(keeps, keep_sems), load(arrivals, arrived_sems)))
+    for at, out in enumerate(outs):
+        for copy in copies[at]:
+            copy.wait()
+        out[...] = (keep_ref[at].astype(F32) + arrived_ref[at].astype(F32)).astype(BF16)
+
+
+def assemble_kernel(*refs):
+    blocks_hbm, parts_ref, total_ref, sems, out_sem = refs[9:]
+    copies = load([(refs[at], parts_ref.at[at]) for at in range(9)], sems)
+    for unit, first in enumerate((0, 4)):
+        for copy in copies[first : first + 4]:
+            copy.wait()
+        total = sum(parts_ref[first + step].astype(F32) for step in range(4))
+        total_ref[:, :, unit * 128 : unit * 128 + 128] = total.astype(BF16)
+    copies[8].wait()
+    total_ref[:, :, 256:] = parts_ref[8]
+    save, = load([(total_ref, blocks_hbm.at[:, :, pl.ds(0, 384)])], out_sem)
+    save.wait()
+
+
+def share_kernel(landed_hbm, qkv_ref, out_ref, up_ref, down_ref, merge_ref, landed_ref, sems):
     parts = [pl.ds(p * 16, 16) for p in range(4)]
     loads = load([(landed_hbm.at[p], landed_ref.at[p]) for p in parts], sems)
+    down, up, merge = ([0.0] * 4 for _ in range(3))
+    shared = 0.0
     for chip in range(64):
+        z, y = chip // 16, chip // 2 % 4
         if chip % 16 == 0:
-            loads[chip // 16].wait()
-        yield chip, landed_ref[chip].astype(F32)
-
-
-def down_kernel(landed_hbm, down_ref, landed_ref, sems):
-    down_ref[...] = sum(block for _, block in arrive(landed_hbm, landed_ref, sems))
-
-
-def share_kernel(landed_hbm, qkv_ref, out_ref, up_ref, merge_ref, landed_ref, sems):
-    shared = jnp.zeros((16, 1024), F32)
-    merge = [jnp.zeros((16, 256), F32) for _ in range(4)]
-    for chip, block in arrive(landed_hbm, landed_ref, sems):
-        y = chip // 2 % 4
-        shared = shared + block[:, :1024]
-        merge[y] = merge[y] + block[:, 1024:]
+            loads[z].wait()
+        block = landed_ref[chip].astype(F32)
+        down[z] = down[z] + block[:, :128]
+        up[y] = up[y] + block[:, 128:256]
+        shared = shared + block[:, 256:768]
+        merge[y] = merge[y] + block[:, 768:]
     for block in range(4):
-        rows = shared[block * 4 : block * 4 + 4]
-        up_ref[:, block * 512 : block * 512 + 512] = rows[:, :512]
-        out_ref[:, block * 128 : block * 128 + 128] = rows[:, 512:640]
-        qkv_ref[:, block * 384 : block * 384 + 384] = rows[:, 640:]
+        down_ref[:, block * 128 : block * 128 + 128] = down[block]
+        rows = slice(block * 4, block * 4 + 4)
+        out_ref[:, block * 128 : block * 128 + 128] = shared[rows, :128]
+        qkv_ref[:, block * 384 : block * 384 + 384] = shared[rows, 128:]
         for y in range(4):
-            merge_ref[y * 4 : y * 4 + 4, block * 256 : block * 256 + 256] = merge[y][
-                block * 4 : block * 4 + 4
-            ]
+            at = block * 512 + y * 128
+            up_ref[:, at : at + 128] = up[y][rows]
+            merge_ref[y * 4 : y * 4 + 4, block * 256 : block * 256 + 256] = merge[y][rows]
 
 
 def call(kernel, inputs, held, outputs, saved, scratch, micros, kind=BF16, free=(), aliases=(),
@@ -461,15 +489,22 @@
     return pltpu.SemaphoreType.DMA((count,))
 
 
-def pair_sum(keep, send, width, place, blocks=None):
-    arrived = lax.ppermute(send, "core", [(0, 1), (1, 0)])
-    blocks, = call(
-        functools.partial(pair_kernel, place=place),
-        [keep, arrived] + ([] if blocks is None else [blocks]), 0, [(64, 16, width)], 0,
-        [vmem(*keep.shape), vmem(*keep.shape), dmas(4), dmas(4), dmas(4)],
-        2, free=(1,), aliases={} if blocks is None else {2: 0},
-    )
-    return blocks
+def exchanged(send):
+    return lax.ppermute(send, "core", [(0, 1), (1, 0)])
+
+
+def ring_parts(where, keep, send, axis, shift):
+    count = keep.shape[0]
+    outs = call(
+        functools.partial(ring_kernel, shift=shift),
+        [where, keep, exchanged(send)], 1, [(64, 16, 128)] * count, count,
+        [vmem(*keep.shape), vmem(*keep.shape), dmas(count), dmas(count)], 2, free=(2,),
+    )
+    moved = [
+        lax.ppermute(outs[step], axis, [(i, (i + step) % 4) for i in range(4)])
+        for step in (1, 2, 3)
+    ]
+    return outs, [outs[0], *moved, *outs[4:]]
 
 
 def shifted_block(block, down, right):
@@ -523,7 +558,7 @@
     by_feature, field, hidden_shape = (512, TOKENS), (TOKENS, 512), (TOKENS, 2048)
     all_probs, near_shape, corner = (16, TOKENS, TOKENS), (MERGED, 1536), (PACKED, 512)
     places = window_places()
-    where = lax.axis_index(("y", "core")).reshape(1)
+    where = lax.axis_index(("z", "y", "core")).reshape(1)
     quads = roll_back(tokens, cotangent)
 
     (level_two, near0, near1, near2, near3, tokens_in, packed, keys_t, attended, first_t,
@@ -533,10 +568,11 @@
          jnp.asarray(places, BF16), jnp.asarray(places[1].T, F32), w_qkv, *quads,
          w_out, w_up, w_down, w_merge], 7,
         [(MERGED, 1024)] + [near_shape] * 4 + [field, (12, TOKENS, 128), by_feature, by_feature,
-         by_feature, field, field, all_probs, hidden_shape, (64, 16, 512), (64, 16, 512)], 12,
+         by_feature, field, field, all_probs, hidden_shape, (4, 64, 16, 128), (4, 64, 16, 128)],
+        12,
         [vmem(4, *corner), pltpu.VMEM((TOKENS, TOKENS), F32), vmem(*by_feature), vmem(*by_feature),
          vmem(*hidden_shape), vmem(*hidden_shape), vmem(*all_probs), vmem(*w_out.shape),
-         vmem(*w_up.shape), vmem(*w_down.shape), vmem(*w_merge.shape), vmem(2, 64, 16, 512),
+         vmem(*w_up.shape), vmem(*w_down.shape), vmem(*w_merge.shape), vmem(2, 4, 64, 16, 128),
          dmas(4), dmas(4), dmas(4)],
         20, free=range(7, 11),
     )
@@ -546,18 +582,14 @@
     middle_grad, keep, send = call(
         middle_kernel,
         [where, grad_after, middle, attended, w_down, slope, w_up], 4,
-        [field, (64, 16, 640), (64, 16, 640)], 1,
-        [vmem(*w_down.shape), vmem(*hidden_shape), vmem(*w_up.shape), vmem(2, 64, 16, 640),
+        [field, (5, 64, 16, 128), (5, 64, 16, 128)], 1,
+        [vmem(*w_down.shape), vmem(*hidden_shape), vmem(*w_up.shape), vmem(2, 5, 64, 16, 128),
          dmas(3), dmas(4)],
         7,
     )
-    down_blocks = pair_sum(down_keep, down_send, 512, 0)
-    middle_grad, down_blocks = lax.optimization_barrier((middle_grad, down_blocks))
-    landed = lax.all_to_all(down_blocks, PAIRS, 0, 0, tiled=True)
-    grad_down, = call(
-        down_kernel, [landed], 0, [(16, 512)], 1, [vmem(64, 16, 512), dmas(4)], 1, kind=F32,
-        weight=60,
-    )
+    down_sums, down_parts = ring_parts(where, down_keep, down_send, "z", 3)
+    up_sums, up_parts = ring_parts(where, keep, send, "y", 1)
+    middle_grad, *_ = lax.optimization_barrier((middle_grad, down_sums[0], up_sums[0]))
     *corners, late_keep, late_send = call(
         backward_kernel,
         [where, tokens_in, packed, keys_t, attended, middle_grad, first_t,
@@ -569,14 +601,21 @@
          vmem(2, 64, 16, 640), dmas(4), dmas(5), dmas(2)],
         12, free=range(12, 15),
     )
-    blocks = pair_sum(keep, send, 1280, 0)
-    late_keep, grad_down = lax.optimization_barrier((late_keep, grad_down))
-    blocks = pair_sum(late_keep, late_send, 1280, 640, blocks)
+    blocks, = call(
+        assemble_kernel, [*down_parts, *up_parts], 0, [(64, 16, 1024)], 0,
+        [vmem(9, 64, 16, 128), vmem(64, 16, 384), dmas(9), dmas(1)], 2, free=range(9), weight=60,
+    )
+    blocks, = call(
+        functools.partial(pair_kernel, place=384),
+        [late_keep, exchanged(late_send), blocks], 0, [blocks.shape], 0,
+        [vmem(64, 16, 640), vmem(64, 16, 640), dmas(4), dmas(4), dmas(4)], 2, free=(1,),
+        aliases={2: 0},
+    )
     corners = send_forth(corners)
     blocks, *corners = lax.optimization_barrier((blocks, *corners))
     landed = lax.all_to_all(blocks, PAIRS, 0, 0, tiled=True)
-    grad_qkv, grad_out, grad_up, grad_merge = call(
-        share_kernel, [landed], 0, [(4, 1536), (4, 512), (4, 2048), (16, 1024)], 4,
+    grad_qkv, grad_out, grad_up, grad_down, grad_merge = call(
+        share_kernel, [landed], 0, [(4, 1536), (4, 512), (4, 2048), (16, 512), (16, 1024)], 5,
         [vmem(*blocks.shape), dmas(4)], 3, kind=F32,
     )
     grad_tokens = from_corners([c[:MERGED].reshape(6, 6, 2, 512) for c in corners])

time: 137 us -> 138 us (level)
  waiting for transfers between devices: 36.5 us -> 44.5 us
  Pallas kernels: 55.6 us -> 50.7 us
  starting transfers between devices: 36.1 us -> 33.1 us
    ppermute x3 -> x9, starting transfers between devices: 2.03 us -> 10.9 us  [the longest x6 8.86 us: ring_parts(): lax.ppermute(outs[step], axis, [(i, (i + step) % 4) for i in range(4)])]
    all_to_all x1 -> x0, starting transfers between devices: 8.71 us -> none  [body(): landed = lax.all_to_all(down_blocks, PAIRS, 0, 0, tiled=True)]
    ppermute x3, waiting for transfers between devices: 0.01 us -> 6.76 us  [body(): lax.ppermute(block, 'y', [(i, (i + step) % 4) for i in range(4)])]
    ppermute x3 -> x9, waiting for transfers between devices: 0.01 us -> 6.16 us  [the longest x3 6.14 us: exchanged(): return lax.ppermute(send, 'core', [(0, 1), (1, 0)])]
    all_to_all x1, waiting for transfers between devices: 32.8 us -> 27.6 us  [body(): landed = lax.all_to_all(blocks, PAIRS, 0, 0, tiled=True)]
    pallas_call x8, Pallas kernels: 55.6 us -> 50.7 us  [call(): pl.pallas_call(kernel, out_shape=[jax.ShapeDtypeStruct(shape, kind) for s...]
    ppermute x6, starting transfers between devices: 13.2 us -> 11.6 us  [shifted_block(): return lax.ppermute(block, GRID, route)]
  transfers between devices with their start and end apart: 14 -> 19, of which waited for: 4 -> 7; matrix products, arithmetic and copies ran while one was open for 2% -> 2% of each run, Pallas kernels for 22% -> 12%
where the time goes in v9:
time: 138 us; the launch traced here: 137 us
  Pallas kernels  50.7 us (37%)
  waiting for transfers between devices  44.5 us (32%)
  starting transfers between devices  33.1 us (24%)
  local copies, waits for them, and re-layouts  5.14 us (4%)
  other arithmetic  2.75 us (2%)
    pallas_call x8, Pallas kernels, call(): pl.pallas_call(kernel, out_shape=[jax.ShapeDtypeStruct(shape, kind) for s...  50.7 us
    all_to_all x1, waiting for transfers between devices, body(): landed = lax.all_to_all(blocks, PAIRS, 0, 0, tiled=True)  27.6 us
    ppermute x6, starting transfers between devices, shifted_block(): return lax.ppermute(block, GRID, route)  11.6 us
    ppermute x6, starting transfers between devices, ring_parts(): lax.ppermute(outs[step], axis, [(i, (i + step) % 4) for i in range(4)])  8.86 us
    all_to_all x1, starting transfers between devices, body(): landed = lax.all_to_all(blocks, PAIRS, 0, 0, tiled=True)  7.35 us
    ppermute x3, waiting for transfers between devices, body(): lax.ppermute(block, 'y', [(i, (i + step) % 4) for i in range(4)])  6.76 us
    ppermute x3, waiting for transfers between devices, exchanged(): return lax.ppermute(send, 'core', [(0, 1), (1, 0)])  6.14 us
    ppermute x6, waiting for transfers between devices, shifted_block(): return lax.ppermute(block, GRID, route)  3.94 us
  transfers between devices with their start and end apart: 19, of which 7 were waited for; matrix products, arithmetic and copies ran while one was open for 2% of the time, Pallas kernels for 12%

profile of v9, /device:TPU:0, one launch (start us, length us, event | category | flops | bytes accessed | tf_op | source)
XLA Modules:
  0.0 137.4 jit_solution(4424421577258586444)
XLA Ops:
  0.6 0.9 fusion.1
  1.6 1.2 fusion
  2.9 5.1 %collective-permute-start = (bf16[108,512]{1,0:T(8,128)(2,1)S(1)}, bf16[108,512]{1,0:T(8,128)(2,1)S(1)}, u32[]{:S(2)}, u32[]{:S(2)}) collective-permute-start(bf16[108,512]{1,0:T(8,128)(2,1)S(1)} %pad_maximum_fusion.1), channel_id=1, source_target_pairs={{0,15},{1,0},{2,1},{3,2},{4,3},{5,4},{6,5},{7,6},{8,7},{9,8},{10,9... | collective-permute-start | bytes 331784 | tf_op jit(solution)/shard_map/ppermute | solution.py:515
  8.0 4.1 %collective-permute-start.1 = (bf16[108,512]{1,0:T(8,128)(2,1)S(1)}, bf16[108,512]{1,0:T(8,128)(2,1)S(1)}, u32[]{:S(2)}, u32[]{:S(2)}) collective-permute-start(bf16[108,512]{1,0:T(8,128)(2,1)S(1)} %pad_maximum_fusion.2), channel_id=1, source_target_pairs={{0,112},{1,113},{2,114},{3,115},{4,116},{5,117},{6,118},{7,119},{8... | collective-permute-start | bytes 331784 | tf_op jit(solution)/shard_map/ppermute | solution.py:515
  12.8 0.7 pad_maximum_fusion.quad0_hbm
  13.5 1.2 collective-permute-done.1.quad2_hbm
  14.7 1.9 %collective-permute-done.2.quad3_hbm = bf16[108,512]{1,0:T(8,128)(2,1)S(1)} collective-permute-done((bf16[108,512]{1,0:T(8,128)(2,1)S(1)}, bf16[108,512]{1,0:T(8,128)(2,1)S(1)}, u32[]{:S(2)}, u32[]{:S(2)}) %collective-permute-start.2) | collective-permute-done | bytes 110624 | tf_op jit(solution)/shard_map/ppermute | solution.py:515
  16.6 0.6 copy-done.14
  17.2 23.5 %shard_map.189 = (bf16[72,1024]{1,0:T(8,128)(2,1)}, bf16[72,1536]{1,0:T(8,128)(2,1)}, bf16[72,1536]{1,0:T(8,128)(2,1)}, bf16[72,1536]{1,0:T(8,128)(2,1)}, bf16[7...) custom-call(s32[1]{0:T(128)} %bitcast.where_ref, ...), custom_call_target="tpu_custom_call" | custom-call | flops 20000000000 | bytes 20000000 | tf_op jit(solution)/shard_map/pallas_call | solution.py:470
  40.7 9.3 %shard_map.190 = (bf16[288,512]{1,0:T(8,128)(2,1)}, bf16[5,64,16,128]{3,2,1,0:T(8,128)(2,1)}, bf16[5,64,16,128]{3,2,1,0:T(8,128)(2,1)}) custom-call(s32[1]{0:T(128)} %bitcast.where_ref, bf16[288,512]{1,0:T(8,128)(2,1)} %get-tuple-element.56.grad_after_ref, bf16[288,512]{1,0:T(8,128)(2,1)} %get-tuple-element.57.middle_ref, ...), custom_call_target="tpu_custom_call" | custom-call | flops 7000000000 | bytes 7000000 | tf_op jit(solution)/shard_map/pallas_call | solution.py:470
  50.7 4.0 %collective-permute-done.3.arrived_hbm = bf16[4,64,16,128]{3,2,1,0:T(8,128)(2,1)S(1)} collective-permute-done((bf16[4,64,16,128]{3,2,1,0:T(8,128)(2,1)S(1)}, bf16[4,64,16,128]{3,2,1,0:T(8,128)(2,1)S(1)}, u32[]{:S(2)}, u32[]{:S(2)}) %collective-permute-start.3) | collective-permute-done | bytes 1048608 | tf_op jit(solution)/shard_map/ppermute | solution.py:493
  55.7 2.1 %collective-permute-start.6 = (bf16[72,1536]{1,0:T(8,128)(2,1)S(1)}, bf16[72,1536]{1,0:T(8,128)(2,1)S(1)}, u32[]{:S(2)}, u32[]{:S(2)}) collective-permute-start(bf16[72,1536]{1,0:T(8,128)(2,1)S(1)} %copy-done.7), channel_id=1, source_target_pairs={{0,8},{4,12},{8,0},{12,4},{1,9},{5,13},{9,1},{13,5},{2,10},{6,14},... | collective-permute-start | bytes 663560 | tf_op jit(solution)/shard_map/ppermute | solution.py:581
  57.9 1.2 collective-permute-start.7
  59.0 2.7 %collective-permute-start.10 = (bf16[64,16,128]{2,1,0:T(8,128)(2,1)S(1)}, bf16[64,16,128]{2,1,0:T(8,128)(2,1)S(1)}, u32[]{:S(2)}, u32[]{:S(2)}) collective-permute-start(bf16[64,16,128]{2,1,0:T(8,128)(2,1)S(1)} %get-tuple-element.77), channel_id=1, source_target_pairs={{0,64},{32,96},{64,0},{96,32},{1,65},{33,97},{65,1},{97,33},{2,66}... | collective-permute-start | bytes 786440 | tf_op jit(solution)/shard_map/ppermute | solution.py:504
  61.7 0.6 shard_map.192
  62.3 6.8 %collective-permute-done.5.near1_hbm = bf16[72,1536]{1,0:T(8,128)(2,1)S(1)} collective-permute-done((bf16[72,1536]{1,0:T(8,128)(2,1)S(1)}, bf16[72,1536]{1,0:T(8,128)(2,1)S(1)}, u32[]{:S(2)}, u32[]{:S(2)}) %collective-permute-start.5) | collective-permute-done | bytes 221216 | tf_op jit(solution)/shard_map/ppermute | solution.py:581
  69.0 2.6 %collective-permute-start.11 = (bf16[64,16,128]{2,1,0:T(8,128)(2,1)S(1)}, bf16[64,16,128]{2,1,0:T(8,128)(2,1)S(1)}, u32[]{:S(2)}, u32[]{:S(2)}) collective-permute-start(bf16[64,16,128]{2,1,0:T(8,128)(2,1)S(1)} %get-tuple-element.78), channel_id=1, source_target_pairs={{0,96},{32,0},{64,32},{96,64},{1,97},{33,1},{65,33},{97,65},{2,98}... | collective-permute-start | bytes 786440 | tf_op jit(solution)/shard_map/ppermute | solution.py:504
  71.7 1.0 collective-permute-start.13
  72.7 2.5 %collective-permute-start.14 = (bf16[64,16,128]{2,1,0:T(8,128)(2,1)S(1)}, bf16[64,16,128]{2,1,0:T(8,128)(2,1)S(1)}, u32[]{:S(2)}, u32[]{:S(2)}) collective-permute-start(bf16[64,16,128]{2,1,0:T(8,128)(2,1)S(1)} %get-tuple-element.81), channel_id=1, source_target_pairs={{0,12},{4,0},{8,4},{12,8},{1,13},{5,1},{9,5},{13,9},{2,14},{6,2},{... | collective-permute-start | bytes 786440 | tf_op jit(solution)/shard_map/ppermute | solution.py:504
  75.2 13.5 %shard_map.193 = (bf16[108,512]{1,0:T(8,128)(2,1)}, bf16[108,512]{1,0:T(8,128)(2,1)}, bf16[108,512]{1,0:T(8,128)(2,1)}, bf16[108,512]{1,0:T(8,128)(2,1)}, bf16[6...) custom-call(s32[1]{0:T(128)} %bitcast.where_ref, bf16[288,512]{1,0:T(8,128)(2,1)} %get-tuple-element.52.tokens_ref, ...), custom_call_target="tpu_custom_call" | custom-call | flops 12000000000 | bytes 12000000 | tf_op jit(solution)/shard_map/pallas_call | solution.py:470
  88.9 1.8 %collective-permute-start.17 = (bf16[108,512]{1,0:T(8,128)(2,1)}, bf16[108,512]{1,0:T(8,128)(2,1)S(1)}, u32[]{:S(2)}, u32[]{:S(2)}) collective-permute-start(bf16[108,512]{1,0:T(8,128)(2,1)} %get-tuple-element.85), channel_id=1, source_target_pairs={{0,1},{1,2},{2,3},{3,4},{4,5},{5,6},{6,7},{7,8},{8,9},{9,10},{10,1... | collective-permute-start | bytes 331784 | tf_op jit(solution)/shard_map/ppermute | solution.py:515
  90.7 1.5 %collective-permute-start.8 = (bf16[64,16,640]{2,1,0:T(8,128)(2,1)}, bf16[64,16,640]{2,1,0:T(8,128)(2,1)S(1)}, u32[]{:S(2)}, u32[]{:S(2)}) collective-permute-start(bf16[64,16,640]{2,1,0:T(8,128)(2,1)} %get-tuple-element.75), channel_id=1, source_target_pairs={{0,1},{1,0},{2,3},{3,2},{4,5},{5,4},{6,7},{7,6},{8,9},{9,8},{10,11... | collective-permute-start | bytes 3932168 | tf_op jit(solution)/shard_map/ppermute | solution.py:493
  92.2 0.7 shard_map.194.refs_0_
  92.9 2.1 %collective-permute-done.8.arrived_hbm = bf16[64,16,640]{2,1,0:T(8,128)(2,1)S(1)} collective-permute-done((bf16[64,16,640]{2,1,0:T(8,128)(2,1)}, bf16[64,16,640]{2,1,0:T(8,128)(2,1)S(1)}, u32[]{:S(2)}, u32[]{:S(2)}) %collective-permute-start.8) | collective-permute-done | bytes 1310752 | tf_op jit(solution)/shard_map/ppermute | solution.py:493
  95.1 1.4 %shard_map.195 = bf16[64,16,1024]{2,1,0:T(8,128)(2,1)S(1)} custom-call(bf16[64,16,640]{2,1,0:T(8,128)(2,1)S(1)} %copy-done.1, bf16[64,16,640]{2,1,0:T(8,128)(2,1)S(1)} %collective-permute-done.8.arrived_hbm, bf16[64,16,1024]{2,1,0:T(8,128)(2,1)S(1)} %shard_map.194.refs_0_), custom_call_target="tpu_custom_call", output_to_operand_aliasing={{}: (2, {})} | custom-call | flops 2000000000 | bytes 2000000 | tf_op jit(solution)/shard_map/pallas_call | solution.py:470
  96.5 1.3 copy-done
  97.8 0.8 collective-permute-done.15
  98.7 7.3 %all-to-all-start = ((bf16[64,16,1024]{2,1,0:T(8,128)(2,1)}), bf16[64,16,1024]{2,1,0:T(8,128)(2,1)S(1)}, u32[]{:S(2)}, u32[]{:S(2)}) async-start(bf16[64,16,1024]{2,1,0:T(8,128)(2,1)} %copy-done), calls=%async_computation | async-start | bytes 4194304 | tf_op jit(solution)/shard_map/all_to_all | solution.py:616
  106.5 0.9 maximum_bitcast_fusion.1
  107.4 1.1 maximum_bitcast_fusion
  108.5 27.6 %all-to-all-done.landed_hbm = bf16[64,16,1024]{2,1,0:T(8,128)(2,1)S(1)} async-done(((bf16[64,16,1024]{2,1,0:T(8,128)(2,1)}), bf16[64,16,1024]{2,1,0:T(8,128)(2,1)S(1)}, u32[]{:S(2)}, u32[]{:S(2)}) %all-to-all-start) | async-done | bytes 2097184 | tf_op jit(solution)/shard_map/all_to_all | solution.py:616
  136.1 1.1 shard_map.196
  (82 shorter events, 2.9 us)
Async XLA Ops:
  2.9 10.6 %collective-permute-start = (bf16[108,512]{1,0:T(8,128)(2,1)S(1)}, bf16[108,512]{1,0:T(8,128)(2,1)S(1)}, u32[]{:S(2)}, u32[]{:S(2)}) collective-permute-start(bf16[108,512]{1,0:T(8,128)(2,1)S(1)} %pad_maximum_fusion.1), channel_id=1, source_target_pairs={{0,15},{1,0},{2,1},{3,2},{4,3},{5,4},{6,5},{7,6},{8,7},{9,8},{10,9... | collective-permute-start | bytes 331784 | tf_op jit(solution)/shard_map/ppermute | solution.py:515
  8.0 6.6 %collective-permute-start.1 = (bf16[108,512]{1,0:T(8,128)(2,1)S(1)}, bf16[108,512]{1,0:T(8,128)(2,1)S(1)}, u32[]{:S(2)}, u32[]{:S(2)}) collective-permute-start(bf16[108,512]{1,0:T(8,128)(2,1)S(1)} %pad_maximum_fusion.2), channel_id=1, source_target_pairs={{0,112},{1,113},{2,114},{3,115},{4,116},{5,117},{6,118},{7,119},{8... | collective-permute-start | bytes 331784 | tf_op jit(solution)/shard_map/ppermute | solution.py:515
  12.3 4.3 %collective-permute-start.2 = (bf16[108,512]{1,0:T(8,128)(2,1)S(1)}, bf16[108,512]{1,0:T(8,128)(2,1)S(1)}, u32[]{:S(2)}, u32[]{:S(2)}) collective-permute-start(bf16[108,512]{1,0:T(8,128)(2,1)S(1)} %pad_maximum_fusion.3), channel_id=1, source_target_pairs={{0,127},{1,112},{2,113},{3,114},{4,115},{5,116},{6,117},{7,118},{8... | collective-permute-start | bytes 331784 | tf_op jit(solution)/shard_map/ppermute | solution.py:515
  13.5 3.1 %copy-start.12 = (bf16[108,512]{1,0:T(8,128)(2,1)}, bf16[108,512]{1,0:T(8,128)(2,1)S(1)}, u32[]{:S(2)}) copy-start(bf16[108,512]{1,0:T(8,128)(2,1)S(1)} %collective-permute-done.quad1_hbm) | copy-start | bytes 331780
  14.7 1.9 %copy-start.13 = (bf16[108,512]{1,0:T(8,128)(2,1)}, bf16[108,512]{1,0:T(8,128)(2,1)S(1)}, u32[]{:S(2)}) copy-start(bf16[108,512]{1,0:T(8,128)(2,1)S(1)} %collective-permute-done.1.quad2_hbm) | copy-start | bytes 331780
  40.7 9.5 %copy-start.5 = (bf16[4,64,16,128]{3,2,1,0:T(8,128)(2,1)S(1)}, bf16[4,64,16,128]{3,2,1,0:T(8,128)(2,1)}, u32[]{:S(2)}) copy-start(bf16[4,64,16,128]{3,2,1,0:T(8,128)(2,1)} %get-tuple-element.61) | copy-start | bytes 3145732
  40.7 14.0 %copy-start.3 = (bf16[4,64,16,128]{3,2,1,0:T(8,128)(2,1)S(1)}, bf16[4,64,16,128]{3,2,1,0:T(8,128)(2,1)}, u32[]{:S(2)}) copy-start(bf16[4,64,16,128]{3,2,1,0:T(8,128)(2,1)} %get-tuple-element.60.keep_hbm) | copy-start | bytes 3145732
  50.1 9.0 %collective-permute-start.4 = (bf16[5,64,16,128]{3,2,1,0:T(8,128)(2,1)}, bf16[5,64,16,128]{3,2,1,0:T(8,128)(2,1)S(1)}, u32[]{:S(2)}, u32[]{:S(2)}) collective-permute-start(bf16[5,64,16,128]{3,2,1,0:T(8,128)(2,1)} %get-tuple-element.64), channel_id=1, source_target_pairs={{0,1},{1,0},{2,3},{3,2},{4,5},{5,4},{6,7},{7,6},{8,9},{9,8},{10,11... | collective-permute-start | bytes 3932168 | tf_op jit(solution)/shard_map/ppermute | solution.py:493
  50.2 4.5 %collective-permute-start.3 = (bf16[4,64,16,128]{3,2,1,0:T(8,128)(2,1)S(1)}, bf16[4,64,16,128]{3,2,1,0:T(8,128)(2,1)S(1)}, u32[]{:S(2)}, u32[]{:S(2)}) collective-permute-start(bf16[4,64,16,128]{3,2,1,0:T(8,128)(2,1)S(1)} %copy-done.5), channel_id=1, source_target_pairs={{0,1},{1,0},{2,3},{3,2},{4,5},{5,4},{6,7},{7,6},{8,9},{9,8},{10,11... | collective-permute-start | bytes 3145736 | tf_op jit(solution)/shard_map/ppermute | solution.py:493
  54.7 1.0 copy-start.7
  54.7 3.2 %copy-start.6 = (bf16[72,1536]{1,0:T(8,128)(2,1)S(1)}, bf16[72,1536]{1,0:T(8,128)(2,1)}, u32[]{:S(2)}) copy-start(bf16[72,1536]{1,0:T(8,128)(2,1)} %get-tuple-element.72) | copy-start | bytes 663556
  54.7 7.0 %copy-start.2 = (bf16[5,64,16,128]{3,2,1,0:T(8,128)(2,1)S(1)}, bf16[5,64,16,128]{3,2,1,0:T(8,128)(2,1)}, u32[]{:S(2)}) copy-start(bf16[5,64,16,128]{3,2,1,0:T(8,128)(2,1)} %get-tuple-element.63.keep_hbm) | copy-start | bytes 3932164
  55.2 17.5 %collective-permute-start.9 = (bf16[64,16,128]{2,1,0:T(8,128)(2,1)S(1)}, bf16[64,16,128]{2,1,0:T(8,128)(2,1)S(1)}, u32[]{:S(2)}, u32[]{:S(2)}) collective-permute-start(bf16[64,16,128]{2,1,0:T(8,128)(2,1)S(1)} %get-tuple-element.76), channel_id=1, source_target_pairs={{0,32},{32,64},{64,96},{96,0},{1,33},{33,65},{65,97},{97,1},{2,34}... | collective-permute-start | bytes 786440 | tf_op jit(solution)/shard_map/ppermute | solution.py:504
  55.6 13.4 %collective-permute-start.5 = (bf16[72,1536]{1,0:T(8,128)(2,1)S(1)}, bf16[72,1536]{1,0:T(8,128)(2,1)S(1)}, u32[]{:S(2)}, u32[]{:S(2)}) collective-permute-start(bf16[72,1536]{1,0:T(8,128)(2,1)S(1)} %copy-done.8), channel_id=1, source_target_pairs={{0,4},{4,8},{8,12},{12,0},{1,5},{5,9},{9,13},{13,1},{2,6},{6,10},{... | collective-permute-start | bytes 663560 | tf_op jit(solution)/shard_map/ppermute | solution.py:581
  55.7 15.9 %collective-permute-start.6 = (bf16[72,1536]{1,0:T(8,128)(2,1)S(1)}, bf16[72,1536]{1,0:T(8,128)(2,1)S(1)}, u32[]{:S(2)}, u32[]{:S(2)}) collective-permute-start(bf16[72,1536]{1,0:T(8,128)(2,1)S(1)} %copy-done.7), channel_id=1, source_target_pairs={{0,8},{4,12},{8,0},{12,4},{1,9},{5,13},{9,1},{13,5},{2,10},{6,14},... | collective-permute-start | bytes 663560 | tf_op jit(solution)/shard_map/ppermute | solution.py:581
  57.9 13.8 %collective-permute-start.7 = (bf16[72,1536]{1,0:T(8,128)(2,1)S(1)}, bf16[72,1536]{1,0:T(8,128)(2,1)S(1)}, u32[]{:S(2)}, u32[]{:S(2)}) collective-permute-start(bf16[72,1536]{1,0:T(8,128)(2,1)S(1)} %copy-done.6), channel_id=1, source_target_pairs={{0,12},{4,0},{8,4},{12,8},{1,13},{5,1},{9,5},{13,9},{2,14},{6,2},{... | collective-permute-start | bytes 663560 | tf_op jit(solution)/shard_map/ppermute | solution.py:581
  59.0 29.7 %collective-permute-start.10 = (bf16[64,16,128]{2,1,0:T(8,128)(2,1)S(1)}, bf16[64,16,128]{2,1,0:T(8,128)(2,1)S(1)}, u32[]{:S(2)}, u32[]{:S(2)}) collective-permute-start(bf16[64,16,128]{2,1,0:T(8,128)(2,1)S(1)} %get-tuple-element.77), channel_id=1, source_target_pairs={{0,64},{32,96},{64,0},{96,32},{1,65},{33,97},{65,1},{97,33},{2,66}... | collective-permute-start | bytes 786440 | tf_op jit(solution)/shard_map/ppermute | solution.py:504
  69.0 6.2 %copy-start.9 = (bf16[72,1536]{1,0:T(8,128)(2,1)}, bf16[72,1536]{1,0:T(8,128)(2,1)S(1)}, u32[]{:S(2)}) copy-start(bf16[72,1536]{1,0:T(8,128)(2,1)S(1)} %collective-permute-done.5.near1_hbm) | copy-start | bytes 663556
  69.0 19.8 %collective-permute-start.11 = (bf16[64,16,128]{2,1,0:T(8,128)(2,1)S(1)}, bf16[64,16,128]{2,1,0:T(8,128)(2,1)S(1)}, u32[]{:S(2)}, u32[]{:S(2)}) collective-permute-start(bf16[64,16,128]{2,1,0:T(8,128)(2,1)S(1)} %get-tuple-element.78), channel_id=1, source_target_pairs={{0,96},{32,0},{64,32},{96,64},{1,97},{33,1},{65,33},{97,65},{2,98}... | collective-permute-start | bytes 786440 | tf_op jit(solution)/shard_map/ppermute | solution.py:504
  71.7 3.6 %copy-start.10 = (bf16[72,1536]{1,0:T(8,128)(2,1)}, bf16[72,1536]{1,0:T(8,128)(2,1)S(1)}, u32[]{:S(2)}) copy-start(bf16[72,1536]{1,0:T(8,128)(2,1)S(1)} %collective-permute-done.6.near2_hbm) | copy-start | bytes 663556
  71.7 17.2 %collective-permute-start.12 = (bf16[64,16,128]{2,1,0:T(8,128)(2,1)S(1)}, bf16[64,16,128]{2,1,0:T(8,128)(2,1)S(1)}, u32[]{:S(2)}, u32[]{:S(2)}) collective-permute-start(bf16[64,16,128]{2,1,0:T(8,128)(2,1)S(1)} %get-tuple-element.79), channel_id=1, source_target_pairs={{0,4},{4,8},{8,12},{12,0},{1,5},{5,9},{9,13},{13,1},{2,6},{6,10},{... | collective-permute-start | bytes 786440 | tf_op jit(solution)/shard_map/ppermute | solution.py:504
  71.7 3.5 %copy-start.11 = (bf16[72,1536]{1,0:T(8,128)(2,1)}, bf16[72,1536]{1,0:T(8,128)(2,1)S(1)}, u32[]{:S(2)}) copy-start(bf16[72,1536]{1,0:T(8,128)(2,1)S(1)} %collective-permute-done.7.near3_hbm) | copy-start | bytes 663556
  71.7 19.0 %collective-permute-start.13 = (bf16[64,16,128]{2,1,0:T(8,128)(2,1)S(1)}, bf16[64,16,128]{2,1,0:T(8,128)(2,1)S(1)}, u32[]{:S(2)}, u32[]{:S(2)}) collective-permute-start(bf16[64,16,128]{2,1,0:T(8,128)(2,1)S(1)} %get-tuple-element.80), channel_id=1, source_target_pairs={{0,8},{4,12},{8,0},{12,4},{1,9},{5,13},{9,1},{13,5},{2,10},{6,14},... | collective-permute-start | bytes 786440 | tf_op jit(solution)/shard_map/ppermute | solution.py:504
  72.7 19.5 %collective-permute-start.14 = (bf16[64,16,128]{2,1,0:T(8,128)(2,1)S(1)}, bf16[64,16,128]{2,1,0:T(8,128)(2,1)S(1)}, u32[]{:S(2)}, u32[]{:S(2)}) collective-permute-start(bf16[64,16,128]{2,1,0:T(8,128)(2,1)S(1)} %get-tuple-element.81), channel_id=1, source_target_pairs={{0,12},{4,0},{8,4},{12,8},{1,13},{5,1},{9,5},{13,9},{2,14},{6,2},{... | collective-permute-start | bytes 786440 | tf_op jit(solution)/shard_map/ppermute | solution.py:504
  88.7 9.9 %collective-permute-start.15 = (bf16[108,512]{1,0:T(8,128)(2,1)}, bf16[108,512]{1,0:T(8,128)(2,1)S(1)}, u32[]{:S(2)}, u32[]{:S(2)}) collective-permute-start(bf16[108,512]{1,0:T(8,128)(2,1)} %get-tuple-element.83), channel_id=1, source_target_pairs={{0,17},{1,18},{2,19},{3,20},{4,21},{5,22},{6,23},{7,24},{8,25},{9,... | collective-permute-start | bytes 331784 | tf_op jit(solution)/shard_map/ppermute | solution.py:515
  88.8 9.8 %collective-permute-start.16 = (bf16[108,512]{1,0:T(8,128)(2,1)}, bf16[108,512]{1,0:T(8,128)(2,1)S(1)}, u32[]{:S(2)}, u32[]{:S(2)}) collective-permute-start(bf16[108,512]{1,0:T(8,128)(2,1)} %get-tuple-element.84), channel_id=1, source_target_pairs={{0,16},{1,17},{2,18},{3,19},{4,20},{5,21},{6,22},{7,23},{8,24},{9,... | collective-permute-start | bytes 331784 | tf_op jit(solution)/shard_map/ppermute | solution.py:515
  88.9 9.7 %collective-permute-start.17 = (bf16[108,512]{1,0:T(8,128)(2,1)}, bf16[108,512]{1,0:T(8,128)(2,1)S(1)}, u32[]{:S(2)}, u32[]{:S(2)}) collective-permute-start(bf16[108,512]{1,0:T(8,128)(2,1)} %get-tuple-element.85), channel_id=1, source_target_pairs={{0,1},{1,2},{2,3},{3,4},{4,5},{5,6},{6,7},{7,8},{8,9},{9,10},{10,1... | collective-permute-start | bytes 331784 | tf_op jit(solution)/shard_map/ppermute | solution.py:515
  90.7 4.4 %collective-permute-start.8 = (bf16[64,16,640]{2,1,0:T(8,128)(2,1)}, bf16[64,16,640]{2,1,0:T(8,128)(2,1)S(1)}, u32[]{:S(2)}, u32[]{:S(2)}) collective-permute-start(bf16[64,16,640]{2,1,0:T(8,128)(2,1)} %get-tuple-element.75), channel_id=1, source_target_pairs={{0,1},{1,0},{2,3},{3,2},{4,5},{5,4},{6,7},{7,6},{8,9},{9,8},{10,11... | collective-permute-start | bytes 3932168 | tf_op jit(solution)/shard_map/ppermute | solution.py:493
  92.2 2.9 %copy-start.1 = (bf16[64,16,640]{2,1,0:T(8,128)(2,1)S(1)}, bf16[64,16,640]{2,1,0:T(8,128)(2,1)}, u32[]{:S(2)}) copy-start(bf16[64,16,640]{2,1,0:T(8,128)(2,1)} %get-tuple-element.74.keep_hbm) | copy-start | bytes 3932164
  96.5 1.3 copy-start
  98.7 7.6 %copy-start.4 = (bf16[108,512]{1,0:T(8,128)(2,1)S(1)}, bf16[108,512]{1,0:T(8,128)(2,1)}, u32[]{:S(2)}) copy-start(bf16[108,512]{1,0:T(8,128)(2,1)} %get-tuple-element.90) | copy-start | bytes 331780
  98.7 37.5 %all-to-all-start = ((bf16[64,16,1024]{2,1,0:T(8,128)(2,1)}), bf16[64,16,1024]{2,1,0:T(8,128)(2,1)S(1)}, u32[]{:S(2)}, u32[]{:S(2)}) async-start(bf16[64,16,1024]{2,1,0:T(8,128)(2,1)} %copy-done), calls=%async_computation | async-start | bytes 4194304 | tf_op jit(solution)/shard_map/all_to_all | solution.py:616
  (2 other events, 1.6 us)

commit v10 on v9

--- a/solution.py
+++ b/solution.py
@@ -129,19 +129,21 @@
 
 
 def forward_kernel(
-    where_ref, order_ref, cot_order_ref, ids_ref, places_ref, cols_t_ref, w_qkv,
-    quad0_hbm, quad1_hbm, quad2_hbm, quad3_hbm, w_out_hbm, w_up_hbm, w_down_hbm, w_merge_hbm,
+    where_ref, order_ref, cot_order_ref, ids_ref, places_ref, cols_t_ref,
+    quad0_hbm, quad1_hbm, quad2_hbm, quad3_hbm, w_qkv_hbm, w_out_hbm, w_up_hbm, w_down_hbm, w_merge_hbm,
     level_two_ref, near0, near1, near2, near3, tokens_ref, packed_ref, keys_t_ref,
     attended_ref, first_t_ref, middle_ref, grad_after_ref, probs_hbm, slope_hbm, keep_hbm, send_hbm,
-    quads_ref, bias_ref, query_t, values_t, slope_ref, hidden_ref, probs_ref, w_out, w_up, w_down,
+    quads_ref, bias_ref, query_t, values_t, slope_ref, hidden_ref, probs_ref, w_qkv, w_out, w_up, w_down,
     w_merge, slots, quad_sems, in_sems, out_sems,
 ):
     quads = (quad0_hbm, quad1_hbm, quad2_hbm, quad3_hbm)
     quads = load([(quads[q], quads_ref.at[q]) for q in range(4)], quad_sems)
     weights = load(
-        [(w_out_hbm, w_out), (w_up_hbm, w_up), (w_down_hbm, w_down), (w_merge_hbm, w_merge)],
+        [(w_qkv_hbm, w_qkv), (w_out_hbm, w_out), (w_up_hbm, w_up), (w_down_hbm, w_down),
+         (w_merge_hbm, w_merge)],
         in_sems,
     )
+    query_t[...] = jnp.zeros_like(query_t)
     ids = ids_ref[...].astype(F32).astype(BF16)
     by_row = dot(places_ref[0], ids) * places_ref[1].astype(F32)
     by_col = dot(ids, places_ref[0], 0, 1) * cols_t_ref[...]
@@ -156,21 +158,23 @@
     first_norm = normalize(tokens)[0].astype(BF16)
     first_t_ref[...] = dot(eye(512), first_norm, 1, 1).astype(BF16)
     by_lane = eye(128)
+    weights[0].wait()
     for part in range(3):
         wide = dot(first_norm, w_qkv[:, part * 512 : part * 512 + 512])
         wide = (wide * QUERY_SCALE if part == 0 else wide).astype(BF16)
         for group in range(4):
             grid = wide[:, group * 128 : group * 128 + 128]
             packed_ref[part * 4 + group] = grid
-            turned = (query_t, keys_t_ref, values_t)[part]
-            turned[group * 128 : group * 128 + 128, :] = dot(by_lane, grid, 1, 1).astype(BF16)
-
-    head_of_row = lax.broadcasted_iota(jnp.int32, (128, TOKENS), 0) >> 5
+            turned = dot(by_lane, grid, 1, 1).astype(BF16)
+            if part:
+                (keys_t_ref, values_t)[part - 1][group * 128 : group * 128 + 128, :] = turned
+                continue
+            for head in range(4):
+                rows = slice(head * HEAD, head * HEAD + HEAD)
+                query_t[group * 4 + head, rows, :] = turned[rows]
 
     def scores_of(head):
-        queries = query_t[head // 4 * 128 : head // 4 * 128 + 128, :]
-        masked = jnp.where(head_of_row == head % 4, queries, jnp.zeros_like(queries))
-        return dot(packed_ref[4 + head // 4], masked)
+        return dot(packed_ref[4 + head // 4], query_t[head])
 
     ahead = scores_of(0)
     for head in range(16):
@@ -186,15 +190,15 @@
     saves = load([(probs_ref, probs_hbm)], out_sems.at[pl.ds(0, 1)])
 
     attended = dot(eye(TOKENS), attended_ref[...], 1, 1).astype(BF16)
-    weights[0].wait()
+    weights[1].wait()
     attn_out = dot(attended, w_out[...]).astype(BF16)
     narrow_middle = (tokens + attn_out.astype(F32)).astype(BF16)
     middle_ref[...] = narrow_middle
     middle = narrow_middle.astype(F32)
     second_norm = normalize(middle)[0].astype(BF16)
     mlp = jnp.zeros((TOKENS, 512), F32)
-    weights[1].wait()
     weights[2].wait()
+    weights[3].wait()
     ahead = dot(second_norm, w_up[:, :512])
     for part in range(4):
         cols = slice(part * 512, part * 512 + 512)
@@ -224,7 +228,7 @@
         near[:, :512] = block
         near[:, 512:] = cotangent
 
-    weights[3].wait()
+    weights[4].wait()
     level_two_ref[...] = sum(
         dot(merged_norm[p], w_merge[p * 512 : p * 512 + 512]) for p in range(4)
     ).astype(BF16)
@@ -318,36 +322,35 @@
     wide = dot(middle_grad, w_out[...], 1, 1).astype(BF16)
     for group in range(4):
         grad_heads[group] = wide[:, group * 128 : group * 128 + 128]
-    grad_heads_t[...] = dot(w_out[...], middle_grad, 1, 1).astype(BF16)
-    products[...] = grad_heads_t[...].astype(F32) * attended_ref[...].astype(F32)
-
-    head_of_row = lax.broadcasted_iota(jnp.int32, (128, TOKENS), 0) >> 5
+    upstream_t = dot(w_out[...], middle_grad, 1, 1).astype(BF16)
+    products[...] = upstream_t.astype(F32) * attended_ref[...].astype(F32)
+    grad_heads_t[...] = jnp.zeros_like(grad_heads_t)
+    for head in range(16):
+        rows = slice(head % 4 * HEAD, head % 4 * HEAD + HEAD)
+        grad_heads_t[head, rows, :] = upstream_t[head * HEAD : head * HEAD + HEAD]
+
     head_of_lane = lax.broadcasted_iota(jnp.int32, (TOKENS, 128), 1) >> 5
 
-    def attend_back(group):
+    for group in range(4):
         loads[group].wait()
         queries = packed_ref[group]
         values = packed_ref[8 + group]
         upstream = grad_heads[group]
-        upstream_t = grad_heads_t[slice(group * 128, group * 128 + 128), :]
         grad_keys = jnp.zeros((TOKENS, 128), F32)
         grad_values = jnp.zeros((TOKENS, 128), F32)
-        for head in range(4):
-            at = slice(group * 128 + head * HEAD, group * 128 + head * HEAD + HEAD)
-            masked_t = jnp.where(head_of_row == head, upstream_t, jnp.zeros_like(upstream_t))
-            weights = probs_ref[group * 4 + head]
+        for part in range(4):
+            head = group * 4 + part
+            at = slice(head * HEAD, head * HEAD + HEAD)
+            weights = probs_ref[head]
             total = jnp.sum(products[at, :], axis=0, keepdims=True)
-            grad_weights = dot(values, masked_t)
-            scores = (weights.astype(F32) * ((grad_weights - total) * (1 / LOG2E))).astype(BF16)
-            in_head = head_of_lane == head
-            grad_keys += dot(scores, jnp.where(in_head, queries, jnp.zeros_like(queries)))
-            grad_values += dot(weights, jnp.where(in_head, upstream, jnp.zeros_like(upstream)))
-            query_grad_t[at, :] = (dot(keys_t_ref[at, :], scores) * QUERY_SCALE).astype(BF16)
-        packed_grad[4 + group] = grad_keys.astype(BF16)
+            grad_weights = dot(values, grad_heads_t[head])
+            scores = (weights.astype(F32) * (grad_weights - total)).astype(BF16)
+            in_head = head_of_lane == part
+            grad_keys = jnp.where(in_head, dot(scores, queries), grad_keys)
+            grad_values = jnp.where(in_head, dot(weights, upstream), grad_values)
+            query_grad_t[at, :] = (dot(keys_t_ref[at, :], scores) * HEAD ** (-0.5)).astype(BF16)
+        packed_grad[4 + group] = (grad_keys * (1 / LOG2E)).astype(BF16)
         packed_grad[8 + group] = grad_values.astype(BF16)
-
-    for group in range(4):
-        attend_back(group)
 
     for copy in nears:
         copy.wait()
@@ -460,7 +463,7 @@
 
 
 def call(kernel, inputs, held, outputs, saved, scratch, micros, kind=BF16, free=(), aliases=(),
-         weight=1):
+         weight=1, loose=False):
     whole, there = pl.BlockSpec(memory_space=pltpu.VMEM), pl.BlockSpec(memory_space=pltpu.HBM)
     specs = [whole if at < held else there for at in range(len(inputs))]
     for at in free:
@@ -471,7 +474,10 @@
         kernel,
         out_shape=[jax.ShapeDtypeStruct(shape, kind) for shape in outputs],
         in_specs=specs,
-        out_specs=[whole if at < saved else there for at in range(len(outputs))],
+        out_specs=[
+            pl.BlockSpec(memory_space=pl.ANY) if loose else whole if at < saved else there
+            for at in range(len(outputs))
+        ],
         scratch_shapes=scratch,
         input_output_aliases=dict(aliases),
         compiler_params=pltpu.CompilerParams(vmem_limit_bytes=(56 if micros > 5 else 14) * 2**20),
@@ -493,12 +499,12 @@
     return lax.ppermute(send, "core", [(0, 1), (1, 0)])
 
 
-def ring_parts(where, keep, send, axis, shift):
+def ring_parts(where, keep, arrived, axis, shift, weight):
     count = keep.shape[0]
     outs = call(
         functools.partial(ring_kernel, shift=shift),
-        [where, keep, exchanged(send)], 1, [(64, 16, 128)] * count, count,
-        [vmem(*keep.shape), vmem(*keep.shape), dmas(count), dmas(count)], 2, free=(2,),
+        [where, keep, arrived], 1, [(64, 16, 128)] * count, count,
+        [vmem(*keep.shape), vmem(*keep.shape), dmas(count), dmas(count)], 2, free=(2,), weight=weight,
     )
     moved = [
         lax.ppermute(outs[step], axis, [(i, (i + step) % 4) for i in range(4)])
@@ -565,16 +571,16 @@
      middle, grad_after, probs, slope, down_keep, down_send) = call(
         forward_kernel,
         [where, jnp.asarray(order, BF16), jnp.asarray(cot_order, BF16), window_ids,
-         jnp.asarray(places, BF16), jnp.asarray(places[1].T, F32), w_qkv, *quads,
-         w_out, w_up, w_down, w_merge], 7,
+         jnp.asarray(places, BF16), jnp.asarray(places[1].T, F32), *quads, w_qkv,
+         w_out, w_up, w_down, w_merge], 6,
         [(MERGED, 1024)] + [near_shape] * 4 + [field, (12, TOKENS, 128), by_feature, by_feature,
          by_feature, field, field, all_probs, hidden_shape, (4, 64, 16, 128), (4, 64, 16, 128)],
         12,
-        [vmem(4, *corner), pltpu.VMEM((TOKENS, TOKENS), F32), vmem(*by_feature), vmem(*by_feature),
-         vmem(*hidden_shape), vmem(*hidden_shape), vmem(*all_probs), vmem(*w_out.shape),
+        [vmem(4, *corner), pltpu.VMEM((TOKENS, TOKENS), F32), vmem(16, 128, TOKENS), vmem(*by_feature),
+         vmem(*hidden_shape), vmem(*hidden_shape), vmem(*all_probs), vmem(*w_qkv.shape), vmem(*w_out.shape),
          vmem(*w_up.shape), vmem(*w_down.shape), vmem(*w_merge.shape), vmem(2, 4, 64, 16, 128),
-         dmas(4), dmas(4), dmas(4)],
-        20, free=range(7, 11),
+         dmas(4), dmas(5), dmas(4)],
+        20, free=range(6, 10),
     )
     near = [near0]
     for step, block in ((1, near1), (2, near2), (3, near3)):
@@ -587,8 +593,9 @@
          dmas(3), dmas(4)],
         7,
     )
-    down_sums, down_parts = ring_parts(where, down_keep, down_send, "z", 3)
-    up_sums, up_parts = ring_parts(where, keep, send, "y", 1)
+    down_keep, *near = lax.optimization_barrier((down_keep, *near))
+    down_sums, down_parts = ring_parts(where, down_keep, exchanged(down_send), "z", 3, 60)
+    up_sums, up_parts = ring_parts(where, keep, exchanged(send), "y", 1, 1)
     middle_grad, *_ = lax.optimization_barrier((middle_grad, down_sums[0], up_sums[0]))
     *corners, late_keep, late_send = call(
         backward_kernel,
@@ -596,7 +603,7 @@
          jnp.asarray(order.transpose(0, 2, 1), BF16), jnp.asarray(level_order, BF16), level_two,
          w_out, *near, probs, w_qkv], 11,
         [corner] * 4 + [(64, 16, 640)] * 2, 4,
-        [vmem(4, TOKENS, 128), vmem(*by_feature), pltpu.VMEM(by_feature, F32), vmem(*by_feature),
+        [vmem(4, TOKENS, 128), vmem(16, 128, TOKENS), pltpu.VMEM(by_feature, F32), vmem(*by_feature),
          vmem(12, TOKENS, 128), vmem(*all_probs), vmem(*w_qkv.shape), vmem(4, *near_shape),
          vmem(2, 64, 16, 640), dmas(4), dmas(5), dmas(2)],
         12, free=range(12, 15),
@@ -604,12 +611,13 @@
     blocks, = call(
         assemble_kernel, [*down_parts, *up_parts], 0, [(64, 16, 1024)], 0,
         [vmem(9, 64, 16, 128), vmem(64, 16, 384), dmas(9), dmas(1)], 2, free=range(9), weight=60,
+        loose=True,
     )
     blocks, = call(
         functools.partial(pair_kernel, place=384),
         [late_keep, exchanged(late_send), blocks], 0, [blocks.shape], 0,
-        [vmem(64, 16, 640), vmem(64, 16, 640), dmas(4), dmas(4), dmas(4)], 2, free=(1,),
-        aliases={2: 0},
+        [vmem(64, 16, 640), vmem(64, 16, 640), dmas(4), dmas(4), dmas(4)], 2, free=(1, 2),
+        aliases={2: 0}, loose=True,
     )
     corners = send_forth(corners)
     blocks, *corners = lax.optimization_barrier((blocks, *corners))

time: 138 us -> 135 us (0.978)
  waiting for transfers between devices: 44.5 us -> 40.5 us
  starting transfers between devices: 33.1 us -> 34.5 us
    ppermute x6, waiting for transfers between devices: 0.02 us -> 6.1 us  [ring_parts(): lax.ppermute(outs[step], axis, [(i, (i + step) % 4) for i in range(4)])]
    ppermute x3, waiting for transfers between devices: 6.76 us -> 1.57 us  [body(): lax.ppermute(block, 'y', [(i, (i + step) % 4) for i in range(4)])]
    ppermute x3, waiting for transfers between devices: 6.14 us -> 2.12 us  [exchanged(): return lax.ppermute(send, 'core', [(0, 1), (1, 0)])]
    ppermute x3, starting transfers between devices: 2.05 us -> 4.29 us  [exchanged(): return lax.ppermute(send, 'core', [(0, 1), (1, 0)])]
    ppermute x6, starting transfers between devices: 11.6 us -> 9.86 us  [shifted_block(): return lax.ppermute(block, GRID, route)]
    all_to_all x1, starting transfers between devices: 7.35 us -> 9.03 us  [body(): landed = lax.all_to_all(blocks, PAIRS, 0, 0, tiled=True)]
  transfers between devices with their start and end apart: 19 -> 19, of which waited for: 7 -> 7; matrix products, arithmetic and copies ran while one was open for 2% -> 2% of each run, Pallas kernels for 12% -> 19%
where the time goes in v10:
time: 135 us; the launch traced here: 134 us
  Pallas kernels  50.5 us (37%)
  waiting for transfers between devices  40.5 us (30%)
  starting transfers between devices  34.5 us (26%)
  local copies, waits for them, and re-layouts  4.87 us (4%)
  other arithmetic  2.74 us (2%)
    pallas_call x8, Pallas kernels, call(): pl.pallas_call(kernel, out_shape=[jax.ShapeDtypeStruct(shape, kind) for s...  50.5 us
    all_to_all x1, waiting for transfers between devices, body(): landed = lax.all_to_all(blocks, PAIRS, 0, 0, tiled=True)  27.6 us
    ppermute x6, starting transfers between devices, shifted_block(): return lax.ppermute(block, GRID, route)  9.86 us
    all_to_all x1, starting transfers between devices, body(): landed = lax.all_to_all(blocks, PAIRS, 0, 0, tiled=True)  9.03 us
    ppermute x6, starting transfers between devices, ring_parts(): lax.ppermute(outs[step], axis, [(i, (i + step) % 4) for i in range(4)])  7.67 us
    ppermute x6, waiting for transfers between devices, ring_parts(): lax.ppermute(outs[step], axis, [(i, (i + step) % 4) for i in range(4)])  6.1 us
    ppermute x3, starting transfers between devices, exchanged(): return lax.ppermute(send, 'core', [(0, 1), (1, 0)])  4.29 us
    ppermute x3, starting transfers between devices, body(): lax.ppermute(block, 'y', [(i, (i + step) % 4) for i in range(4)])  3.69 us
  transfers between devices with their start and end apart: 19, of which 7 were waited for; matrix products, arithmetic and copies ran while one was open for 2% of the time, Pallas kernels for 19%

profile of v10, /device:TPU:0, one launch (start us, length us, event | category | flops | bytes accessed | tf_op | source)
XLA Modules:
  0.0 134.4 jit_solution(1091227169287727427)
XLA Ops:
  0.6 0.9 fusion.1
  1.6 1.2 fusion
  2.9 5.1 %collective-permute-start = (bf16[108,512]{1,0:T(8,128)(2,1)S(1)}, bf16[108,512]{1,0:T(8,128)(2,1)S(1)}, u32[]{:S(2)}, u32[]{:S(2)}) collective-permute-start(bf16[108,512]{1,0:T(8,128)(2,1)S(1)} %pad_maximum_fusion.1), channel_id=1, source_target_pairs={{0,15},{1,0},{2,1},{3,2},{4,3},{5,4},{6,5},{7,6},{8,7},{9,8},{10,9... | collective-permute-start | bytes 331784 | tf_op jit(solution)/shard_map/ppermute | solution.py:521
  8.0 4.1 %collective-permute-start.1 = (bf16[108,512]{1,0:T(8,128)(2,1)S(1)}, bf16[108,512]{1,0:T(8,128)(2,1)S(1)}, u32[]{:S(2)}, u32[]{:S(2)}) collective-permute-start(bf16[108,512]{1,0:T(8,128)(2,1)S(1)} %pad_maximum_fusion.2), channel_id=1, source_target_pairs={{0,112},{1,113},{2,114},{3,115},{4,116},{5,117},{6,118},{7,119},{8... | collective-permute-start | bytes 331784 | tf_op jit(solution)/shard_map/ppermute | solution.py:521
  12.3 0.4 collective-permute-start.2
  12.8 0.7 pad_maximum_fusion.quad0_hbm
  13.5 1.2 collective-permute-done.1.quad2_hbm
  14.7 1.9 %collective-permute-done.2.quad3_hbm = bf16[108,512]{1,0:T(8,128)(2,1)S(1)} collective-permute-done((bf16[108,512]{1,0:T(8,128)(2,1)S(1)}, bf16[108,512]{1,0:T(8,128)(2,1)S(1)}, u32[]{:S(2)}, u32[]{:S(2)}) %collective-permute-start.2) | collective-permute-done | bytes 110624 | tf_op jit(solution)/shard_map/ppermute | solution.py:521
  16.6 0.6 copy-done.10
  17.2 23.6 %shard_map.189 = (bf16[72,1024]{1,0:T(8,128)(2,1)}, bf16[72,1536]{1,0:T(8,128)(2,1)}, bf16[72,1536]{1,0:T(8,128)(2,1)}, bf16[72,1536]{1,0:T(8,128)(2,1)}, bf16[7...) custom-call(s32[1]{0:T(128)} %bitcast.where_ref, ...), custom_call_target="tpu_custom_call" | custom-call | flops 20000000000 | bytes 20000000 | tf_op jit(solution)/shard_map/pallas_call | solution.py:473
  41.0 2.4 %collective-permute-start.4 = (bf16[72,1536]{1,0:T(8,128)(2,1)}, bf16[72,1536]{1,0:T(8,128)(2,1)S(1)}, u32[]{:S(2)}, u32[]{:S(2)}) collective-permute-start(bf16[72,1536]{1,0:T(8,128)(2,1)} %get-tuple-element.68), channel_id=1, source_target_pairs={{0,8},{4,12},{8,0},{12,4},{1,9},{5,13},{9,1},{13,5},{2,10},{6,14},... | collective-permute-start | bytes 663560 | tf_op jit(solution)/shard_map/ppermute | solution.py:587
  43.4 1.2 collective-permute-start.5
  44.6 9.3 %shard_map.190 = (bf16[288,512]{1,0:T(8,128)(2,1)}, bf16[5,64,16,128]{3,2,1,0:T(8,128)(2,1)}, bf16[5,64,16,128]{3,2,1,0:T(8,128)(2,1)}) custom-call(s32[1]{0:T(128)} %bitcast.where_ref, bf16[288,512]{1,0:T(8,128)(2,1)} %get-tuple-element.61.grad_after_ref, bf16[288,512]{1,0:T(8,128)(2,1)} %get-tuple-element.62.middle_ref, ...), custom_call_target="tpu_custom_call" | custom-call | flops 7000000000 | bytes 7000000 | tf_op jit(solution)/shard_map/pallas_call | solution.py:473
  53.9 1.0 collective-permute-done.3.near1_hbm
  54.9 0.6 collective-permute-done.5.near3_hbm
  55.5 0.5 shard_map.191
  56.2 3.1 %collective-permute-start.10 = (bf16[64,16,128]{2,1,0:T(8,128)(2,1)S(1)}, bf16[64,16,128]{2,1,0:T(8,128)(2,1)S(1)}, u32[]{:S(2)}, u32[]{:S(2)}) collective-permute-start(bf16[64,16,128]{2,1,0:T(8,128)(2,1)S(1)} %get-tuple-element.87), channel_id=1, source_target_pairs={{0,64},{32,96},{64,0},{96,32},{1,65},{33,97},{65,1},{97,33},{2,66}... | collective-permute-start | bytes 786440 | tf_op jit(solution)/shard_map/ppermute | solution.py:510
  59.3 0.7 collective-permute-start.11
  60.0 0.6 shard_map.192
  60.9 3.6 %collective-permute-start.13 = (bf16[64,16,128]{2,1,0:T(8,128)(2,1)S(1)}, bf16[64,16,128]{2,1,0:T(8,128)(2,1)S(1)}, u32[]{:S(2)}, u32[]{:S(2)}) collective-permute-start(bf16[64,16,128]{2,1,0:T(8,128)(2,1)S(1)} %get-tuple-element.90), channel_id=1, source_target_pairs={{0,8},{4,12},{8,0},{12,4},{1,9},{5,13},{9,1},{13,5},{2,10},{6,14},... | collective-permute-start | bytes 786440 | tf_op jit(solution)/shard_map/ppermute | solution.py:510
  64.5 6.1 %collective-permute-done.9.refs_1_ = bf16[64,16,128]{2,1,0:T(8,128)(2,1)S(1)} collective-permute-done((bf16[64,16,128]{2,1,0:T(8,128)(2,1)S(1)}, bf16[64,16,128]{2,1,0:T(8,128)(2,1)S(1)}, u32[]{:S(2)}, u32[]{:S(2)}) %collective-permute-start.9) | collective-permute-done | bytes 262176 | tf_op jit(solution)/shard_map/ppermute | solution.py:510
  70.6 13.3 %shard_map.193 = (bf16[108,512]{1,0:T(8,128)(2,1)}, bf16[108,512]{1,0:T(8,128)(2,1)}, bf16[108,512]{1,0:T(8,128)(2,1)}, bf16[108,512]{1,0:T(8,128)(2,1)}, bf16[6...) custom-call(s32[1]{0:T(128)} %bitcast.where_ref, bf16[288,512]{1,0:T(8,128)(2,1)} %get-tuple-element.57.tokens_ref, ...), custom_call_target="tpu_custom_call" | custom-call | flops 12000000000 | bytes 12000000 | tf_op jit(solution)/shard_map/pallas_call | solution.py:473
  84.2 4.1 %collective-permute-start.8 = (bf16[64,16,640]{2,1,0:T(8,128)(2,1)}, bf16[64,16,640]{2,1,0:T(8,128)(2,1)S(1)}, u32[]{:S(2)}, u32[]{:S(2)}) collective-permute-start(bf16[64,16,640]{2,1,0:T(8,128)(2,1)} %get-tuple-element.85), channel_id=1, source_target_pairs={{0,1},{1,0},{2,3},{3,2},{4,5},{5,4},{6,7},{7,6},{8,9},{9,8},{10,11... | collective-permute-start | bytes 3932168 | tf_op jit(solution)/shard_map/ppermute | solution.py:499
  88.3 0.7 shard_map.194.refs_0_
  89.1 2.1 %collective-permute-done.8.arrived_hbm = bf16[64,16,640]{2,1,0:T(8,128)(2,1)S(1)} collective-permute-done((bf16[64,16,640]{2,1,0:T(8,128)(2,1)}, bf16[64,16,640]{2,1,0:T(8,128)(2,1)S(1)}, u32[]{:S(2)}, u32[]{:S(2)}) %collective-permute-start.8) | collective-permute-done | bytes 1310752 | tf_op jit(solution)/shard_map/ppermute | solution.py:499
  91.2 1.4 %shard_map.195 = bf16[64,16,1024]{2,1,0:T(8,128)(2,1)S(1)} custom-call(bf16[64,16,640]{2,1,0:T(8,128)(2,1)S(1)} %copy-done.1, bf16[64,16,640]{2,1,0:T(8,128)(2,1)S(1)} %collective-permute-done.8.arrived_hbm, bf16[64,16,1024]{2,1,0:T(8,128)(2,1)S(1)} %shard_map.194.refs_0_), custom_call_target="tpu_custom_call", output_to_operand_aliasing={{}: (2, {})} | custom-call | flops 2000000000 | bytes 2000000 | tf_op jit(solution)/shard_map/pallas_call | solution.py:473
  92.6 1.3 %copy-done = bf16[64,16,1024]{2,1,0:T(8,128)(2,1)} copy-done((bf16[64,16,1024]{2,1,0:T(8,128)(2,1)}, bf16[64,16,1024]{2,1,0:T(8,128)(2,1)S(1)}, u32[]{:S(2)}) %copy-start) | copy-done | bytes 2097176
  94.0 9.0 %all-to-all-start = ((bf16[64,16,1024]{2,1,0:T(8,128)(2,1)}), bf16[64,16,1024]{2,1,0:T(8,128)(2,1)S(1)}, u32[]{:S(2)}, u32[]{:S(2)}) async-start(bf16[64,16,1024]{2,1,0:T(8,128)(2,1)} %copy-done), calls=%async_computation | async-start | bytes 4194304 | tf_op jit(solution)/shard_map/all_to_all | solution.py:624
  103.5 0.9 maximum_bitcast_fusion.1
  104.3 1.1 maximum_bitcast_fusion
  105.5 27.6 %all-to-all-done.landed_hbm = bf16[64,16,1024]{2,1,0:T(8,128)(2,1)S(1)} async-done(((bf16[64,16,1024]{2,1,0:T(8,128)(2,1)}), bf16[64,16,1024]{2,1,0:T(8,128)(2,1)S(1)}, u32[]{:S(2)}, u32[]{:S(2)}) %all-to-all-start) | async-done | bytes 2097184 | tf_op jit(solution)/shard_map/all_to_all | solution.py:624
  133.1 1.1 shard_map.196
  (74 shorter events, 1.6 us)
Async XLA Ops:
  2.9 10.6 %collective-permute-start = (bf16[108,512]{1,0:T(8,128)(2,1)S(1)}, bf16[108,512]{1,0:T(8,128)(2,1)S(1)}, u32[]{:S(2)}, u32[]{:S(2)}) collective-permute-start(bf16[108,512]{1,0:T(8,128)(2,1)S(1)} %pad_maximum_fusion.1), channel_id=1, source_target_pairs={{0,15},{1,0},{2,1},{3,2},{4,3},{5,4},{6,5},{7,6},{8,7},{9,8},{10,9... | collective-permute-start | bytes 331784 | tf_op jit(solution)/shard_map/ppermute | solution.py:521
  8.0 6.6 %collective-permute-start.1 = (bf16[108,512]{1,0:T(8,128)(2,1)S(1)}, bf16[108,512]{1,0:T(8,128)(2,1)S(1)}, u32[]{:S(2)}, u32[]{:S(2)}) collective-permute-start(bf16[108,512]{1,0:T(8,128)(2,1)S(1)} %pad_maximum_fusion.2), channel_id=1, source_target_pairs={{0,112},{1,113},{2,114},{3,115},{4,116},{5,117},{6,118},{7,119},{8... | collective-permute-start | bytes 331784 | tf_op jit(solution)/shard_map/ppermute | solution.py:521
  12.3 4.3 %collective-permute-start.2 = (bf16[108,512]{1,0:T(8,128)(2,1)S(1)}, bf16[108,512]{1,0:T(8,128)(2,1)S(1)}, u32[]{:S(2)}, u32[]{:S(2)}) collective-permute-start(bf16[108,512]{1,0:T(8,128)(2,1)S(1)} %pad_maximum_fusion.3), channel_id=1, source_target_pairs={{0,127},{1,112},{2,113},{3,114},{4,115},{5,116},{6,117},{7,118},{8... | collective-permute-start | bytes 331784 | tf_op jit(solution)/shard_map/ppermute | solution.py:521
  13.5 3.1 %copy-start.8 = (bf16[108,512]{1,0:T(8,128)(2,1)}, bf16[108,512]{1,0:T(8,128)(2,1)S(1)}, u32[]{:S(2)}) copy-start(bf16[108,512]{1,0:T(8,128)(2,1)S(1)} %collective-permute-done.quad1_hbm) | copy-start | bytes 331780
  14.7 1.9 %copy-start.9 = (bf16[108,512]{1,0:T(8,128)(2,1)}, bf16[108,512]{1,0:T(8,128)(2,1)S(1)}, u32[]{:S(2)}) copy-start(bf16[108,512]{1,0:T(8,128)(2,1)S(1)} %collective-permute-done.1.quad2_hbm) | copy-start | bytes 331780
  16.6 0.6 copy-start.10
  40.8 14.7 %collective-permute-start.6 = (bf16[4,64,16,128]{3,2,1,0:T(8,128)(2,1)}, bf16[4,64,16,128]{3,2,1,0:T(8,128)(2,1)S(1)}, u32[]{:S(2)}, u32[]{:S(2)}) collective-permute-start(bf16[4,64,16,128]{3,2,1,0:T(8,128)(2,1)} %get-tuple-element.71), channel_id=1, source_target_pairs={{0,1},{1,0},{2,3},{3,2},{4,5},{5,4},{6,7},{7,6},{8,9},{9,8},{10,11... | collective-permute-start | bytes 3145736 | tf_op jit(solution)/shard_map/ppermute | solution.py:499
  40.9 14.0 %collective-permute-start.3 = (bf16[72,1536]{1,0:T(8,128)(2,1)}, bf16[72,1536]{1,0:T(8,128)(2,1)S(1)}, u32[]{:S(2)}, u32[]{:S(2)}) collective-permute-start(bf16[72,1536]{1,0:T(8,128)(2,1)} %get-tuple-element.67), channel_id=1, source_target_pairs={{0,4},{4,8},{8,12},{12,0},{1,5},{5,9},{9,13},{13,1},{2,6},{6,10},{... | collective-permute-start | bytes 663560 | tf_op jit(solution)/shard_map/ppermute | solution.py:587
  41.0 13.9 %collective-permute-start.4 = (bf16[72,1536]{1,0:T(8,128)(2,1)}, bf16[72,1536]{1,0:T(8,128)(2,1)S(1)}, u32[]{:S(2)}, u32[]{:S(2)}) collective-permute-start(bf16[72,1536]{1,0:T(8,128)(2,1)} %get-tuple-element.68), channel_id=1, source_target_pairs={{0,8},{4,12},{8,0},{12,4},{1,9},{5,13},{9,1},{13,5},{2,10},{6,14},... | collective-permute-start | bytes 663560 | tf_op jit(solution)/shard_map/ppermute | solution.py:587
  43.4 12.1 %collective-permute-start.5 = (bf16[72,1536]{1,0:T(8,128)(2,1)}, bf16[72,1536]{1,0:T(8,128)(2,1)S(1)}, u32[]{:S(2)}, u32[]{:S(2)}) collective-permute-start(bf16[72,1536]{1,0:T(8,128)(2,1)} %get-tuple-element.69), channel_id=1, source_target_pairs={{0,12},{4,0},{8,4},{12,8},{1,13},{5,1},{9,5},{13,9},{2,14},{6,2},{... | collective-permute-start | bytes 663560 | tf_op jit(solution)/shard_map/ppermute | solution.py:587
  44.6 10.9 %copy-start.3 = (bf16[4,64,16,128]{3,2,1,0:T(8,128)(2,1)S(1)}, bf16[4,64,16,128]{3,2,1,0:T(8,128)(2,1)}, u32[]{:S(2)}) copy-start(bf16[4,64,16,128]{3,2,1,0:T(8,128)(2,1)} %get-tuple-element.70.keep_hbm) | copy-start | bytes 3145732
  53.9 6.2 %collective-permute-start.7 = (bf16[5,64,16,128]{3,2,1,0:T(8,128)(2,1)}, bf16[5,64,16,128]{3,2,1,0:T(8,128)(2,1)S(1)}, u32[]{:S(2)}, u32[]{:S(2)}) collective-permute-start(bf16[5,64,16,128]{3,2,1,0:T(8,128)(2,1)} %get-tuple-element.74), channel_id=1, source_target_pairs={{0,1},{1,0},{2,3},{3,2},{4,5},{5,4},{6,7},{7,6},{8,9},{9,8},{10,11... | collective-permute-start | bytes 3932168 | tf_op jit(solution)/shard_map/ppermute | solution.py:499
  54.9 1.1 copy-start.5
  54.9 1.1 copy-start.6
  55.5 0.7 copy-start.7
  55.5 4.5 %copy-start.2 = (bf16[5,64,16,128]{3,2,1,0:T(8,128)(2,1)S(1)}, bf16[5,64,16,128]{3,2,1,0:T(8,128)(2,1)}, u32[]{:S(2)}) copy-start(bf16[5,64,16,128]{3,2,1,0:T(8,128)(2,1)} %get-tuple-element.73.keep_hbm) | copy-start | bytes 3932164
  56.2 14.4 %collective-permute-start.9 = (bf16[64,16,128]{2,1,0:T(8,128)(2,1)S(1)}, bf16[64,16,128]{2,1,0:T(8,128)(2,1)S(1)}, u32[]{:S(2)}, u32[]{:S(2)}) collective-permute-start(bf16[64,16,128]{2,1,0:T(8,128)(2,1)S(1)} %get-tuple-element.86), channel_id=1, source_target_pairs={{0,32},{32,64},{64,96},{96,0},{1,33},{33,65},{65,97},{97,1},{2,34}... | collective-permute-start | bytes 786440 | tf_op jit(solution)/shard_map/ppermute | solution.py:510
  56.2 27.7 %collective-permute-start.10 = (bf16[64,16,128]{2,1,0:T(8,128)(2,1)S(1)}, bf16[64,16,128]{2,1,0:T(8,128)(2,1)S(1)}, u32[]{:S(2)}, u32[]{:S(2)}) collective-permute-start(bf16[64,16,128]{2,1,0:T(8,128)(2,1)S(1)} %get-tuple-element.87), channel_id=1, source_target_pairs={{0,64},{32,96},{64,0},{96,32},{1,65},{33,97},{65,1},{97,33},{2,66}... | collective-permute-start | bytes 786440 | tf_op jit(solution)/shard_map/ppermute | solution.py:510
  59.3 24.7 %collective-permute-start.11 = (bf16[64,16,128]{2,1,0:T(8,128)(2,1)S(1)}, bf16[64,16,128]{2,1,0:T(8,128)(2,1)S(1)}, u32[]{:S(2)}, u32[]{:S(2)}) collective-permute-start(bf16[64,16,128]{2,1,0:T(8,128)(2,1)S(1)} %get-tuple-element.88), channel_id=1, source_target_pairs={{0,96},{32,0},{64,32},{96,64},{1,97},{33,1},{65,33},{97,65},{2,98}... | collective-permute-start | bytes 786440 | tf_op jit(solution)/shard_map/ppermute | solution.py:510
  60.6 23.4 %collective-permute-start.12 = (bf16[64,16,128]{2,1,0:T(8,128)(2,1)S(1)}, bf16[64,16,128]{2,1,0:T(8,128)(2,1)S(1)}, u32[]{:S(2)}, u32[]{:S(2)}) collective-permute-start(bf16[64,16,128]{2,1,0:T(8,128)(2,1)S(1)} %get-tuple-element.89), channel_id=1, source_target_pairs={{0,4},{4,8},{8,12},{12,0},{1,5},{5,9},{9,13},{13,1},{2,6},{6,10},{... | collective-permute-start | bytes 786440 | tf_op jit(solution)/shard_map/ppermute | solution.py:510
  60.9 23.2 %collective-permute-start.13 = (bf16[64,16,128]{2,1,0:T(8,128)(2,1)S(1)}, bf16[64,16,128]{2,1,0:T(8,128)(2,1)S(1)}, u32[]{:S(2)}, u32[]{:S(2)}) collective-permute-start(bf16[64,16,128]{2,1,0:T(8,128)(2,1)S(1)} %get-tuple-element.90), channel_id=1, source_target_pairs={{0,8},{4,12},{8,0},{12,4},{1,9},{5,13},{9,1},{13,5},{2,10},{6,14},... | collective-permute-start | bytes 786440 | tf_op jit(solution)/shard_map/ppermute | solution.py:510
  70.6 17.7 %collective-permute-start.14 = (bf16[64,16,128]{2,1,0:T(8,128)(2,1)S(1)}, bf16[64,16,128]{2,1,0:T(8,128)(2,1)S(1)}, u32[]{:S(2)}, u32[]{:S(2)}) collective-permute-start(bf16[64,16,128]{2,1,0:T(8,128)(2,1)S(1)} %get-tuple-element.91), channel_id=1, source_target_pairs={{0,12},{4,0},{8,4},{12,8},{1,13},{5,1},{9,5},{13,9},{2,14},{6,2},{... | collective-permute-start | bytes 786440 | tf_op jit(solution)/shard_map/ppermute | solution.py:510
  83.9 10.0 %collective-permute-start.15 = (bf16[108,512]{1,0:T(8,128)(2,1)}, bf16[108,512]{1,0:T(8,128)(2,1)S(1)}, u32[]{:S(2)}, u32[]{:S(2)}) collective-permute-start(bf16[108,512]{1,0:T(8,128)(2,1)} %get-tuple-element.93), channel_id=1, source_target_pairs={{0,17},{1,18},{2,19},{3,20},{4,21},{5,22},{6,23},{7,24},{8,25},{9,... | collective-permute-start | bytes 331784 | tf_op jit(solution)/shard_map/ppermute | solution.py:521
  84.0 10.0 %collective-permute-start.16 = (bf16[108,512]{1,0:T(8,128)(2,1)}, bf16[108,512]{1,0:T(8,128)(2,1)S(1)}, u32[]{:S(2)}, u32[]{:S(2)}) collective-permute-start(bf16[108,512]{1,0:T(8,128)(2,1)} %get-tuple-element.94), channel_id=1, source_target_pairs={{0,16},{1,17},{2,18},{3,19},{4,20},{5,21},{6,22},{7,23},{8,24},{9,... | collective-permute-start | bytes 331784 | tf_op jit(solution)/shard_map/ppermute | solution.py:521
  84.1 9.9 %collective-permute-start.17 = (bf16[108,512]{1,0:T(8,128)(2,1)}, bf16[108,512]{1,0:T(8,128)(2,1)S(1)}, u32[]{:S(2)}, u32[]{:S(2)}) collective-permute-start(bf16[108,512]{1,0:T(8,128)(2,1)} %get-tuple-element.95), channel_id=1, source_target_pairs={{0,1},{1,2},{2,3},{3,4},{4,5},{5,6},{6,7},{7,8},{8,9},{9,10},{10,1... | collective-permute-start | bytes 331784 | tf_op jit(solution)/shard_map/ppermute | solution.py:521
  84.2 7.0 %collective-permute-start.8 = (bf16[64,16,640]{2,1,0:T(8,128)(2,1)}, bf16[64,16,640]{2,1,0:T(8,128)(2,1)S(1)}, u32[]{:S(2)}, u32[]{:S(2)}) collective-permute-start(bf16[64,16,640]{2,1,0:T(8,128)(2,1)} %get-tuple-element.85), channel_id=1, source_target_pairs={{0,1},{1,0},{2,3},{3,2},{4,5},{5,4},{6,7},{7,6},{8,9},{9,8},{10,11... | collective-permute-start | bytes 3932168 | tf_op jit(solution)/shard_map/ppermute | solution.py:499
  88.3 2.9 %copy-start.1 = (bf16[64,16,640]{2,1,0:T(8,128)(2,1)S(1)}, bf16[64,16,640]{2,1,0:T(8,128)(2,1)}, u32[]{:S(2)}) copy-start(bf16[64,16,640]{2,1,0:T(8,128)(2,1)} %get-tuple-element.84.keep_hbm) | copy-start | bytes 3932164
  92.6 1.4 %copy-start = (bf16[64,16,1024]{2,1,0:T(8,128)(2,1)}, bf16[64,16,1024]{2,1,0:T(8,128)(2,1)S(1)}, u32[]{:S(2)}) copy-start(bf16[64,16,1024]{2,1,0:T(8,128)(2,1)S(1)} %shard_map.195) | copy-start | bytes 6291460
  94.0 9.3 %copy-start.4 = (bf16[108,512]{1,0:T(8,128)(2,1)S(1)}, bf16[108,512]{1,0:T(8,128)(2,1)}, u32[]{:S(2)}) copy-start(bf16[108,512]{1,0:T(8,128)(2,1)} %get-tuple-element.100) | copy-start | bytes 331780
  94.0 39.1 %all-to-all-start = ((bf16[64,16,1024]{2,1,0:T(8,128)(2,1)}), bf16[64,16,1024]{2,1,0:T(8,128)(2,1)S(1)}, u32[]{:S(2)}, u32[]{:S(2)}) async-start(bf16[64,16,1024]{2,1,0:T(8,128)(2,1)} %copy-done), calls=%async_computation | async-start | bytes 4194304 | tf_op jit(solution)/shard_map/all_to_all | solution.py:624

commit v11 on v10

--- a/solution.py
+++ b/solution.py
@@ -77,10 +77,8 @@
     return inverse_std * (upstream - mean_grad - normed * mean_cross)
 
 
-def eye(size):
-    rows = lax.broadcasted_iota(jnp.int32, (size, 1), 0)
-    cols = lax.broadcasted_iota(jnp.int32, (1, size), 1)
-    return jnp.where(rows == cols, 1.0, 0.0).astype(BF16)
+def turned(values):
+    return jnp.swapaxes(values.astype(F32), 0, 1).astype(BF16)
 
 
 def weave(grads, slots, cols):
@@ -155,23 +153,22 @@
     tokens_ref[...] = tokens.astype(BF16)
     halves = sum(dot(cot_order_ref[q], quads_ref[q]) for q in range(4))
     cotangent = jnp.concatenate([halves[:MERGED], halves[MERGED:]], axis=1).astype(BF16)
-    first_norm = normalize(tokens)[0].astype(BF16)
-    first_t_ref[...] = dot(eye(512), first_norm, 1, 1).astype(BF16)
-    by_lane = eye(128)
+    normed_in = normalize(tokens)[0]
+    first_norm = normed_in.astype(BF16)
+    first_t_ref[...] = turned(normed_in)
     weights[0].wait()
     for part in range(3):
         wide = dot(first_norm, w_qkv[:, part * 512 : part * 512 + 512])
-        wide = (wide * QUERY_SCALE if part == 0 else wide).astype(BF16)
+        wide = wide * QUERY_SCALE if part == 0 else wide
         for group in range(4):
-            grid = wide[:, group * 128 : group * 128 + 128]
-            packed_ref[part * 4 + group] = grid
-            turned = dot(by_lane, grid, 1, 1).astype(BF16)
-            if part:
-                (keys_t_ref, values_t)[part - 1][group * 128 : group * 128 + 128, :] = turned
-                continue
-            for head in range(4):
-                rows = slice(head * HEAD, head * HEAD + HEAD)
-                query_t[group * 4 + head, rows, :] = turned[rows]
+            packed_ref[part * 4 + group] = wide[:, group * 128 : group * 128 + 128].astype(BF16)
+        by_feature = turned(wide)
+        if part:
+            (keys_t_ref, values_t)[part - 1][...] = by_feature
+            continue
+        for head in range(16):
+            rows = slice(head % 4 * HEAD, head % 4 * HEAD + HEAD)
+            query_t[head, rows, :] = by_feature[head * HEAD : head * HEAD + HEAD]
 
     def scores_of(head):
         return dot(packed_ref[4 + head // 4], query_t[head])
@@ -189,7 +186,7 @@
         attended_ref[at, :] = dot(values_t[at, :], probs).astype(BF16)
     saves = load([(probs_ref, probs_hbm)], out_sems.at[pl.ds(0, 1)])
 
-    attended = dot(eye(TOKENS), attended_ref[...], 1, 1).astype(BF16)
+    attended = turned(attended_ref[...])
     weights[1].wait()
     attn_out = dot(attended, w_out[...]).astype(BF16)
     narrow_middle = (tokens + attn_out.astype(F32)).astype(BF16)
@@ -266,7 +263,7 @@
     core = where_ref[0] & 1
     grad_after = grad_after_ref[...]
     normed_mid, inverse_mid = normalize(middle_ref[...].astype(F32))
-    second_t = dot(eye(512), normed_mid.astype(BF16), 1, 1).astype(BF16)
+    second_t = turned(normed_mid)
 
     def save(units, at):
         return load(
@@ -358,11 +355,8 @@
     grad = dot(near[:, :512], near[:, 512:], 0, 0)
     weave([grad[:, q * 256 : q * 256 + 256] for q in range(4)], slots, slice(384, 640))
 
-    identity = eye(TOKENS)
     for group in range(4):
-        packed_grad[group] = dot(
-            identity, query_grad_t[group * 128 : group * 128 + 128, :], 1, 1
-        ).astype(BF16)
+        packed_grad[group] = turned(query_grad_t[group * 128 : group * 128 + 128, :])
     first_t = first_t_ref[...]
     loads[4].wait()
     back_qkv = jnp.zeros((TOKENS, 512), F32)
@@ -410,37 +404,57 @@
         save.wait()
 
 
-def ring_kernel(where_ref, keep_hbm, arrived_hbm, *refs, shift):
-    *outs, keep_ref, arrived_ref, keep_sems, arrived_sems = refs
-    me = (where_ref[0] >> shift) & 3
-    units = [(me + step) & 3 for step in range(4)] + list(range(4, len(outs)))
+def pair_total(keep_hbm, arrived_hbm, units, keep_ref, arrived_ref, keep_sems, arrived_sems):
     keeps = [(keep_hbm.at[unit], keep_ref.at[at]) for at, unit in enumerate(units)]
     arrivals = [(arrived_hbm.at[unit], arrived_ref.at[at]) for at, unit in enumerate(units)]
     copies = list(zip(load(keeps, keep_sems), load(arrivals, arrived_sems)))
-    for at, out in enumerate(outs):
+    for at in range(len(units)):
         for copy in copies[at]:
             copy.wait()
-        out[...] = (keep_ref[at].astype(F32) + arrived_ref[at].astype(F32)).astype(BF16)
+        yield at, (keep_ref[at].astype(F32) + arrived_ref[at].astype(F32)).astype(BF16)
+
+
+def ring_kernel(where_ref, keep_hbm, arrived_hbm, own, send1, send2, send3, *scratch):
+    z = where_ref[0] >> 3
+    units = [(z + step) & 3 for step in range(4)]
+    for at, total in pair_total(keep_hbm, arrived_hbm, units, *scratch):
+        (own, send1, send2, send3)[at][...] = total
+
+
+def halves_kernel(where_ref, keep_hbm, arrived_hbm, own, send, out, *scratch):
+    half = (where_ref[0] >> 1) & 1
+    units = [half * 2, half * 2 + 1, 2 - half * 2, 3 - half * 2, 4]
+    for at, total in pair_total(keep_hbm, arrived_hbm, units, *scratch):
+        if at == 4:
+            out[...] = total
+        else:
+            (own, send)[at // 2][:, :, at % 2 * 128 : at % 2 * 128 + 128] = total
 
 
 def assemble_kernel(*refs):
-    blocks_hbm, parts_ref, total_ref, sems, out_sem = refs[9:]
-    copies = load([(refs[at], parts_ref.at[at]) for at in range(9)], sems)
-    for unit, first in enumerate((0, 4)):
-        for copy in copies[first : first + 4]:
-            copy.wait()
-        total = sum(parts_ref[first + step].astype(F32) for step in range(4))
-        total_ref[:, :, unit * 128 : unit * 128 + 128] = total.astype(BF16)
-    copies[8].wait()
-    total_ref[:, :, 256:] = parts_ref[8]
-    save, = load([(total_ref, blocks_hbm.at[:, :, pl.ds(0, 384)])], out_sem)
+    downs, ups, out_hbm, blocks_hbm = refs[:4], refs[4:6], refs[6], refs[7]
+    down_ref, up_ref, total_ref, sems, out_sem = refs[8:]
+    copies = load(
+        [(downs[at], down_ref.at[at]) for at in range(4)]
+        + [(ups[at], up_ref.at[at]) for at in range(2)]
+        + [(out_hbm, total_ref.at[:, :, pl.ds(384, 128)])],
+        sems,
+    )
+    for copy in copies[:4]:
+        copy.wait()
+    total = sum(down_ref[step].astype(F32) for step in range(4))
+    total_ref[:, :, :128] = total.astype(BF16)
+    for copy in copies[4:]:
+        copy.wait()
+    total_ref[:, :, 128:384] = (up_ref[0].astype(F32) + up_ref[1].astype(F32)).astype(BF16)
+    save, = load([(total_ref, blocks_hbm.at[:, :, pl.ds(0, 512)])], out_sem)
     save.wait()
 
 
 def share_kernel(landed_hbm, qkv_ref, out_ref, up_ref, down_ref, merge_ref, landed_ref, sems):
     parts = [pl.ds(p * 16, 16) for p in range(4)]
     loads = load([(landed_hbm.at[p], landed_ref.at[p]) for p in parts], sems)
-    down, up, merge = ([0.0] * 4 for _ in range(3))
+    down, up, merge = [0.0] * 4, [0.0] * 2, [0.0] * 4
     shared = 0.0
     for chip in range(64):
         z, y = chip // 16, chip // 2 % 4
@@ -448,17 +462,18 @@
             loads[z].wait()
         block = landed_ref[chip].astype(F32)
         down[z] = down[z] + block[:, :128]
-        up[y] = up[y] + block[:, 128:256]
-        shared = shared + block[:, 256:768]
-        merge[y] = merge[y] + block[:, 768:]
+        up[y % 2] = up[y % 2] + block[:, 128:384]
+        shared = shared + block[:, 384:896]
+        merge[y] = merge[y] + block[:, 896:]
     for block in range(4):
         down_ref[:, block * 128 : block * 128 + 128] = down[block]
         rows = slice(block * 4, block * 4 + 4)
         out_ref[:, block * 128 : block * 128 + 128] = shared[rows, :128]
         qkv_ref[:, block * 384 : block * 384 + 384] = shared[rows, 128:]
+        for half in range(2):
+            at = block * 512 + half * 256
+            up_ref[:, at : at + 256] = up[half][rows]
         for y in range(4):
-            at = block * 512 + y * 128
-            up_ref[:, at : at + 128] = up[y][rows]
             merge_ref[y * 4 : y * 4 + 4, block * 256 : block * 256 + 256] = merge[y][rows]
 
 
@@ -499,18 +514,8 @@
     return lax.ppermute(send, "core", [(0, 1), (1, 0)])
 
 
-def ring_parts(where, keep, arrived, axis, shift, weight):
-    count = keep.shape[0]
-    outs = call(
-        functools.partial(ring_kernel, shift=shift),
-        [where, keep, arrived], 1, [(64, 16, 128)] * count, count,
-        [vmem(*keep.shape), vmem(*keep.shape), dmas(count), dmas(count)], 2, free=(2,), weight=weight,
-    )
-    moved = [
-        lax.ppermute(outs[step], axis, [(i, (i + step) % 4) for i in range(4)])
-        for step in (1, 2, 3)
-    ]
-    return outs, [outs[0], *moved, *outs[4:]]
+def pair_scratch(count):
+    return [vmem(count, 64, 16, 128), vmem(count, 64, 16, 128), dmas(count), dmas(count)]
 
 
 def shifted_block(block, down, right):
@@ -594,9 +599,19 @@
         7,
     )
     down_keep, *near = lax.optimization_barrier((down_keep, *near))
-    down_sums, down_parts = ring_parts(where, down_keep, exchanged(down_send), "z", 3, 60)
-    up_sums, up_parts = ring_parts(where, keep, exchanged(send), "y", 1, 1)
-    middle_grad, *_ = lax.optimization_barrier((middle_grad, down_sums[0], up_sums[0]))
+    down_own, *down_sends = call(
+        ring_kernel, [where, down_keep, exchanged(down_send)], 1, [(64, 16, 128)] * 4, 4,
+        pair_scratch(4), 2, free=(2,), weight=60,
+    )
+    downs = [down_own]
+    for step, block in enumerate(down_sends, 1):
+        downs.append(lax.ppermute(block, "z", [(i, (i + step) % 4) for i in range(4)]))
+    up_own, up_send, out_sum = call(
+        halves_kernel, [where, keep, exchanged(send)], 1,
+        [(64, 16, 256), (64, 16, 256), (64, 16, 128)], 3, pair_scratch(5), 2, free=(2,),
+    )
+    up_arrived = lax.ppermute(up_send, "y", [(i, i ^ 1) for i in range(4)])
+    middle_grad, *_ = lax.optimization_barrier((middle_grad, down_own, up_own))
     *corners, late_keep, late_send = call(
         backward_kernel,
         [where, tokens_in, packed, keys_t, attended, middle_grad, first_t,
@@ -609,12 +624,13 @@
         12, free=range(12, 15),
     )
     blocks, = call(
-        assemble_kernel, [*down_parts, *up_parts], 0, [(64, 16, 1024)], 0,
-        [vmem(9, 64, 16, 128), vmem(64, 16, 384), dmas(9), dmas(1)], 2, free=range(9), weight=60,
+        assemble_kernel, [*downs, up_own, up_arrived, out_sum], 0, [(64, 16, 1152)], 0,
+        [vmem(4, 64, 16, 128), vmem(2, 64, 16, 256), vmem(64, 16, 512), dmas(7), dmas(1)], 2,
+        free=range(7), weight=60,
         loose=True,
     )
     blocks, = call(
-        functools.partial(pair_kernel, place=384),
+        functools.partial(pair_kernel, place=512),
         [late_keep, exchanged(late_send), blocks], 0, [blocks.shape], 0,
         [vmem(64, 16, 640), vmem(64, 16, 640), dmas(4), dmas(4), dmas(4)], 2, free=(1, 2),
         aliases={2: 0}, loose=True,

time: 135 us -> 127 us (0.941)
  starting transfers between devices: 34.5 us -> 31.1 us
  waiting for transfers between devices: 40.5 us -> 37.4 us
  Pallas kernels: 50.5 us -> 49.1 us
    ppermute x6 -> x4, waiting for transfers between devices: 6.1 us -> 0.01 us  [the longest x3 0.01 us: body(): lax.ppermute(block, 'z', [(i, (i + step) % 4) for i in range(4)])]
    ppermute x6 -> x4, starting transfers between devices: 7.67 us -> 4.4 us  [the longest x3 3.86 us: body(): lax.ppermute(block, 'z', [(i, (i + step) % 4) for i in range(4)])]
    ppermute x6, starting transfers between devices: 9.86 us -> 12.9 us  [shifted_block(): return lax.ppermute(block, GRID, route)]
    ppermute x3, starting transfers between devices: 4.29 us -> 1.65 us  [exchanged(): return lax.ppermute(send, 'core', [(0, 1), (1, 0)])]
    all_to_all x1, waiting for transfers between devices: 27.6 us -> 29.6 us  [body(): landed = lax.all_to_all(blocks, PAIRS, 0, 0, tiled=True)]
  transfers between devices with their start and end apart: 19 -> 17, of which waited for: 7 -> 8; matrix products, arithmetic and copies ran while one was open for 2% -> 3% of each run, Pallas kernels for 19% -> 20%
where the time goes in v11:
time: 127 us; the launch traced here: 126 us
  Pallas kernels  49.1 us (39%)
  waiting for transfers between devices  37.4 us (29%)
  starting transfers between devices  31.1 us (24%)
  local copies, waits for them, and re-layouts  4.92 us (4%)
  other arithmetic  2.74 us (2%)
    pallas_call x8, Pallas kernels, call(): pl.pallas_call(kernel, out_shape=[jax.ShapeDtypeStruct(shape, kind) for s...  49.1 us
    all_to_all x1, waiting for transfers between devices, body(): landed = lax.all_to_all(blocks, PAIRS, 0, 0, tiled=True)  29.6 us
    ppermute x6, starting transfers between devices, shifted_block(): return lax.ppermute(block, GRID, route)  12.9 us
    all_to_all x1, starting transfers between devices, body(): landed = lax.all_to_all(blocks, PAIRS, 0, 0, tiled=True)  8.42 us
    ppermute x6, waiting for transfers between devices, shifted_block(): return lax.ppermute(block, GRID, route)  3.97 us
    ppermute x3, starting transfers between devices, body(): lax.ppermute(block, 'z', [(i, (i + step) % 4) for i in range(4)])  3.86 us
    ppermute x3, starting transfers between devices, body(): lax.ppermute(block, 'y', [(i, (i + step) % 4) for i in range(4)])  3.72 us
  transfers between devices with their start and end apart: 17, of which 8 were waited for; matrix products, arithmetic and copies ran while one was open for 3% of the time, Pallas kernels for 20%

profile of v11, /device:TPU:0, one launch (start us, length us, event | category | flops | bytes accessed | tf_op | source)
XLA Modules:
  0.0 126.5 jit_solution(7226256946224108565)
XLA Ops:
  0.6 0.9 fusion.1
  1.6 1.2 fusion
  2.9 5.1 %collective-permute-start = (bf16[108,512]{1,0:T(8,128)(2,1)S(1)}, bf16[108,512]{1,0:T(8,128)(2,1)S(1)}, u32[]{:S(2)}, u32[]{:S(2)}) collective-permute-start(bf16[108,512]{1,0:T(8,128)(2,1)S(1)} %pad_maximum_fusion.1), channel_id=1, source_target_pairs={{0,15},{1,0},{2,1},{3,2},{4,3},{5,4},{6,5},{7,6},{8,7},{9,8},{10,9... | collective-permute-start | bytes 331784 | tf_op jit(solution)/shard_map/ppermute | solution.py:526
  8.0 4.1 %collective-permute-start.1 = (bf16[108,512]{1,0:T(8,128)(2,1)S(1)}, bf16[108,512]{1,0:T(8,128)(2,1)S(1)}, u32[]{:S(2)}, u32[]{:S(2)}) collective-permute-start(bf16[108,512]{1,0:T(8,128)(2,1)S(1)} %pad_maximum_fusion.2), channel_id=1, source_target_pairs={{0,112},{1,113},{2,114},{3,115},{4,116},{5,117},{6,118},{7,119},{8... | collective-permute-start | bytes 331784 | tf_op jit(solution)/shard_map/ppermute | solution.py:526
  12.8 0.7 pad_maximum_fusion.quad0_hbm
  13.5 1.2 collective-permute-done.1.quad2_hbm
  14.7 1.9 %collective-permute-done.2.quad3_hbm = bf16[108,512]{1,0:T(8,128)(2,1)S(1)} collective-permute-done((bf16[108,512]{1,0:T(8,128)(2,1)S(1)}, bf16[108,512]{1,0:T(8,128)(2,1)S(1)}, u32[]{:S(2)}, u32[]{:S(2)}) %collective-permute-start.2) | collective-permute-done | bytes 110624 | tf_op jit(solution)/shard_map/ppermute | solution.py:526
  16.6 0.6 copy-done.10
  17.2 22.4 %shard_map.189 = (bf16[72,1024]{1,0:T(8,128)(2,1)}, bf16[72,1536]{1,0:T(8,128)(2,1)}, bf16[72,1536]{1,0:T(8,128)(2,1)}, bf16[72,1536]{1,0:T(8,128)(2,1)}, bf16[7...) custom-call(s32[1]{0:T(128)} %bitcast.where_ref, ...), custom_call_target="tpu_custom_call" | custom-call | flops 20000000000 | bytes 20000000 | tf_op jit(solution)/shard_map/pallas_call | solution.py:488
  39.8 2.5 %collective-permute-start.4 = (bf16[72,1536]{1,0:T(8,128)(2,1)}, bf16[72,1536]{1,0:T(8,128)(2,1)S(1)}, u32[]{:S(2)}, u32[]{:S(2)}) collective-permute-start(bf16[72,1536]{1,0:T(8,128)(2,1)} %get-tuple-element.66), channel_id=1, source_target_pairs={{0,8},{4,12},{8,0},{12,4},{1,9},{5,13},{9,1},{13,5},{2,10},{6,14},... | collective-permute-start | bytes 663560 | tf_op jit(solution)/shard_map/ppermute | solution.py:592
  42.2 1.2 collective-permute-start.5
  43.4 9.2 %shard_map.190 = (bf16[288,512]{1,0:T(8,128)(2,1)}, bf16[5,64,16,128]{3,2,1,0:T(8,128)(2,1)}, bf16[5,64,16,128]{3,2,1,0:T(8,128)(2,1)}) custom-call(s32[1]{0:T(128)} %bitcast.where_ref, bf16[288,512]{1,0:T(8,128)(2,1)} %get-tuple-element.59.grad_after_ref, bf16[288,512]{1,0:T(8,128)(2,1)} %get-tuple-element.60.middle_ref, ...), custom_call_target="tpu_custom_call" | custom-call | flops 7000000000 | bytes 7000000 | tf_op jit(solution)/shard_map/pallas_call | solution.py:488
  52.7 1.0 collective-permute-done.3.near1_hbm
  53.7 0.6 collective-permute-done.5.near3_hbm
  55.0 3.1 %collective-permute-start.10 = (bf16[64,16,128]{2,1,0:T(8,128)(2,1)S(1)}, bf16[64,16,128]{2,1,0:T(8,128)(2,1)S(1)}, u32[]{:S(2)}, u32[]{:S(2)}) collective-permute-start(bf16[64,16,128]{2,1,0:T(8,128)(2,1)S(1)} %get-tuple-element.85), channel_id=1, source_target_pairs={{0,64},{32,96},{64,0},{96,32},{1,65},{33,97},{65,1},{97,33},{2,66}... | collective-permute-start | bytes 786440 | tf_op jit(solution)/shard_map/ppermute | solution.py:608
  58.1 0.8 collective-permute-start.11
  58.9 0.6 shard_map.192
  59.5 0.5 collective-permute-start.12
  60.0 13.0 %shard_map.193 = (bf16[108,512]{1,0:T(8,128)(2,1)}, bf16[108,512]{1,0:T(8,128)(2,1)}, bf16[108,512]{1,0:T(8,128)(2,1)}, bf16[108,512]{1,0:T(8,128)(2,1)}, bf16[6...) custom-call(s32[1]{0:T(128)} %bitcast.where_ref, bf16[288,512]{1,0:T(8,128)(2,1)} %get-tuple-element.55.tokens_ref, ...), custom_call_target="tpu_custom_call" | custom-call | flops 12000000000 | bytes 12000000 | tf_op jit(solution)/shard_map/pallas_call | solution.py:488
  73.0 1.7 %collective-permute-start.13 = (bf16[108,512]{1,0:T(8,128)(2,1)}, bf16[108,512]{1,0:T(8,128)(2,1)S(1)}, u32[]{:S(2)}, u32[]{:S(2)}) collective-permute-start(bf16[108,512]{1,0:T(8,128)(2,1)} %get-tuple-element.89), channel_id=1, source_target_pairs={{0,17},{1,18},{2,19},{3,20},{4,21},{5,22},{6,23},{7,24},{8,25},{9,... | collective-permute-start | bytes 331784 | tf_op jit(solution)/shard_map/ppermute | solution.py:526
  74.8 1.5 %collective-permute-start.14 = (bf16[108,512]{1,0:T(8,128)(2,1)}, bf16[108,512]{1,0:T(8,128)(2,1)S(1)}, u32[]{:S(2)}, u32[]{:S(2)}) collective-permute-start(bf16[108,512]{1,0:T(8,128)(2,1)} %get-tuple-element.90), channel_id=1, source_target_pairs={{0,16},{1,17},{2,18},{3,19},{4,20},{5,21},{6,22},{7,23},{8,24},{9,... | collective-permute-start | bytes 331784 | tf_op jit(solution)/shard_map/ppermute | solution.py:526
  76.3 1.5 %collective-permute-start.8 = (bf16[64,16,640]{2,1,0:T(8,128)(2,1)}, bf16[64,16,640]{2,1,0:T(8,128)(2,1)S(1)}, u32[]{:S(2)}, u32[]{:S(2)}) collective-permute-start(bf16[64,16,640]{2,1,0:T(8,128)(2,1)} %get-tuple-element.83), channel_id=1, source_target_pairs={{0,1},{1,0},{2,3},{3,2},{4,5},{5,4},{6,7},{7,6},{8,9},{9,8},{10,11... | collective-permute-start | bytes 3932168 | tf_op jit(solution)/shard_map/ppermute | solution.py:514
  77.8 0.6 shard_map.194.refs_0_
  78.4 2.3 %collective-permute-done.8.arrived_hbm = bf16[64,16,640]{2,1,0:T(8,128)(2,1)S(1)} collective-permute-done((bf16[64,16,640]{2,1,0:T(8,128)(2,1)}, bf16[64,16,640]{2,1,0:T(8,128)(2,1)S(1)}, u32[]{:S(2)}, u32[]{:S(2)}) %collective-permute-start.8) | collective-permute-done | bytes 1310752 | tf_op jit(solution)/shard_map/ppermute | solution.py:514
  80.7 1.4 %shard_map.195 = bf16[64,16,1152]{2,1,0:T(8,128)(2,1)S(1)} custom-call(bf16[64,16,640]{2,1,0:T(8,128)(2,1)S(1)} %copy-done.1, bf16[64,16,640]{2,1,0:T(8,128)(2,1)S(1)} %collective-permute-done.8.arrived_hbm, bf16[64,16,1152]{2,1,0:T(8,128)(2,1)S(1)} %shard_map.194.refs_0_), custom_call_target="tpu_custom_call", output_to_operand_aliasing={{}: (2, {})} | custom-call | flops 2000000000 | bytes 2000000 | tf_op jit(solution)/shard_map/pallas_call | solution.py:488
  82.1 1.4 %copy-done = bf16[64,16,1152]{2,1,0:T(8,128)(2,1)} copy-done((bf16[64,16,1152]{2,1,0:T(8,128)(2,1)}, bf16[64,16,1152]{2,1,0:T(8,128)(2,1)S(1)}, u32[]{:S(2)}) %copy-start) | copy-done | bytes 2359320
  83.5 0.6 collective-permute-done.13
  84.3 8.4 %all-to-all-start = ((bf16[64,16,1152]{2,1,0:T(8,128)(2,1)}), bf16[64,16,1152]{2,1,0:T(8,128)(2,1)S(1)}, u32[]{:S(2)}, u32[]{:S(2)}) async-start(bf16[64,16,1152]{2,1,0:T(8,128)(2,1)} %copy-done), calls=%async_computation | async-start | bytes 4718592 | tf_op jit(solution)/shard_map/all_to_all | solution.py:640
  93.2 0.9 maximum_bitcast_fusion.1
  94.1 1.1 maximum_bitcast_fusion
  95.2 29.6 %all-to-all-done.landed_hbm = bf16[64,16,1152]{2,1,0:T(8,128)(2,1)S(1)} async-done(((bf16[64,16,1152]{2,1,0:T(8,128)(2,1)}), bf16[64,16,1152]{2,1,0:T(8,128)(2,1)S(1)}, u32[]{:S(2)}, u32[]{:S(2)}) %all-to-all-start) | async-done | bytes 2359328 | tf_op jit(solution)/shard_map/all_to_all | solution.py:640
  124.8 1.5 %shard_map.196 = (f32[4,1536]{1,0:T(4,128)}, f32[4,512]{1,0:T(4,128)}, f32[4,2048]{1,0:T(4,128)}, f32[16,512]{1,0:T(8,128)}, f32[16,1024]{1,0:T(8,128)}) custom-call(bf16[64,16,1152]{2,1,0:T(8,128)(2,1)S(1)} %all-to-all-done.landed_hbm), custom_call_target="tpu_custom_call" | custom-call | flops 3000000000 | bytes 3000000 | tf_op jit(solution)/shard_map/pallas_call | solution.py:488
  (70 shorter events, 2.3 us)
Async XLA Ops:
  2.9 10.6 %collective-permute-start = (bf16[108,512]{1,0:T(8,128)(2,1)S(1)}, bf16[108,512]{1,0:T(8,128)(2,1)S(1)}, u32[]{:S(2)}, u32[]{:S(2)}) collective-permute-start(bf16[108,512]{1,0:T(8,128)(2,1)S(1)} %pad_maximum_fusion.1), channel_id=1, source_target_pairs={{0,15},{1,0},{2,1},{3,2},{4,3},{5,4},{6,5},{7,6},{8,7},{9,8},{10,9... | collective-permute-start | bytes 331784 | tf_op jit(solution)/shard_map/ppermute | solution.py:526
  8.0 6.6 %collective-permute-start.1 = (bf16[108,512]{1,0:T(8,128)(2,1)S(1)}, bf16[108,512]{1,0:T(8,128)(2,1)S(1)}, u32[]{:S(2)}, u32[]{:S(2)}) collective-permute-start(bf16[108,512]{1,0:T(8,128)(2,1)S(1)} %pad_maximum_fusion.2), channel_id=1, source_target_pairs={{0,112},{1,113},{2,114},{3,115},{4,116},{5,117},{6,118},{7,119},{8... | collective-permute-start | bytes 331784 | tf_op jit(solution)/shard_map/ppermute | solution.py:526
  12.3 4.3 %collective-permute-start.2 = (bf16[108,512]{1,0:T(8,128)(2,1)S(1)}, bf16[108,512]{1,0:T(8,128)(2,1)S(1)}, u32[]{:S(2)}, u32[]{:S(2)}) collective-permute-start(bf16[108,512]{1,0:T(8,128)(2,1)S(1)} %pad_maximum_fusion.3), channel_id=1, source_target_pairs={{0,127},{1,112},{2,113},{3,114},{4,115},{5,116},{6,117},{7,118},{8... | collective-permute-start | bytes 331784 | tf_op jit(solution)/shard_map/ppermute | solution.py:526
  13.5 3.1 %copy-start.8 = (bf16[108,512]{1,0:T(8,128)(2,1)}, bf16[108,512]{1,0:T(8,128)(2,1)S(1)}, u32[]{:S(2)}) copy-start(bf16[108,512]{1,0:T(8,128)(2,1)S(1)} %collective-permute-done.quad1_hbm) | copy-start | bytes 331780
  14.7 1.9 %copy-start.9 = (bf16[108,512]{1,0:T(8,128)(2,1)}, bf16[108,512]{1,0:T(8,128)(2,1)S(1)}, u32[]{:S(2)}) copy-start(bf16[108,512]{1,0:T(8,128)(2,1)S(1)} %collective-permute-done.1.quad2_hbm) | copy-start | bytes 331780
  16.6 0.6 copy-start.10
  39.6 14.7 %collective-permute-start.6 = (bf16[4,64,16,128]{3,2,1,0:T(8,128)(2,1)}, bf16[4,64,16,128]{3,2,1,0:T(8,128)(2,1)S(1)}, u32[]{:S(2)}, u32[]{:S(2)}) collective-permute-start(bf16[4,64,16,128]{3,2,1,0:T(8,128)(2,1)} %get-tuple-element.69), channel_id=1, source_target_pairs={{0,1},{1,0},{2,3},{3,2},{4,5},{5,4},{6,7},{7,6},{8,9},{9,8},{10,11... | collective-permute-start | bytes 3145736 | tf_op jit(solution)/shard_map/ppermute | solution.py:514
  39.7 14.0 %collective-permute-start.3 = (bf16[72,1536]{1,0:T(8,128)(2,1)}, bf16[72,1536]{1,0:T(8,128)(2,1)S(1)}, u32[]{:S(2)}, u32[]{:S(2)}) collective-permute-start(bf16[72,1536]{1,0:T(8,128)(2,1)} %get-tuple-element.65), channel_id=1, source_target_pairs={{0,4},{4,8},{8,12},{12,0},{1,5},{5,9},{9,13},{13,1},{2,6},{6,10},{... | collective-permute-start | bytes 663560 | tf_op jit(solution)/shard_map/ppermute | solution.py:592
  39.8 13.9 %collective-permute-start.4 = (bf16[72,1536]{1,0:T(8,128)(2,1)}, bf16[72,1536]{1,0:T(8,128)(2,1)S(1)}, u32[]{:S(2)}, u32[]{:S(2)}) collective-permute-start(bf16[72,1536]{1,0:T(8,128)(2,1)} %get-tuple-element.66), channel_id=1, source_target_pairs={{0,8},{4,12},{8,0},{12,4},{1,9},{5,13},{9,1},{13,5},{2,10},{6,14},... | collective-permute-start | bytes 663560 | tf_op jit(solution)/shard_map/ppermute | solution.py:592
  42.2 12.1 %collective-permute-start.5 = (bf16[72,1536]{1,0:T(8,128)(2,1)}, bf16[72,1536]{1,0:T(8,128)(2,1)S(1)}, u32[]{:S(2)}, u32[]{:S(2)}) collective-permute-start(bf16[72,1536]{1,0:T(8,128)(2,1)} %get-tuple-element.67), channel_id=1, source_target_pairs={{0,12},{4,0},{8,4},{12,8},{1,13},{5,1},{9,5},{13,9},{2,14},{6,2},{... | collective-permute-start | bytes 663560 | tf_op jit(solution)/shard_map/ppermute | solution.py:592
  43.4 10.9 %copy-start.3 = (bf16[4,64,16,128]{3,2,1,0:T(8,128)(2,1)S(1)}, bf16[4,64,16,128]{3,2,1,0:T(8,128)(2,1)}, u32[]{:S(2)}) copy-start(bf16[4,64,16,128]{3,2,1,0:T(8,128)(2,1)} %get-tuple-element.68.keep_hbm) | copy-start | bytes 3145732
  52.6 6.2 %collective-permute-start.7 = (bf16[5,64,16,128]{3,2,1,0:T(8,128)(2,1)}, bf16[5,64,16,128]{3,2,1,0:T(8,128)(2,1)S(1)}, u32[]{:S(2)}, u32[]{:S(2)}) collective-permute-start(bf16[5,64,16,128]{3,2,1,0:T(8,128)(2,1)} %get-tuple-element.72), channel_id=1, source_target_pairs={{0,1},{1,0},{2,3},{3,2},{4,5},{5,4},{6,7},{7,6},{8,9},{9,8},{10,11... | collective-permute-start | bytes 3932168 | tf_op jit(solution)/shard_map/ppermute | solution.py:514
  53.7 1.1 copy-start.5
  53.7 1.1 copy-start.6
  54.3 0.7 copy-start.7
  54.3 4.6 %copy-start.2 = (bf16[5,64,16,128]{3,2,1,0:T(8,128)(2,1)S(1)}, bf16[5,64,16,128]{3,2,1,0:T(8,128)(2,1)}, u32[]{:S(2)}) copy-start(bf16[5,64,16,128]{3,2,1,0:T(8,128)(2,1)} %get-tuple-element.71.keep_hbm) | copy-start | bytes 3932164
  55.0 19.8 %collective-permute-start.9 = (bf16[64,16,128]{2,1,0:T(8,128)(2,1)S(1)}, bf16[64,16,128]{2,1,0:T(8,128)(2,1)S(1)}, u32[]{:S(2)}, u32[]{:S(2)}) collective-permute-start(bf16[64,16,128]{2,1,0:T(8,128)(2,1)S(1)} %get-tuple-element.84), channel_id=1, source_target_pairs={{0,32},{32,64},{64,96},{96,0},{1,33},{33,65},{65,97},{97,1},{2,34}... | collective-permute-start | bytes 786440 | tf_op jit(solution)/shard_map/ppermute | solution.py:608
  55.0 21.3 %collective-permute-start.10 = (bf16[64,16,128]{2,1,0:T(8,128)(2,1)S(1)}, bf16[64,16,128]{2,1,0:T(8,128)(2,1)S(1)}, u32[]{:S(2)}, u32[]{:S(2)}) collective-permute-start(bf16[64,16,128]{2,1,0:T(8,128)(2,1)S(1)} %get-tuple-element.85), channel_id=1, source_target_pairs={{0,64},{32,96},{64,0},{96,32},{1,65},{33,97},{65,1},{97,33},{2,66}... | collective-permute-start | bytes 786440 | tf_op jit(solution)/shard_map/ppermute | solution.py:608
  58.1 18.2 %collective-permute-start.11 = (bf16[64,16,128]{2,1,0:T(8,128)(2,1)S(1)}, bf16[64,16,128]{2,1,0:T(8,128)(2,1)S(1)}, u32[]{:S(2)}, u32[]{:S(2)}) collective-permute-start(bf16[64,16,128]{2,1,0:T(8,128)(2,1)S(1)} %get-tuple-element.86), channel_id=1, source_target_pairs={{0,96},{32,0},{64,32},{96,64},{1,97},{33,1},{65,33},{97,65},{2,98}... | collective-permute-start | bytes 786440 | tf_op jit(solution)/shard_map/ppermute | solution.py:608
  59.5 18.3 %collective-permute-start.12 = (bf16[64,16,256]{2,1,0:T(8,128)(2,1)S(1)}, bf16[64,16,256]{2,1,0:T(8,128)(2,1)S(1)}, u32[]{:S(2)}, u32[]{:S(2)}) collective-permute-start(bf16[64,16,256]{2,1,0:T(8,128)(2,1)S(1)} %get-tuple-element.87), channel_id=1, source_target_pairs={{0,4},{4,0},{8,12},{12,8},{1,5},{5,1},{9,13},{13,9},{2,6},{6,2},{1... | collective-permute-start | bytes 1572872 | tf_op jit(solution)/shard_map/ppermute | solution.py:613
  73.0 11.0 %collective-permute-start.13 = (bf16[108,512]{1,0:T(8,128)(2,1)}, bf16[108,512]{1,0:T(8,128)(2,1)S(1)}, u32[]{:S(2)}, u32[]{:S(2)}) collective-permute-start(bf16[108,512]{1,0:T(8,128)(2,1)} %get-tuple-element.89), channel_id=1, source_target_pairs={{0,17},{1,18},{2,19},{3,20},{4,21},{5,22},{6,23},{7,24},{8,25},{9,... | collective-permute-start | bytes 331784 | tf_op jit(solution)/shard_map/ppermute | solution.py:526
  74.8 9.3 %collective-permute-start.14 = (bf16[108,512]{1,0:T(8,128)(2,1)}, bf16[108,512]{1,0:T(8,128)(2,1)S(1)}, u32[]{:S(2)}, u32[]{:S(2)}) collective-permute-start(bf16[108,512]{1,0:T(8,128)(2,1)} %get-tuple-element.90), channel_id=1, source_target_pairs={{0,16},{1,17},{2,18},{3,19},{4,20},{5,21},{6,22},{7,23},{8,24},{9,... | collective-permute-start | bytes 331784 | tf_op jit(solution)/shard_map/ppermute | solution.py:526
  76.3 8.0 %collective-permute-start.15 = (bf16[108,512]{1,0:T(8,128)(2,1)}, bf16[108,512]{1,0:T(8,128)(2,1)S(1)}, u32[]{:S(2)}, u32[]{:S(2)}) collective-permute-start(bf16[108,512]{1,0:T(8,128)(2,1)} %get-tuple-element.91), channel_id=1, source_target_pairs={{0,1},{1,2},{2,3},{3,4},{4,5},{5,6},{6,7},{7,8},{8,9},{9,10},{10,1... | collective-permute-start | bytes 331784 | tf_op jit(solution)/shard_map/ppermute | solution.py:526
  76.3 4.4 %collective-permute-start.8 = (bf16[64,16,640]{2,1,0:T(8,128)(2,1)}, bf16[64,16,640]{2,1,0:T(8,128)(2,1)S(1)}, u32[]{:S(2)}, u32[]{:S(2)}) collective-permute-start(bf16[64,16,640]{2,1,0:T(8,128)(2,1)} %get-tuple-element.83), channel_id=1, source_target_pairs={{0,1},{1,0},{2,3},{3,2},{4,5},{5,4},{6,7},{7,6},{8,9},{9,8},{10,11... | collective-permute-start | bytes 3932168 | tf_op jit(solution)/shard_map/ppermute | solution.py:514
  77.8 2.9 %copy-start.1 = (bf16[64,16,640]{2,1,0:T(8,128)(2,1)S(1)}, bf16[64,16,640]{2,1,0:T(8,128)(2,1)}, u32[]{:S(2)}) copy-start(bf16[64,16,640]{2,1,0:T(8,128)(2,1)} %get-tuple-element.82.keep_hbm) | copy-start | bytes 3932164
  82.1 1.4 %copy-start = (bf16[64,16,1152]{2,1,0:T(8,128)(2,1)}, bf16[64,16,1152]{2,1,0:T(8,128)(2,1)S(1)}, u32[]{:S(2)}) copy-start(bf16[64,16,1152]{2,1,0:T(8,128)(2,1)S(1)} %shard_map.195) | copy-start | bytes 7077892
  84.3 8.7 %copy-start.4 = (bf16[108,512]{1,0:T(8,128)(2,1)S(1)}, bf16[108,512]{1,0:T(8,128)(2,1)}, u32[]{:S(2)}) copy-start(bf16[108,512]{1,0:T(8,128)(2,1)} %get-tuple-element.96) | copy-start | bytes 331780
  84.3 40.5 %all-to-all-start = ((bf16[64,16,1152]{2,1,0:T(8,128)(2,1)}), bf16[64,16,1152]{2,1,0:T(8,128)(2,1)S(1)}, u32[]{:S(2)}, u32[]{:S(2)}) async-start(bf16[64,16,1152]{2,1,0:T(8,128)(2,1)} %copy-done), calls=%async_computation | async-start | bytes 4718592 | tf_op jit(solution)/shard_map/all_to_all | solution.py:640

commit v12 on v11

--- a/solution.py
+++ b/solution.py
@@ -12,6 +12,7 @@
 WIN = 12
 TOKENS = 2 * WIN * WIN
 MERGED = TOKENS // 4
+MAIN = 256
 EPS = 1e-05
 LOG2E = 1.4426950408889634
 QUERY_SCALE = HEAD ** (-0.5) * LOG2E
@@ -81,6 +82,28 @@
     return jnp.swapaxes(values.astype(F32), 0, 1).astype(BF16)
 
 
+def own_block(shape):
+    rows = lax.broadcasted_iota(jnp.int32, shape, 0) >> 5
+    return rows == lax.broadcasted_iota(jnp.int32, shape, 1) >> 5
+
+
+def spread_rest(values):
+    wide = jnp.concatenate([values] * 4, axis=1)
+    return jnp.where(own_block(wide.shape), wide, 0.0).astype(BF16)
+
+
+def gather_rest(blocks):
+    kept = jnp.where(own_block(blocks.shape), blocks, 0.0)
+    kept = kept + pltpu.roll(kept, 64, 1)
+    kept = kept + pltpu.roll(kept, 32, 1)
+    return kept[:, :HEAD]
+
+
+def stack_rest(values):
+    tall = jnp.concatenate([values[MAIN:]] * 4, axis=0)
+    return jnp.where(own_block(tall.shape), tall, jnp.zeros_like(tall))
+
+
 def weave(grads, slots, cols):
     tiles = [grad.reshape(64, 8, grad.shape[-1]) for grad in grads]
     turned = [pltpu.roll(tile, 4, 1) for tile in tiles]
@@ -128,12 +151,19 @@
 
 def forward_kernel(
     where_ref, order_ref, cot_order_ref, ids_ref, places_ref, cols_t_ref,
-    quad0_hbm, quad1_hbm, quad2_hbm, quad3_hbm, w_qkv_hbm, w_out_hbm, w_up_hbm, w_down_hbm, w_merge_hbm,
-    level_two_ref, near0, near1, near2, near3, tokens_ref, packed_ref, keys_t_ref,
-    attended_ref, first_t_ref, middle_ref, grad_after_ref, probs_hbm, slope_hbm, keep_hbm, send_hbm,
-    quads_ref, bias_ref, query_t, values_t, slope_ref, hidden_ref, probs_ref, w_qkv, w_out, w_up, w_down,
-    w_merge, slots, quad_sems, in_sems, out_sems,
+    quad0_hbm, quad1_hbm, quad2_hbm, quad3_hbm, w_qkv_hbm, w_out_hbm, w_up_hbm, w_down_hbm,
+    w_merge_hbm,
+    level_two_ref, grad_after_ref, near0, near1, near2, near3, tokens_hbm, packed_hbm, keys_t_hbm,
+    attended_hbm, first_t_hbm, middle_hbm, probs_hbm, rest_hbm, slope_hbm, keep_hbm, send_hbm,
+    quads_ref, bias_ref, bias_rest, query_t, query_rest, values_t, slope_ref, hidden_ref,
+    probs_ref, rest_ref, w_qkv, w_out, w_up, w_down, w_merge, slots, near_ref, tokens_ref,
+    packed_ref, keys_t_ref, attended_ref, first_t_ref, middle_ref, quad_sems, in_sems, out_sems,
 ):
+    saves = []
+
+    def save(*pairs):
+        saves.extend(load(pairs, out_sems.at[pl.ds(len(saves), len(pairs))]))
+
     quads = (quad0_hbm, quad1_hbm, quad2_hbm, quad3_hbm)
     quads = load([(quads[q], quads_ref.at[q]) for q in range(4)], quad_sems)
     weights = load(
@@ -145,8 +175,11 @@
     ids = ids_ref[...].astype(F32).astype(BF16)
     by_row = dot(places_ref[0], ids) * places_ref[1].astype(F32)
     by_col = dot(ids, places_ref[0], 0, 1) * cols_t_ref[...]
-    alike = jnp.sum(by_row, axis=1, keepdims=True) == jnp.sum(by_col, axis=0, keepdims=True)
-    bias_ref[...] = jnp.where(alike, 0.0, -1e30)
+    by_row = jnp.sum(by_row, axis=1, keepdims=True)
+    by_col = jnp.sum(by_col, axis=0, keepdims=True)
+    rest = jnp.concatenate([by_col[:, MAIN:]] * 4, axis=1)
+    bias_ref[...] = jnp.where(by_row == by_col[:, :MAIN], 0.0, -1e30)
+    bias_rest[...] = jnp.where(by_row == rest, 0.0, -1e30)
     for quad in quads:
         quad.wait()
     tokens = sum(dot(order_ref[q], quads_ref[q]) for q in range(4))
@@ -156,41 +189,57 @@
     normed_in = normalize(tokens)[0]
     first_norm = normed_in.astype(BF16)
     first_t_ref[...] = turned(normed_in)
+    save((tokens_ref, tokens_hbm), (first_t_ref, first_t_hbm))
     weights[0].wait()
     for part in range(3):
         wide = dot(first_norm, w_qkv[:, part * 512 : part * 512 + 512])
         wide = wide * QUERY_SCALE if part == 0 else wide
         for group in range(4):
             packed_ref[part * 4 + group] = wide[:, group * 128 : group * 128 + 128].astype(BF16)
-        by_feature = turned(wide)
+        by_feature = jnp.swapaxes(wide, 0, 1)
         if part:
-            (keys_t_ref, values_t)[part - 1][...] = by_feature
+            (keys_t_ref, values_t)[part - 1][...] = by_feature.astype(BF16)
             continue
         for head in range(16):
             rows = slice(head % 4 * HEAD, head % 4 * HEAD + HEAD)
-            query_t[head, rows, :] = by_feature[head * HEAD : head * HEAD + HEAD]
-
-    def scores_of(head):
-        return dot(packed_ref[4 + head // 4], query_t[head])
+            own = by_feature[head * HEAD : head * HEAD + HEAD, :MAIN]
+            query_t[head, rows, :] = own.astype(BF16)
+        for group in range(4):
+            rest = by_feature[group * 128 : group * 128 + 128, MAIN:]
+            query_rest[group] = spread_rest(rest)
+    save((packed_ref, packed_hbm), (keys_t_ref, keys_t_hbm))
+
+    def scores_of(at):
+        group, head = at // 5, at % 5
+        turn = query_rest[group] if head == 4 else query_t[group * 4 + head]
+        return dot(packed_ref[4 + group], turn)
 
     ahead = scores_of(0)
-    for head in range(16):
-        scores = ahead + bias_ref[...]
-        if head < 15:
-            ahead = scores_of(head + 1)
+    for at in range(20):
+        group, head = at // 5, at % 5
+        scores = ahead + (bias_rest if head == 4 else bias_ref)[...]
+        if at < 19:
+            ahead = scores_of(at + 1)
         raised = jnp.exp2(scores - jnp.max(scores, axis=0, keepdims=True))
         inverse = 1.0 / jnp.sum(raised, axis=0, keepdims=True)
         probs = (raised * inverse).astype(BF16)
-        probs_ref[head] = probs
-        at = slice(head * HEAD, head * HEAD + HEAD)
-        attended_ref[at, :] = dot(values_t[at, :], probs).astype(BF16)
-    saves = load([(probs_ref, probs_hbm)], out_sems.at[pl.ds(0, 1)])
+        if head == 4:
+            rest_ref[group] = probs
+            rows = slice(group * 128, group * 128 + 128)
+            rest = gather_rest(dot(values_t[rows, :], probs))
+            attended_ref[rows, MAIN:] = rest.astype(BF16)
+        else:
+            probs_ref[group * 4 + head] = probs
+            rows = slice(group * 128 + head * HEAD, group * 128 + head * HEAD + HEAD)
+            attended_ref[rows, :MAIN] = dot(values_t[rows, :], probs).astype(BF16)
+    save((probs_ref, probs_hbm), (rest_ref, rest_hbm), (attended_ref, attended_hbm))
 
     attended = turned(attended_ref[...])
     weights[1].wait()
     attn_out = dot(attended, w_out[...]).astype(BF16)
     narrow_middle = (tokens + attn_out.astype(F32)).astype(BF16)
     middle_ref[...] = narrow_middle
+    save((middle_ref, middle_hbm))
     middle = narrow_middle.astype(F32)
     second_norm = normalize(middle)[0].astype(BF16)
     mlp = jnp.zeros((TOKENS, 512), F32)
@@ -207,7 +256,7 @@
         hidden_ref[:, cols] = hidden
         slope_ref[:, cols] = (cumulative + before * density * 0.3989422804014327).astype(BF16)
         mlp = mlp + dot(hidden, w_down[cols])
-    saves += load([(slope_ref, slope_hbm)], out_sems.at[pl.ds(1, 1)])
+    save((slope_ref, slope_hbm))
     after_mlp = (middle + mlp).astype(BF16)
     pieces, inverse_out = merge_norm(after_mlp.astype(F32))
     merged_norm = [v.astype(BF16) for v in pieces]
@@ -222,8 +271,9 @@
         block = blocks[step]
         for own in range(1, 4):
             block = jnp.where(y == own, blocks[(own + step) % 4], block)
-        near[:, :512] = block
-        near[:, 512:] = cotangent
+        near_ref[step, :, :512] = block
+        near_ref[step, :, 512:] = cotangent
+        save((near_ref.at[step], near))
 
     weights[4].wait()
     level_two_ref[...] = sum(
@@ -247,11 +297,9 @@
                 slots[parity, unit, part * 16 : part * 16 + 16] = grad[
                     :, parity, :, unit * 128 : unit * 128 + 128
                 ]
-    saves += load(
-        [(slots.at[core], keep_hbm), (slots.at[1 - core], send_hbm)], out_sems.at[pl.ds(2, 2)]
-    )
-    for save in saves:
-        save.wait()
+    save((slots.at[core], keep_hbm), (slots.at[1 - core], send_hbm))
+    for copy in saves:
+        copy.wait()
 
 
 def middle_kernel(
@@ -259,7 +307,13 @@
     middle_grad_ref, keep_hbm, send_hbm,
     w_down, slope_ref, w_up, slots, sems, out_sems,
 ):
-    loads = load([(w_down_hbm, w_down), (slope_hbm, slope_ref), (w_up_hbm, w_up)], sems)
+    loads = []
+    for part in range(4):
+        cols = pl.ds(part * 512, 512)
+        pairs = [(w_down_hbm.at[cols], w_down.at[cols])]
+        pairs += [(slope_hbm.at[:, cols], slope_ref.at[part])]
+        pairs += [(w_up_hbm.at[:, cols], w_up.at[part])]
+        loads.append(load(pairs, sems.at[pl.ds(part * 3, 3)]))
     core = where_ref[0] & 1
     grad_after = grad_after_ref[...]
     normed_mid, inverse_mid = normalize(middle_ref[...].astype(F32))
@@ -274,15 +328,15 @@
 
     back_up = jnp.zeros((TOKENS, 512), F32)
     grads_up = []
-    for copy in loads:
-        copy.wait()
     for part in range(4):
         cols = slice(part * 512, part * 512 + 512)
+        for copy in loads[part]:
+            copy.wait()
         grad_before = (
-            dot(grad_after, w_down[cols], 1, 1) * slope_ref[:, cols].astype(F32)
+            dot(grad_after, w_down[cols], 1, 1) * slope_ref[part].astype(F32)
         ).astype(BF16)
         grads_up.append(dot(second_t, grad_before))
-        back_up = back_up + dot(grad_before, w_up[:, cols], 1, 1)
+        back_up = back_up + dot(grad_before, w_up[part], 1, 1)
     for unit in range(4):
         cols = slice(unit * 128, unit * 128 + 128)
         weave([grad[:, cols] for grad in grads_up], slots.at[:, unit], slice(0, 128))
@@ -300,16 +354,20 @@
 
 
 def backward_kernel(
-    where_ref, tokens_ref, packed_ref, keys_t_ref, attended_ref, middle_grad_ref,
-    first_t_ref, order_ref, level_order_ref, level_two_ref, w_out,
-    near0_hbm, near1_hbm, near2_hbm, near3_hbm, probs_hbm, w_qkv_hbm,
+    where_ref, middle_grad_ref, attended_ref, w_out,
+    near0_hbm, near1_hbm, near2_hbm, near3_hbm, packed_hbm, keys_t_hbm, probs_hbm, rest_hbm,
+    w_qkv_hbm, first_t_hbm, tokens_hbm, order_hbm, level_order_hbm, level_two_hbm,
     out0, out1, out2, out3, keep_hbm, send_hbm,
-    grad_heads, grad_heads_t, products, query_grad_t, packed_grad, probs_ref, w_qkv, near_ref,
-    slots, near_sems, sems, out_sems,
+    grad_heads, grad_heads_t, grad_heads_rest, products, query_grad_t, packed_grad, probs_ref,
+    near_ref, packed_ref, keys_t_ref, rest_ref, w_qkv, first_t_ref, tokens_ref, order_ref,
+    level_order_ref, level_two_ref, slots, near_sems, sems, out_sems,
 ):
     loads = load(
-        [(probs_hbm.at[pl.ds(g * 4, 4)], probs_ref.at[pl.ds(g * 4, 4)]) for g in range(4)]
-        + [(w_qkv_hbm, w_qkv)],
+        [(packed_hbm, packed_ref), (keys_t_hbm, keys_t_ref), (rest_hbm, rest_ref)]
+        + [(probs_hbm.at[pl.ds(g * 4, 4)], probs_ref.at[pl.ds(g * 4, 4)]) for g in range(4)]
+        + [(w_qkv_hbm, w_qkv), (first_t_hbm, first_t_ref), (tokens_hbm, tokens_ref),
+           (order_hbm, order_ref), (level_order_hbm, level_order_ref),
+           (level_two_hbm, level_two_ref)],
         sems,
     )
     nears = (near0_hbm, near1_hbm, near2_hbm, near3_hbm)
@@ -324,28 +382,44 @@
     grad_heads_t[...] = jnp.zeros_like(grad_heads_t)
     for head in range(16):
         rows = slice(head % 4 * HEAD, head % 4 * HEAD + HEAD)
-        grad_heads_t[head, rows, :] = upstream_t[head * HEAD : head * HEAD + HEAD]
+        grad_heads_t[head, rows, :] = upstream_t[head * HEAD : head * HEAD + HEAD, :MAIN]
+    for group in range(4):
+        rest = upstream_t[group * 128 : group * 128 + 128].astype(F32)
+        grad_heads_rest[group] = spread_rest(rest[:, MAIN:])
 
     head_of_lane = lax.broadcasted_iota(jnp.int32, (TOKENS, 128), 1) >> 5
-
+    for copy in loads[:3]:
+        copy.wait()
     for group in range(4):
-        loads[group].wait()
+        loads[3 + group].wait()
+        rows = slice(group * 128, group * 128 + 128)
         queries = packed_ref[group]
         values = packed_ref[8 + group]
         upstream = grad_heads[group]
         grad_keys = jnp.zeros((TOKENS, 128), F32)
         grad_values = jnp.zeros((TOKENS, 128), F32)
+        totals = []
         for part in range(4):
             head = group * 4 + part
             at = slice(head * HEAD, head * HEAD + HEAD)
             weights = probs_ref[head]
             total = jnp.sum(products[at, :], axis=0, keepdims=True)
+            totals.append(total[:, MAIN:])
             grad_weights = dot(values, grad_heads_t[head])
-            scores = (weights.astype(F32) * (grad_weights - total)).astype(BF16)
+            scores = (weights.astype(F32) * (grad_weights - total[:, :MAIN])).astype(BF16)
             in_head = head_of_lane == part
-            grad_keys = jnp.where(in_head, dot(scores, queries), grad_keys)
-            grad_values = jnp.where(in_head, dot(weights, upstream), grad_values)
-            query_grad_t[at, :] = (dot(keys_t_ref[at, :], scores) * HEAD ** (-0.5)).astype(BF16)
+            grad_keys = jnp.where(in_head, dot(scores, queries[:MAIN]), grad_keys)
+            grad_values = jnp.where(in_head, dot(weights, upstream[:MAIN]), grad_values)
+            query_grad = dot(keys_t_ref[at, :], scores) * HEAD ** (-0.5)
+            query_grad_t[at, :MAIN] = query_grad.astype(BF16)
+        weights = rest_ref[group]
+        total = jnp.concatenate(totals, axis=1)
+        grad_weights = dot(values, grad_heads_rest[group])
+        scores = (weights.astype(F32) * (grad_weights - total)).astype(BF16)
+        grad_keys = grad_keys + dot(scores, stack_rest(queries))
+        grad_values = grad_values + dot(weights, stack_rest(upstream))
+        query_grad = gather_rest(dot(keys_t_ref[rows, :], scores)) * HEAD ** (-0.5)
+        query_grad_t[rows, MAIN:] = query_grad.astype(BF16)
         packed_grad[4 + group] = (grad_keys * (1 / LOG2E)).astype(BF16)
         packed_grad[8 + group] = grad_values.astype(BF16)
 
@@ -357,8 +431,9 @@
 
     for group in range(4):
         packed_grad[group] = turned(query_grad_t[group * 128 : group * 128 + 128, :])
+    for copy in loads[7:]:
+        copy.wait()
     first_t = first_t_ref[...]
-    loads[4].wait()
     back_qkv = jnp.zeros((TOKENS, 512), F32)
     grads = []
     for part in range(3):
@@ -567,24 +642,28 @@
     order, cot_order = token_order(), cotangent_order()
     level_order = np.concatenate([cot_order[:, :MERGED], cot_order[:, MERGED:]]).transpose(0, 2, 1)
     by_feature, field, hidden_shape = (512, TOKENS), (TOKENS, 512), (TOKENS, 2048)
-    all_probs, near_shape, corner = (16, TOKENS, TOKENS), (MERGED, 1536), (PACKED, 512)
+    near_shape, corner = (MERGED, 1536), (PACKED, 512)
     places = window_places()
     where = lax.axis_index(("z", "y", "core")).reshape(1)
     quads = roll_back(tokens, cotangent)
 
-    (level_two, near0, near1, near2, near3, tokens_in, packed, keys_t, attended, first_t,
-     middle, grad_after, probs, slope, down_keep, down_send) = call(
+    probs_shape, rest_shape = (16, TOKENS, MAIN), (4, TOKENS, 128)
+    packed_shape, down_shape = (12, TOKENS, 128), (4, 64, 16, 128)
+    (level_two, grad_after, near0, near1, near2, near3, tokens_in, packed, keys_t, attended,
+     first_t, middle, probs, rest, slope, down_keep, down_send) = call(
         forward_kernel,
         [where, jnp.asarray(order, BF16), jnp.asarray(cot_order, BF16), window_ids,
          jnp.asarray(places, BF16), jnp.asarray(places[1].T, F32), *quads, w_qkv,
          w_out, w_up, w_down, w_merge], 6,
-        [(MERGED, 1024)] + [near_shape] * 4 + [field, (12, TOKENS, 128), by_feature, by_feature,
-         by_feature, field, field, all_probs, hidden_shape, (4, 64, 16, 128), (4, 64, 16, 128)],
-        12,
-        [vmem(4, *corner), pltpu.VMEM((TOKENS, TOKENS), F32), vmem(16, 128, TOKENS), vmem(*by_feature),
-         vmem(*hidden_shape), vmem(*hidden_shape), vmem(*all_probs), vmem(*w_qkv.shape), vmem(*w_out.shape),
-         vmem(*w_up.shape), vmem(*w_down.shape), vmem(*w_merge.shape), vmem(2, 4, 64, 16, 128),
-         dmas(4), dmas(5), dmas(4)],
+        [(MERGED, 1024), field] + [near_shape] * 4 + [field, packed_shape, by_feature, by_feature,
+         by_feature, field, probs_shape, rest_shape, hidden_shape, down_shape, down_shape], 2,
+        [vmem(4, *corner), pltpu.VMEM((TOKENS, MAIN), F32), pltpu.VMEM((TOKENS, 128), F32),
+         vmem(16, 128, MAIN), vmem(4, 128, 128), vmem(*by_feature), vmem(*hidden_shape),
+         vmem(*hidden_shape), vmem(*probs_shape), vmem(*rest_shape), vmem(*w_qkv.shape),
+         vmem(*w_out.shape), vmem(*w_up.shape), vmem(*w_down.shape), vmem(*w_merge.shape),
+         vmem(2, *down_shape), vmem(4, *near_shape), vmem(*field), vmem(*packed_shape),
+         vmem(*by_feature), vmem(*by_feature), vmem(*by_feature), vmem(*field),
+         dmas(4), dmas(5), dmas(15)],
         20, free=range(6, 10),
     )
     near = [near0]
@@ -594,8 +673,8 @@
         middle_kernel,
         [where, grad_after, middle, attended, w_down, slope, w_up], 4,
         [field, (5, 64, 16, 128), (5, 64, 16, 128)], 1,
-        [vmem(*w_down.shape), vmem(*hidden_shape), vmem(*w_up.shape), vmem(2, 5, 64, 16, 128),
-         dmas(3), dmas(4)],
+        [vmem(*w_down.shape), vmem(4, TOKENS, 512), vmem(4, 512, 512), vmem(2, 5, 64, 16, 128),
+         dmas(12), dmas(4)],
         7,
     )
     down_keep, *near = lax.optimization_barrier((down_keep, *near))
@@ -614,14 +693,17 @@
     middle_grad, *_ = lax.optimization_barrier((middle_grad, down_own, up_own))
     *corners, late_keep, late_send = call(
         backward_kernel,
-        [where, tokens_in, packed, keys_t, attended, middle_grad, first_t,
-         jnp.asarray(order.transpose(0, 2, 1), BF16), jnp.asarray(level_order, BF16), level_two,
-         w_out, *near, probs, w_qkv], 11,
+        [where, middle_grad, attended, w_out, *near, packed, keys_t, probs, rest, w_qkv, first_t,
+         tokens_in, jnp.asarray(order.transpose(0, 2, 1), BF16), jnp.asarray(level_order, BF16),
+         level_two], 4,
         [corner] * 4 + [(64, 16, 640)] * 2, 4,
-        [vmem(4, TOKENS, 128), vmem(16, 128, TOKENS), pltpu.VMEM(by_feature, F32), vmem(*by_feature),
-         vmem(12, TOKENS, 128), vmem(*all_probs), vmem(*w_qkv.shape), vmem(4, *near_shape),
-         vmem(2, 64, 16, 640), dmas(4), dmas(5), dmas(2)],
-        12, free=range(12, 15),
+        [vmem(4, TOKENS, 128), vmem(16, 128, MAIN), vmem(4, 128, 128),
+         pltpu.VMEM(by_feature, F32), vmem(*by_feature), vmem(*packed_shape), vmem(*probs_shape),
+         vmem(4, *near_shape), vmem(*packed_shape), vmem(*by_feature), vmem(*rest_shape),
+         vmem(*w_qkv.shape), vmem(*by_feature), vmem(*field), vmem(4, PACKED, TOKENS),
+         vmem(8, PACKED, MERGED), vmem(MERGED, 1024), vmem(2, 64, 16, 640),
+         dmas(4), dmas(13), dmas(2)],
+        12, free=range(5, 8),
     )
     blocks, = call(
         assemble_kernel, [*downs, up_own, up_arrived, out_sum], 0, [(64, 16, 1152)], 0,

time: 127 us -> 127 us (level)
  no operation moved by 1% of the time
where the time goes in v12:
time: 127 us; the launch traced here: 126 us
  Pallas kernels  48.6 us (38%)
  waiting for transfers between devices  37.4 us (29%)
  starting transfers between devices  31.3 us (25%)
  local copies, waits for them, and re-layouts  4.93 us (4%)
  other arithmetic  2.74 us (2%)
    pallas_call x8, Pallas kernels, call(): pl.pallas_call(kernel, out_shape=[jax.ShapeDtypeStruct(shape, kind) for s...  48.6 us
    all_to_all x1, waiting for transfers between devices, body(): landed = lax.all_to_all(blocks, PAIRS, 0, 0, tiled=True)  29.6 us
    ppermute x6, starting transfers between devices, shifted_block(): return lax.ppermute(block, GRID, route)  12.9 us
    all_to_all x1, starting transfers between devices, body(): landed = lax.all_to_all(blocks, PAIRS, 0, 0, tiled=True)  8.41 us
    ppermute x6, waiting for transfers between devices, shifted_block(): return lax.ppermute(block, GRID, route)  3.98 us
    ppermute x3, starting transfers between devices, body(): lax.ppermute(block, 'z', [(i, (i + step) % 4) for i in range(4)])  3.86 us
    ppermute x3, starting transfers between devices, body(): lax.ppermute(block, 'y', [(i, (i + step) % 4) for i in range(4)])  3.73 us
  transfers between devices with their start and end apart: 17, of which 8 were waited for; matrix products, arithmetic and copies ran while one was open for 3% of the time, Pallas kernels for 20%

profile of v12, /device:TPU:0, one launch (start us, length us, event | category | flops | bytes accessed | tf_op | source)
XLA Modules:
  0.0 126.2 jit_solution(5664437643503816943)
XLA Ops:
  0.6 0.9 fusion.1
  1.6 1.2 fusion
  2.9 5.1 %collective-permute-start = (bf16[108,512]{1,0:T(8,128)(2,1)S(1)}, bf16[108,512]{1,0:T(8,128)(2,1)S(1)}, u32[]{:S(2)}, u32[]{:S(2)}) collective-permute-start(bf16[108,512]{1,0:T(8,128)(2,1)S(1)} %pad_maximum_fusion.1), channel_id=1, source_target_pairs={{0,15},{1,0},{2,1},{3,2},{4,3},{5,4},{6,5},{7,6},{8,7},{9,8},{10,9... | collective-permute-start | bytes 331784 | tf_op jit(solution)/shard_map/ppermute | solution.py:601
  8.0 4.1 %collective-permute-start.1 = (bf16[108,512]{1,0:T(8,128)(2,1)S(1)}, bf16[108,512]{1,0:T(8,128)(2,1)S(1)}, u32[]{:S(2)}, u32[]{:S(2)}) collective-permute-start(bf16[108,512]{1,0:T(8,128)(2,1)S(1)} %pad_maximum_fusion.2), channel_id=1, source_target_pairs={{0,112},{1,113},{2,114},{3,115},{4,116},{5,117},{6,118},{7,119},{8... | collective-permute-start | bytes 331784 | tf_op jit(solution)/shard_map/ppermute | solution.py:601
  12.8 0.7 pad_maximum_fusion.quad0_hbm
  13.5 1.2 collective-permute-done.1.quad2_hbm
  14.7 1.9 %collective-permute-done.2.quad3_hbm = bf16[108,512]{1,0:T(8,128)(2,1)S(1)} collective-permute-done((bf16[108,512]{1,0:T(8,128)(2,1)S(1)}, bf16[108,512]{1,0:T(8,128)(2,1)S(1)}, u32[]{:S(2)}, u32[]{:S(2)}) %collective-permute-start.2) | collective-permute-done | bytes 110624 | tf_op jit(solution)/shard_map/ppermute | solution.py:601
  16.6 0.6 copy-done.10
  17.2 21.9 %shard_map.189 = (bf16[72,1024]{1,0:T(8,128)(2,1)}, bf16[288,512]{1,0:T(8,128)(2,1)}, bf16[72,1536]{1,0:T(8,128)(2,1)}, bf16[72,1536]{1,0:T(8,128)(2,1)}, bf16[7...) custom-call(s32[1]{0:T(128)} %bitcast.where_ref, ...), custom_call_target="tpu_custom_call" | custom-call | flops 20000000000 | bytes 20000000 | tf_op jit(solution)/shard_map/pallas_call | solution.py:563
  39.5 2.5 %collective-permute-start.4 = (bf16[72,1536]{1,0:T(8,128)(2,1)}, bf16[72,1536]{1,0:T(8,128)(2,1)S(1)}, u32[]{:S(2)}, u32[]{:S(2)}) collective-permute-start(bf16[72,1536]{1,0:T(8,128)(2,1)} %get-tuple-element.64), channel_id=1, source_target_pairs={{0,8},{4,12},{8,0},{12,4},{1,9},{5,13},{9,1},{13,5},{2,10},{6,14},... | collective-permute-start | bytes 663560 | tf_op jit(solution)/shard_map/ppermute | solution.py:671
  42.0 1.2 collective-permute-start.5
  43.1 9.2 %shard_map.190 = (bf16[288,512]{1,0:T(8,128)(2,1)}, bf16[5,64,16,128]{3,2,1,0:T(8,128)(2,1)}, bf16[5,64,16,128]{3,2,1,0:T(8,128)(2,1)}) custom-call(s32[1]{0:T(128)} %bitcast.where_ref, bf16[288,512]{1,0:T(8,128)(2,1)} %get-tuple-element.56.grad_after_ref, bf16[288,512]{1,0:T(8,128)(2,1)} %get-tuple-element.57.middle_ref, ...), custom_call_target="tpu_custom_call" | custom-call | flops 7000000000 | bytes 7000000 | tf_op jit(solution)/shard_map/pallas_call | solution.py:563
  52.4 1.0 collective-permute-done.3.near1_hbm
  53.4 0.6 collective-permute-done.5.near3_hbm
  54.7 3.1 %collective-permute-start.10 = (bf16[64,16,128]{2,1,0:T(8,128)(2,1)S(1)}, bf16[64,16,128]{2,1,0:T(8,128)(2,1)S(1)}, u32[]{:S(2)}, u32[]{:S(2)}) collective-permute-start(bf16[64,16,128]{2,1,0:T(8,128)(2,1)S(1)} %get-tuple-element.87), channel_id=1, source_target_pairs={{0,64},{32,96},{64,0},{96,32},{1,65},{33,97},{65,1},{97,33},{2,66}... | collective-permute-start | bytes 786440 | tf_op jit(solution)/shard_map/ppermute | solution.py:687
  57.8 0.8 collective-permute-start.11
  58.6 0.6 shard_map.192
  59.2 0.5 collective-permute-start.12
  59.8 12.9 %shard_map.193 = (bf16[108,512]{1,0:T(8,128)(2,1)}, bf16[108,512]{1,0:T(8,128)(2,1)}, bf16[108,512]{1,0:T(8,128)(2,1)}, bf16[108,512]{1,0:T(8,128)(2,1)}, bf16[6...) custom-call(s32[1]{0:T(128)} %bitcast.where_ref, bf16[288,512]{1,0:T(8,128)(2,1)} %get-tuple-element.72.middle_grad_ref, ...), custom_call_target="tpu_custom_call" | custom-call | flops 12000000000 | bytes 12000000 | tf_op jit(solution)/shard_map/pallas_call | solution.py:563
  72.7 1.7 %collective-permute-start.13 = (bf16[108,512]{1,0:T(8,128)(2,1)}, bf16[108,512]{1,0:T(8,128)(2,1)S(1)}, u32[]{:S(2)}, u32[]{:S(2)}) collective-permute-start(bf16[108,512]{1,0:T(8,128)(2,1)} %get-tuple-element.91), channel_id=1, source_target_pairs={{0,17},{1,18},{2,19},{3,20},{4,21},{5,22},{6,23},{7,24},{8,25},{9,... | collective-permute-start | bytes 331784 | tf_op jit(solution)/shard_map/ppermute | solution.py:601
  74.5 1.5 %collective-permute-start.14 = (bf16[108,512]{1,0:T(8,128)(2,1)}, bf16[108,512]{1,0:T(8,128)(2,1)S(1)}, u32[]{:S(2)}, u32[]{:S(2)}) collective-permute-start(bf16[108,512]{1,0:T(8,128)(2,1)} %get-tuple-element.92), channel_id=1, source_target_pairs={{0,16},{1,17},{2,18},{3,19},{4,20},{5,21},{6,22},{7,23},{8,24},{9,... | collective-permute-start | bytes 331784 | tf_op jit(solution)/shard_map/ppermute | solution.py:601
  76.0 1.5 %collective-permute-start.8 = (bf16[64,16,640]{2,1,0:T(8,128)(2,1)}, bf16[64,16,640]{2,1,0:T(8,128)(2,1)S(1)}, u32[]{:S(2)}, u32[]{:S(2)}) collective-permute-start(bf16[64,16,640]{2,1,0:T(8,128)(2,1)} %get-tuple-element.85), channel_id=1, source_target_pairs={{0,1},{1,0},{2,3},{3,2},{4,5},{5,4},{6,7},{7,6},{8,9},{9,8},{10,11... | collective-permute-start | bytes 3932168 | tf_op jit(solution)/shard_map/ppermute | solution.py:589
  77.5 0.6 shard_map.194.refs_0_
  78.1 2.3 %collective-permute-done.8.arrived_hbm = bf16[64,16,640]{2,1,0:T(8,128)(2,1)S(1)} collective-permute-done((bf16[64,16,640]{2,1,0:T(8,128)(2,1)}, bf16[64,16,640]{2,1,0:T(8,128)(2,1)S(1)}, u32[]{:S(2)}, u32[]{:S(2)}) %collective-permute-start.8) | collective-permute-done | bytes 1310752 | tf_op jit(solution)/shard_map/ppermute | solution.py:589
  80.3 1.4 %shard_map.195 = bf16[64,16,1152]{2,1,0:T(8,128)(2,1)S(1)} custom-call(bf16[64,16,640]{2,1,0:T(8,128)(2,1)S(1)} %copy-done.1, bf16[64,16,640]{2,1,0:T(8,128)(2,1)S(1)} %collective-permute-done.8.arrived_hbm, bf16[64,16,1152]{2,1,0:T(8,128)(2,1)S(1)} %shard_map.194.refs_0_), custom_call_target="tpu_custom_call", output_to_operand_aliasing={{}: (2, {})} | custom-call | flops 2000000000 | bytes 2000000 | tf_op jit(solution)/shard_map/pallas_call | solution.py:563
  81.7 1.4 %copy-done = bf16[64,16,1152]{2,1,0:T(8,128)(2,1)} copy-done((bf16[64,16,1152]{2,1,0:T(8,128)(2,1)}, bf16[64,16,1152]{2,1,0:T(8,128)(2,1)S(1)}, u32[]{:S(2)}) %copy-start) | copy-done | bytes 2359320
  83.2 0.6 collective-permute-done.13
  84.0 8.4 %all-to-all-start = ((bf16[64,16,1152]{2,1,0:T(8,128)(2,1)}), bf16[64,16,1152]{2,1,0:T(8,128)(2,1)S(1)}, u32[]{:S(2)}, u32[]{:S(2)}) async-start(bf16[64,16,1152]{2,1,0:T(8,128)(2,1)} %copy-done), calls=%async_computation | async-start | bytes 4718592 | tf_op jit(solution)/shard_map/all_to_all | solution.py:722
  92.9 0.9 maximum_bitcast_fusion.1
  93.8 1.1 maximum_bitcast_fusion
  94.9 29.6 %all-to-all-done.landed_hbm = bf16[64,16,1152]{2,1,0:T(8,128)(2,1)S(1)} async-done(((bf16[64,16,1152]{2,1,0:T(8,128)(2,1)}), bf16[64,16,1152]{2,1,0:T(8,128)(2,1)S(1)}, u32[]{:S(2)}, u32[]{:S(2)}) %all-to-all-start) | async-done | bytes 2359328 | tf_op jit(solution)/shard_map/all_to_all | solution.py:722
  124.5 1.5 %shard_map.196 = (f32[4,1536]{1,0:T(4,128)}, f32[4,512]{1,0:T(4,128)}, f32[4,2048]{1,0:T(4,128)}, f32[16,512]{1,0:T(8,128)}, f32[16,1024]{1,0:T(8,128)}) custom-call(bf16[64,16,1152]{2,1,0:T(8,128)(2,1)S(1)} %all-to-all-done.landed_hbm), custom_call_target="tpu_custom_call" | custom-call | flops 3000000000 | bytes 3000000 | tf_op jit(solution)/shard_map/pallas_call | solution.py:563
  (70 shorter events, 2.5 us)
Async XLA Ops:
  2.9 10.6 %collective-permute-start = (bf16[108,512]{1,0:T(8,128)(2,1)S(1)}, bf16[108,512]{1,0:T(8,128)(2,1)S(1)}, u32[]{:S(2)}, u32[]{:S(2)}) collective-permute-start(bf16[108,512]{1,0:T(8,128)(2,1)S(1)} %pad_maximum_fusion.1), channel_id=1, source_target_pairs={{0,15},{1,0},{2,1},{3,2},{4,3},{5,4},{6,5},{7,6},{8,7},{9,8},{10,9... | collective-permute-start | bytes 331784 | tf_op jit(solution)/shard_map/ppermute | solution.py:601
  8.0 6.6 %collective-permute-start.1 = (bf16[108,512]{1,0:T(8,128)(2,1)S(1)}, bf16[108,512]{1,0:T(8,128)(2,1)S(1)}, u32[]{:S(2)}, u32[]{:S(2)}) collective-permute-start(bf16[108,512]{1,0:T(8,128)(2,1)S(1)} %pad_maximum_fusion.2), channel_id=1, source_target_pairs={{0,112},{1,113},{2,114},{3,115},{4,116},{5,117},{6,118},{7,119},{8... | collective-permute-start | bytes 331784 | tf_op jit(solution)/shard_map/ppermute | solution.py:601
  12.3 4.3 %collective-permute-start.2 = (bf16[108,512]{1,0:T(8,128)(2,1)S(1)}, bf16[108,512]{1,0:T(8,128)(2,1)S(1)}, u32[]{:S(2)}, u32[]{:S(2)}) collective-permute-start(bf16[108,512]{1,0:T(8,128)(2,1)S(1)} %pad_maximum_fusion.3), channel_id=1, source_target_pairs={{0,127},{1,112},{2,113},{3,114},{4,115},{5,116},{6,117},{7,118},{8... | collective-permute-start | bytes 331784 | tf_op jit(solution)/shard_map/ppermute | solution.py:601
  13.5 3.1 %copy-start.8 = (bf16[108,512]{1,0:T(8,128)(2,1)}, bf16[108,512]{1,0:T(8,128)(2,1)S(1)}, u32[]{:S(2)}) copy-start(bf16[108,512]{1,0:T(8,128)(2,1)S(1)} %collective-permute-done.quad1_hbm) | copy-start | bytes 331780
  14.7 1.9 %copy-start.9 = (bf16[108,512]{1,0:T(8,128)(2,1)}, bf16[108,512]{1,0:T(8,128)(2,1)S(1)}, u32[]{:S(2)}) copy-start(bf16[108,512]{1,0:T(8,128)(2,1)S(1)} %collective-permute-done.1.quad2_hbm) | copy-start | bytes 331780
  16.6 0.6 copy-start.10
  39.1 14.9 %collective-permute-start.6 = (bf16[4,64,16,128]{3,2,1,0:T(8,128)(2,1)}, bf16[4,64,16,128]{3,2,1,0:T(8,128)(2,1)S(1)}, u32[]{:S(2)}, u32[]{:S(2)}) collective-permute-start(bf16[4,64,16,128]{3,2,1,0:T(8,128)(2,1)} %get-tuple-element.67), channel_id=1, source_target_pairs={{0,1},{1,0},{2,3},{3,2},{4,5},{5,4},{6,7},{7,6},{8,9},{9,8},{10,11... | collective-permute-start | bytes 3145736 | tf_op jit(solution)/shard_map/ppermute | solution.py:589
  39.4 14.0 %collective-permute-start.3 = (bf16[72,1536]{1,0:T(8,128)(2,1)}, bf16[72,1536]{1,0:T(8,128)(2,1)S(1)}, u32[]{:S(2)}, u32[]{:S(2)}) collective-permute-start(bf16[72,1536]{1,0:T(8,128)(2,1)} %get-tuple-element.63), channel_id=1, source_target_pairs={{0,4},{4,8},{8,12},{12,0},{1,5},{5,9},{9,13},{13,1},{2,6},{6,10},{... | collective-permute-start | bytes 663560 | tf_op jit(solution)/shard_map/ppermute | solution.py:671
  39.5 13.9 %collective-permute-start.4 = (bf16[72,1536]{1,0:T(8,128)(2,1)}, bf16[72,1536]{1,0:T(8,128)(2,1)S(1)}, u32[]{:S(2)}, u32[]{:S(2)}) collective-permute-start(bf16[72,1536]{1,0:T(8,128)(2,1)} %get-tuple-element.64), channel_id=1, source_target_pairs={{0,8},{4,12},{8,0},{12,4},{1,9},{5,13},{9,1},{13,5},{2,10},{6,14},... | collective-permute-start | bytes 663560 | tf_op jit(solution)/shard_map/ppermute | solution.py:671
  42.0 12.1 %collective-permute-start.5 = (bf16[72,1536]{1,0:T(8,128)(2,1)}, bf16[72,1536]{1,0:T(8,128)(2,1)S(1)}, u32[]{:S(2)}, u32[]{:S(2)}) collective-permute-start(bf16[72,1536]{1,0:T(8,128)(2,1)} %get-tuple-element.65), channel_id=1, source_target_pairs={{0,12},{4,0},{8,4},{12,8},{1,13},{5,1},{9,5},{13,9},{2,14},{6,2},{... | collective-permute-start | bytes 663560 | tf_op jit(solution)/shard_map/ppermute | solution.py:671
  43.1 10.9 %copy-start.3 = (bf16[4,64,16,128]{3,2,1,0:T(8,128)(2,1)S(1)}, bf16[4,64,16,128]{3,2,1,0:T(8,128)(2,1)}, u32[]{:S(2)}) copy-start(bf16[4,64,16,128]{3,2,1,0:T(8,128)(2,1)} %get-tuple-element.66.keep_hbm) | copy-start | bytes 3145732
  52.3 6.3 %collective-permute-start.7 = (bf16[5,64,16,128]{3,2,1,0:T(8,128)(2,1)}, bf16[5,64,16,128]{3,2,1,0:T(8,128)(2,1)S(1)}, u32[]{:S(2)}, u32[]{:S(2)}) collective-permute-start(bf16[5,64,16,128]{3,2,1,0:T(8,128)(2,1)} %get-tuple-element.70), channel_id=1, source_target_pairs={{0,1},{1,0},{2,3},{3,2},{4,5},{5,4},{6,7},{7,6},{8,9},{9,8},{10,11... | collective-permute-start | bytes 3932168 | tf_op jit(solution)/shard_map/ppermute | solution.py:589
  53.4 1.1 copy-start.5
  53.4 1.1 copy-start.6
  54.0 0.7 copy-start.7
  54.0 4.6 %copy-start.2 = (bf16[5,64,16,128]{3,2,1,0:T(8,128)(2,1)S(1)}, bf16[5,64,16,128]{3,2,1,0:T(8,128)(2,1)}, u32[]{:S(2)}) copy-start(bf16[5,64,16,128]{3,2,1,0:T(8,128)(2,1)} %get-tuple-element.69.keep_hbm) | copy-start | bytes 3932164
  54.7 19.7 %collective-permute-start.9 = (bf16[64,16,128]{2,1,0:T(8,128)(2,1)S(1)}, bf16[64,16,128]{2,1,0:T(8,128)(2,1)S(1)}, u32[]{:S(2)}, u32[]{:S(2)}) collective-permute-start(bf16[64,16,128]{2,1,0:T(8,128)(2,1)S(1)} %get-tuple-element.86), channel_id=1, source_target_pairs={{0,32},{32,64},{64,96},{96,0},{1,33},{33,65},{65,97},{97,1},{2,34}... | collective-permute-start | bytes 786440 | tf_op jit(solution)/shard_map/ppermute | solution.py:687
  54.7 21.3 %collective-permute-start.10 = (bf16[64,16,128]{2,1,0:T(8,128)(2,1)S(1)}, bf16[64,16,128]{2,1,0:T(8,128)(2,1)S(1)}, u32[]{:S(2)}, u32[]{:S(2)}) collective-permute-start(bf16[64,16,128]{2,1,0:T(8,128)(2,1)S(1)} %get-tuple-element.87), channel_id=1, source_target_pairs={{0,64},{32,96},{64,0},{96,32},{1,65},{33,97},{65,1},{97,33},{2,66}... | collective-permute-start | bytes 786440 | tf_op jit(solution)/shard_map/ppermute | solution.py:687
  57.8 18.2 %collective-permute-start.11 = (bf16[64,16,128]{2,1,0:T(8,128)(2,1)S(1)}, bf16[64,16,128]{2,1,0:T(8,128)(2,1)S(1)}, u32[]{:S(2)}, u32[]{:S(2)}) collective-permute-start(bf16[64,16,128]{2,1,0:T(8,128)(2,1)S(1)} %get-tuple-element.88), channel_id=1, source_target_pairs={{0,96},{32,0},{64,32},{96,64},{1,97},{33,1},{65,33},{97,65},{2,98}... | collective-permute-start | bytes 786440 | tf_op jit(solution)/shard_map/ppermute | solution.py:687
  59.2 18.3 %collective-permute-start.12 = (bf16[64,16,256]{2,1,0:T(8,128)(2,1)S(1)}, bf16[64,16,256]{2,1,0:T(8,128)(2,1)S(1)}, u32[]{:S(2)}, u32[]{:S(2)}) collective-permute-start(bf16[64,16,256]{2,1,0:T(8,128)(2,1)S(1)} %get-tuple-element.89), channel_id=1, source_target_pairs={{0,4},{4,0},{8,12},{12,8},{1,5},{5,1},{9,13},{13,9},{2,6},{6,2},{1... | collective-permute-start | bytes 1572872 | tf_op jit(solution)/shard_map/ppermute | solution.py:692
  72.7 11.0 %collective-permute-start.13 = (bf16[108,512]{1,0:T(8,128)(2,1)}, bf16[108,512]{1,0:T(8,128)(2,1)S(1)}, u32[]{:S(2)}, u32[]{:S(2)}) collective-permute-start(bf16[108,512]{1,0:T(8,128)(2,1)} %get-tuple-element.91), channel_id=1, source_target_pairs={{0,17},{1,18},{2,19},{3,20},{4,21},{5,22},{6,23},{7,24},{8,25},{9,... | collective-permute-start | bytes 331784 | tf_op jit(solution)/shard_map/ppermute | solution.py:601
  74.5 9.3 %collective-permute-start.14 = (bf16[108,512]{1,0:T(8,128)(2,1)}, bf16[108,512]{1,0:T(8,128)(2,1)S(1)}, u32[]{:S(2)}, u32[]{:S(2)}) collective-permute-start(bf16[108,512]{1,0:T(8,128)(2,1)} %get-tuple-element.92), channel_id=1, source_target_pairs={{0,16},{1,17},{2,18},{3,19},{4,20},{5,21},{6,22},{7,23},{8,24},{9,... | collective-permute-start | bytes 331784 | tf_op jit(solution)/shard_map/ppermute | solution.py:601
  76.0 8.0 %collective-permute-start.15 = (bf16[108,512]{1,0:T(8,128)(2,1)}, bf16[108,512]{1,0:T(8,128)(2,1)S(1)}, u32[]{:S(2)}, u32[]{:S(2)}) collective-permute-start(bf16[108,512]{1,0:T(8,128)(2,1)} %get-tuple-element.93), channel_id=1, source_target_pairs={{0,1},{1,2},{2,3},{3,4},{4,5},{5,6},{6,7},{7,8},{8,9},{9,10},{10,1... | collective-permute-start | bytes 331784 | tf_op jit(solution)/shard_map/ppermute | solution.py:601
  76.0 4.4 %collective-permute-start.8 = (bf16[64,16,640]{2,1,0:T(8,128)(2,1)}, bf16[64,16,640]{2,1,0:T(8,128)(2,1)S(1)}, u32[]{:S(2)}, u32[]{:S(2)}) collective-permute-start(bf16[64,16,640]{2,1,0:T(8,128)(2,1)} %get-tuple-element.85), channel_id=1, source_target_pairs={{0,1},{1,0},{2,3},{3,2},{4,5},{5,4},{6,7},{7,6},{8,9},{9,8},{10,11... | collective-permute-start | bytes 3932168 | tf_op jit(solution)/shard_map/ppermute | solution.py:589
  77.5 2.9 %copy-start.1 = (bf16[64,16,640]{2,1,0:T(8,128)(2,1)S(1)}, bf16[64,16,640]{2,1,0:T(8,128)(2,1)}, u32[]{:S(2)}) copy-start(bf16[64,16,640]{2,1,0:T(8,128)(2,1)} %get-tuple-element.84.keep_hbm) | copy-start | bytes 3932164
  81.7 1.4 %copy-start = (bf16[64,16,1152]{2,1,0:T(8,128)(2,1)}, bf16[64,16,1152]{2,1,0:T(8,128)(2,1)S(1)}, u32[]{:S(2)}) copy-start(bf16[64,16,1152]{2,1,0:T(8,128)(2,1)S(1)} %shard_map.195) | copy-start | bytes 7077892
  84.0 8.7 %copy-start.4 = (bf16[108,512]{1,0:T(8,128)(2,1)S(1)}, bf16[108,512]{1,0:T(8,128)(2,1)}, u32[]{:S(2)}) copy-start(bf16[108,512]{1,0:T(8,128)(2,1)} %get-tuple-element.98) | copy-start | bytes 331780
  84.0 40.5 %all-to-all-start = ((bf16[64,16,1152]{2,1,0:T(8,128)(2,1)}), bf16[64,16,1152]{2,1,0:T(8,128)(2,1)S(1)}, u32[]{:S(2)}, u32[]{:S(2)}) async-start(bf16[64,16,1152]{2,1,0:T(8,128)(2,1)} %copy-done), calls=%async_computation | async-start | bytes 4718592 | tf_op jit(solution)/shard_map/all_to_all | solution.py:722

commit v13 on v12

--- a/solution.py
+++ b/solution.py
@@ -82,6 +82,10 @@
     return jnp.swapaxes(values.astype(F32), 0, 1).astype(BF16)
 
 
+def block_of(at, size):
+    return pl.ds(pl.multiple_of(at * size, size), size)
+
+
 def own_block(shape):
     rows = lax.broadcasted_iota(jnp.int32, shape, 0) >> 5
     return rows == lax.broadcasted_iota(jnp.int32, shape, 1) >> 5
@@ -157,7 +161,7 @@
     attended_hbm, first_t_hbm, middle_hbm, probs_hbm, rest_hbm, slope_hbm, keep_hbm, send_hbm,
     quads_ref, bias_ref, bias_rest, query_t, query_rest, values_t, slope_ref, hidden_ref,
     probs_ref, rest_ref, w_qkv, w_out, w_up, w_down, w_merge, slots, near_ref, tokens_ref,
-    packed_ref, keys_t_ref, attended_ref, first_t_ref, middle_ref, quad_sems, in_sems, out_sems,
+    packed_ref, keys_t_ref, attended_ref, first_t_ref, middle_ref, mlp_ref, quad_sems, in_sems, out_sems,
 ):
     saves = []
 
@@ -167,8 +171,8 @@
     quads = (quad0_hbm, quad1_hbm, quad2_hbm, quad3_hbm)
     quads = load([(quads[q], quads_ref.at[q]) for q in range(4)], quad_sems)
     weights = load(
-        [(w_qkv_hbm, w_qkv), (w_out_hbm, w_out), (w_up_hbm, w_up), (w_down_hbm, w_down),
-         (w_merge_hbm, w_merge)],
+        [(w_qkv_hbm, w_qkv), (w_out_hbm, w_out), (w_down_hbm, w_down), (w_merge_hbm, w_merge)]
+        + [(w_up_hbm.at[:, pl.ds(p * 512, 512)], w_up.at[p]) for p in range(4)],
         in_sems,
     )
     query_t[...] = jnp.zeros_like(query_t)
@@ -209,29 +213,29 @@
             query_rest[group] = spread_rest(rest)
     save((packed_ref, packed_hbm), (keys_t_ref, keys_t_hbm))
 
-    def scores_of(at):
-        group, head = at // 5, at % 5
-        turn = query_rest[group] if head == 4 else query_t[group * 4 + head]
-        return dot(packed_ref[4 + group], turn)
-
-    ahead = scores_of(0)
-    for at in range(20):
-        group, head = at // 5, at % 5
-        scores = ahead + (bias_rest if head == 4 else bias_ref)[...]
-        if at < 19:
-            ahead = scores_of(at + 1)
-        raised = jnp.exp2(scores - jnp.max(scores, axis=0, keepdims=True))
-        inverse = 1.0 / jnp.sum(raised, axis=0, keepdims=True)
-        probs = (raised * inverse).astype(BF16)
-        if head == 4:
-            rest_ref[group] = probs
-            rows = slice(group * 128, group * 128 + 128)
-            rest = gather_rest(dot(values_t[rows, :], probs))
-            attended_ref[rows, MAIN:] = rest.astype(BF16)
-        else:
-            probs_ref[group * 4 + head] = probs
-            rows = slice(group * 128 + head * HEAD, group * 128 + head * HEAD + HEAD)
-            attended_ref[rows, :MAIN] = dot(values_t[rows, :], probs).astype(BF16)
+    def attend(group, _):
+        keys = packed_ref[4 + group]
+        ahead = dot(keys, query_t[group * 4])
+        for head in range(5):
+            scores = ahead + (bias_rest if head == 4 else bias_ref)[...]
+            if head < 4:
+                turn = query_rest[group] if head == 3 else query_t[group * 4 + head + 1]
+                ahead = dot(keys, turn)
+            raised = jnp.exp2(scores - jnp.max(scores, axis=0, keepdims=True))
+            inverse = 1.0 / jnp.sum(raised, axis=0, keepdims=True)
+            probs = (raised * inverse).astype(BF16)
+            if head == 4:
+                rest_ref[group] = probs
+                rows = block_of(group, 128)
+                rest = gather_rest(dot(values_t[rows, :], probs))
+                attended_ref[rows, MAIN:] = rest.astype(BF16)
+            else:
+                probs_ref[group * 4 + head] = probs
+                rows = block_of(group * 4 + head, HEAD)
+                attended_ref[rows, :MAIN] = dot(values_t[rows, :], probs).astype(BF16)
+        return 0
+
+    lax.fori_loop(0, 4, attend, 0)
     save((probs_ref, probs_hbm), (rest_ref, rest_hbm), (attended_ref, attended_hbm))
 
     attended = turned(attended_ref[...])
@@ -242,22 +246,22 @@
     save((middle_ref, middle_hbm))
     middle = narrow_middle.astype(F32)
     second_norm = normalize(middle)[0].astype(BF16)
-    mlp = jnp.zeros((TOKENS, 512), F32)
-    weights[2].wait()
-    weights[3].wait()
-    ahead = dot(second_norm, w_up[:, :512])
-    for part in range(4):
-        cols = slice(part * 512, part * 512 + 512)
-        before = ahead
-        if part < 3:
-            ahead = dot(second_norm, w_up[:, part * 512 + 512 : part * 512 + 1024])
+    mlp_ref[...] = middle
+    for at in (2, 4, 5, 6, 7):
+        weights[at].wait()
+
+    def feed(part, _):
+        before = dot(second_norm, w_up[part])
         cumulative, density = gelu_parts(before)
         hidden = (before * cumulative).astype(BF16)
-        hidden_ref[:, cols] = hidden
-        slope_ref[:, cols] = (cumulative + before * density * 0.3989422804014327).astype(BF16)
-        mlp = mlp + dot(hidden, w_down[cols])
+        hidden_ref[part] = hidden
+        slope_ref[part] = (cumulative + before * density * 0.3989422804014327).astype(BF16)
+        mlp_ref[...] += dot(hidden, w_down[block_of(part, 512), :])
+        return 0
+
+    lax.fori_loop(0, 4, feed, 0)
     save((slope_ref, slope_hbm))
-    after_mlp = (middle + mlp).astype(BF16)
+    after_mlp = mlp_ref[...].astype(BF16)
     pieces, inverse_out = merge_norm(after_mlp.astype(F32))
     merged_norm = [v.astype(BF16) for v in pieces]
     order = near_order()
@@ -275,7 +279,7 @@
         near_ref[step, :, 512:] = cotangent
         save((near_ref.at[step], near))
 
-    weights[4].wait()
+    weights[3].wait()
     level_two_ref[...] = sum(
         dot(merged_norm[p], w_merge[p * 512 : p * 512 + 512]) for p in range(4)
     ).astype(BF16)
@@ -289,14 +293,16 @@
     ).astype(BF16)
     grad_after_ref[...] = grad_after
     core = where_ref[0] & 1
-    for part in range(4):
-        grad = dot(hidden_ref[:, part * 512 : part * 512 + 512], grad_after, 0, 0).astype(BF16)
-        grad = grad.reshape(16, 2, 16, 512)
+
+    def down(part, _):
+        grad = dot(hidden_ref[part], grad_after, 0, 0).astype(BF16).reshape(16, 2, 16, 512)
+        chips = block_of(part, 16)
         for unit in range(4):
             for parity in range(2):
-                slots[parity, unit, part * 16 : part * 16 + 16] = grad[
-                    :, parity, :, unit * 128 : unit * 128 + 128
-                ]
+                slots[parity, unit, chips] = grad[:, parity, :, unit * 128 : unit * 128 + 128]
+        return 0
+
+    lax.fori_loop(0, 4, down, 0)
     save((slots.at[core], keep_hbm), (slots.at[1 - core], send_hbm))
     for copy in saves:
         copy.wait()
@@ -305,13 +311,13 @@
 def middle_kernel(
     where_ref, grad_after_ref, middle_ref, attended_ref, w_down_hbm, slope_hbm, w_up_hbm,
     middle_grad_ref, keep_hbm, send_hbm,
-    w_down, slope_ref, w_up, slots, sems, out_sems,
+    w_down, slope_ref, w_up, slots, grads_ref, back_ref, sems, out_sems,
 ):
     loads = []
     for part in range(4):
         cols = pl.ds(part * 512, 512)
         pairs = [(w_down_hbm.at[cols], w_down.at[cols])]
-        pairs += [(slope_hbm.at[:, cols], slope_ref.at[part])]
+        pairs += [(slope_hbm.at[part], slope_ref.at[part])]
         pairs += [(w_up_hbm.at[:, cols], w_up.at[part])]
         loads.append(load(pairs, sems.at[pl.ds(part * 3, 3)]))
     core = where_ref[0] & 1
@@ -326,23 +332,28 @@
             out_sems.at[pl.ds(at, 2)],
         )
 
-    back_up = jnp.zeros((TOKENS, 512), F32)
-    grads_up = []
-    for part in range(4):
-        cols = slice(part * 512, part * 512 + 512)
-        for copy in loads[part]:
-            copy.wait()
-        grad_before = (
-            dot(grad_after, w_down[cols], 1, 1) * slope_ref[part].astype(F32)
-        ).astype(BF16)
-        grads_up.append(dot(second_t, grad_before))
-        back_up = back_up + dot(grad_before, w_up[part], 1, 1)
-    for unit in range(4):
-        cols = slice(unit * 128, unit * 128 + 128)
-        weave([grad[:, cols] for grad in grads_up], slots.at[:, unit], slice(0, 128))
+    back_ref[...] = jnp.zeros_like(back_ref)
+    for copy in sum(loads, []):
+        copy.wait()
+
+    def back(part, _):
+        grad_before = dot(grad_after, w_down[block_of(part, 512), :], 1, 1)
+        grad_before = (grad_before * slope_ref[part].astype(F32)).astype(BF16)
+        grads_ref[part] = dot(second_t, grad_before)
+        back_ref[...] += dot(grad_before, w_up[part], 1, 1)
+        return 0
+
+    lax.fori_loop(0, 4, back, 0)
+
+    def lay_out(unit, _):
+        cols = block_of(unit, 128)
+        weave([grads_ref[p, :, cols] for p in range(4)], slots.at[:, unit], slice(0, 128))
+        return 0
+
+    lax.fori_loop(0, 4, lay_out, 0)
     saves = save(pl.ds(0, 4), 0)
     middle_grad = (
-        grad_after.astype(F32) + norm_back(normed_mid, inverse_mid, back_up)
+        grad_after.astype(F32) + norm_back(normed_mid, inverse_mid, back_ref[...])
     ).astype(BF16)
     middle_grad_ref[...] = middle_grad
     grad = dot(attended_ref[...], middle_grad)
@@ -360,12 +371,13 @@
     out0, out1, out2, out3, keep_hbm, send_hbm,
     grad_heads, grad_heads_t, grad_heads_rest, products, query_grad_t, packed_grad, probs_ref,
     near_ref, packed_ref, keys_t_ref, rest_ref, w_qkv, first_t_ref, tokens_ref, order_ref,
-    level_order_ref, level_two_ref, slots, near_sems, sems, out_sems,
+    level_order_ref, level_two_ref, slots, grads_ref, back_ref, near_sems, sems, out_sems,
 ):
     loads = load(
         [(packed_hbm, packed_ref), (keys_t_hbm, keys_t_ref), (rest_hbm, rest_ref)]
         + [(probs_hbm.at[pl.ds(g * 4, 4)], probs_ref.at[pl.ds(g * 4, 4)]) for g in range(4)]
-        + [(w_qkv_hbm, w_qkv), (first_t_hbm, first_t_ref), (tokens_hbm, tokens_ref),
+        + [(w_qkv_hbm.at[:, pl.ds(p * 512, 512)], w_qkv.at[p]) for p in range(3)]
+        + [(first_t_hbm, first_t_ref), (tokens_hbm, tokens_ref),
            (order_hbm, order_ref), (level_order_hbm, level_order_ref),
            (level_two_hbm, level_two_ref)],
         sems,
@@ -388,11 +400,11 @@
         grad_heads_rest[group] = spread_rest(rest[:, MAIN:])
 
     head_of_lane = lax.broadcasted_iota(jnp.int32, (TOKENS, 128), 1) >> 5
-    for copy in loads[:3]:
-        copy.wait()
-    for group in range(4):
-        loads[3 + group].wait()
-        rows = slice(group * 128, group * 128 + 128)
+    for copy in loads[:7]:
+        copy.wait()
+
+    def attend_back(group, _):
+        rows = block_of(group, 128)
         queries = packed_ref[group]
         values = packed_ref[8 + group]
         upstream = grad_heads[group]
@@ -401,7 +413,7 @@
         totals = []
         for part in range(4):
             head = group * 4 + part
-            at = slice(head * HEAD, head * HEAD + HEAD)
+            at = block_of(head, HEAD)
             weights = probs_ref[head]
             total = jnp.sum(products[at, :], axis=0, keepdims=True)
             totals.append(total[:, MAIN:])
@@ -422,6 +434,9 @@
         query_grad_t[rows, MAIN:] = query_grad.astype(BF16)
         packed_grad[4 + group] = (grad_keys * (1 / LOG2E)).astype(BF16)
         packed_grad[8 + group] = grad_values.astype(BF16)
+        return 0
+
+    lax.fori_loop(0, 4, attend_back, 0)
 
     for copy in nears:
         copy.wait()
@@ -434,19 +449,22 @@
     for copy in loads[7:]:
         copy.wait()
     first_t = first_t_ref[...]
-    back_qkv = jnp.zeros((TOKENS, 512), F32)
-    grads = []
-    for part in range(3):
+    back_ref[...] = jnp.zeros_like(back_ref)
+
+    def project_back(part, _):
         wide = jnp.concatenate([packed_grad[part * 4 + g] for g in range(4)], axis=1)
-        grad = dot(first_t, wide)
-        grads += [grad[:, q * 128 : q * 128 + 128] for q in range(4)]
-        back_qkv = back_qkv + dot(wide, w_qkv[:, part * 512 : part * 512 + 512], 1, 1)
+        grads_ref[part] = dot(first_t, wide)
+        back_ref[...] += dot(wide, w_qkv[part], 1, 1)
+        return 0
+
+    lax.fori_loop(0, 3, project_back, 0)
+    grads = [grads_ref[q // 4, :, q % 4 * 128 : q % 4 * 128 + 128] for q in range(12)]
     for part in range(3):
         weave([grads[q * 3 + part] for q in range(4)], slots, slice(part * 128, part * 128 + 128))
     saves = load([(slots.at[core], keep_hbm), (slots.at[1 - core], send_hbm)], out_sems)
 
     normed_in, inverse_in = normalize(tokens_ref[...].astype(F32))
-    grad_first = back_qkv.astype(BF16).astype(F32)
+    grad_first = back_ref[...].astype(BF16).astype(F32)
     grad_tokens = (
         middle_grad.astype(F32) + norm_back(normed_in, inverse_in, grad_first)
     ).astype(BF16)
@@ -641,7 +659,7 @@
 def body(tokens, window_ids, cotangent, w_qkv, w_out, w_up, w_down, w_merge):
     order, cot_order = token_order(), cotangent_order()
     level_order = np.concatenate([cot_order[:, :MERGED], cot_order[:, MERGED:]]).transpose(0, 2, 1)
-    by_feature, field, hidden_shape = (512, TOKENS), (TOKENS, 512), (TOKENS, 2048)
+    by_feature, field, hidden_shape = (512, TOKENS), (TOKENS, 512), (4, TOKENS, 512)
     near_shape, corner = (MERGED, 1536), (PACKED, 512)
     places = window_places()
     where = lax.axis_index(("z", "y", "core")).reshape(1)
@@ -660,10 +678,10 @@
         [vmem(4, *corner), pltpu.VMEM((TOKENS, MAIN), F32), pltpu.VMEM((TOKENS, 128), F32),
          vmem(16, 128, MAIN), vmem(4, 128, 128), vmem(*by_feature), vmem(*hidden_shape),
          vmem(*hidden_shape), vmem(*probs_shape), vmem(*rest_shape), vmem(*w_qkv.shape),
-         vmem(*w_out.shape), vmem(*w_up.shape), vmem(*w_down.shape), vmem(*w_merge.shape),
+         vmem(*w_out.shape), vmem(4, 512, 512), vmem(*w_down.shape), vmem(*w_merge.shape),
          vmem(2, *down_shape), vmem(4, *near_shape), vmem(*field), vmem(*packed_shape),
          vmem(*by_feature), vmem(*by_feature), vmem(*by_feature), vmem(*field),
-         dmas(4), dmas(5), dmas(15)],
+         pltpu.VMEM(field, F32), dmas(4), dmas(8), dmas(15)],
         20, free=range(6, 10),
     )
     near = [near0]
@@ -674,7 +692,7 @@
         [where, grad_after, middle, attended, w_down, slope, w_up], 4,
         [field, (5, 64, 16, 128), (5, 64, 16, 128)], 1,
         [vmem(*w_down.shape), vmem(4, TOKENS, 512), vmem(4, 512, 512), vmem(2, 5, 64, 16, 128),
-         dmas(12), dmas(4)],
+         pltpu.VMEM((4, 512, 512), F32), pltpu.VMEM(field, F32), dmas(12), dmas(4)],
         7,
     )
     down_keep, *near = lax.optimization_barrier((down_keep, *near))
@@ -700,9 +718,9 @@
         [vmem(4, TOKENS, 128), vmem(16, 128, MAIN), vmem(4, 128, 128),
          pltpu.VMEM(by_feature, F32), vmem(*by_feature), vmem(*packed_shape), vmem(*probs_shape),
          vmem(4, *near_shape), vmem(*packed_shape), vmem(*by_feature), vmem(*rest_shape),
-         vmem(*w_qkv.shape), vmem(*by_feature), vmem(*field), vmem(4, PACKED, TOKENS),
+         vmem(3, 512, 512), vmem(*by_feature), vmem(*field), vmem(4, PACKED, TOKENS),
          vmem(8, PACKED, MERGED), vmem(MERGED, 1024), vmem(2, 64, 16, 640),
-         dmas(4), dmas(13), dmas(2)],
+         pltpu.VMEM((3, 512, 512), F32), pltpu.VMEM(field, F32), dmas(4), dmas(15), dmas(2)],
         12, free=range(5, 8),
     )
     blocks, = call(

time: 127 us -> 134 us (1.055)
  Pallas kernels: 48.6 us -> 57 us
  waiting for transfers between devices: 37.4 us -> 35.7 us
    pallas_call x8, Pallas kernels: 48.6 us -> 57 us  [call(): pl.pallas_call(kernel, out_shape=[jax.ShapeDtypeStruct(shape, kind) for s...]
    ppermute x3, waiting for transfers between devices: 1.62 us -> 0.01 us  [body(): lax.ppermute(block, 'y', [(i, (i + step) % 4) for i in range(4)])]
  transfers between devices with their start and end apart: 17 -> 17, of which waited for: 8 -> 4; matrix products, arithmetic and copies ran while one was open for 3% -> 2% of each run, Pallas kernels for 20% -> 22%
where the time goes in v13:
time: 134 us
  Pallas kernels  57 us (43%)
  waiting for transfers between devices  35.7 us (27%)
  starting transfers between devices  32.1 us (24%)
  local copies, waits for them, and re-layouts  5.03 us (4%)
  other arithmetic  2.74 us (2%)
    pallas_call x8, Pallas kernels, call(): pl.pallas_call(kernel, out_shape=[jax.ShapeDtypeStruct(shape, kind) for s...  57 us
    all_to_all x1, waiting for transfers between devices, body(): landed = lax.all_to_all(blocks, PAIRS, 0, 0, tiled=True)  30.3 us
    ppermute x6, starting transfers between devices, shifted_block(): return lax.ppermute(block, GRID, route)  14 us
    all_to_all x1, starting transfers between devices, body(): landed = lax.all_to_all(blocks, PAIRS, 0, 0, tiled=True)  8.05 us
    ppermute x3, starting transfers between devices, body(): lax.ppermute(block, 'y', [(i, (i + step) % 4) for i in range(4)])  3.74 us
    ppermute x3, starting transfers between devices, body(): lax.ppermute(block, 'z', [(i, (i + step) % 4) for i in range(4)])  3.64 us
    ppermute x6, waiting for transfers between devices, shifted_block(): return lax.ppermute(block, GRID, route)  3.11 us
  transfers between devices with their start and end apart: 17, of which 4 were waited for; matrix products, arithmetic and copies ran while one was open for 2% of the time, Pallas kernels for 22%

profile of v13, /device:TPU:0, one launch (start us, length us, event | category | flops | bytes accessed | tf_op | source)
XLA Modules:
  0.0 133.8 jit_solution(6141030702107079540)
XLA Ops:
  0.6 0.9 fusion.1
  1.6 1.2 fusion
  2.9 5.1 %collective-permute-start = (bf16[108,512]{1,0:T(8,128)(2,1)S(1)}, bf16[108,512]{1,0:T(8,128)(2,1)S(1)}, u32[]{:S(2)}, u32[]{:S(2)}) collective-permute-start(bf16[108,512]{1,0:T(8,128)(2,1)S(1)} %pad_maximum_fusion.1), channel_id=1, source_target_pairs={{0,15},{1,0},{2,1},{3,2},{4,3},{5,4},{6,5},{7,6},{8,7},{9,8},{10,9... | collective-permute-start | bytes 331784 | tf_op jit(solution)/shard_map/ppermute | solution.py:619
  8.0 4.1 %collective-permute-start.1 = (bf16[108,512]{1,0:T(8,128)(2,1)S(1)}, bf16[108,512]{1,0:T(8,128)(2,1)S(1)}, u32[]{:S(2)}, u32[]{:S(2)}) collective-permute-start(bf16[108,512]{1,0:T(8,128)(2,1)S(1)} %pad_maximum_fusion.2), channel_id=1, source_target_pairs={{0,112},{1,113},{2,114},{3,115},{4,116},{5,117},{6,118},{7,119},{8... | collective-permute-start | bytes 331784 | tf_op jit(solution)/shard_map/ppermute | solution.py:619
  12.3 0.4 collective-permute-start.2
  12.8 0.7 pad_maximum_fusion.quad0_hbm
  13.5 1.2 collective-permute-done.1.quad2_hbm
  14.7 1.9 %collective-permute-done.2.quad3_hbm = bf16[108,512]{1,0:T(8,128)(2,1)S(1)} collective-permute-done((bf16[108,512]{1,0:T(8,128)(2,1)S(1)}, bf16[108,512]{1,0:T(8,128)(2,1)S(1)}, u32[]{:S(2)}, u32[]{:S(2)}) %collective-permute-start.2) | collective-permute-done | bytes 110624 | tf_op jit(solution)/shard_map/ppermute | solution.py:619
  16.6 0.6 copy-done.10
  17.2 25.8 %shard_map.189 = (bf16[72,1024]{1,0:T(8,128)(2,1)}, bf16[288,512]{1,0:T(8,128)(2,1)}, bf16[72,1536]{1,0:T(8,128)(2,1)}, bf16[72,1536]{1,0:T(8,128)(2,1)}, bf16[7...) custom-call(s32[1]{0:T(128)} %bitcast.where_ref, ...), custom_call_target="tpu_custom_call" | custom-call | flops 20000000000 | bytes 20000000 | tf_op jit(solution)/shard_map/pallas_call | solution.py:581
  43.2 2.5 %collective-permute-start.4 = (bf16[72,1536]{1,0:T(8,128)(2,1)}, bf16[72,1536]{1,0:T(8,128)(2,1)S(1)}, u32[]{:S(2)}, u32[]{:S(2)}) collective-permute-start(bf16[72,1536]{1,0:T(8,128)(2,1)} %get-tuple-element.64), channel_id=1, source_target_pairs={{0,8},{4,12},{8,0},{12,4},{1,9},{5,13},{9,1},{13,5},{2,10},{6,14},... | collective-permute-start | bytes 663560 | tf_op jit(solution)/shard_map/ppermute | solution.py:689
  45.7 1.2 collective-permute-start.5
  46.8 10.7 %shard_map.190 = (bf16[288,512]{1,0:T(8,128)(2,1)}, bf16[5,64,16,128]{3,2,1,0:T(8,128)(2,1)}, bf16[5,64,16,128]{3,2,1,0:T(8,128)(2,1)}) custom-call(s32[1]{0:T(128)} %bitcast.where_ref, bf16[288,512]{1,0:T(8,128)(2,1)} %get-tuple-element.56.grad_after_ref, bf16[288,512]{1,0:T(8,128)(2,1)} %get-tuple-element.57.middle_ref, ...), custom_call_target="tpu_custom_call" | custom-call | flops 7000000000 | bytes 7000000 | tf_op jit(solution)/shard_map/pallas_call | solution.py:581
  57.9 0.5 shard_map.191
  58.6 2.9 %collective-permute-start.10 = (bf16[64,16,128]{2,1,0:T(8,128)(2,1)S(1)}, bf16[64,16,128]{2,1,0:T(8,128)(2,1)S(1)}, u32[]{:S(2)}, u32[]{:S(2)}) collective-permute-start(bf16[64,16,128]{2,1,0:T(8,128)(2,1)S(1)} %get-tuple-element.87), channel_id=1, source_target_pairs={{0,64},{32,96},{64,0},{96,32},{1,65},{33,97},{65,1},{97,33},{2,66}... | collective-permute-start | bytes 786440 | tf_op jit(solution)/shard_map/ppermute | solution.py:705
  61.5 0.8 collective-permute-start.11
  62.3 0.6 shard_map.192
  62.9 0.8 collective-permute-start.12
  63.7 16.0 %shard_map.193 = (bf16[108,512]{1,0:T(8,128)(2,1)}, bf16[108,512]{1,0:T(8,128)(2,1)}, bf16[108,512]{1,0:T(8,128)(2,1)}, bf16[108,512]{1,0:T(8,128)(2,1)}, bf16[6...) custom-call(s32[1]{0:T(128)} %bitcast.where_ref, bf16[288,512]{1,0:T(8,128)(2,1)} %get-tuple-element.72.middle_grad_ref, ...), custom_call_target="tpu_custom_call" | custom-call | flops 12000000000 | bytes 12000000 | tf_op jit(solution)/shard_map/pallas_call | solution.py:581
  79.8 2.4 %collective-permute-start.13 = (bf16[108,512]{1,0:T(8,128)(2,1)}, bf16[108,512]{1,0:T(8,128)(2,1)S(1)}, u32[]{:S(2)}, u32[]{:S(2)}) collective-permute-start(bf16[108,512]{1,0:T(8,128)(2,1)} %get-tuple-element.91), channel_id=1, source_target_pairs={{0,17},{1,18},{2,19},{3,20},{4,21},{5,22},{6,23},{7,24},{8,25},{9,... | collective-permute-start | bytes 331784 | tf_op jit(solution)/shard_map/ppermute | solution.py:619
  82.2 1.0 collective-permute-start.14
  83.2 1.0 collective-permute-start.15
  84.1 1.5 %collective-permute-start.8 = (bf16[64,16,640]{2,1,0:T(8,128)(2,1)}, bf16[64,16,640]{2,1,0:T(8,128)(2,1)S(1)}, u32[]{:S(2)}, u32[]{:S(2)}) collective-permute-start(bf16[64,16,640]{2,1,0:T(8,128)(2,1)} %get-tuple-element.85), channel_id=1, source_target_pairs={{0,1},{1,0},{2,3},{3,2},{4,5},{5,4},{6,7},{7,6},{8,9},{9,8},{10,11... | collective-permute-start | bytes 3932168 | tf_op jit(solution)/shard_map/ppermute | solution.py:607
  85.6 0.6 shard_map.194.refs_0_
  86.2 2.3 %collective-permute-done.8.arrived_hbm = bf16[64,16,640]{2,1,0:T(8,128)(2,1)S(1)} collective-permute-done((bf16[64,16,640]{2,1,0:T(8,128)(2,1)}, bf16[64,16,640]{2,1,0:T(8,128)(2,1)S(1)}, u32[]{:S(2)}, u32[]{:S(2)}) %collective-permute-start.8) | collective-permute-done | bytes 1310752 | tf_op jit(solution)/shard_map/ppermute | solution.py:607
  88.5 1.4 %shard_map.195 = bf16[64,16,1152]{2,1,0:T(8,128)(2,1)S(1)} custom-call(bf16[64,16,640]{2,1,0:T(8,128)(2,1)S(1)} %copy-done.1, bf16[64,16,640]{2,1,0:T(8,128)(2,1)S(1)} %collective-permute-done.8.arrived_hbm, bf16[64,16,1152]{2,1,0:T(8,128)(2,1)S(1)} %shard_map.194.refs_0_), custom_call_target="tpu_custom_call", output_to_operand_aliasing={{}: (2, {})} | custom-call | flops 2000000000 | bytes 2000000 | tf_op jit(solution)/shard_map/pallas_call | solution.py:581
  89.9 1.4 %copy-done = bf16[64,16,1152]{2,1,0:T(8,128)(2,1)} copy-done((bf16[64,16,1152]{2,1,0:T(8,128)(2,1)}, bf16[64,16,1152]{2,1,0:T(8,128)(2,1)S(1)}, u32[]{:S(2)}) %copy-start) | copy-done | bytes 2359320
  91.3 8.0 %all-to-all-start = ((bf16[64,16,1152]{2,1,0:T(8,128)(2,1)}), bf16[64,16,1152]{2,1,0:T(8,128)(2,1)S(1)}, u32[]{:S(2)}, u32[]{:S(2)}) async-start(bf16[64,16,1152]{2,1,0:T(8,128)(2,1)} %copy-done), calls=%async_computation | async-start | bytes 4718592 | tf_op jit(solution)/shard_map/all_to_all | solution.py:740
  99.8 0.9 maximum_bitcast_fusion.1
  100.7 1.1 maximum_bitcast_fusion
  101.8 30.3 %all-to-all-done.landed_hbm = bf16[64,16,1152]{2,1,0:T(8,128)(2,1)S(1)} async-done(((bf16[64,16,1152]{2,1,0:T(8,128)(2,1)}), bf16[64,16,1152]{2,1,0:T(8,128)(2,1)S(1)}, u32[]{:S(2)}, u32[]{:S(2)}) %all-to-all-start) | async-done | bytes 2359328 | tf_op jit(solution)/shard_map/all_to_all | solution.py:740
  132.1 1.5 %shard_map.196 = (f32[4,1536]{1,0:T(4,128)}, f32[4,512]{1,0:T(4,128)}, f32[4,2048]{1,0:T(4,128)}, f32[16,512]{1,0:T(8,128)}, f32[16,1024]{1,0:T(8,128)}) custom-call(bf16[64,16,1152]{2,1,0:T(8,128)(2,1)S(1)} %all-to-all-done.landed_hbm), custom_call_target="tpu_custom_call" | custom-call | flops 3000000000 | bytes 3000000 | tf_op jit(solution)/shard_map/pallas_call | solution.py:581
  (70 shorter events, 1.4 us)
Async XLA Ops:
  2.9 10.6 %collective-permute-start = (bf16[108,512]{1,0:T(8,128)(2,1)S(1)}, bf16[108,512]{1,0:T(8,128)(2,1)S(1)}, u32[]{:S(2)}, u32[]{:S(2)}) collective-permute-start(bf16[108,512]{1,0:T(8,128)(2,1)S(1)} %pad_maximum_fusion.1), channel_id=1, source_target_pairs={{0,15},{1,0},{2,1},{3,2},{4,3},{5,4},{6,5},{7,6},{8,7},{9,8},{10,9... | collective-permute-start | bytes 331784 | tf_op jit(solution)/shard_map/ppermute | solution.py:619
  8.0 6.6 %collective-permute-start.1 = (bf16[108,512]{1,0:T(8,128)(2,1)S(1)}, bf16[108,512]{1,0:T(8,128)(2,1)S(1)}, u32[]{:S(2)}, u32[]{:S(2)}) collective-permute-start(bf16[108,512]{1,0:T(8,128)(2,1)S(1)} %pad_maximum_fusion.2), channel_id=1, source_target_pairs={{0,112},{1,113},{2,114},{3,115},{4,116},{5,117},{6,118},{7,119},{8... | collective-permute-start | bytes 331784 | tf_op jit(solution)/shard_map/ppermute | solution.py:619
  12.3 4.3 %collective-permute-start.2 = (bf16[108,512]{1,0:T(8,128)(2,1)S(1)}, bf16[108,512]{1,0:T(8,128)(2,1)S(1)}, u32[]{:S(2)}, u32[]{:S(2)}) collective-permute-start(bf16[108,512]{1,0:T(8,128)(2,1)S(1)} %pad_maximum_fusion.3), channel_id=1, source_target_pairs={{0,127},{1,112},{2,113},{3,114},{4,115},{5,116},{6,117},{7,118},{8... | collective-permute-start | bytes 331784 | tf_op jit(solution)/shard_map/ppermute | solution.py:619
  13.5 3.1 %copy-start.8 = (bf16[108,512]{1,0:T(8,128)(2,1)}, bf16[108,512]{1,0:T(8,128)(2,1)S(1)}, u32[]{:S(2)}) copy-start(bf16[108,512]{1,0:T(8,128)(2,1)S(1)} %collective-permute-done.quad1_hbm) | copy-start | bytes 331780
  14.7 1.9 %copy-start.9 = (bf16[108,512]{1,0:T(8,128)(2,1)}, bf16[108,512]{1,0:T(8,128)(2,1)S(1)}, u32[]{:S(2)}) copy-start(bf16[108,512]{1,0:T(8,128)(2,1)S(1)} %collective-permute-done.1.quad2_hbm) | copy-start | bytes 331780
  16.6 0.6 copy-start.10
  43.0 14.9 %collective-permute-start.6 = (bf16[4,64,16,128]{3,2,1,0:T(8,128)(2,1)}, bf16[4,64,16,128]{3,2,1,0:T(8,128)(2,1)S(1)}, u32[]{:S(2)}, u32[]{:S(2)}) collective-permute-start(bf16[4,64,16,128]{3,2,1,0:T(8,128)(2,1)} %get-tuple-element.67), channel_id=1, source_target_pairs={{0,1},{1,0},{2,3},{3,2},{4,5},{5,4},{6,7},{7,6},{8,9},{9,8},{10,11... | collective-permute-start | bytes 3145736 | tf_op jit(solution)/shard_map/ppermute | solution.py:607
  43.1 14.7 %collective-permute-start.3 = (bf16[72,1536]{1,0:T(8,128)(2,1)}, bf16[72,1536]{1,0:T(8,128)(2,1)S(1)}, u32[]{:S(2)}, u32[]{:S(2)}) collective-permute-start(bf16[72,1536]{1,0:T(8,128)(2,1)} %get-tuple-element.63), channel_id=1, source_target_pairs={{0,4},{4,8},{8,12},{12,0},{1,5},{5,9},{9,13},{13,1},{2,6},{6,10},{... | collective-permute-start | bytes 663560 | tf_op jit(solution)/shard_map/ppermute | solution.py:689
  43.2 14.6 %collective-permute-start.4 = (bf16[72,1536]{1,0:T(8,128)(2,1)}, bf16[72,1536]{1,0:T(8,128)(2,1)S(1)}, u32[]{:S(2)}, u32[]{:S(2)}) collective-permute-start(bf16[72,1536]{1,0:T(8,128)(2,1)} %get-tuple-element.64), channel_id=1, source_target_pairs={{0,8},{4,12},{8,0},{12,4},{1,9},{5,13},{9,1},{13,5},{2,10},{6,14},... | collective-permute-start | bytes 663560 | tf_op jit(solution)/shard_map/ppermute | solution.py:689
  45.7 12.2 %collective-permute-start.5 = (bf16[72,1536]{1,0:T(8,128)(2,1)}, bf16[72,1536]{1,0:T(8,128)(2,1)S(1)}, u32[]{:S(2)}, u32[]{:S(2)}) collective-permute-start(bf16[72,1536]{1,0:T(8,128)(2,1)} %get-tuple-element.65), channel_id=1, source_target_pairs={{0,12},{4,0},{8,4},{12,8},{1,13},{5,1},{9,5},{13,9},{2,14},{6,2},{... | collective-permute-start | bytes 663560 | tf_op jit(solution)/shard_map/ppermute | solution.py:689
  46.8 11.0 %copy-start.3 = (bf16[4,64,16,128]{3,2,1,0:T(8,128)(2,1)S(1)}, bf16[4,64,16,128]{3,2,1,0:T(8,128)(2,1)}, u32[]{:S(2)}) copy-start(bf16[4,64,16,128]{3,2,1,0:T(8,128)(2,1)} %get-tuple-element.66.keep_hbm) | copy-start | bytes 3145732
  57.5 4.8 %collective-permute-start.7 = (bf16[5,64,16,128]{3,2,1,0:T(8,128)(2,1)}, bf16[5,64,16,128]{3,2,1,0:T(8,128)(2,1)S(1)}, u32[]{:S(2)}, u32[]{:S(2)}) collective-permute-start(bf16[5,64,16,128]{3,2,1,0:T(8,128)(2,1)} %get-tuple-element.70), channel_id=1, source_target_pairs={{0,1},{1,0},{2,3},{3,2},{4,5},{5,4},{6,7},{7,6},{8,9},{9,8},{10,11... | collective-permute-start | bytes 3932168 | tf_op jit(solution)/shard_map/ppermute | solution.py:607
  57.8 0.7 copy-start.5
  57.8 0.7 copy-start.6
  57.8 0.8 copy-start.7
  57.8 4.4 %copy-start.2 = (bf16[5,64,16,128]{3,2,1,0:T(8,128)(2,1)S(1)}, bf16[5,64,16,128]{3,2,1,0:T(8,128)(2,1)}, u32[]{:S(2)}) copy-start(bf16[5,64,16,128]{3,2,1,0:T(8,128)(2,1)} %get-tuple-element.69.keep_hbm) | copy-start | bytes 3932164
  58.6 23.5 %collective-permute-start.9 = (bf16[64,16,128]{2,1,0:T(8,128)(2,1)S(1)}, bf16[64,16,128]{2,1,0:T(8,128)(2,1)S(1)}, u32[]{:S(2)}, u32[]{:S(2)}) collective-permute-start(bf16[64,16,128]{2,1,0:T(8,128)(2,1)S(1)} %get-tuple-element.86), channel_id=1, source_target_pairs={{0,32},{32,64},{64,96},{96,0},{1,33},{33,65},{65,97},{97,1},{2,34}... | collective-permute-start | bytes 786440 | tf_op jit(solution)/shard_map/ppermute | solution.py:705
  58.6 24.5 %collective-permute-start.10 = (bf16[64,16,128]{2,1,0:T(8,128)(2,1)S(1)}, bf16[64,16,128]{2,1,0:T(8,128)(2,1)S(1)}, u32[]{:S(2)}, u32[]{:S(2)}) collective-permute-start(bf16[64,16,128]{2,1,0:T(8,128)(2,1)S(1)} %get-tuple-element.87), channel_id=1, source_target_pairs={{0,64},{32,96},{64,0},{96,32},{1,65},{33,97},{65,1},{97,33},{2,66}... | collective-permute-start | bytes 786440 | tf_op jit(solution)/shard_map/ppermute | solution.py:705
  61.5 22.6 %collective-permute-start.11 = (bf16[64,16,128]{2,1,0:T(8,128)(2,1)S(1)}, bf16[64,16,128]{2,1,0:T(8,128)(2,1)S(1)}, u32[]{:S(2)}, u32[]{:S(2)}) collective-permute-start(bf16[64,16,128]{2,1,0:T(8,128)(2,1)S(1)} %get-tuple-element.88), channel_id=1, source_target_pairs={{0,96},{32,0},{64,32},{96,64},{1,97},{33,1},{65,33},{97,65},{2,98}... | collective-permute-start | bytes 786440 | tf_op jit(solution)/shard_map/ppermute | solution.py:705
  62.9 22.7 %collective-permute-start.12 = (bf16[64,16,256]{2,1,0:T(8,128)(2,1)S(1)}, bf16[64,16,256]{2,1,0:T(8,128)(2,1)S(1)}, u32[]{:S(2)}, u32[]{:S(2)}) collective-permute-start(bf16[64,16,256]{2,1,0:T(8,128)(2,1)S(1)} %get-tuple-element.89), channel_id=1, source_target_pairs={{0,4},{4,0},{8,12},{12,8},{1,5},{5,1},{9,13},{13,9},{2,6},{6,2},{1... | collective-permute-start | bytes 1572872 | tf_op jit(solution)/shard_map/ppermute | solution.py:710
  79.8 11.5 %collective-permute-start.13 = (bf16[108,512]{1,0:T(8,128)(2,1)}, bf16[108,512]{1,0:T(8,128)(2,1)S(1)}, u32[]{:S(2)}, u32[]{:S(2)}) collective-permute-start(bf16[108,512]{1,0:T(8,128)(2,1)} %get-tuple-element.91), channel_id=1, source_target_pairs={{0,17},{1,18},{2,19},{3,20},{4,21},{5,22},{6,23},{7,24},{8,25},{9,... | collective-permute-start | bytes 331784 | tf_op jit(solution)/shard_map/ppermute | solution.py:619
  82.2 9.1 %collective-permute-start.14 = (bf16[108,512]{1,0:T(8,128)(2,1)}, bf16[108,512]{1,0:T(8,128)(2,1)S(1)}, u32[]{:S(2)}, u32[]{:S(2)}) collective-permute-start(bf16[108,512]{1,0:T(8,128)(2,1)} %get-tuple-element.92), channel_id=1, source_target_pairs={{0,16},{1,17},{2,18},{3,19},{4,20},{5,21},{6,22},{7,23},{8,24},{9,... | collective-permute-start | bytes 331784 | tf_op jit(solution)/shard_map/ppermute | solution.py:619
  83.2 8.1 %collective-permute-start.15 = (bf16[108,512]{1,0:T(8,128)(2,1)}, bf16[108,512]{1,0:T(8,128)(2,1)S(1)}, u32[]{:S(2)}, u32[]{:S(2)}) collective-permute-start(bf16[108,512]{1,0:T(8,128)(2,1)} %get-tuple-element.93), channel_id=1, source_target_pairs={{0,1},{1,2},{2,3},{3,4},{4,5},{5,6},{6,7},{7,8},{8,9},{9,10},{10,1... | collective-permute-start | bytes 331784 | tf_op jit(solution)/shard_map/ppermute | solution.py:619
  84.1 4.4 %collective-permute-start.8 = (bf16[64,16,640]{2,1,0:T(8,128)(2,1)}, bf16[64,16,640]{2,1,0:T(8,128)(2,1)S(1)}, u32[]{:S(2)}, u32[]{:S(2)}) collective-permute-start(bf16[64,16,640]{2,1,0:T(8,128)(2,1)} %get-tuple-element.85), channel_id=1, source_target_pairs={{0,1},{1,0},{2,3},{3,2},{4,5},{5,4},{6,7},{7,6},{8,9},{9,8},{10,11... | collective-permute-start | bytes 3932168 | tf_op jit(solution)/shard_map/ppermute | solution.py:607
  85.6 2.9 %copy-start.1 = (bf16[64,16,640]{2,1,0:T(8,128)(2,1)S(1)}, bf16[64,16,640]{2,1,0:T(8,128)(2,1)}, u32[]{:S(2)}) copy-start(bf16[64,16,640]{2,1,0:T(8,128)(2,1)} %get-tuple-element.84.keep_hbm) | copy-start | bytes 3932164
  89.9 1.4 %copy-start = (bf16[64,16,1152]{2,1,0:T(8,128)(2,1)}, bf16[64,16,1152]{2,1,0:T(8,128)(2,1)S(1)}, u32[]{:S(2)}) copy-start(bf16[64,16,1152]{2,1,0:T(8,128)(2,1)S(1)} %shard_map.195) | copy-start | bytes 7077892
  91.3 8.3 %copy-start.4 = (bf16[108,512]{1,0:T(8,128)(2,1)S(1)}, bf16[108,512]{1,0:T(8,128)(2,1)}, u32[]{:S(2)}) copy-start(bf16[108,512]{1,0:T(8,128)(2,1)} %get-tuple-element.98) | copy-start | bytes 331780
  91.3 40.8 %all-to-all-start = ((bf16[64,16,1152]{2,1,0:T(8,128)(2,1)}), bf16[64,16,1152]{2,1,0:T(8,128)(2,1)S(1)}, u32[]{:S(2)}, u32[]{:S(2)}) async-start(bf16[64,16,1152]{2,1,0:T(8,128)(2,1)} %copy-done), calls=%async_computation | async-start | bytes 4718592 | tf_op jit(solution)/shard_map/all_to_all | solution.py:740

commit v14 on v12

--- a/solution.py
+++ b/solution.py
@@ -711,6 +711,7 @@
         free=range(7), weight=60,
         loose=True,
     )
+    blocks, *corners = lax.optimization_barrier((blocks, *corners))
     blocks, = call(
         functools.partial(pair_kernel, place=512),
         [late_keep, exchanged(late_send), blocks], 0, [blocks.shape], 0,

time: 127 us -> 125 us (0.984)
  starting transfers between devices: 31.3 us -> 28.5 us
  waiting for transfers between devices: 37.4 us -> 38.8 us
    ppermute x6, waiting for transfers between devices: 3.98 us -> 8.72 us  [shifted_block(): return lax.ppermute(block, GRID, route)]
    ppermute x3, waiting for transfers between devices: 2.26 us -> 0.01 us  [exchanged(): return lax.ppermute(send, 'core', [(0, 1), (1, 0)])]
    all_to_all x1, starting transfers between devices: 8.41 us -> 6.94 us  [body(): landed = lax.all_to_all(blocks, PAIRS, 0, 0, tiled=True)]
    ppermute x3, starting transfers between devices: 1.83 us -> 0.43 us  [exchanged(): return lax.ppermute(send, 'core', [(0, 1), (1, 0)])]
where the time goes in v14:
time: 125 us
  Pallas kernels  48.5 us (39%)
  waiting for transfers between devices  38.8 us (31%)
  starting transfers between devices  28.5 us (23%)
  local copies, waits for them, and re-layouts  5.19 us (4%)
  other arithmetic  2.74 us (2%)
  between operations  1.26 us (1%)
    pallas_call x8, Pallas kernels, call(): pl.pallas_call(kernel, out_shape=[jax.ShapeDtypeStruct(shape, kind) for s...  48.5 us
    all_to_all x1, waiting for transfers between devices, body(): landed = lax.all_to_all(blocks, PAIRS, 0, 0, tiled=True)  28.5 us
    ppermute x6, starting transfers between devices, shifted_block(): return lax.ppermute(block, GRID, route)  13 us
    ppermute x6, waiting for transfers between devices, shifted_block(): return lax.ppermute(block, GRID, route)  8.72 us
    all_to_all x1, starting transfers between devices, body(): landed = lax.all_to_all(blocks, PAIRS, 0, 0, tiled=True)  6.94 us
    ppermute x3, starting transfers between devices, body(): lax.ppermute(block, 'z', [(i, (i + step) % 4) for i in range(4)])  3.87 us
    ppermute x3, starting transfers between devices, body(): lax.ppermute(block, 'y', [(i, (i + step) % 4) for i in range(4)])  3.73 us
    unnamed x28, local copies, waits for them, and re-layouts  2.51 us
  transfers between devices with their start and end apart: 17, of which 8 were waited for; matrix products, arithmetic and copies ran while one was open for 3% of the time, Pallas kernels for 20%

profile of v14, /device:TPU:0, one launch (start us, length us, event | category | flops | bytes accessed | tf_op | source)
XLA Modules:
  0.0 125.1 jit_solution(6615713838509142570)
XLA Ops:
  0.6 0.9 fusion.1
  1.6 1.2 fusion
  2.9 5.1 %collective-permute-start = (bf16[108,512]{1,0:T(8,128)(2,1)S(1)}, bf16[108,512]{1,0:T(8,128)(2,1)S(1)}, u32[]{:S(2)}, u32[]{:S(2)}) collective-permute-start(bf16[108,512]{1,0:T(8,128)(2,1)S(1)} %pad_maximum_fusion.1), channel_id=1, source_target_pairs={{0,15},{1,0},{2,1},{3,2},{4,3},{5,4},{6,5},{7,6},{8,7},{9,8},{10,9... | collective-permute-start | bytes 331784 | tf_op jit(solution)/shard_map/ppermute | solution.py:601
  8.0 4.1 %collective-permute-start.1 = (bf16[108,512]{1,0:T(8,128)(2,1)S(1)}, bf16[108,512]{1,0:T(8,128)(2,1)S(1)}, u32[]{:S(2)}, u32[]{:S(2)}) collective-permute-start(bf16[108,512]{1,0:T(8,128)(2,1)S(1)} %pad_maximum_fusion.2), channel_id=1, source_target_pairs={{0,112},{1,113},{2,114},{3,115},{4,116},{5,117},{6,118},{7,119},{8... | collective-permute-start | bytes 331784 | tf_op jit(solution)/shard_map/ppermute | solution.py:601
  12.3 0.4 collective-permute-start.2
  12.8 0.7 pad_maximum_fusion.quad0_hbm
  13.5 1.2 collective-permute-done.1.quad2_hbm
  14.7 1.9 %collective-permute-done.2.quad3_hbm = bf16[108,512]{1,0:T(8,128)(2,1)S(1)} collective-permute-done((bf16[108,512]{1,0:T(8,128)(2,1)S(1)}, bf16[108,512]{1,0:T(8,128)(2,1)S(1)}, u32[]{:S(2)}, u32[]{:S(2)}) %collective-permute-start.2) | collective-permute-done | bytes 110624 | tf_op jit(solution)/shard_map/ppermute | solution.py:601
  16.6 0.6 copy-done.10
  17.2 21.9 %shard_map.189 = (bf16[72,1024]{1,0:T(8,128)(2,1)}, bf16[288,512]{1,0:T(8,128)(2,1)}, bf16[72,1536]{1,0:T(8,128)(2,1)}, bf16[72,1536]{1,0:T(8,128)(2,1)}, bf16[7...) custom-call(s32[1]{0:T(128)} %bitcast.where_ref, ...), custom_call_target="tpu_custom_call" | custom-call | flops 20000000000 | bytes 20000000 | tf_op jit(solution)/shard_map/pallas_call | solution.py:563
  39.5 2.5 %collective-permute-start.4 = (bf16[72,1536]{1,0:T(8,128)(2,1)}, bf16[72,1536]{1,0:T(8,128)(2,1)S(1)}, u32[]{:S(2)}, u32[]{:S(2)}) collective-permute-start(bf16[72,1536]{1,0:T(8,128)(2,1)} %get-tuple-element.69), channel_id=1, source_target_pairs={{0,8},{4,12},{8,0},{12,4},{1,9},{5,13},{9,1},{13,5},{2,10},{6,14},... | collective-permute-start | bytes 663560 | tf_op jit(solution)/shard_map/ppermute | solution.py:671
  42.0 1.2 collective-permute-start.5
  43.1 9.1 %shard_map.190 = (bf16[288,512]{1,0:T(8,128)(2,1)}, bf16[5,64,16,128]{3,2,1,0:T(8,128)(2,1)}, bf16[5,64,16,128]{3,2,1,0:T(8,128)(2,1)}) custom-call(s32[1]{0:T(128)} %bitcast.where_ref, bf16[288,512]{1,0:T(8,128)(2,1)} %get-tuple-element.61.grad_after_ref, bf16[288,512]{1,0:T(8,128)(2,1)} %get-tuple-element.62.middle_ref, ...), custom_call_target="tpu_custom_call" | custom-call | flops 7000000000 | bytes 7000000 | tf_op jit(solution)/shard_map/pallas_call | solution.py:563
  52.4 1.0 collective-permute-done.3.near1_hbm
  53.4 0.6 collective-permute-done.5.near3_hbm
  54.0 0.5 shard_map.191
  54.7 3.1 %collective-permute-start.10 = (bf16[64,16,128]{2,1,0:T(8,128)(2,1)S(1)}, bf16[64,16,128]{2,1,0:T(8,128)(2,1)S(1)}, u32[]{:S(2)}, u32[]{:S(2)}) collective-permute-start(bf16[64,16,128]{2,1,0:T(8,128)(2,1)S(1)} %get-tuple-element.92), channel_id=1, source_target_pairs={{0,64},{32,96},{64,0},{96,32},{1,65},{33,97},{65,1},{97,33},{2,66}... | collective-permute-start | bytes 786440 | tf_op jit(solution)/shard_map/ppermute | solution.py:687
  57.8 0.8 collective-permute-start.11
  58.6 0.6 shard_map.192
  59.2 0.5 collective-permute-start.12
  59.8 12.9 %shard_map.193 = (bf16[108,512]{1,0:T(8,128)(2,1)}, bf16[108,512]{1,0:T(8,128)(2,1)}, bf16[108,512]{1,0:T(8,128)(2,1)}, bf16[108,512]{1,0:T(8,128)(2,1)}, bf16[6...) custom-call(s32[1]{0:T(128)} %bitcast.where_ref, bf16[288,512]{1,0:T(8,128)(2,1)} %get-tuple-element.77.middle_grad_ref, ...), custom_call_target="tpu_custom_call" | custom-call | flops 12000000000 | bytes 12000000 | tf_op jit(solution)/shard_map/pallas_call | solution.py:563
  72.9 0.6 shard_map.194.refs_0_
  73.7 3.2 %collective-permute-start.13 = (bf16[108,512]{1,0:T(8,128)(2,1)S(1)}, bf16[108,512]{1,0:T(8,128)(2,1)S(1)}, u32[]{:S(2)}, u32[]{:S(2)}) collective-permute-start(bf16[108,512]{1,0:T(8,128)(2,1)S(1)} %copy-done.13), channel_id=1, source_target_pairs={{0,17},{1,18},{2,19},{3,20},{4,21},{5,22},{6,23},{7,24},{8,25},{9,... | collective-permute-start | bytes 331784 | tf_op jit(solution)/shard_map/ppermute | solution.py:601
  77.1 1.4 %shard_map.195 = bf16[64,16,1152]{2,1,0:T(8,128)(2,1)S(1)} custom-call(bf16[64,16,640]{2,1,0:T(8,128)(2,1)S(1)} %copy-done.1, bf16[64,16,640]{2,1,0:T(8,128)(2,1)S(1)} %collective-permute-done.8.arrived_hbm, bf16[64,16,1152]{2,1,0:T(8,128)(2,1)S(1)} %shard_map.194.refs_0_), custom_call_target="tpu_custom_call", output_to_operand_aliasing={{}: (2, {})} | custom-call | flops 2000000000 | bytes 2000000 | tf_op jit(solution)/shard_map/pallas_call | solution.py:563
  78.5 1.4 %copy-done = bf16[64,16,1152]{2,1,0:T(8,128)(2,1)} copy-done((bf16[64,16,1152]{2,1,0:T(8,128)(2,1)}, bf16[64,16,1152]{2,1,0:T(8,128)(2,1)S(1)}, u32[]{:S(2)}) %copy-start) | copy-done | bytes 2359320
  79.9 4.5 %collective-permute-done.13 = bf16[108,512]{1,0:T(8,128)(2,1)S(1)} collective-permute-done((bf16[108,512]{1,0:T(8,128)(2,1)S(1)}, bf16[108,512]{1,0:T(8,128)(2,1)S(1)}, u32[]{:S(2)}, u32[]{:S(2)}) %collective-permute-start.13) | collective-permute-done | bytes 110624 | tf_op jit(solution)/shard_map/ppermute | solution.py:601
  84.4 0.8 collective-permute-done.14
  85.5 6.9 %all-to-all-start = ((bf16[64,16,1152]{2,1,0:T(8,128)(2,1)}), bf16[64,16,1152]{2,1,0:T(8,128)(2,1)S(1)}, u32[]{:S(2)}, u32[]{:S(2)}) async-start(bf16[64,16,1152]{2,1,0:T(8,128)(2,1)} %copy-done), calls=%async_computation | async-start | bytes 4718592 | tf_op jit(solution)/shard_map/all_to_all | solution.py:723
  92.9 0.9 maximum_bitcast_fusion.1
  93.8 1.1 maximum_bitcast_fusion
  95.0 28.5 %all-to-all-done.landed_hbm = bf16[64,16,1152]{2,1,0:T(8,128)(2,1)S(1)} async-done(((bf16[64,16,1152]{2,1,0:T(8,128)(2,1)}), bf16[64,16,1152]{2,1,0:T(8,128)(2,1)S(1)}, u32[]{:S(2)}, u32[]{:S(2)}) %all-to-all-start) | async-done | bytes 2359328 | tf_op jit(solution)/shard_map/all_to_all | solution.py:723
  123.4 1.5 %shard_map.196 = (f32[4,1536]{1,0:T(4,128)}, f32[4,512]{1,0:T(4,128)}, f32[4,2048]{1,0:T(4,128)}, f32[16,512]{1,0:T(8,128)}, f32[16,1024]{1,0:T(8,128)}) custom-call(bf16[64,16,1152]{2,1,0:T(8,128)(2,1)S(1)} %all-to-all-done.landed_hbm), custom_call_target="tpu_custom_call" | custom-call | flops 3000000000 | bytes 3000000 | tf_op jit(solution)/shard_map/pallas_call | solution.py:563
  (76 shorter events, 2.1 us)
Async XLA Ops:
  2.9 10.6 %collective-permute-start = (bf16[108,512]{1,0:T(8,128)(2,1)S(1)}, bf16[108,512]{1,0:T(8,128)(2,1)S(1)}, u32[]{:S(2)}, u32[]{:S(2)}) collective-permute-start(bf16[108,512]{1,0:T(8,128)(2,1)S(1)} %pad_maximum_fusion.1), channel_id=1, source_target_pairs={{0,15},{1,0},{2,1},{3,2},{4,3},{5,4},{6,5},{7,6},{8,7},{9,8},{10,9... | collective-permute-start | bytes 331784 | tf_op jit(solution)/shard_map/ppermute | solution.py:601
  8.0 6.6 %collective-permute-start.1 = (bf16[108,512]{1,0:T(8,128)(2,1)S(1)}, bf16[108,512]{1,0:T(8,128)(2,1)S(1)}, u32[]{:S(2)}, u32[]{:S(2)}) collective-permute-start(bf16[108,512]{1,0:T(8,128)(2,1)S(1)} %pad_maximum_fusion.2), channel_id=1, source_target_pairs={{0,112},{1,113},{2,114},{3,115},{4,116},{5,117},{6,118},{7,119},{8... | collective-permute-start | bytes 331784 | tf_op jit(solution)/shard_map/ppermute | solution.py:601
  12.3 4.3 %collective-permute-start.2 = (bf16[108,512]{1,0:T(8,128)(2,1)S(1)}, bf16[108,512]{1,0:T(8,128)(2,1)S(1)}, u32[]{:S(2)}, u32[]{:S(2)}) collective-permute-start(bf16[108,512]{1,0:T(8,128)(2,1)S(1)} %pad_maximum_fusion.3), channel_id=1, source_target_pairs={{0,127},{1,112},{2,113},{3,114},{4,115},{5,116},{6,117},{7,118},{8... | collective-permute-start | bytes 331784 | tf_op jit(solution)/shard_map/ppermute | solution.py:601
  13.5 3.1 %copy-start.8 = (bf16[108,512]{1,0:T(8,128)(2,1)}, bf16[108,512]{1,0:T(8,128)(2,1)S(1)}, u32[]{:S(2)}) copy-start(bf16[108,512]{1,0:T(8,128)(2,1)S(1)} %collective-permute-done.quad1_hbm) | copy-start | bytes 331780
  14.7 1.9 %copy-start.9 = (bf16[108,512]{1,0:T(8,128)(2,1)}, bf16[108,512]{1,0:T(8,128)(2,1)S(1)}, u32[]{:S(2)}) copy-start(bf16[108,512]{1,0:T(8,128)(2,1)S(1)} %collective-permute-done.1.quad2_hbm) | copy-start | bytes 331780
  16.6 0.6 copy-start.10
  39.1 14.9 %collective-permute-start.6 = (bf16[4,64,16,128]{3,2,1,0:T(8,128)(2,1)}, bf16[4,64,16,128]{3,2,1,0:T(8,128)(2,1)S(1)}, u32[]{:S(2)}, u32[]{:S(2)}) collective-permute-start(bf16[4,64,16,128]{3,2,1,0:T(8,128)(2,1)} %get-tuple-element.72), channel_id=1, source_target_pairs={{0,1},{1,0},{2,3},{3,2},{4,5},{5,4},{6,7},{7,6},{8,9},{9,8},{10,11... | collective-permute-start | bytes 3145736 | tf_op jit(solution)/shard_map/ppermute | solution.py:589
  39.4 14.0 %collective-permute-start.3 = (bf16[72,1536]{1,0:T(8,128)(2,1)}, bf16[72,1536]{1,0:T(8,128)(2,1)S(1)}, u32[]{:S(2)}, u32[]{:S(2)}) collective-permute-start(bf16[72,1536]{1,0:T(8,128)(2,1)} %get-tuple-element.68), channel_id=1, source_target_pairs={{0,4},{4,8},{8,12},{12,0},{1,5},{5,9},{9,13},{13,1},{2,6},{6,10},{... | collective-permute-start | bytes 663560 | tf_op jit(solution)/shard_map/ppermute | solution.py:671
  39.5 13.9 %collective-permute-start.4 = (bf16[72,1536]{1,0:T(8,128)(2,1)}, bf16[72,1536]{1,0:T(8,128)(2,1)S(1)}, u32[]{:S(2)}, u32[]{:S(2)}) collective-permute-start(bf16[72,1536]{1,0:T(8,128)(2,1)} %get-tuple-element.69), channel_id=1, source_target_pairs={{0,8},{4,12},{8,0},{12,4},{1,9},{5,13},{9,1},{13,5},{2,10},{6,14},... | collective-permute-start | bytes 663560 | tf_op jit(solution)/shard_map/ppermute | solution.py:671
  42.0 12.1 %collective-permute-start.5 = (bf16[72,1536]{1,0:T(8,128)(2,1)}, bf16[72,1536]{1,0:T(8,128)(2,1)S(1)}, u32[]{:S(2)}, u32[]{:S(2)}) collective-permute-start(bf16[72,1536]{1,0:T(8,128)(2,1)} %get-tuple-element.70), channel_id=1, source_target_pairs={{0,12},{4,0},{8,4},{12,8},{1,13},{5,1},{9,5},{13,9},{2,14},{6,2},{... | collective-permute-start | bytes 663560 | tf_op jit(solution)/shard_map/ppermute | solution.py:671
  43.1 10.9 %copy-start.3 = (bf16[4,64,16,128]{3,2,1,0:T(8,128)(2,1)S(1)}, bf16[4,64,16,128]{3,2,1,0:T(8,128)(2,1)}, u32[]{:S(2)}) copy-start(bf16[4,64,16,128]{3,2,1,0:T(8,128)(2,1)} %get-tuple-element.71.keep_hbm) | copy-start | bytes 3145732
  52.3 6.3 %collective-permute-start.7 = (bf16[5,64,16,128]{3,2,1,0:T(8,128)(2,1)}, bf16[5,64,16,128]{3,2,1,0:T(8,128)(2,1)S(1)}, u32[]{:S(2)}, u32[]{:S(2)}) collective-permute-start(bf16[5,64,16,128]{3,2,1,0:T(8,128)(2,1)} %get-tuple-element.75), channel_id=1, source_target_pairs={{0,1},{1,0},{2,3},{3,2},{4,5},{5,4},{6,7},{7,6},{8,9},{9,8},{10,11... | collective-permute-start | bytes 3932168 | tf_op jit(solution)/shard_map/ppermute | solution.py:589
  53.4 1.1 copy-start.5
  53.4 1.1 copy-start.6
  54.0 0.7 copy-start.7
  54.0 4.6 %copy-start.2 = (bf16[5,64,16,128]{3,2,1,0:T(8,128)(2,1)S(1)}, bf16[5,64,16,128]{3,2,1,0:T(8,128)(2,1)}, u32[]{:S(2)}) copy-start(bf16[5,64,16,128]{3,2,1,0:T(8,128)(2,1)} %get-tuple-element.74.keep_hbm) | copy-start | bytes 3932164
  54.7 18.1 %collective-permute-start.9 = (bf16[64,16,128]{2,1,0:T(8,128)(2,1)S(1)}, bf16[64,16,128]{2,1,0:T(8,128)(2,1)S(1)}, u32[]{:S(2)}, u32[]{:S(2)}) collective-permute-start(bf16[64,16,128]{2,1,0:T(8,128)(2,1)S(1)} %get-tuple-element.91), channel_id=1, source_target_pairs={{0,32},{32,64},{64,96},{96,0},{1,33},{33,65},{65,97},{97,1},{2,34}... | collective-permute-start | bytes 786440 | tf_op jit(solution)/shard_map/ppermute | solution.py:687
  54.7 18.1 %collective-permute-start.10 = (bf16[64,16,128]{2,1,0:T(8,128)(2,1)S(1)}, bf16[64,16,128]{2,1,0:T(8,128)(2,1)S(1)}, u32[]{:S(2)}, u32[]{:S(2)}) collective-permute-start(bf16[64,16,128]{2,1,0:T(8,128)(2,1)S(1)} %get-tuple-element.92), channel_id=1, source_target_pairs={{0,64},{32,96},{64,0},{96,32},{1,65},{33,97},{65,1},{97,33},{2,66}... | collective-permute-start | bytes 786440 | tf_op jit(solution)/shard_map/ppermute | solution.py:687
  57.8 15.0 %collective-permute-start.11 = (bf16[64,16,128]{2,1,0:T(8,128)(2,1)S(1)}, bf16[64,16,128]{2,1,0:T(8,128)(2,1)S(1)}, u32[]{:S(2)}, u32[]{:S(2)}) collective-permute-start(bf16[64,16,128]{2,1,0:T(8,128)(2,1)S(1)} %get-tuple-element.93), channel_id=1, source_target_pairs={{0,96},{32,0},{64,32},{96,64},{1,97},{33,1},{65,33},{97,65},{2,98}... | collective-permute-start | bytes 786440 | tf_op jit(solution)/shard_map/ppermute | solution.py:687
  59.2 13.6 %collective-permute-start.12 = (bf16[64,16,256]{2,1,0:T(8,128)(2,1)S(1)}, bf16[64,16,256]{2,1,0:T(8,128)(2,1)S(1)}, u32[]{:S(2)}, u32[]{:S(2)}) collective-permute-start(bf16[64,16,256]{2,1,0:T(8,128)(2,1)S(1)} %get-tuple-element.94), channel_id=1, source_target_pairs={{0,4},{4,0},{8,12},{12,8},{1,5},{5,1},{9,13},{13,9},{2,6},{6,2},{1... | collective-permute-start | bytes 1572872 | tf_op jit(solution)/shard_map/ppermute | solution.py:692
  72.7 4.4 %collective-permute-start.8 = (bf16[64,16,640]{2,1,0:T(8,128)(2,1)}, bf16[64,16,640]{2,1,0:T(8,128)(2,1)S(1)}, u32[]{:S(2)}, u32[]{:S(2)}) collective-permute-start(bf16[64,16,640]{2,1,0:T(8,128)(2,1)} %get-tuple-element.90), channel_id=1, source_target_pairs={{0,1},{1,0},{2,3},{3,2},{4,5},{5,4},{6,7},{7,6},{8,9},{9,8},{10,11... | collective-permute-start | bytes 3932168 | tf_op jit(solution)/shard_map/ppermute | solution.py:589
  72.8 0.9 copy-start.13
  72.8 4.1 %copy-start.12 = (bf16[108,512]{1,0:T(8,128)(2,1)S(1)}, bf16[108,512]{1,0:T(8,128)(2,1)}, u32[]{:S(2)}) copy-start(bf16[108,512]{1,0:T(8,128)(2,1)} %get-tuple-element.102) | copy-start | bytes 331780
  72.8 4.1 %copy-start.11 = (bf16[108,512]{1,0:T(8,128)(2,1)S(1)}, bf16[108,512]{1,0:T(8,128)(2,1)}, u32[]{:S(2)}) copy-start(bf16[108,512]{1,0:T(8,128)(2,1)} %get-tuple-element.103) | copy-start | bytes 331780
  72.8 4.2 %copy-start.1 = (bf16[64,16,640]{2,1,0:T(8,128)(2,1)S(1)}, bf16[64,16,640]{2,1,0:T(8,128)(2,1)}, u32[]{:S(2)}) copy-start(bf16[64,16,640]{2,1,0:T(8,128)(2,1)} %get-tuple-element.89.keep_hbm) | copy-start | bytes 3932164
  73.7 10.7 %collective-permute-start.13 = (bf16[108,512]{1,0:T(8,128)(2,1)S(1)}, bf16[108,512]{1,0:T(8,128)(2,1)S(1)}, u32[]{:S(2)}, u32[]{:S(2)}) collective-permute-start(bf16[108,512]{1,0:T(8,128)(2,1)S(1)} %copy-done.13), channel_id=1, source_target_pairs={{0,17},{1,18},{2,19},{3,20},{4,21},{5,22},{6,23},{7,24},{8,25},{9,... | collective-permute-start | bytes 331784 | tf_op jit(solution)/shard_map/ppermute | solution.py:601
  76.9 8.3 %collective-permute-start.14 = (bf16[108,512]{1,0:T(8,128)(2,1)S(1)}, bf16[108,512]{1,0:T(8,128)(2,1)S(1)}, u32[]{:S(2)}, u32[]{:S(2)}) collective-permute-start(bf16[108,512]{1,0:T(8,128)(2,1)S(1)} %copy-done.12), channel_id=1, source_target_pairs={{0,16},{1,17},{2,18},{3,19},{4,20},{5,21},{6,22},{7,23},{8,24},{9,... | collective-permute-start | bytes 331784 | tf_op jit(solution)/shard_map/ppermute | solution.py:601
  76.9 8.6 %collective-permute-start.15 = (bf16[108,512]{1,0:T(8,128)(2,1)S(1)}, bf16[108,512]{1,0:T(8,128)(2,1)S(1)}, u32[]{:S(2)}, u32[]{:S(2)}) collective-permute-start(bf16[108,512]{1,0:T(8,128)(2,1)S(1)} %copy-done.11), channel_id=1, source_target_pairs={{0,1},{1,2},{2,3},{3,4},{4,5},{5,6},{6,7},{7,8},{8,9},{9,10},{10,1... | collective-permute-start | bytes 331784 | tf_op jit(solution)/shard_map/ppermute | solution.py:601
  78.5 1.4 %copy-start = (bf16[64,16,1152]{2,1,0:T(8,128)(2,1)}, bf16[64,16,1152]{2,1,0:T(8,128)(2,1)S(1)}, u32[]{:S(2)}) copy-start(bf16[64,16,1152]{2,1,0:T(8,128)(2,1)S(1)} %shard_map.195) | copy-start | bytes 7077892
  79.9 12.8 %copy-start.4 = (bf16[108,512]{1,0:T(8,128)(2,1)S(1)}, bf16[108,512]{1,0:T(8,128)(2,1)}, u32[]{:S(2)}) copy-start(bf16[108,512]{1,0:T(8,128)(2,1)} %get-tuple-element.108) | copy-start | bytes 331780
  85.5 37.9 %all-to-all-start = ((bf16[64,16,1152]{2,1,0:T(8,128)(2,1)}), bf16[64,16,1152]{2,1,0:T(8,128)(2,1)S(1)}, u32[]{:S(2)}, u32[]{:S(2)}) async-start(bf16[64,16,1152]{2,1,0:T(8,128)(2,1)} %copy-done), calls=%async_computation | async-start | bytes 4718592 | tf_op jit(solution)/shard_map/all_to_all | solution.py:723

commit v15 on v14

--- a/solution.py
+++ b/solution.py
@@ -719,7 +719,6 @@
         aliases={2: 0}, loose=True,
     )
     corners = send_forth(corners)
-    blocks, *corners = lax.optimization_barrier((blocks, *corners))
     landed = lax.all_to_all(blocks, PAIRS, 0, 0, tiled=True)
     grad_qkv, grad_out, grad_up, grad_down, grad_merge = call(
         share_kernel, [landed], 0, [(4, 1536), (4, 512), (4, 2048), (16, 512), (16, 1024)], 5,

time: 125 us -> 129 us (1.032)
  starting transfers between devices: 28.5 us -> 31.2 us
  waiting for transfers between devices: 38.8 us -> 40.2 us
    all_to_all x1, waiting for transfers between devices: 28.5 us -> 0.01 us  [body(): landed = lax.all_to_all(blocks, PAIRS, 0, 0, tiled=True)]
    ppermute x6, waiting for transfers between devices: 8.72 us -> 36 us  [shifted_block(): return lax.ppermute(block, GRID, route)]
    ppermute x3, waiting for transfers between devices: 0.01 us -> 2.57 us  [exchanged(): return lax.ppermute(send, 'core', [(0, 1), (1, 0)])]
    all_to_all x1, starting transfers between devices: 6.94 us -> 9.09 us  [body(): landed = lax.all_to_all(blocks, PAIRS, 0, 0, tiled=True)]
  transfers between devices with their start and end apart: 17 -> 17, of which waited for: 8 -> 7; matrix products, arithmetic and copies ran while one was open for 3% -> 2% of each run, Pallas kernels for 20% -> 18%
where the time goes in v15:
time: 129 us
  Pallas kernels  48.5 us (38%)
  waiting for transfers between devices  40.2 us (31%)
  starting transfers between devices  31.2 us (24%)
  local copies, waits for them, and re-layouts  4.97 us (4%)
  other arithmetic  2.75 us (2%)
    pallas_call x8, Pallas kernels, call(): pl.pallas_call(kernel, out_shape=[jax.ShapeDtypeStruct(shape, kind) for s...  48.5 us
    ppermute x6, waiting for transfers between devices, shifted_block(): return lax.ppermute(block, GRID, route)  36 us
    ppermute x6, starting transfers between devices, shifted_block(): return lax.ppermute(block, GRID, route)  13.5 us
    all_to_all x1, starting transfers between devices, body(): landed = lax.all_to_all(blocks, PAIRS, 0, 0, tiled=True)  9.09 us
    ppermute x3, starting transfers between devices, body(): lax.ppermute(block, 'z', [(i, (i + step) % 4) for i in range(4)])  3.87 us
    ppermute x3, starting transfers between devices, body(): lax.ppermute(block, 'y', [(i, (i + step) % 4) for i in range(4)])  3.73 us
  transfers between devices with their start and end apart: 17, of which 7 were waited for; matrix products, arithmetic and copies ran while one was open for 2% of the time, Pallas kernels for 18%

profile of v15, /device:TPU:0, one launch (start us, length us, event | category | flops | bytes accessed | tf_op | source)
XLA Modules:
  0.0 128.9 jit_solution(3386735909479978904)
XLA Ops:
  0.6 0.9 fusion.1
  1.6 1.2 fusion
  2.9 5.1 %collective-permute-start = (bf16[108,512]{1,0:T(8,128)(2,1)S(1)}, bf16[108,512]{1,0:T(8,128)(2,1)S(1)}, u32[]{:S(2)}, u32[]{:S(2)}) collective-permute-start(bf16[108,512]{1,0:T(8,128)(2,1)S(1)} %pad_maximum_fusion.1), channel_id=1, source_target_pairs={{0,15},{1,0},{2,1},{3,2},{4,3},{5,4},{6,5},{7,6},{8,7},{9,8},{10,9... | collective-permute-start | bytes 331784 | tf_op jit(solution)/shard_map/ppermute | solution.py:601
  8.0 4.1 %collective-permute-start.1 = (bf16[108,512]{1,0:T(8,128)(2,1)S(1)}, bf16[108,512]{1,0:T(8,128)(2,1)S(1)}, u32[]{:S(2)}, u32[]{:S(2)}) collective-permute-start(bf16[108,512]{1,0:T(8,128)(2,1)S(1)} %pad_maximum_fusion.2), channel_id=1, source_target_pairs={{0,112},{1,113},{2,114},{3,115},{4,116},{5,117},{6,118},{7,119},{8... | collective-permute-start | bytes 331784 | tf_op jit(solution)/shard_map/ppermute | solution.py:601
  12.8 0.7 pad_maximum_fusion.quad0_hbm
  13.5 1.2 collective-permute-done.1.quad2_hbm
  14.7 1.9 %collective-permute-done.2.quad3_hbm = bf16[108,512]{1,0:T(8,128)(2,1)S(1)} collective-permute-done((bf16[108,512]{1,0:T(8,128)(2,1)S(1)}, bf16[108,512]{1,0:T(8,128)(2,1)S(1)}, u32[]{:S(2)}, u32[]{:S(2)}) %collective-permute-start.2) | collective-permute-done | bytes 110624 | tf_op jit(solution)/shard_map/ppermute | solution.py:601
  16.6 0.6 copy-done.13
  17.2 21.9 %shard_map.189 = (bf16[72,1024]{1,0:T(8,128)(2,1)}, bf16[288,512]{1,0:T(8,128)(2,1)}, bf16[72,1536]{1,0:T(8,128)(2,1)}, bf16[72,1536]{1,0:T(8,128)(2,1)}, bf16[7...) custom-call(s32[1]{0:T(128)} %bitcast.where_ref, ...), custom_call_target="tpu_custom_call" | custom-call | flops 20000000000 | bytes 20000000 | tf_op jit(solution)/shard_map/pallas_call | solution.py:563
  39.5 2.5 %collective-permute-start.4 = (bf16[72,1536]{1,0:T(8,128)(2,1)}, bf16[72,1536]{1,0:T(8,128)(2,1)S(1)}, u32[]{:S(2)}, u32[]{:S(2)}) collective-permute-start(bf16[72,1536]{1,0:T(8,128)(2,1)} %get-tuple-element.59), channel_id=1, source_target_pairs={{0,8},{4,12},{8,0},{12,4},{1,9},{5,13},{9,1},{13,5},{2,10},{6,14},... | collective-permute-start | bytes 663560 | tf_op jit(solution)/shard_map/ppermute | solution.py:671
  42.0 1.2 collective-permute-start.5
  43.1 9.1 %shard_map.191 = (bf16[288,512]{1,0:T(8,128)(2,1)}, bf16[5,64,16,128]{3,2,1,0:T(8,128)(2,1)}, bf16[5,64,16,128]{3,2,1,0:T(8,128)(2,1)}) custom-call(s32[1]{0:T(128)} %bitcast.where_ref, bf16[288,512]{1,0:T(8,128)(2,1)} %get-tuple-element.67.grad_after_ref, bf16[288,512]{1,0:T(8,128)(2,1)} %get-tuple-element.68.middle_ref, ...), custom_call_target="tpu_custom_call" | custom-call | flops 7000000000 | bytes 7000000 | tf_op jit(solution)/shard_map/pallas_call | solution.py:563
  52.4 1.0 collective-permute-done.3.near1_hbm
  53.4 0.6 collective-permute-done.5.near3_hbm
  54.7 3.1 %collective-permute-start.8 = (bf16[64,16,128]{2,1,0:T(8,128)(2,1)S(1)}, bf16[64,16,128]{2,1,0:T(8,128)(2,1)S(1)}, u32[]{:S(2)}, u32[]{:S(2)}) collective-permute-start(bf16[64,16,128]{2,1,0:T(8,128)(2,1)S(1)} %get-tuple-element.65), channel_id=1, source_target_pairs={{0,64},{32,96},{64,0},{96,32},{1,65},{33,97},{65,1},{97,33},{2,66}... | collective-permute-start | bytes 786440 | tf_op jit(solution)/shard_map/ppermute | solution.py:687
  57.8 0.8 collective-permute-start.9
  58.6 0.6 shard_map.192
  59.2 0.5 collective-permute-start.11
  59.8 12.9 %shard_map.194 = (bf16[108,512]{1,0:T(8,128)(2,1)}, bf16[108,512]{1,0:T(8,128)(2,1)}, bf16[108,512]{1,0:T(8,128)(2,1)}, bf16[108,512]{1,0:T(8,128)(2,1)}, bf16[6...) custom-call(s32[1]{0:T(128)} %bitcast.where_ref, bf16[288,512]{1,0:T(8,128)(2,1)} %get-tuple-element.77.middle_grad_ref, ...), custom_call_target="tpu_custom_call" | custom-call | flops 12000000000 | bytes 12000000 | tf_op jit(solution)/shard_map/pallas_call | solution.py:563
  72.8 0.6 shard_map.193.refs_0_
  73.4 2.6 %collective-permute-done.15.arrived_hbm = bf16[64,16,640]{2,1,0:T(8,128)(2,1)S(1)} collective-permute-done((bf16[64,16,640]{2,1,0:T(8,128)(2,1)}, bf16[64,16,640]{2,1,0:T(8,128)(2,1)S(1)}, u32[]{:S(2)}, u32[]{:S(2)}) %collective-permute-start.15) | collective-permute-done | bytes 1310752 | tf_op jit(solution)/shard_map/ppermute | solution.py:589
  76.0 1.4 %shard_map.195 = bf16[64,16,1152]{2,1,0:T(8,128)(2,1)S(1)} custom-call(bf16[64,16,640]{2,1,0:T(8,128)(2,1)S(1)} %copy-done.1, bf16[64,16,640]{2,1,0:T(8,128)(2,1)S(1)} %collective-permute-done.15.arrived_hbm, bf16[64,16,1152]{2,1,0:T(8,128)(2,1)S(1)} %shard_map.193.refs_0_), custom_call_target="tpu_custom_call", output_to_operand_aliasing={{}: (2, {})} | custom-call | flops 2000000000 | bytes 2000000 | tf_op jit(solution)/shard_map/pallas_call | solution.py:563
  77.4 1.4 %copy-done = bf16[64,16,1152]{2,1,0:T(8,128)(2,1)} copy-done((bf16[64,16,1152]{2,1,0:T(8,128)(2,1)}, bf16[64,16,1152]{2,1,0:T(8,128)(2,1)S(1)}, u32[]{:S(2)}) %copy-start) | copy-done | bytes 2359320
  78.8 9.1 %all-to-all-start = ((bf16[64,16,1152]{2,1,0:T(8,128)(2,1)}), bf16[64,16,1152]{2,1,0:T(8,128)(2,1)S(1)}, u32[]{:S(2)}, u32[]{:S(2)}) async-start(bf16[64,16,1152]{2,1,0:T(8,128)(2,1)} %copy-done), calls=%async_computation | async-start | bytes 4718592 | tf_op jit(solution)/shard_map/all_to_all | solution.py:722
  88.0 0.8 collective-permute-start.12
  88.9 1.5 %collective-permute-start.13 = (bf16[108,512]{1,0:T(8,128)(2,1)S(1)}, bf16[108,512]{1,0:T(8,128)(2,1)S(1)}, u32[]{:S(2)}, u32[]{:S(2)}) collective-permute-start(bf16[108,512]{1,0:T(8,128)(2,1)S(1)} %copy-done.10), channel_id=1, source_target_pairs={{0,16},{1,17},{2,18},{3,19},{4,20},{5,21},{6,22},{7,23},{8,24},{9,... | collective-permute-start | bytes 331784 | tf_op jit(solution)/shard_map/ppermute | solution.py:601
  90.4 1.6 %collective-permute-start.14 = (bf16[108,512]{1,0:T(8,128)(2,1)S(1)}, bf16[108,512]{1,0:T(8,128)(2,1)S(1)}, u32[]{:S(2)}, u32[]{:S(2)}) collective-permute-start(bf16[108,512]{1,0:T(8,128)(2,1)S(1)} %copy-done.8), channel_id=1, source_target_pairs={{0,1},{1,2},{2,3},{3,4},{4,5},{5,6},{6,7},{7,8},{8,9},{9,10},{10,1... | collective-permute-start | bytes 331784 | tf_op jit(solution)/shard_map/ppermute | solution.py:601
  92.0 31.7 %collective-permute-done.12 = bf16[108,512]{1,0:T(8,128)(2,1)S(1)} collective-permute-done((bf16[108,512]{1,0:T(8,128)(2,1)S(1)}, bf16[108,512]{1,0:T(8,128)(2,1)S(1)}, u32[]{:S(2)}, u32[]{:S(2)}) %collective-permute-start.12) | collective-permute-done | bytes 110624 | tf_op jit(solution)/shard_map/ppermute | solution.py:601
  123.8 1.2 collective-permute-done.13
  125.2 0.9 maximum_bitcast_fusion.1
  126.1 1.1 maximum_bitcast_fusion
  127.2 1.5 %shard_map.196 = (f32[4,1536]{1,0:T(4,128)}, f32[4,512]{1,0:T(4,128)}, f32[4,2048]{1,0:T(4,128)}, f32[16,512]{1,0:T(8,128)}, f32[16,1024]{1,0:T(8,128)}) custom-call(bf16[64,16,1152]{2,1,0:T(8,128)(2,1)S(1)} %all-to-all-done.landed_hbm), custom_call_target="tpu_custom_call" | custom-call | flops 3000000000 | bytes 3000000 | tf_op jit(solution)/shard_map/pallas_call | solution.py:563
  (78 shorter events, 2.3 us)
Async XLA Ops:
  2.9 10.6 %collective-permute-start = (bf16[108,512]{1,0:T(8,128)(2,1)S(1)}, bf16[108,512]{1,0:T(8,128)(2,1)S(1)}, u32[]{:S(2)}, u32[]{:S(2)}) collective-permute-start(bf16[108,512]{1,0:T(8,128)(2,1)S(1)} %pad_maximum_fusion.1), channel_id=1, source_target_pairs={{0,15},{1,0},{2,1},{3,2},{4,3},{5,4},{6,5},{7,6},{8,7},{9,8},{10,9... | collective-permute-start | bytes 331784 | tf_op jit(solution)/shard_map/ppermute | solution.py:601
  8.0 6.6 %collective-permute-start.1 = (bf16[108,512]{1,0:T(8,128)(2,1)S(1)}, bf16[108,512]{1,0:T(8,128)(2,1)S(1)}, u32[]{:S(2)}, u32[]{:S(2)}) collective-permute-start(bf16[108,512]{1,0:T(8,128)(2,1)S(1)} %pad_maximum_fusion.2), channel_id=1, source_target_pairs={{0,112},{1,113},{2,114},{3,115},{4,116},{5,117},{6,118},{7,119},{8... | collective-permute-start | bytes 331784 | tf_op jit(solution)/shard_map/ppermute | solution.py:601
  12.3 4.3 %collective-permute-start.2 = (bf16[108,512]{1,0:T(8,128)(2,1)S(1)}, bf16[108,512]{1,0:T(8,128)(2,1)S(1)}, u32[]{:S(2)}, u32[]{:S(2)}) collective-permute-start(bf16[108,512]{1,0:T(8,128)(2,1)S(1)} %pad_maximum_fusion.3), channel_id=1, source_target_pairs={{0,127},{1,112},{2,113},{3,114},{4,115},{5,116},{6,117},{7,118},{8... | collective-permute-start | bytes 331784 | tf_op jit(solution)/shard_map/ppermute | solution.py:601
  13.5 3.1 %copy-start.9 = (bf16[108,512]{1,0:T(8,128)(2,1)}, bf16[108,512]{1,0:T(8,128)(2,1)S(1)}, u32[]{:S(2)}) copy-start(bf16[108,512]{1,0:T(8,128)(2,1)S(1)} %collective-permute-done.quad1_hbm) | copy-start | bytes 331780
  14.7 1.9 %copy-start.11 = (bf16[108,512]{1,0:T(8,128)(2,1)}, bf16[108,512]{1,0:T(8,128)(2,1)S(1)}, u32[]{:S(2)}) copy-start(bf16[108,512]{1,0:T(8,128)(2,1)S(1)} %collective-permute-done.1.quad2_hbm) | copy-start | bytes 331780
  16.6 0.6 copy-start.13
  39.1 14.9 %collective-permute-start.6 = (bf16[4,64,16,128]{3,2,1,0:T(8,128)(2,1)}, bf16[4,64,16,128]{3,2,1,0:T(8,128)(2,1)S(1)}, u32[]{:S(2)}, u32[]{:S(2)}) collective-permute-start(bf16[4,64,16,128]{3,2,1,0:T(8,128)(2,1)} %get-tuple-element.62), channel_id=1, source_target_pairs={{0,1},{1,0},{2,3},{3,2},{4,5},{5,4},{6,7},{7,6},{8,9},{9,8},{10,11... | collective-permute-start | bytes 3145736 | tf_op jit(solution)/shard_map/ppermute | solution.py:589
  39.4 14.0 %collective-permute-start.3 = (bf16[72,1536]{1,0:T(8,128)(2,1)}, bf16[72,1536]{1,0:T(8,128)(2,1)S(1)}, u32[]{:S(2)}, u32[]{:S(2)}) collective-permute-start(bf16[72,1536]{1,0:T(8,128)(2,1)} %get-tuple-element.58), channel_id=1, source_target_pairs={{0,4},{4,8},{8,12},{12,0},{1,5},{5,9},{9,13},{13,1},{2,6},{6,10},{... | collective-permute-start | bytes 663560 | tf_op jit(solution)/shard_map/ppermute | solution.py:671
  39.5 13.9 %collective-permute-start.4 = (bf16[72,1536]{1,0:T(8,128)(2,1)}, bf16[72,1536]{1,0:T(8,128)(2,1)S(1)}, u32[]{:S(2)}, u32[]{:S(2)}) collective-permute-start(bf16[72,1536]{1,0:T(8,128)(2,1)} %get-tuple-element.59), channel_id=1, source_target_pairs={{0,8},{4,12},{8,0},{12,4},{1,9},{5,13},{9,1},{13,5},{2,10},{6,14},... | collective-permute-start | bytes 663560 | tf_op jit(solution)/shard_map/ppermute | solution.py:671
  42.0 12.1 %collective-permute-start.5 = (bf16[72,1536]{1,0:T(8,128)(2,1)}, bf16[72,1536]{1,0:T(8,128)(2,1)S(1)}, u32[]{:S(2)}, u32[]{:S(2)}) collective-permute-start(bf16[72,1536]{1,0:T(8,128)(2,1)} %get-tuple-element.60), channel_id=1, source_target_pairs={{0,12},{4,0},{8,4},{12,8},{1,13},{5,1},{9,5},{13,9},{2,14},{6,2},{... | collective-permute-start | bytes 663560 | tf_op jit(solution)/shard_map/ppermute | solution.py:671
  43.1 10.9 %copy-start.3 = (bf16[4,64,16,128]{3,2,1,0:T(8,128)(2,1)S(1)}, bf16[4,64,16,128]{3,2,1,0:T(8,128)(2,1)}, u32[]{:S(2)}) copy-start(bf16[4,64,16,128]{3,2,1,0:T(8,128)(2,1)} %get-tuple-element.61.keep_hbm) | copy-start | bytes 3145732
  52.3 6.3 %collective-permute-start.10 = (bf16[5,64,16,128]{3,2,1,0:T(8,128)(2,1)}, bf16[5,64,16,128]{3,2,1,0:T(8,128)(2,1)S(1)}, u32[]{:S(2)}, u32[]{:S(2)}) collective-permute-start(bf16[5,64,16,128]{3,2,1,0:T(8,128)(2,1)} %get-tuple-element.72), channel_id=1, source_target_pairs={{0,1},{1,0},{2,3},{3,2},{4,5},{5,4},{6,7},{7,6},{8,9},{9,8},{10,11... | collective-permute-start | bytes 3932168 | tf_op jit(solution)/shard_map/ppermute | solution.py:589
  53.4 1.1 copy-start.5
  53.4 1.1 copy-start.6
  54.0 0.7 copy-start.7
  54.0 4.6 %copy-start.2 = (bf16[5,64,16,128]{3,2,1,0:T(8,128)(2,1)S(1)}, bf16[5,64,16,128]{3,2,1,0:T(8,128)(2,1)}, u32[]{:S(2)}) copy-start(bf16[5,64,16,128]{3,2,1,0:T(8,128)(2,1)} %get-tuple-element.71.keep_hbm) | copy-start | bytes 3932164
  54.7 18.0 %collective-permute-start.7 = (bf16[64,16,128]{2,1,0:T(8,128)(2,1)S(1)}, bf16[64,16,128]{2,1,0:T(8,128)(2,1)S(1)}, u32[]{:S(2)}, u32[]{:S(2)}) collective-permute-start(bf16[64,16,128]{2,1,0:T(8,128)(2,1)S(1)} %get-tuple-element.64), channel_id=1, source_target_pairs={{0,32},{32,64},{64,96},{96,0},{1,33},{33,65},{65,97},{97,1},{2,34}... | collective-permute-start | bytes 786440 | tf_op jit(solution)/shard_map/ppermute | solution.py:687
  54.7 18.1 %collective-permute-start.8 = (bf16[64,16,128]{2,1,0:T(8,128)(2,1)S(1)}, bf16[64,16,128]{2,1,0:T(8,128)(2,1)S(1)}, u32[]{:S(2)}, u32[]{:S(2)}) collective-permute-start(bf16[64,16,128]{2,1,0:T(8,128)(2,1)S(1)} %get-tuple-element.65), channel_id=1, source_target_pairs={{0,64},{32,96},{64,0},{96,32},{1,65},{33,97},{65,1},{97,33},{2,66}... | collective-permute-start | bytes 786440 | tf_op jit(solution)/shard_map/ppermute | solution.py:687
  57.8 15.0 %collective-permute-start.9 = (bf16[64,16,128]{2,1,0:T(8,128)(2,1)S(1)}, bf16[64,16,128]{2,1,0:T(8,128)(2,1)S(1)}, u32[]{:S(2)}, u32[]{:S(2)}) collective-permute-start(bf16[64,16,128]{2,1,0:T(8,128)(2,1)S(1)} %get-tuple-element.66), channel_id=1, source_target_pairs={{0,96},{32,0},{64,32},{96,64},{1,97},{33,1},{65,33},{97,65},{2,98}... | collective-permute-start | bytes 786440 | tf_op jit(solution)/shard_map/ppermute | solution.py:687
  59.2 13.6 %collective-permute-start.11 = (bf16[64,16,256]{2,1,0:T(8,128)(2,1)S(1)}, bf16[64,16,256]{2,1,0:T(8,128)(2,1)S(1)}, u32[]{:S(2)}, u32[]{:S(2)}) collective-permute-start(bf16[64,16,256]{2,1,0:T(8,128)(2,1)S(1)} %get-tuple-element.74), channel_id=1, source_target_pairs={{0,4},{4,0},{8,12},{12,8},{1,5},{5,1},{9,13},{13,9},{2,6},{6,2},{1... | collective-permute-start | bytes 1572872 | tf_op jit(solution)/shard_map/ppermute | solution.py:692
  72.7 3.3 %collective-permute-start.15 = (bf16[64,16,640]{2,1,0:T(8,128)(2,1)}, bf16[64,16,640]{2,1,0:T(8,128)(2,1)S(1)}, u32[]{:S(2)}, u32[]{:S(2)}) collective-permute-start(bf16[64,16,640]{2,1,0:T(8,128)(2,1)} %get-tuple-element.98), channel_id=1, source_target_pairs={{0,1},{1,0},{2,3},{3,2},{4,5},{5,4},{6,7},{7,6},{8,9},{9,8},{10,11... | collective-permute-start | bytes 3932168 | tf_op jit(solution)/shard_map/ppermute | solution.py:589
  72.8 3.2 %copy-start.1 = (bf16[64,16,640]{2,1,0:T(8,128)(2,1)S(1)}, bf16[64,16,640]{2,1,0:T(8,128)(2,1)}, u32[]{:S(2)}) copy-start(bf16[64,16,640]{2,1,0:T(8,128)(2,1)} %get-tuple-element.97.keep_hbm) | copy-start | bytes 3932164
  77.4 1.4 %copy-start = (bf16[64,16,1152]{2,1,0:T(8,128)(2,1)}, bf16[64,16,1152]{2,1,0:T(8,128)(2,1)S(1)}, u32[]{:S(2)}) copy-start(bf16[64,16,1152]{2,1,0:T(8,128)(2,1)S(1)} %shard_map.195) | copy-start | bytes 7077892
  78.8 9.1 %copy-start.4 = (bf16[108,512]{1,0:T(8,128)(2,1)S(1)}, bf16[108,512]{1,0:T(8,128)(2,1)}, u32[]{:S(2)}) copy-start(bf16[108,512]{1,0:T(8,128)(2,1)} %get-tuple-element.96) | copy-start | bytes 331780
  78.8 9.2 %copy-start.12 = (bf16[108,512]{1,0:T(8,128)(2,1)S(1)}, bf16[108,512]{1,0:T(8,128)(2,1)}, u32[]{:S(2)}) copy-start(bf16[108,512]{1,0:T(8,128)(2,1)} %get-tuple-element.93) | copy-start | bytes 331780
  78.8 10.1 %copy-start.10 = (bf16[108,512]{1,0:T(8,128)(2,1)S(1)}, bf16[108,512]{1,0:T(8,128)(2,1)}, u32[]{:S(2)}) copy-start(bf16[108,512]{1,0:T(8,128)(2,1)} %get-tuple-element.94) | copy-start | bytes 331780
  78.8 11.6 %copy-start.8 = (bf16[108,512]{1,0:T(8,128)(2,1)S(1)}, bf16[108,512]{1,0:T(8,128)(2,1)}, u32[]{:S(2)}) copy-start(bf16[108,512]{1,0:T(8,128)(2,1)} %get-tuple-element.95) | copy-start | bytes 331780
  78.8 48.4 %all-to-all-start = ((bf16[64,16,1152]{2,1,0:T(8,128)(2,1)}), bf16[64,16,1152]{2,1,0:T(8,128)(2,1)S(1)}, u32[]{:S(2)}, u32[]{:S(2)}) async-start(bf16[64,16,1152]{2,1,0:T(8,128)(2,1)} %copy-done), calls=%async_computation | async-start | bytes 4718592 | tf_op jit(solution)/shard_map/all_to_all | solution.py:722
  88.0 35.7 %collective-permute-start.12 = (bf16[108,512]{1,0:T(8,128)(2,1)S(1)}, bf16[108,512]{1,0:T(8,128)(2,1)S(1)}, u32[]{:S(2)}, u32[]{:S(2)}) collective-permute-start(bf16[108,512]{1,0:T(8,128)(2,1)S(1)} %copy-done.12), channel_id=1, source_target_pairs={{0,17},{1,18},{2,19},{3,20},{4,21},{5,22},{6,23},{7,24},{8,25},{9,... | collective-permute-start | bytes 331784 | tf_op jit(solution)/shard_map/ppermute | solution.py:601
  88.9 36.1 %collective-permute-start.13 = (bf16[108,512]{1,0:T(8,128)(2,1)S(1)}, bf16[108,512]{1,0:T(8,128)(2,1)S(1)}, u32[]{:S(2)}, u32[]{:S(2)}) collective-permute-start(bf16[108,512]{1,0:T(8,128)(2,1)S(1)} %copy-done.10), channel_id=1, source_target_pairs={{0,16},{1,17},{2,18},{3,19},{4,20},{5,21},{6,22},{7,23},{8,24},{9,... | collective-permute-start | bytes 331784 | tf_op jit(solution)/shard_map/ppermute | solution.py:601
  90.4 34.6 %collective-permute-start.14 = (bf16[108,512]{1,0:T(8,128)(2,1)S(1)}, bf16[108,512]{1,0:T(8,128)(2,1)S(1)}, u32[]{:S(2)}, u32[]{:S(2)}) collective-permute-start(bf16[108,512]{1,0:T(8,128)(2,1)S(1)} %copy-done.8), channel_id=1, source_target_pairs={{0,1},{1,2},{2,3},{3,4},{4,5},{5,6},{6,7},{7,8},{8,9},{9,10},{10,1... | collective-permute-start | bytes 331784 | tf_op jit(solution)/shard_map/ppermute | solution.py:601

commit v16 on v14

--- a/solution.py
+++ b/solution.py
@@ -614,12 +614,10 @@
         for corner, cot in zip(quadrants(tokens), quadrants(cotangent))
     ]
     upper_left, upper_right, lower_left, lower_right = corners
-    return [
-        lower_right,
-        shifted_block(lower_left, 0, -1),
-        shifted_block(upper_right, -1, 0),
-        shifted_block(upper_left, -1, -1),
-    ]
+    from_both = shifted_block(upper_left, -1, -1)
+    from_below = shifted_block(upper_right, -1, 0)
+    from_right = shifted_block(lower_left, 0, -1)
+    return [lower_right, from_right, from_below, from_both]
 
 
 def send_forth(corners):

time: 125 us -> 125 us (level)
  no operation moved by 1% of the time
where the time goes in v16:
time: 125 us
  Pallas kernels  48.5 us (39%)
  waiting for transfers between devices  38.8 us (31%)
  starting transfers between devices  28.5 us (23%)
  local copies, waits for them, and re-layouts  5.19 us (4%)
  other arithmetic  2.74 us (2%)
  between operations  1.26 us (1%)
    pallas_call x8, Pallas kernels, call(): pl.pallas_call(kernel, out_shape=[jax.ShapeDtypeStruct(shape, kind) for s...  48.5 us
    all_to_all x1, waiting for transfers between devices, body(): landed = lax.all_to_all(blocks, PAIRS, 0, 0, tiled=True)  28.5 us
    ppermute x6, starting transfers between devices, shifted_block(): return lax.ppermute(block, GRID, route)  13 us
    ppermute x6, waiting for transfers between devices, shifted_block(): return lax.ppermute(block, GRID, route)  8.72 us
    all_to_all x1, starting transfers between devices, body(): landed = lax.all_to_all(blocks, PAIRS, 0, 0, tiled=True)  6.94 us
    ppermute x3, starting transfers between devices, body(): lax.ppermute(block, 'z', [(i, (i + step) % 4) for i in range(4)])  3.87 us
    ppermute x3, starting transfers between devices, body(): lax.ppermute(block, 'y', [(i, (i + step) % 4) for i in range(4)])  3.73 us
    unnamed x28, local copies, waits for them, and re-layouts  2.51 us
  transfers between devices with their start and end apart: 17, of which 8 were waited for; matrix products, arithmetic and copies ran while one was open for 3% of the time, Pallas kernels for 20%

profile of v16, /device:TPU:0, one launch (start us, length us, event | category | flops | bytes accessed | tf_op | source)
XLA Modules:
  0.0 125.1 jit_solution(6615713838509142570)
XLA Ops:
  0.6 0.9 fusion.1
  1.6 1.2 fusion
  2.9 5.1 %collective-permute-start = (bf16[108,512]{1,0:T(8,128)(2,1)S(1)}, bf16[108,512]{1,0:T(8,128)(2,1)S(1)}, u32[]{:S(2)}, u32[]{:S(2)}) collective-permute-start(bf16[108,512]{1,0:T(8,128)(2,1)S(1)} %pad_maximum_fusion.1), channel_id=1, source_target_pairs={{0,15},{1,0},{2,1},{3,2},{4,3},{5,4},{6,5},{7,6},{8,7},{9,8},{10,9... | collective-permute-start | bytes 331784 | tf_op jit(solution)/shard_map/ppermute | solution.py:601
  8.0 4.1 %collective-permute-start.1 = (bf16[108,512]{1,0:T(8,128)(2,1)S(1)}, bf16[108,512]{1,0:T(8,128)(2,1)S(1)}, u32[]{:S(2)}, u32[]{:S(2)}) collective-permute-start(bf16[108,512]{1,0:T(8,128)(2,1)S(1)} %pad_maximum_fusion.2), channel_id=1, source_target_pairs={{0,112},{1,113},{2,114},{3,115},{4,116},{5,117},{6,118},{7,119},{8... | collective-permute-start | bytes 331784 | tf_op jit(solution)/shard_map/ppermute | solution.py:601
  12.3 0.4 collective-permute-start.2
  12.8 0.7 pad_maximum_fusion.quad0_hbm
  13.5 1.2 collective-permute-done.1.quad2_hbm
  14.7 1.9 %collective-permute-done.2.quad3_hbm = bf16[108,512]{1,0:T(8,128)(2,1)S(1)} collective-permute-done((bf16[108,512]{1,0:T(8,128)(2,1)S(1)}, bf16[108,512]{1,0:T(8,128)(2,1)S(1)}, u32[]{:S(2)}, u32[]{:S(2)}) %collective-permute-start.2) | collective-permute-done | bytes 110624 | tf_op jit(solution)/shard_map/ppermute | solution.py:601
  16.6 0.6 copy-done.10
  17.2 21.9 %shard_map.189 = (bf16[72,1024]{1,0:T(8,128)(2,1)}, bf16[288,512]{1,0:T(8,128)(2,1)}, bf16[72,1536]{1,0:T(8,128)(2,1)}, bf16[72,1536]{1,0:T(8,128)(2,1)}, bf16[7...) custom-call(s32[1]{0:T(128)} %bitcast.where_ref, ...), custom_call_target="tpu_custom_call" | custom-call | flops 20000000000 | bytes 20000000 | tf_op jit(solution)/shard_map/pallas_call | solution.py:563
  39.5 2.5 %collective-permute-start.4 = (bf16[72,1536]{1,0:T(8,128)(2,1)}, bf16[72,1536]{1,0:T(8,128)(2,1)S(1)}, u32[]{:S(2)}, u32[]{:S(2)}) collective-permute-start(bf16[72,1536]{1,0:T(8,128)(2,1)} %get-tuple-element.69), channel_id=1, source_target_pairs={{0,8},{4,12},{8,0},{12,4},{1,9},{5,13},{9,1},{13,5},{2,10},{6,14},... | collective-permute-start | bytes 663560 | tf_op jit(solution)/shard_map/ppermute | solution.py:669
  42.0 1.2 collective-permute-start.5
  43.1 9.1 %shard_map.190 = (bf16[288,512]{1,0:T(8,128)(2,1)}, bf16[5,64,16,128]{3,2,1,0:T(8,128)(2,1)}, bf16[5,64,16,128]{3,2,1,0:T(8,128)(2,1)}) custom-call(s32[1]{0:T(128)} %bitcast.where_ref, bf16[288,512]{1,0:T(8,128)(2,1)} %get-tuple-element.61.grad_after_ref, bf16[288,512]{1,0:T(8,128)(2,1)} %get-tuple-element.62.middle_ref, ...), custom_call_target="tpu_custom_call" | custom-call | flops 7000000000 | bytes 7000000 | tf_op jit(solution)/shard_map/pallas_call | solution.py:563
  52.4 1.0 collective-permute-done.3.near1_hbm
  53.4 0.6 collective-permute-done.5.near3_hbm
  54.0 0.5 shard_map.191
  54.7 3.1 %collective-permute-start.10 = (bf16[64,16,128]{2,1,0:T(8,128)(2,1)S(1)}, bf16[64,16,128]{2,1,0:T(8,128)(2,1)S(1)}, u32[]{:S(2)}, u32[]{:S(2)}) collective-permute-start(bf16[64,16,128]{2,1,0:T(8,128)(2,1)S(1)} %get-tuple-element.92), channel_id=1, source_target_pairs={{0,64},{32,96},{64,0},{96,32},{1,65},{33,97},{65,1},{97,33},{2,66}... | collective-permute-start | bytes 786440 | tf_op jit(solution)/shard_map/ppermute | solution.py:685
  57.8 0.8 collective-permute-start.11
  58.6 0.6 shard_map.192
  59.2 0.5 collective-permute-start.12
  59.8 12.9 %shard_map.193 = (bf16[108,512]{1,0:T(8,128)(2,1)}, bf16[108,512]{1,0:T(8,128)(2,1)}, bf16[108,512]{1,0:T(8,128)(2,1)}, bf16[108,512]{1,0:T(8,128)(2,1)}, bf16[6...) custom-call(s32[1]{0:T(128)} %bitcast.where_ref, bf16[288,512]{1,0:T(8,128)(2,1)} %get-tuple-element.77.middle_grad_ref, ...), custom_call_target="tpu_custom_call" | custom-call | flops 12000000000 | bytes 12000000 | tf_op jit(solution)/shard_map/pallas_call | solution.py:563
  72.9 0.6 shard_map.194.refs_0_
  73.7 3.2 %collective-permute-start.13 = (bf16[108,512]{1,0:T(8,128)(2,1)S(1)}, bf16[108,512]{1,0:T(8,128)(2,1)S(1)}, u32[]{:S(2)}, u32[]{:S(2)}) collective-permute-start(bf16[108,512]{1,0:T(8,128)(2,1)S(1)} %copy-done.13), channel_id=1, source_target_pairs={{0,17},{1,18},{2,19},{3,20},{4,21},{5,22},{6,23},{7,24},{8,25},{9,... | collective-permute-start | bytes 331784 | tf_op jit(solution)/shard_map/ppermute | solution.py:601
  77.1 1.4 %shard_map.195 = bf16[64,16,1152]{2,1,0:T(8,128)(2,1)S(1)} custom-call(bf16[64,16,640]{2,1,0:T(8,128)(2,1)S(1)} %copy-done.1, bf16[64,16,640]{2,1,0:T(8,128)(2,1)S(1)} %collective-permute-done.8.arrived_hbm, bf16[64,16,1152]{2,1,0:T(8,128)(2,1)S(1)} %shard_map.194.refs_0_), custom_call_target="tpu_custom_call", output_to_operand_aliasing={{}: (2, {})} | custom-call | flops 2000000000 | bytes 2000000 | tf_op jit(solution)/shard_map/pallas_call | solution.py:563
  78.5 1.4 %copy-done = bf16[64,16,1152]{2,1,0:T(8,128)(2,1)} copy-done((bf16[64,16,1152]{2,1,0:T(8,128)(2,1)}, bf16[64,16,1152]{2,1,0:T(8,128)(2,1)S(1)}, u32[]{:S(2)}) %copy-start) | copy-done | bytes 2359320
  79.9 4.5 %collective-permute-done.13 = bf16[108,512]{1,0:T(8,128)(2,1)S(1)} collective-permute-done((bf16[108,512]{1,0:T(8,128)(2,1)S(1)}, bf16[108,512]{1,0:T(8,128)(2,1)S(1)}, u32[]{:S(2)}, u32[]{:S(2)}) %collective-permute-start.13) | collective-permute-done | bytes 110624 | tf_op jit(solution)/shard_map/ppermute | solution.py:601
  84.4 0.8 collective-permute-done.14
  85.5 6.9 %all-to-all-start = ((bf16[64,16,1152]{2,1,0:T(8,128)(2,1)}), bf16[64,16,1152]{2,1,0:T(8,128)(2,1)S(1)}, u32[]{:S(2)}, u32[]{:S(2)}) async-start(bf16[64,16,1152]{2,1,0:T(8,128)(2,1)} %copy-done), calls=%async_computation | async-start | bytes 4718592 | tf_op jit(solution)/shard_map/all_to_all | solution.py:721
  92.9 0.9 maximum_bitcast_fusion.1
  93.8 1.1 maximum_bitcast_fusion
  95.0 28.5 %all-to-all-done.landed_hbm = bf16[64,16,1152]{2,1,0:T(8,128)(2,1)S(1)} async-done(((bf16[64,16,1152]{2,1,0:T(8,128)(2,1)}), bf16[64,16,1152]{2,1,0:T(8,128)(2,1)S(1)}, u32[]{:S(2)}, u32[]{:S(2)}) %all-to-all-start) | async-done | bytes 2359328 | tf_op jit(solution)/shard_map/all_to_all | solution.py:721
  123.4 1.5 %shard_map.196 = (f32[4,1536]{1,0:T(4,128)}, f32[4,512]{1,0:T(4,128)}, f32[4,2048]{1,0:T(4,128)}, f32[16,512]{1,0:T(8,128)}, f32[16,1024]{1,0:T(8,128)}) custom-call(bf16[64,16,1152]{2,1,0:T(8,128)(2,1)S(1)} %all-to-all-done.landed_hbm), custom_call_target="tpu_custom_call" | custom-call | flops 3000000000 | bytes 3000000 | tf_op jit(solution)/shard_map/pallas_call | solution.py:563
  (76 shorter events, 2.1 us)
Async XLA Ops:
  2.9 10.6 %collective-permute-start = (bf16[108,512]{1,0:T(8,128)(2,1)S(1)}, bf16[108,512]{1,0:T(8,128)(2,1)S(1)}, u32[]{:S(2)}, u32[]{:S(2)}) collective-permute-start(bf16[108,512]{1,0:T(8,128)(2,1)S(1)} %pad_maximum_fusion.1), channel_id=1, source_target_pairs={{0,15},{1,0},{2,1},{3,2},{4,3},{5,4},{6,5},{7,6},{8,7},{9,8},{10,9... | collective-permute-start | bytes 331784 | tf_op jit(solution)/shard_map/ppermute | solution.py:601
  8.0 6.6 %collective-permute-start.1 = (bf16[108,512]{1,0:T(8,128)(2,1)S(1)}, bf16[108,512]{1,0:T(8,128)(2,1)S(1)}, u32[]{:S(2)}, u32[]{:S(2)}) collective-permute-start(bf16[108,512]{1,0:T(8,128)(2,1)S(1)} %pad_maximum_fusion.2), channel_id=1, source_target_pairs={{0,112},{1,113},{2,114},{3,115},{4,116},{5,117},{6,118},{7,119},{8... | collective-permute-start | bytes 331784 | tf_op jit(solution)/shard_map/ppermute | solution.py:601
  12.3 4.3 %collective-permute-start.2 = (bf16[108,512]{1,0:T(8,128)(2,1)S(1)}, bf16[108,512]{1,0:T(8,128)(2,1)S(1)}, u32[]{:S(2)}, u32[]{:S(2)}) collective-permute-start(bf16[108,512]{1,0:T(8,128)(2,1)S(1)} %pad_maximum_fusion.3), channel_id=1, source_target_pairs={{0,127},{1,112},{2,113},{3,114},{4,115},{5,116},{6,117},{7,118},{8... | collective-permute-start | bytes 331784 | tf_op jit(solution)/shard_map/ppermute | solution.py:601
  13.5 3.1 %copy-start.8 = (bf16[108,512]{1,0:T(8,128)(2,1)}, bf16[108,512]{1,0:T(8,128)(2,1)S(1)}, u32[]{:S(2)}) copy-start(bf16[108,512]{1,0:T(8,128)(2,1)S(1)} %collective-permute-done.quad1_hbm) | copy-start | bytes 331780
  14.7 1.9 %copy-start.9 = (bf16[108,512]{1,0:T(8,128)(2,1)}, bf16[108,512]{1,0:T(8,128)(2,1)S(1)}, u32[]{:S(2)}) copy-start(bf16[108,512]{1,0:T(8,128)(2,1)S(1)} %collective-permute-done.1.quad2_hbm) | copy-start | bytes 331780
  16.6 0.6 copy-start.10
  39.1 14.9 %collective-permute-start.6 = (bf16[4,64,16,128]{3,2,1,0:T(8,128)(2,1)}, bf16[4,64,16,128]{3,2,1,0:T(8,128)(2,1)S(1)}, u32[]{:S(2)}, u32[]{:S(2)}) collective-permute-start(bf16[4,64,16,128]{3,2,1,0:T(8,128)(2,1)} %get-tuple-element.72), channel_id=1, source_target_pairs={{0,1},{1,0},{2,3},{3,2},{4,5},{5,4},{6,7},{7,6},{8,9},{9,8},{10,11... | collective-permute-start | bytes 3145736 | tf_op jit(solution)/shard_map/ppermute | solution.py:589
  39.4 14.0 %collective-permute-start.3 = (bf16[72,1536]{1,0:T(8,128)(2,1)}, bf16[72,1536]{1,0:T(8,128)(2,1)S(1)}, u32[]{:S(2)}, u32[]{:S(2)}) collective-permute-start(bf16[72,1536]{1,0:T(8,128)(2,1)} %get-tuple-element.68), channel_id=1, source_target_pairs={{0,4},{4,8},{8,12},{12,0},{1,5},{5,9},{9,13},{13,1},{2,6},{6,10},{... | collective-permute-start | bytes 663560 | tf_op jit(solution)/shard_map/ppermute | solution.py:669
  39.5 13.9 %collective-permute-start.4 = (bf16[72,1536]{1,0:T(8,128)(2,1)}, bf16[72,1536]{1,0:T(8,128)(2,1)S(1)}, u32[]{:S(2)}, u32[]{:S(2)}) collective-permute-start(bf16[72,1536]{1,0:T(8,128)(2,1)} %get-tuple-element.69), channel_id=1, source_target_pairs={{0,8},{4,12},{8,0},{12,4},{1,9},{5,13},{9,1},{13,5},{2,10},{6,14},... | collective-permute-start | bytes 663560 | tf_op jit(solution)/shard_map/ppermute | solution.py:669
  42.0 12.1 %collective-permute-start.5 = (bf16[72,1536]{1,0:T(8,128)(2,1)}, bf16[72,1536]{1,0:T(8,128)(2,1)S(1)}, u32[]{:S(2)}, u32[]{:S(2)}) collective-permute-start(bf16[72,1536]{1,0:T(8,128)(2,1)} %get-tuple-element.70), channel_id=1, source_target_pairs={{0,12},{4,0},{8,4},{12,8},{1,13},{5,1},{9,5},{13,9},{2,14},{6,2},{... | collective-permute-start | bytes 663560 | tf_op jit(solution)/shard_map/ppermute | solution.py:669
  43.1 10.9 %copy-start.3 = (bf16[4,64,16,128]{3,2,1,0:T(8,128)(2,1)S(1)}, bf16[4,64,16,128]{3,2,1,0:T(8,128)(2,1)}, u32[]{:S(2)}) copy-start(bf16[4,64,16,128]{3,2,1,0:T(8,128)(2,1)} %get-tuple-element.71.keep_hbm) | copy-start | bytes 3145732
  52.3 6.3 %collective-permute-start.7 = (bf16[5,64,16,128]{3,2,1,0:T(8,128)(2,1)}, bf16[5,64,16,128]{3,2,1,0:T(8,128)(2,1)S(1)}, u32[]{:S(2)}, u32[]{:S(2)}) collective-permute-start(bf16[5,64,16,128]{3,2,1,0:T(8,128)(2,1)} %get-tuple-element.75), channel_id=1, source_target_pairs={{0,1},{1,0},{2,3},{3,2},{4,5},{5,4},{6,7},{7,6},{8,9},{9,8},{10,11... | collective-permute-start | bytes 3932168 | tf_op jit(solution)/shard_map/ppermute | solution.py:589
  53.4 1.1 copy-start.5
  53.4 1.1 copy-start.6
  54.0 0.7 copy-start.7
  54.0 4.6 %copy-start.2 = (bf16[5,64,16,128]{3,2,1,0:T(8,128)(2,1)S(1)}, bf16[5,64,16,128]{3,2,1,0:T(8,128)(2,1)}, u32[]{:S(2)}) copy-start(bf16[5,64,16,128]{3,2,1,0:T(8,128)(2,1)} %get-tuple-element.74.keep_hbm) | copy-start | bytes 3932164
  54.7 18.1 %collective-permute-start.9 = (bf16[64,16,128]{2,1,0:T(8,128)(2,1)S(1)}, bf16[64,16,128]{2,1,0:T(8,128)(2,1)S(1)}, u32[]{:S(2)}, u32[]{:S(2)}) collective-permute-start(bf16[64,16,128]{2,1,0:T(8,128)(2,1)S(1)} %get-tuple-element.91), channel_id=1, source_target_pairs={{0,32},{32,64},{64,96},{96,0},{1,33},{33,65},{65,97},{97,1},{2,34}... | collective-permute-start | bytes 786440 | tf_op jit(solution)/shard_map/ppermute | solution.py:685
  54.7 18.1 %collective-permute-start.10 = (bf16[64,16,128]{2,1,0:T(8,128)(2,1)S(1)}, bf16[64,16,128]{2,1,0:T(8,128)(2,1)S(1)}, u32[]{:S(2)}, u32[]{:S(2)}) collective-permute-start(bf16[64,16,128]{2,1,0:T(8,128)(2,1)S(1)} %get-tuple-element.92), channel_id=1, source_target_pairs={{0,64},{32,96},{64,0},{96,32},{1,65},{33,97},{65,1},{97,33},{2,66}... | collective-permute-start | bytes 786440 | tf_op jit(solution)/shard_map/ppermute | solution.py:685
  57.8 15.0 %collective-permute-start.11 = (bf16[64,16,128]{2,1,0:T(8,128)(2,1)S(1)}, bf16[64,16,128]{2,1,0:T(8,128)(2,1)S(1)}, u32[]{:S(2)}, u32[]{:S(2)}) collective-permute-start(bf16[64,16,128]{2,1,0:T(8,128)(2,1)S(1)} %get-tuple-element.93), channel_id=1, source_target_pairs={{0,96},{32,0},{64,32},{96,64},{1,97},{33,1},{65,33},{97,65},{2,98}... | collective-permute-start | bytes 786440 | tf_op jit(solution)/shard_map/ppermute | solution.py:685
  59.2 13.6 %collective-permute-start.12 = (bf16[64,16,256]{2,1,0:T(8,128)(2,1)S(1)}, bf16[64,16,256]{2,1,0:T(8,128)(2,1)S(1)}, u32[]{:S(2)}, u32[]{:S(2)}) collective-permute-start(bf16[64,16,256]{2,1,0:T(8,128)(2,1)S(1)} %get-tuple-element.94), channel_id=1, source_target_pairs={{0,4},{4,0},{8,12},{12,8},{1,5},{5,1},{9,13},{13,9},{2,6},{6,2},{1... | collective-permute-start | bytes 1572872 | tf_op jit(solution)/shard_map/ppermute | solution.py:690
  72.7 4.4 %collective-permute-start.8 = (bf16[64,16,640]{2,1,0:T(8,128)(2,1)}, bf16[64,16,640]{2,1,0:T(8,128)(2,1)S(1)}, u32[]{:S(2)}, u32[]{:S(2)}) collective-permute-start(bf16[64,16,640]{2,1,0:T(8,128)(2,1)} %get-tuple-element.90), channel_id=1, source_target_pairs={{0,1},{1,0},{2,3},{3,2},{4,5},{5,4},{6,7},{7,6},{8,9},{9,8},{10,11... | collective-permute-start | bytes 3932168 | tf_op jit(solution)/shard_map/ppermute | solution.py:589
  72.8 0.9 copy-start.13
  72.8 4.1 %copy-start.12 = (bf16[108,512]{1,0:T(8,128)(2,1)S(1)}, bf16[108,512]{1,0:T(8,128)(2,1)}, u32[]{:S(2)}) copy-start(bf16[108,512]{1,0:T(8,128)(2,1)} %get-tuple-element.102) | copy-start | bytes 331780
  72.8 4.1 %copy-start.11 = (bf16[108,512]{1,0:T(8,128)(2,1)S(1)}, bf16[108,512]{1,0:T(8,128)(2,1)}, u32[]{:S(2)}) copy-start(bf16[108,512]{1,0:T(8,128)(2,1)} %get-tuple-element.103) | copy-start | bytes 331780
  72.8 4.2 %copy-start.1 = (bf16[64,16,640]{2,1,0:T(8,128)(2,1)S(1)}, bf16[64,16,640]{2,1,0:T(8,128)(2,1)}, u32[]{:S(2)}) copy-start(bf16[64,16,640]{2,1,0:T(8,128)(2,1)} %get-tuple-element.89.keep_hbm) | copy-start | bytes 3932164
  73.7 10.7 %collective-permute-start.13 = (bf16[108,512]{1,0:T(8,128)(2,1)S(1)}, bf16[108,512]{1,0:T(8,128)(2,1)S(1)}, u32[]{:S(2)}, u32[]{:S(2)}) collective-permute-start(bf16[108,512]{1,0:T(8,128)(2,1)S(1)} %copy-done.13), channel_id=1, source_target_pairs={{0,17},{1,18},{2,19},{3,20},{4,21},{5,22},{6,23},{7,24},{8,25},{9,... | collective-permute-start | bytes 331784 | tf_op jit(solution)/shard_map/ppermute | solution.py:601
  76.9 8.3 %collective-permute-start.14 = (bf16[108,512]{1,0:T(8,128)(2,1)S(1)}, bf16[108,512]{1,0:T(8,128)(2,1)S(1)}, u32[]{:S(2)}, u32[]{:S(2)}) collective-permute-start(bf16[108,512]{1,0:T(8,128)(2,1)S(1)} %copy-done.12), channel_id=1, source_target_pairs={{0,16},{1,17},{2,18},{3,19},{4,20},{5,21},{6,22},{7,23},{8,24},{9,... | collective-permute-start | bytes 331784 | tf_op jit(solution)/shard_map/ppermute | solution.py:601
  76.9 8.6 %collective-permute-start.15 = (bf16[108,512]{1,0:T(8,128)(2,1)S(1)}, bf16[108,512]{1,0:T(8,128)(2,1)S(1)}, u32[]{:S(2)}, u32[]{:S(2)}) collective-permute-start(bf16[108,512]{1,0:T(8,128)(2,1)S(1)} %copy-done.11), channel_id=1, source_target_pairs={{0,1},{1,2},{2,3},{3,4},{4,5},{5,6},{6,7},{7,8},{8,9},{9,10},{10,1... | collective-permute-start | bytes 331784 | tf_op jit(solution)/shard_map/ppermute | solution.py:601
  78.5 1.4 %copy-start = (bf16[64,16,1152]{2,1,0:T(8,128)(2,1)}, bf16[64,16,1152]{2,1,0:T(8,128)(2,1)S(1)}, u32[]{:S(2)}) copy-start(bf16[64,16,1152]{2,1,0:T(8,128)(2,1)S(1)} %shard_map.195) | copy-start | bytes 7077892
  79.9 12.8 %copy-start.4 = (bf16[108,512]{1,0:T(8,128)(2,1)S(1)}, bf16[108,512]{1,0:T(8,128)(2,1)}, u32[]{:S(2)}) copy-start(bf16[108,512]{1,0:T(8,128)(2,1)} %get-tuple-element.108) | copy-start | bytes 331780
  85.5 37.9 %all-to-all-start = ((bf16[64,16,1152]{2,1,0:T(8,128)(2,1)}), bf16[64,16,1152]{2,1,0:T(8,128)(2,1)S(1)}, u32[]{:S(2)}, u32[]{:S(2)}) async-start(bf16[64,16,1152]{2,1,0:T(8,128)(2,1)} %copy-done), calls=%async_computation | async-start | bytes 4718592 | tf_op jit(solution)/shard_map/all_to_all | solution.py:721
